TPU v7x, 32 devices: a whole 2x2x4 slice. The times are simulated.
32 devices in a mesh: batch: 8 (over z, y), seq: 4 (over x, core).
Axes of the slice: x: 2, y: 2, z: 4, core: 2. Of those that a mesh axis runs over, the one named last changes fastest.
Arguments:
- tokens: bfloat16 [4, 8, 1024, 512], P(None, 'batch', 'seq'), may hold values from -6 to 6
- first_length: int32 [4, 8], P(None, 'batch'), may hold values from 512 to 1024, as said below
- cotangent: bfloat16 [4, 8, 1024, 512], P(None, 'batch', 'seq'), may hold values from -6 to 6
- positions: bfloat16 [1024, 512], P(None, ('batch', 'seq')), may hold values from -3 to 3
- inward: bfloat16 [512, 1536], P(('batch', 'seq')), may hold values from -0.25 to 0.25
- intake: bfloat16 [1024], P(('batch', 'seq')), may hold values from -3 to 3
- outward: bfloat16 [512, 512], P(('batch', 'seq')), may hold values from -2 to 2
- outlet: bfloat16 [512], P(('batch', 'seq')), may hold values from -2 to 2
- steady: bfloat16 [512], P(('batch', 'seq')), may hold values from 0.5 to 1.5
- offset: bfloat16 [512], P(('batch', 'seq')), may hold values from -2 to 2
- expand: bfloat16 [512, 2048], P(('batch', 'seq')), may hold values from -0.25 to 0.25
- spread: bfloat16 [2048], P(('batch', 'seq')), may hold values from -2 to 2
- contract: bfloat16 [2048, 512], P(('batch', 'seq')), may hold values from -0.125 to 0.125
- settle: bfloat16 [512], P(('batch', 'seq')), may hold values from -2 to 2
- temper: bfloat16 [512], P(('batch', 'seq')), may hold values from 0.5 to 1.5
- anchor: bfloat16 [512], P(('batch', 'seq')), may hold values from -2 to 2
Outputs:
- layer_output: bfloat16 [4, 8, 1024, 512], P(None, 'batch', 'seq')
- tokens_grad: bfloat16 [4, 8, 1024, 512], P(None, 'batch', 'seq')
- positions_grad: float32 [1024, 512], P(None, ('batch', 'seq'))
- inward_grad: float32 [512, 1536], P(('batch', 'seq'))
- intake_grad: float32 [1024], P(('batch', 'seq'))
- outward_grad: float32 [512, 512], P(('batch', 'seq'))
- outlet_grad: float32 [512], P(('batch', 'seq'))
- steady_grad: float32 [512], P(('batch', 'seq'))
- offset_grad: float32 [512], P(('batch', 'seq'))
- expand_grad: float32 [512, 2048], P(('batch', 'seq'))
- spread_grad: float32 [2048], P(('batch', 'seq'))
- contract_grad: float32 [2048, 512], P(('batch', 'seq'))
- settle_grad: float32 [512], P(('batch', 'seq'))
- temper_grad: float32 [512], P(('batch', 'seq'))
- anchor_grad: float32 [512], P(('batch', 'seq'))
Inputs may be any that keep to these rules, and one draw needn't show every extreme that they name: `first_length`: each entry is 1024 // 2 (a pack of two documents of equal length) or 1024 (a pack of one document); among the packs of one index of batch over all micro-batches, both kinds occur.
All inputs are finite; a program needn't handle non-finite values.
Results may differ from a plain program's by a relative error of at most 0.015.
The roundings to bfloat16 on the way count: a program that leaves them out, or rounds other values in their place, can miss the bound.
Values may be sent and summed in bfloat16 or wider, within the bound.
No kernel may reach another device: no remote copies, remote signals or barrier semaphores. Data moves between devices by JAX's collectives and lax.ppermute only.
A program may use at most 128 MiB of HBM per device.

v0:
```python
import functools

import jax
import jax.numpy as jnp
from jax import lax
from jax.experimental import pallas as pl
from jax.experimental.pallas import tpu as pltpu
from jax.sharding import PartitionSpec as P

AXES = ("batch", "seq")
LANE = 128
TILE = 16
STEP = 256
FAR = 1e30
BEND = 0.7978845608028654
BF = jnp.bfloat16
F32 = jnp.float32
VECTORS = 8


def times(left, right):
    return jnp.dot(left, right, preferred_element_type=F32)


def times_t(left, right):
    return lax.dot_general(left, right, (((1,), (1,)), ((), ())), preferred_element_type=F32)


def t_times(left, right):
    return lax.dot_general(left, right, (((0,), (0,)), ((), ())), preferred_element_type=F32)


def column_sum(values):
    return jnp.sum(values.astype(F32), axis=0, keepdims=True)


def aligned(index, size):
    return pl.ds(pl.multiple_of(index * size, size), size)


def like(shape, kind):
    return jax.ShapeDtypeStruct(shape, kind)


def full(shape):
    return pl.BlockSpec(shape, lambda *_: (0,) * len(shape))


def params(megabytes):
    return pltpu.CompilerParams(vmem_limit_bytes=megabytes * 2**20)


def cost(flops, size, exps=0):
    return pl.CostEstimate(flops=flops, bytes_accessed=size, transcendentals=exps)


class Plan:
    def __init__(self, devices, width, hidden, total_rows):
        self.devices = devices
        self.width = width
        self.hidden = hidden
        self.total_rows = total_rows
        self.own_rows = width // devices
        self.packed = devices == 32 and self.own_rows % TILE == 0
        self.lanes = width // LANE
        self.parts = hidden // width
        self.table_pieces = total_rows // LANE
        self.early_pieces = self.table_pieces + 3 * self.lanes
        self.early_rows = (self.early_pieces + 1) * TILE
        self.late_rows = (self.lanes + hidden // LANE) * TILE + self.lanes * (hidden // devices)
        lengths = [2 * width, width, width, width, hidden, width, width, width]
        self.lengths = lengths
        self.owned = [n // devices for n in lengths]
        self.small_rows = 16
        starts = [0]
        for n in lengths:
            starts.append(starts[-1] + n // LANE)
        self.block_starts = starts

    def place(self, mask):
        return ((mask >> 1) & 3) * 4 + ((mask >> 3) & 3)


def fill_early(plan, me, halves, table_ref, inward_ref, small_ref, stage_ref):
    for mask in range(plan.devices):
        shard = halves[mask & 1].at[plan.place(mask)]
        owner = me ^ mask
        rows = aligned(owner, TILE)
        for piece in range(plan.table_pieces):
            table_ref[piece, rows, :] = shard[piece * TILE : (piece + 1) * TILE, :]
        for piece in range(3 * plan.lanes):
            at = plan.table_pieces + piece
            inward_ref[piece, rows, :] = shard[at * TILE : (at + 1) * TILE, :]
        at = plan.early_pieces * TILE
        stage_ref[pl.ds(owner, 1), :, :] = shard[at : at + TILE, :].astype(F32)[None]
    for vector, length in enumerate(plan.lengths):
        group = LANE // plan.owned[vector]
        for block in range(length // LANE):
            row = jnp.sum(stage_ref[block * group : (block + 1) * group, vector, :], axis=0, keepdims=True)
            at = plan.block_starts[vector] + block
            small_ref[at // plan.lanes : at // plan.lanes + 1, (at % plan.lanes) * LANE : (at % plan.lanes + 1) * LANE] = row


def own_lanes(value, head):
    lane = lax.broadcasted_iota(jnp.int32, value.shape, 1)
    return jnp.where((lane // (LANE // 2)) == head, value, jnp.zeros_like(value))


def causal():
    return lax.broadcasted_iota(jnp.int32, (STEP, STEP), 0) <= lax.broadcasted_iota(
        jnp.int32, (STEP, STEP), 1
    )


def attend_kernel(plan, count, info_ref, *refs):
    pieces, refs = refs[:count], refs[count:]
    if plan.packed:
        halves, refs = refs[:2], refs[2:]
    else:
        table_in, inward_in, small_in = refs[:3]
        refs = refs[3:]
    (lifted_ref, query_ref, key_ref, value_ref, mixed_ref, total_ref, inward_ref, small_ref) = refs[:8]
    low_ref, table_ref, place_ref, stage_ref = refs[8:]
    pair = pl.program_id(0)
    total_rows, width = plan.total_rows, plan.width
    half = total_rows // 2
    split = info_ref[0] < total_rows
    far = jnp.where(split, FAR, 0.0)

    @pl.when(pair == 0)
    def _():
        if plan.packed:
            fill_early(plan, info_ref[1], halves, table_ref, inward_ref, small_ref, stage_ref)
        else:
            table_ref[...] = table_in[...]
            inward_ref[...] = inward_in[...]
            small_ref[...] = small_in[...]
        eye = (
            lax.broadcasted_iota(jnp.int32, (half, half), 0)
            == lax.broadcasted_iota(jnp.int32, (half, half), 1)
        ).astype(BF)
        per_half = half // LANE
        for part in range(2):
            table = jnp.concatenate(
                [table_ref[part * per_half + i] for i in range(per_half)], axis=1
            )
            place_ref[part * half : (part + 1) * half, :] = times_t(eye, table)
        rows = total_rows // count
        for mask in range(count):
            start = (info_ref[2] ^ mask) * rows
            place = start - jnp.where(jnp.logical_and(split, start >= half), half, 0)
            lifted = pieces[mask][...].astype(F32) + place_ref[pl.ds(pl.multiple_of(place, rows), rows), :]
            spot = pl.ds(pl.multiple_of(start, rows), rows)
            lifted_ref[spot, :] = lifted
            low_ref[spot, :] = lifted.astype(BF)

    weights = jnp.concatenate([inward_ref[pair + i * plan.lanes] for i in range(3)], axis=1)
    lanes = aligned(pair, LANE)
    query_bias = small_ref[0:1, lanes]
    value_bias = small_ref[1:2, lanes]
    for block in range(total_rows // STEP):
        spot = slice(block * STEP, (block + 1) * STEP)
        joint = times(low_ref[spot, :], weights)
        query_ref[spot, :] = (joint[:, :LANE] + query_bias).astype(BF) * BF(0.125)
        key_ref[spot, :] = joint[:, LANE : 2 * LANE].astype(BF)
        value_ref[spot, :] = (joint[:, 2 * LANE :] + value_bias).astype(BF)

    keep = causal()
    lower = lax.broadcasted_iota(jnp.int32, (LANE, STEP), 0) < LANE // 2
    for block in range(total_rows // STEP):
        spot = slice(block * STEP, (block + 1) * STEP)
        start = block * STEP
        other = half if start >= half else 0
        query = query_ref[spot, :]
        parts = []
        for head in range(2):
            mine = own_lanes(query, head)
            near = times_t(key_ref[start : start + STEP, :], mine)
            near = jnp.where(keep, near, -FAR)
            peak = jnp.max(near, axis=0, keepdims=True)
            logits = [near]
            if start > other:
                same = times_t(key_ref[other:start, :], mine)
                peak = jnp.maximum(peak, jnp.max(same, axis=0, keepdims=True))
                logits.insert(0, same)
            if other:
                away = times_t(key_ref[:other, :], mine)
                peak = jnp.maximum(peak, jnp.max(away, axis=0, keepdims=True) - far)
            raised = [jnp.exp(piece - peak) for piece in logits]
            total = sum(jnp.sum(piece, axis=0, keepdims=True) for piece in raised)
            low = jnp.concatenate([piece.astype(BF) for piece in raised], axis=0)
            mixed = t_times(value_ref[other : start + STEP, :], low)
            if other:
                away = jnp.exp(away - (peak + far))
                total = total + jnp.sum(away, axis=0, keepdims=True)
                mixed = mixed + t_times(value_ref[:other, :], away.astype(BF))
            parts.append(mixed * (1.0 / total))
            total_ref[0, head : head + 1, spot] = peak + jnp.log(total)
        mixed_ref[spot, :] = jnp.where(lower, parts[0], parts[1]).T.astype(BF)


def attend(plan, info, pieces, weights):
    total_rows, width = plan.total_rows, plan.width
    block = pl.BlockSpec((total_rows, LANE), lambda p, *_: (0, p))
    low = like((total_rows, width), BF)
    inward = (3 * plan.lanes, width, LANE)
    small = (plan.small_rows, width)
    return pl.pallas_call(
        functools.partial(attend_kernel, plan, len(pieces)),
        grid_spec=pltpu.PrefetchScalarGridSpec(
            num_scalar_prefetch=1,
            grid=(plan.lanes,),
            in_specs=[full(v.shape) for v in pieces + weights],
            out_specs=[
                full((total_rows, width)),
                block,
                block,
                block,
                block,
                pl.BlockSpec((1, 8, total_rows), lambda p, *_: (p, 0, 0)),
                full(inward),
                full(small),
            ],
            scratch_shapes=[
                pltpu.VMEM((total_rows, width), BF),
                pltpu.VMEM((plan.table_pieces, width, LANE), BF),
                pltpu.VMEM((total_rows, width), F32),
                pltpu.VMEM((plan.devices, TILE, LANE), F32),
            ],
        ),
        out_shape=[
            like((total_rows, width), F32),
            low,
            low,
            low,
            low,
            like((plan.lanes, 8, total_rows), F32),
            like(inward, BF),
            like(small, F32),
        ],
        compiler_params=params(48),
        cost_estimate=cost(5 * 10**9, 14 * 2**20, 6 * 10**6),
        name="attend",
    )(info, *pieces, *weights)


def norm(rows):
    center = rows - jnp.mean(rows, axis=1, keepdims=True)
    root = lax.rsqrt(jnp.mean(center * center, axis=1, keepdims=True) + 1e-05)
    return center * root, root


def norm_back(upstream, gain, unit, root):
    scaled = upstream * gain
    mean = jnp.mean(scaled, axis=1, keepdims=True)
    slope = jnp.mean(scaled * unit, axis=1, keepdims=True)
    return (scaled - mean - unit * slope) * root


def feed_kernel(plan, count, info_ref, lifted_ref, mixed_ref, *refs):
    upstreams, refs = refs[:count], refs[count:]
    if plan.packed:
        late_in, small_ref = refs[:2]
        refs = refs[2:]
    else:
        outward_in, expand_in, contract_in, small_ref = refs[:4]
        refs = refs[4:]
    results, refs = refs[:count], refs[count:]
    mixed_back_ref, first_back_ref, small_grad_ref = refs[:3]
    refs = refs[3:]
    if plan.packed:
        halves, refs = refs[:2], refs[2:]
    else:
        outward_out, expand_out, contract_out = refs[:3]
        refs = refs[3:]
    (outward_ref, expand_ref, contract_ref, upstream_ref, active_ref, slope_ref,
     outward_sum, expand_sum, contract_sum) = refs
    step = pl.program_id(0)
    width, parts, lanes = plan.width, plan.parts, plan.lanes
    contract_own = plan.hidden // plan.devices
    contract_at = (lanes + parts * lanes) * TILE

    @pl.when(step == 0)
    def _():
        if plan.packed:
            for device in range(plan.devices):
                rows = slice(device * TILE, (device + 1) * TILE)
                shard = late_in.at[device]
                for lane in range(lanes):
                    cut = slice(lane * LANE, (lane + 1) * LANE)
                    outward_ref[rows, cut] = shard[lane * TILE : (lane + 1) * TILE, :]
                    for part in range(parts):
                        at = (lanes + part * lanes + lane) * TILE
                        expand_ref[part, rows, cut] = shard[at : at + TILE, :]
                    at = contract_at + lane * contract_own
                    contract_ref[device * contract_own : (device + 1) * contract_own, cut] = shard[at : at + contract_own, :]
        else:
            outward_ref[...] = outward_in[...]
            expand_ref[...] = expand_in[...]
            contract_ref[...] = contract_in[...]

    for mask in range(count):
        @pl.when(step == mask)
        def _(mask=mask):
            upstream_ref[...] = upstreams[mask][...]

    outlet, steady, offset = (small_ref[i : i + 1, :] for i in (2, 3, 4))
    settle, temper, anchor = (small_ref[i + parts : i + parts + 1, :] for i in (5, 6, 7))
    mixed = mixed_ref[...]
    branch = times(mixed, outward_ref[...]) + outlet
    unit, root = norm(lifted_ref[...] + branch)
    normed = unit * steady + offset
    normed_low = normed.astype(BF)
    lowered = jnp.zeros_like(normed)
    for part in range(parts):
        cut = slice(part * width, (part + 1) * width)
        hidden = times(normed_low, expand_ref[part]) + small_ref[5 + part : 6 + part, :]
        square = hidden * hidden
        bend = jnp.tanh(hidden * (BEND + BEND * 0.044715 * square))
        half = 0.5 + 0.5 * bend
        active = (hidden * half).astype(BF)
        active_ref[:, cut] = active
        slope_ref[:, cut] = half + (0.5 * hidden) * (1.0 - bend * bend) * (
            BEND + 3 * BEND * 0.044715 * square
        )
        lowered = lowered + times(active, contract_ref[cut, :])
    last_unit, last_root = norm(normed + (lowered + settle))
    result = (last_unit * temper + anchor).astype(BF)
    for mask in range(count):
        @pl.when(step == mask)
        def _(mask=mask):
            results[mask][...] = result

    upstream = upstream_ref[...].astype(F32)
    temper_grad = column_sum(upstream * last_unit)
    anchor_grad = column_sum(upstream)
    second_back = norm_back(upstream, temper, last_unit, last_root)
    lowered_back = second_back.astype(BF)
    settle_grad = column_sum(lowered_back)
    normed_back = second_back
    spread_grads = []
    contract_terms = []
    expand_terms = []
    for part in range(parts):
        cut = slice(part * width, (part + 1) * width)
        contract_terms.append(t_times(active_ref[:, cut], lowered_back))
        active_back = times_t(lowered_back, contract_ref[cut, :])
        hidden_back = (active_back * slope_ref[:, cut]).astype(BF)
        spread_grads.append(column_sum(hidden_back))
        expand_terms.append(t_times(normed_low, hidden_back))
        normed_back = normed_back + times_t(hidden_back, expand_ref[part])
    first_back = norm_back(normed_back, steady, unit, root)
    first_back_ref[...] = first_back
    branch_back = first_back.astype(BF)
    mixed_back_ref[...] = times_t(branch_back, outward_ref[...]).astype(BF)
    outward_term = t_times(mixed, branch_back)
    zero = jnp.zeros_like(anchor_grad)
    grads = [zero, zero, column_sum(branch_back), column_sum(normed_back * unit)]
    grads += [column_sum(normed_back)] + spread_grads + [settle_grad, temper_grad, anchor_grad]
    grads += [zero] * (plan.small_rows - len(grads))
    small_term = jnp.concatenate(grads, axis=0)

    @pl.when(step == 0)
    def _():
        small_grad_ref[...] = small_term
        outward_sum[...] = outward_term
        for part in range(parts):
            expand_sum[part] = expand_terms[part]
            contract_sum[part * width : (part + 1) * width, :] = contract_terms[part]

    @pl.when(step > 0)
    def _():
        small_grad_ref[...] += small_term
        outward_sum[...] += outward_term
        for part in range(parts):
            expand_sum[part] += expand_terms[part]
            contract_sum[part * width : (part + 1) * width, :] += contract_terms[part]

    @pl.when(step == count - 1)
    def _():
        if plan.packed:
            for mask in range(plan.devices):
                shard = halves[mask & 1].at[plan.place(mask)]
                owner = info_ref[1] ^ mask
                rows = aligned(owner, TILE)
                wide = aligned(owner, contract_own)
                for lane in range(lanes):
                    cut = slice(lane * LANE, (lane + 1) * LANE)
                    shard[lane * TILE : (lane + 1) * TILE, :] = outward_sum[rows, cut].astype(BF)
                    for part in range(parts):
                        at = (lanes + part * lanes + lane) * TILE
                        shard[at : at + TILE, :] = expand_sum[part, rows, cut].astype(BF)
                    at = contract_at + lane * contract_own
                    shard[at : at + contract_own, :] = contract_sum[wide, cut].astype(BF)
        else:
            outward_out[...] = outward_sum[...].astype(BF)
            expand_out[...] = expand_sum[...].astype(BF)
            contract_out[...] = contract_sum[...].astype(BF)


def feed(plan, info, lifted, mixed, upstreams, weights, small):
    total_rows, width, parts = plan.total_rows, plan.width, plan.parts
    count = len(upstreams)
    size = total_rows // count
    rows = pl.BlockSpec((size, width), lambda i, info: (info[2] ^ i, 0))
    outward, expand, contract = (width, width), (parts, width, width), (parts * width, width)
    if plan.packed:
        grads = [like((plan.devices // 2, plan.late_rows, LANE), BF)] * 2
    else:
        grads = [like(outward, BF), like(expand, BF), like(contract, BF)]
    ends = [like((size, width), BF)] * count
    outs = [like((total_rows, width), BF), like((total_rows, width), F32), like(small.shape, F32)]
    values = pl.pallas_call(
        functools.partial(feed_kernel, plan, count),
        grid_spec=pltpu.PrefetchScalarGridSpec(
            num_scalar_prefetch=1,
            grid=(count,),
            in_specs=[rows, rows] + [full(v.shape) for v in upstreams + weights + [small]],
            out_specs=[full(v.shape) for v in ends]
            + [rows, rows, full(small.shape)]
            + [full(v.shape) for v in grads],
            scratch_shapes=[
                pltpu.VMEM(outward, BF),
                pltpu.VMEM(expand, BF),
                pltpu.VMEM(contract, BF),
                pltpu.VMEM((size, width), BF),
                pltpu.VMEM((size, parts * width), BF),
                pltpu.VMEM((size, parts * width), F32),
                pltpu.VMEM(outward, F32),
                pltpu.VMEM(expand, F32),
                pltpu.VMEM(contract, F32),
            ],
        ),
        out_shape=ends + outs + grads,
        compiler_params=params(60),
        cost_estimate=cost(15 * 10**9, 20 * 2**20, 2 * 10**6),
        name="feed",
    )(info, lifted, mixed, *upstreams, *weights, small)
    return values[:count], values[count : count + 3], values[count + 3 :]


def attend_back_kernel(
    plan, count, info_ref, lifted_ref, query_ref, key_ref, value_ref, mixed_ref, mixed_back_ref,
    total_ref, inward_ref, first_back_ref, small_grad_ref, *refs
):
    tokens, refs = refs[:count], refs[count:]
    if plan.packed:
        halves, refs = refs[:2], refs[2:]
    else:
        table_out, inward_out, small_out = refs[:3]
        refs = refs[3:]
    low_ref, sum_ref, share_ref, score_ref, grad_ref, table_ref, joint_sums, blocks_ref = refs
    pair = pl.program_id(0)
    total_rows, lanes = plan.total_rows, plan.lanes
    half = total_rows // 2
    split = info_ref[0] < total_rows
    far = jnp.where(split, FAR, 0.0)
    blocks = total_rows // STEP

    @pl.when(pair == 0)
    def _():
        low_ref[...] = lifted_ref[...].astype(BF)

    keep = causal()
    lower = lax.broadcasted_iota(jnp.int32, (STEP, LANE), 1) < LANE // 2
    lower_t = lax.broadcasted_iota(jnp.int32, (LANE, STEP), 0) < LANE // 2
    query_parts, key_parts, value_parts = [], [], []
    product = (mixed_ref[...].astype(F32) * mixed_back_ref[...].astype(F32)).T
    scaled_key = key_ref[...] * BF(0.125)
    for head in range(2):
        between = jnp.sum(
            product[head * LANE // 2 : (head + 1) * LANE // 2], axis=0, keepdims=True
        )
        for block in range(blocks):
            start = block * STEP
            spot = slice(start, start + STEP)
            query = own_lanes(query_ref[spot, :], head)
            back = own_lanes(mixed_back_ref[spot, :], head)
            total = total_ref[0, head : head + 1, spot]
            gap = between[:, spot]
            for under in range(block + 1):
                keys = slice(under * STEP, (under + 1) * STEP)
                away = start >= half and under * STEP < half
                logits = times_t(key_ref[keys, :], query)
                share = jnp.exp(logits - (total + far if away else total))
                if under == block:
                    share = jnp.where(keep, share, 0.0)
                share_back = times_t(value_ref[keys, :], back)
                score = share * (share_back - gap)
                share_ref[head, keys, spot] = share.astype(BF)
                score_ref[head, keys, spot] = score.astype(BF)
        queries, keys_, values = [], [], []
        for block in range(blocks):
            start = block * STEP
            spot = slice(start, start + STEP)
            end = start + STEP
            queries.append(t_times(scaled_key[:end], score_ref[head, :end, spot]))
            keys_.append(times(score_ref[head, spot, start:], query_ref[start:, :]))
            values.append(times(share_ref[head, spot, start:], mixed_back_ref[start:, :]))
        query_parts.append(queries)
        key_parts.append(keys_)
        value_parts.append(values)
    weights = jnp.concatenate([inward_ref[pair + i * lanes] for i in range(3)], axis=1)
    joints = []
    for block in range(blocks):
        spot = slice(block * STEP, (block + 1) * STEP)
        query_back = jnp.where(lower_t, query_parts[0][block], query_parts[1][block]).T
        key_back = jnp.where(lower, key_parts[0][block], key_parts[1][block])
        value_back = jnp.where(lower, value_parts[0][block], value_parts[1][block])
        joint = jnp.concatenate([query_back, key_back, value_back], axis=1).astype(BF)
        joints.append(joint)
        term = times_t(joint, weights)

        @pl.when(pair == 0)
        def _():
            sum_ref[spot, :] = term + first_back_ref[spot, :]

        @pl.when(pair > 0)
        def _():
            sum_ref[spot, :] += term

    joint = jnp.concatenate(joints, axis=0)
    grads = t_times(low_ref[...], joint)
    for part in range(3):
        grad_ref[pair + part * lanes] = grads[:, part * LANE : (part + 1) * LANE]
    sums = column_sum(joint)
    joint_sums[pl.ds(pair, 1), :] = sums[:, :LANE]
    joint_sums[pl.ds(pair + lanes, 1), :] = sums[:, 2 * LANE :]

    @pl.when(pair == lanes - 1)
    def _():
        rows = total_rows // count
        for mask in range(count):
            spot = pl.ds(pl.multiple_of((info_ref[2] ^ mask) * rows, rows), rows)
            tokens[mask][...] = sum_ref[spot, :].astype(BF)
        late = sum_ref[half:, :]
        early = sum_ref[:half, :] + jnp.where(split, late, 0.0)
        table_ref[:, :half] = early.T
        table_ref[:, half:] = jnp.where(split, 0.0, late).T
        counted = info_ref[3] > 0
        blocks_ref[: 2 * lanes, :] = joint_sums[: 2 * lanes, :]
        for row in range(2, plan.block_starts[-1] // lanes):
            for lane in range(lanes):
                blocks_ref[row * lanes + lane : row * lanes + lane + 1, :] = small_grad_ref[
                    row : row + 1, lane * LANE : (lane + 1) * LANE
                ]
        if plan.packed:
            for mask in range(plan.devices):
                shard = halves[mask & 1].at[plan.place(mask)]
                owner = info_ref[1] ^ mask
                own = aligned(owner, TILE)
                for piece in range(plan.table_pieces):
                    shard[piece * TILE : (piece + 1) * TILE, :] = table_ref[
                        own, piece * LANE : (piece + 1) * LANE
                    ].astype(BF)
                for piece in range(3 * lanes):
                    at = (plan.table_pieces + piece) * TILE
                    shard[at : at + TILE, :] = grad_ref[piece, own, :].astype(BF)
                rows = [
                    blocks_ref[pl.ds(plan.block_starts[v] + owner * plan.owned[v] // LANE, 1), :]
                    for v in range(VECTORS)
                ]
                rows.append(jnp.zeros((TILE - VECTORS, LANE), F32))
                at = plan.early_pieces * TILE
                shard[at : at + TILE, :] = jnp.concatenate(rows, axis=0).astype(BF)
        else:
            table_out[...] = jnp.where(counted, table_ref[...], 0.0).astype(BF)
            inward_out[...] = jnp.where(counted, grad_ref[...], 0.0).astype(BF)
            small_out[...] = jnp.where(counted, blocks_ref[...], 0.0)


def attend_back(plan, info, count, lifted, saved, mixed_back, inward, first_back, small_grad):
    query, key, value, mixed, totals = saved
    total_rows, width, lanes = plan.total_rows, plan.width, plan.lanes
    block = pl.BlockSpec((total_rows, LANE), lambda p, *_: (0, p))
    blocks = (plan.block_starts[-1], LANE)
    if plan.packed:
        grads = [like((plan.devices // 2, plan.early_rows, LANE), BF)] * 2
    else:
        grads = [like((width, total_rows), BF), like(inward.shape, BF), like(blocks, F32)]
    tokens = [like((total_rows // count, width), BF)] * count
    values = pl.pallas_call(
        functools.partial(attend_back_kernel, plan, count),
        grid_spec=pltpu.PrefetchScalarGridSpec(
            num_scalar_prefetch=1,
            grid=(lanes,),
            in_specs=[
                full(lifted.shape),
                block,
                block,
                block,
                block,
                block,
                pl.BlockSpec((1, 8, total_rows), lambda p, *_: (p, 0, 0)),
                full(inward.shape),
                full(first_back.shape),
                full(small_grad.shape),
            ],
            out_specs=[full(v.shape) for v in tokens + grads],
            scratch_shapes=[
                pltpu.VMEM((total_rows, width), BF),
                pltpu.VMEM((total_rows, width), F32),
                pltpu.VMEM((2, total_rows, total_rows), BF),
                pltpu.VMEM((2, total_rows, total_rows), BF),
                pltpu.VMEM(inward.shape, F32),
                pltpu.VMEM((width, total_rows), F32),
                pltpu.VMEM((8, LANE), F32),
                pltpu.VMEM(blocks, F32),
            ],
        ),
        out_shape=tokens + grads,
        compiler_params=params(60),
        cost_estimate=cost(14 * 10**9, 24 * 2**20, 6 * 10**6),
        name="attend_back",
    )(info, lifted, query, key, value, mixed, mixed_back, totals, inward, first_back, small_grad)
    return values[:count], values[count:]


def pack_early_kernel(plan, info_ref, table_ref, inward_ref, *refs):
    vectors, out_ref = refs[:VECTORS], refs[VECTORS]
    me = info_ref[1]
    for piece in range(plan.table_pieces):
        out_ref[piece * TILE : (piece + 1) * TILE, :] = table_ref[:, piece * LANE : (piece + 1) * LANE]
    for piece in range(3 * plan.lanes):
        at = (plan.table_pieces + piece) * TILE
        out_ref[at : at + TILE, :] = inward_ref[:, piece * LANE : (piece + 1) * LANE]
    lane = lax.broadcasted_iota(jnp.int32, (1, LANE), 1)
    rows = []
    for vector, ref in zip(range(VECTORS), vectors):
        size = plan.owned[vector]
        wide = jnp.concatenate([ref[...].astype(F32)] * (LANE // size), axis=1)
        slot = lax.rem(me, LANE // size)
        rows.append(jnp.where(lane // size == slot, wide, 0.0))
    rows.append(jnp.zeros((TILE - VECTORS, LANE), F32))
    at = plan.early_pieces * TILE
    out_ref[at : at + TILE, :] = jnp.concatenate(rows, axis=0).astype(BF)


def pack_early(plan, info, table, inward, vectors):
    values = [table, inward] + [v.reshape(1, -1) for v in vectors]
    out = (plan.early_rows, LANE)
    return pl.pallas_call(
        functools.partial(pack_early_kernel, plan),
        grid_spec=pltpu.PrefetchScalarGridSpec(
            num_scalar_prefetch=1,
            grid=(1,),
            in_specs=[full(v.shape) for v in values],
            out_specs=full(out),
        ),
        out_shape=like(out, BF),
        name="pack_early",
    )(info, *values)


def pack_late_kernel(plan, outward_ref, expand_ref, contract_ref, out_ref):
    at = 0
    for ref in (outward_ref, expand_ref, contract_ref):
        rows = ref.shape[0]
        for lane in range(ref.shape[1] // LANE):
            out_ref[at : at + rows, :] = ref[:, lane * LANE : (lane + 1) * LANE]
            at += rows


def pack_late(plan, outward, expand, contract):
    return pl.pallas_call(
        functools.partial(pack_late_kernel, plan),
        out_shape=like((plan.late_rows, LANE), BF),
        name="pack_late",
    )(outward, expand, contract)


def fold_kernel(count, *refs):
    total = refs[0][...].astype(F32)
    for ref in refs[1:count]:
        total = total + ref[...].astype(F32)
    size = total.shape[0] // len(refs[count:])
    for index, ref in enumerate(refs[count:]):
        ref[...] = total[index * size : (index + 1) * size].astype(ref.dtype)


def fold(terms, cuts):
    entries, rows, _ = terms[0].shape
    pieces = 4 if rows % 64 == 0 else 3
    size = rows // pieces
    out = like((entries // cuts, rows, LANE), BF)
    return pl.pallas_call(
        functools.partial(fold_kernel, len(terms)),
        grid=(pieces,),
        in_specs=[pl.BlockSpec((entries, size, LANE), lambda i: (0, i, 0))] * len(terms),
        out_specs=[pl.BlockSpec((entries // cuts, size, LANE), lambda i: (0, i, 0))] * cuts,
        out_shape=[out] * cuts,
        cost_estimate=cost(10**6, len(terms) * entries * rows * LANE * 4),
        name="fold",
    )(*terms)


def finish_kernel(plan, count, info_ref, *refs):
    early, late, tokens = refs[:4], refs[4:8], refs[8 : 8 + count]
    (tokens_ref, table_ref, inward_ref, outward_ref, expand_ref, contract_ref) = refs[8 + count : 14 + count]
    vectors = refs[14 + count :]
    early = sum(ref[0].astype(F32) for ref in early)
    late = sum(ref[0].astype(F32) for ref in late)
    for mask in range(count):
        tokens_ref[pl.ds(info_ref[2] ^ mask, 1), :, :] = tokens[mask][...][None]
    for piece in range(plan.table_pieces):
        table_ref[:, piece * LANE : (piece + 1) * LANE] = early[piece * TILE : (piece + 1) * TILE]
    for piece in range(3 * plan.lanes):
        at = (plan.table_pieces + piece) * TILE
        inward_ref[:, piece * LANE : (piece + 1) * LANE] = early[at : at + TILE]
    at = 0
    for ref in (outward_ref, expand_ref, contract_ref):
        rows = ref.shape[0]
        for lane in range(ref.shape[1] // LANE):
            ref[:, lane * LANE : (lane + 1) * LANE] = late[at : at + rows]
            at += rows
    at = plan.early_pieces * TILE
    small = early[at : at + VECTORS]
    for vector, ref in enumerate(vectors):
        size = plan.owned[vector]
        slot = lax.rem(info_ref[1], LANE // size)
        row = pltpu.roll(small, LANE - slot * size, 1)
        ref[...] = row[vector : vector + 1, :size]


def finish(plan, info, micro_count, early, late, tokens):
    rows, width = tokens[0].shape
    own = plan.own_rows
    outs = [
        like((micro_count, rows, width), BF),
        like((own, plan.total_rows), F32),
        like((own, 3 * width), F32),
        like((own, width), F32),
        like((own, plan.hidden), F32),
        like((plan.hidden // plan.devices, width), F32),
    ] + [like((1, n), F32) for n in plan.owned]
    values = early + late + tokens
    return pl.pallas_call(
        functools.partial(finish_kernel, plan, len(tokens)),
        grid_spec=pltpu.PrefetchScalarGridSpec(
            num_scalar_prefetch=1,
            grid=(1,),
            in_specs=[full(v.shape) for v in values],
            out_specs=[full(v.shape) for v in outs],
        ),
        out_shape=outs,
        name="finish",
    )(info, *values)


def settle_kernel(count, share, info_ref, *refs):
    for mask in range(count):
        refs[count][pl.ds((info_ref[2] ^ mask) // share, 1), :, :] = refs[mask][...][None]


def settle_rows(info, micro_count, share, pieces):
    out = (micro_count,) + pieces[0].shape
    return pl.pallas_call(
        functools.partial(settle_kernel, len(pieces), share),
        grid_spec=pltpu.PrefetchScalarGridSpec(
            num_scalar_prefetch=1,
            grid=(1,),
            in_specs=[full(v.shape) for v in pieces],
            out_specs=full(out),
        ),
        out_shape=like(out, BF),
        name="settle_rows",
    )(info, *pieces)


def cut_kernel(*refs):
    refs[2][...] = refs[1][0]


def cut_rows(info, rows, count, share):
    def one(mask):
        return pl.pallas_call(
            cut_kernel,
            grid_spec=pltpu.PrefetchScalarGridSpec(
                num_scalar_prefetch=1,
                grid=(1,),
                in_specs=[
                    pl.BlockSpec((1,) + rows.shape[1:], lambda i, info: ((info[2] ^ mask) // share, 0, 0))
                ],
                out_specs=full(rows.shape[1:]),
            ),
            out_shape=like(rows.shape[1:], BF),
            name="cut_rows",
        )(info, rows)

    return [one(mask) for mask in range(count)]


def local(tokens, first_length, cotangent, positions, inward, intake, outward, outlet, steady, offset,
          expand, spread, contract, settle, temper, anchor):
    micro_count, pack_count, block_rows, width = tokens.shape
    assert pack_count == 1
    devices, count = lax.axis_size(AXES), lax.axis_size("seq")
    me, rank = lax.axis_index(AXES), lax.axis_index("seq")
    share = max(count // micro_count, 1)
    assert share * micro_count == count
    plan = Plan(devices, width, contract.shape[0] * devices, block_rows * count)
    micro = rank // share
    firsts = jnp.where(jnp.arange(micro_count) == micro, first_length[:, 0], 0)
    counted = (rank % share == 0).astype(jnp.int32)
    info = jnp.stack([jnp.sum(firsts), me, rank, counted]).astype(jnp.int32)
    vectors = (intake, outlet, steady, offset, spread, settle, temper, anchor)

    def swap(value, mask):
        return lax.ppermute(value, AXES, [(d, d ^ mask) for d in range(devices)]) if mask else value

    def exchange(pieces):
        return [swap(piece, mask) for mask, piece in enumerate(pieces)]

    rows_in = exchange(cut_rows(info, tokens[:, 0], count, share))
    upstreams = exchange(cut_rows(info, cotangent[:, 0], count, share))
    if plan.packed:
        shard = pack_early(plan, info, positions.T, inward, vectors)[None]
        late_shard = pack_late(plan, outward, expand, contract)
        shard = jnp.concatenate([swap(shard, k << 3) for k in range(4)], axis=0)
        shard = jnp.concatenate([swap(shard, k << 1) for k in range(4)], axis=0)
        early = [shard, swap(shard, 1)]
        late = lax.all_gather(late_shard, AXES, axis=0, tiled=False)
        late = [late]
    else:
        early, late = plain_weights(plan, positions, inward, vectors, outward, expand, contract)
    lifted, query, key, value, mixed, totals, inward_all, small = attend(plan, info, rows_in, early)
    results, (mixed_back, first_back, small_grad), late_grads = feed(
        plan, info, lifted, mixed, upstreams, late, small
    )
    output = settle_rows(info, micro_count, share, exchange(results))
    if plan.packed:
        keep, send = late_grads
        terms = fold([keep, swap(send, 1)], 4)
        terms = [swap(term, k << 1) for k, term in enumerate(terms)]
    token_pieces, early_grads = attend_back(
        plan, info, count, lifted, (query, key, value, mixed, totals), mixed_back, inward_all,
        first_back, small_grad,
    )
    token_pieces = exchange(token_pieces)
    if plan.packed:
        terms = fold(terms, 4)
        late_terms = [swap(term, k << 3) for k, term in enumerate(terms)]
        keep, send = early_grads
        terms = fold([keep, swap(send, 1)], 4)
        terms = fold([swap(term, k << 1) for k, term in enumerate(terms)], 4)
        early_terms = [swap(term, k << 3) for k, term in enumerate(terms)]
        values = finish(plan, info, micro_count, early_terms, late_terms, token_pieces)
        tokens_back, table_t, inward_own, outward_own, expand_own, contract_own = values[:6]
        own = [v.reshape(-1) for v in values[6:]]
        table_own = table_t.T
    else:
        tokens_back = settle_rows(info, micro_count, share, token_pieces)
        table_own, inward_own, outward_own, expand_own, contract_own, own = plain_grads(
            plan, counted, early_grads, late_grads
        )
    return (output[:, None], tokens_back[:, None], table_own, inward_own, own[0], outward_own, own[1], own[2],
            own[3], expand_own, own[4], contract_own, own[5], own[6], own[7])


def plain_weights(plan, positions, inward, vectors, outward, expand, contract):
    lanes, width = plan.lanes, plan.width

    def gather(value, axis=0):
        return lax.all_gather(value, AXES, axis=axis, tiled=True)

    def in_pieces(value, size):
        return value.reshape(value.shape[0], -1, size).transpose(1, 0, 2)

    table = in_pieces(gather(positions, 1).T, LANE)
    small = jnp.concatenate([gather(v) for v in vectors]).astype(F32).reshape(-1, width)
    small = jnp.pad(small, ((0, plan.small_rows - small.shape[0]), (0, 0)))
    early = [table, in_pieces(gather(inward), LANE), small]
    return early, [gather(outward), in_pieces(gather(expand), width), gather(contract)]


def plain_grads(plan, counted, early_grads, late_grads):
    width = plan.width
    table, inward, small = early_grads
    outward, expand, contract = (jnp.where(counted > 0, g, BF(0)) for g in late_grads)

    def scatter(value, axis=0):
        return lax.psum_scatter(value, AXES, scatter_dimension=axis, tiled=True).astype(F32)

    def whole(value):
        return value.transpose(1, 0, 2).reshape(value.shape[1], -1)

    flat = small.reshape(-1)
    own = []
    for vector, length in enumerate(plan.lengths):
        start = plan.block_starts[vector] * LANE
        own.append(scatter(flat[start : start + length]))
    return (scatter(table.T, 1), scatter(whole(inward)), scatter(outward), scatter(whole(expand)),
            scatter(contract), own)


def solution(mesh):
    rows = P(None, "batch", "seq", None)
    table = P(None, AXES)
    matrix = P(AXES, None)
    vector = P(AXES)
    weights = (table, matrix, vector, matrix, vector, vector, vector, matrix, vector, matrix, vector,
               vector, vector)
    return jax.shard_map(
        local,
        mesh=mesh,
        in_specs=(rows, P(None, "batch"), rows) + weights,
        out_specs=(rows, rows) + weights,
        check_vma=False,
    )
```

profile of v0, /device:TPU:0, one launch (start us, length us, event | category | flops | bytes accessed | tf_op | source)
XLA Modules:
  0.0 276.9 jit_solution(5965279783976780603)
XLA Ops:
  11.4 2.2 pack_early.1
  13.7 5.0 %collective-permute-start.5 = (bf16[1,336,128]{2,1,0:T(8,128)(2,1)}, bf16[1,336,128]{2,1,0:T(8,128)(2,1)S(1)}, u32[]{:S(2)}, u32[]{:S(2)}) collective-permute-start(bf16[1,336,128]{2,1,0:T(8,128)(2,1)} %bitcast.43), channel_id=1, source_target_pairs={{0,24},{1,25},{2,26},{3,27},{4,28},{5,29},{6,30},{7,31},{8,16},{9,... | collective-permute-start | bytes 258056 | tf_op jit(solution)/shard_map/ppermute | solution.py:809
  19.3 2.9 %collective-permute-done.5 = bf16[1,336,128]{2,1,0:T(8,128)(2,1)S(1)} collective-permute-done((bf16[1,336,128]{2,1,0:T(8,128)(2,1)}, bf16[1,336,128]{2,1,0:T(8,128)(2,1)S(1)}, u32[]{:S(2)}, u32[]{:S(2)}) %collective-permute-start.5) | collective-permute-done | bytes 86048 | tf_op jit(solution)/shard_map/ppermute | solution.py:809
  22.1 4.2 %collective-permute-done.4 = bf16[1,336,128]{2,1,0:T(8,128)(2,1)S(1)} collective-permute-done((bf16[1,336,128]{2,1,0:T(8,128)(2,1)}, bf16[1,336,128]{2,1,0:T(8,128)(2,1)S(1)}, u32[]{:S(2)}, u32[]{:S(2)}) %collective-permute-start.4) | collective-permute-done | bytes 86048 | tf_op jit(solution)/shard_map/ppermute | solution.py:809
  31.8 6.6 %collective-permute-done.6 = bf16[4,336,128]{2,1,0:T(8,128)(2,1)S(1)} collective-permute-done((bf16[4,336,128]{2,1,0:T(8,128)(2,1)S(1)}, bf16[4,336,128]{2,1,0:T(8,128)(2,1)S(1)}, u32[]{:S(2)}, u32[]{:S(2)}) %collective-permute-start.6) | collective-permute-done | bytes 344096 | tf_op jit(solution)/shard_map/ppermute | solution.py:809
  38.4 10.8 %collective-permute-done.7 = bf16[4,336,128]{2,1,0:T(8,128)(2,1)S(1)} collective-permute-done((bf16[4,336,128]{2,1,0:T(8,128)(2,1)S(1)}, bf16[4,336,128]{2,1,0:T(8,128)(2,1)S(1)}, u32[]{:S(2)}, u32[]{:S(2)}) %collective-permute-start.7) | collective-permute-done | bytes 344096 | tf_op jit(solution)/shard_map/ppermute | solution.py:809
  49.4 2.3 cut_rows.9
  52.3 2.3 cut_rows.10
  56.1 2.3 cut_rows.11
  58.4 2.3 cut_rows.13
  61.4 2.3 cut_rows.8.refs_0_
  63.7 2.3 cut_rows.15
  66.1 2.5 cut_rows.14
  68.6 2.3 cut_rows.12.refs_0_
  72.4 4.7 %collective-permute-done.2.refs_3_ = bf16[256,512]{1,0:T(8,128)(2,1)S(1)} collective-permute-done((bf16[256,512]{1,0:T(8,128)(2,1)}, bf16[256,512]{1,0:T(8,128)(2,1)S(1)}, u32[]{:S(2)}, u32[]{:S(2)}) %collective-permute-start.2) | collective-permute-done | bytes 262176 | tf_op jit(solution)/shard_map/ppermute | solution.py:809
  77.1 22.0 %attend.1 = (f32[1024,512]{1,0:T(8,128)}, bf16[1024,512]{1,0:T(8,128)(2,1)S(1)}, bf16[1024,512]{1,0:T(8,128)(2,1)S(1)}, bf16[1024,512]{1,0:T(8,128)(2,1)S(1)}, b...) custom-call(s32[4]{0:T(128)S(1)} %copy-done.1, ...), custom_call_target="tpu_custom_call" | custom-call | flops 5000000000 | bytes 14680064 | tf_op jit(solution)/shard_map/attend/pallas_call | solution.py:208
  105.2 37.4 %feed.1 = (bf16[256,512]{1,0:T(8,128)(2,1)}, bf16[256,512]{1,0:T(8,128)(2,1)}, bf16[256,512]{1,0:T(8,128)(2,1)}, bf16[256,512]{1,0:T(8,128)(2,1)}, bf16[1024,512...) custom-call(s32[4]{0:T(128)} %pad_add_fusion.refs_0_.info_ref, ...), custom_call_target="tpu_custom_call" | custom-call | flops 15000000512 | bytes 20971520 | tf_op jit(solution)/shard_map/feed/pallas_call | solution.py:413
  143.7 29.1 %attend_back.1 = (bf16[256,512]{1,0:T(8,128)(2,1)}, bf16[256,512]{1,0:T(8,128)(2,1)}, bf16[256,512]{1,0:T(8,128)(2,1)}, bf16[256,512]{1,0:T(8,128)(2,1)}, bf16[1...) custom-call(s32[4]{0:T(128)} %pad_add_fusion.refs_0_.info_ref, f32[1024,512]{1,0:T(8,128)} %get-tuple-element.68.lifted_ref, ...), custom_call_target="tpu_custom_call" | custom-call | flops 14000000000 | bytes 25165824 | tf_op jit(solution)/shard_map/attend_back/pallas_call | solution.py:582
  172.8 3.4 %collective-permute-done.16.refs_1_ = bf16[16,336,128]{2,1,0:T(8,128)(2,1)} collective-permute-done((bf16[16,336,128]{2,1,0:T(8,128)(2,1)}, bf16[16,336,128]{2,1,0:T(8,128)(2,1)}, u32[]{:S(2)}, u32[]{:S(2)}) %collective-permute-start.16) | collective-permute-done | bytes 1376288 | tf_op jit(solution)/shard_map/ppermute | solution.py:809
  176.2 3.7 %fold.4 = (bf16[4,336,128]{2,1,0:T(8,128)(2,1)}, bf16[4,336,128]{2,1,0:T(8,128)(2,1)}, bf16[4,336,128]{2,1,0:T(8,128)(2,1)}, bf16[4,336,128]{2,1,0:T(8,128)(2,1)}) custom-call(bf16[16,336,128]{2,1,0:T(8,128)(2,1)} %get-tuple-element.83.refs_0_, bf16[16,336,128]{2,1,0:T(8,128)(2,1)} %collective-permute-done.16.refs_1_), custom_call_target="tpu_custom_call" | custom-call | flops 1000000 | bytes 5505024 | tf_op jit(solution)/shard_map/fold/pallas_call | solution.py:686
  183.4 4.5 %fold.6 = (bf16[4,576,128]{2,1,0:T(8,128)(2,1)}, bf16[4,576,128]{2,1,0:T(8,128)(2,1)}, bf16[4,576,128]{2,1,0:T(8,128)(2,1)}, bf16[4,576,128]{2,1,0:T(8,128)(2,1)}) custom-call(bf16[16,576,128]{2,1,0:T(8,128)(2,1)} %get-tuple-element.93.refs_0_, bf16[16,576,128]{2,1,0:T(8,128)(2,1)} %copy-done.8), custom_call_target="tpu_custom_call" | custom-call | flops 1000000 | bytes 9437184 | tf_op jit(solution)/shard_map/fold/pallas_call | solution.py:686
  191.4 5.3 %collective-permute-done.14.refs_2_ = bf16[256,512]{1,0:T(8,128)(2,1)S(1)} collective-permute-done((bf16[256,512]{1,0:T(8,128)(2,1)}, bf16[256,512]{1,0:T(8,128)(2,1)S(1)}, u32[]{:S(2)}, u32[]{:S(2)}) %collective-permute-start.14) | collective-permute-done | bytes 262176 | tf_op jit(solution)/shard_map/ppermute | solution.py:809
  197.4 2.0 collective-permute-start.19
  199.4 32.5 %collective-permute-done.18.refs_2_ = bf16[4,336,128]{2,1,0:T(8,128)(2,1)S(1)} collective-permute-done((bf16[4,336,128]{2,1,0:T(8,128)(2,1)}, bf16[4,336,128]{2,1,0:T(8,128)(2,1)S(1)}, u32[]{:S(2)}, u32[]{:S(2)}) %collective-permute-start.18) | collective-permute-done | bytes 344096 | tf_op jit(solution)/shard_map/ppermute | solution.py:809
  234.3 2.9 %fold.5 = (bf16[1,336,128]{2,1,0:T(8,128)(2,1)}, bf16[1,336,128]{2,1,0:T(8,128)(2,1)}, bf16[1,336,128]{2,1,0:T(8,128)(2,1)}, bf16[1,336,128]{2,1,0:T(8,128)(2,1)}) custom-call(bf16[4,336,128]{2,1,0:T(8,128)(2,1)} %get-tuple-element.85.refs_0_, bf16[4,336,128]{2,1,0:T(8,128)(2,1)} %copy-done.12, bf16[4,336,128]{2,1,0:T(8,128)(2,1)} %copy-done.13, ...), custom_call_target="tpu_custom_call" | custom-call | flops 1000000 | bytes 2752512 | tf_op jit(solution)/shard_map/fold/pallas_call | solution.py:686
  238.5 3.7 %fold.7 = (bf16[1,576,128]{2,1,0:T(8,128)(2,1)}, bf16[1,576,128]{2,1,0:T(8,128)(2,1)}, bf16[1,576,128]{2,1,0:T(8,128)(2,1)}, bf16[1,576,128]{2,1,0:T(8,128)(2,1)}) custom-call(bf16[4,576,128]{2,1,0:T(8,128)(2,1)} %get-tuple-element.95.refs_0_, bf16[4,576,128]{2,1,0:T(8,128)(2,1)} %copy-done.9, bf16[4,576,128]{2,1,0:T(8,128)(2,1)} %copy-done.10, ...), custom_call_target="tpu_custom_call" | custom-call | flops 1000000 | bytes 4718592 | tf_op jit(solution)/shard_map/fold/pallas_call | solution.py:686
  243.4 1.9 collective-permute-done.31.refs_10_
  246.6 4.8 %collective-permute-done.32.refs_11_ = bf16[256,512]{1,0:T(8,128)(2,1)} collective-permute-done((bf16[256,512]{1,0:T(8,128)(2,1)S(1)}, bf16[256,512]{1,0:T(8,128)(2,1)}, u32[]{:S(2)}, u32[]{:S(2)}) %collective-permute-start.32) | collective-permute-done | bytes 262176 | tf_op jit(solution)/shard_map/ppermute | solution.py:809
  251.4 3.5 %collective-permute-start.22 = (bf16[1,336,128]{2,1,0:T(8,128)(2,1)S(1)}, bf16[1,336,128]{2,1,0:T(8,128)(2,1)S(1)}, u32[]{:S(2)}, u32[]{:S(2)}) collective-permute-start(bf16[1,336,128]{2,1,0:T(8,128)(2,1)S(1)} %copy-done.29), channel_id=1, source_target_pairs={{0,24},{1,25},{2,26},{3,27},{4,28},{5,29},{6,30},{7,31},{8,16},{9,... | collective-permute-start | bytes 258056 | tf_op jit(solution)/shard_map/ppermute | solution.py:809
  255.0 2.9 %settle_rows.1 = bf16[4,256,512]{2,1,0:T(8,128)(2,1)} custom-call(s32[4]{0:T(128)} %pad_add_fusion.refs_0_.info_ref, bf16[256,512]{1,0:T(8,128)(2,1)} %get-tuple-element.71.refs_0_, bf16[256,512]{1,0:T(8,128)(2,1)} %copy-done.15, bf16[256,512]{1,0:T(8,128)(2,1)} %copy-done.16, bf16[256,512]{1,0:T(8,128)(2,1)} %collective-permute-done.15.refs_3_), custom_call_target="tpu_custom_call" | custom-call | tf_op jit(solution)/shard_map/settle_rows/pallas_call | solution.py:757
  257.9 8.0 %collective-permute-done.21.refs_2_ = bf16[1,336,128]{2,1,0:T(8,128)(2,1)S(1)} collective-permute-done((bf16[1,336,128]{2,1,0:T(8,128)(2,1)S(1)}, bf16[1,336,128]{2,1,0:T(8,128)(2,1)S(1)}, u32[]{:S(2)}, u32[]{:S(2)}) %collective-permute-start.21) | collective-permute-done | bytes 86048 | tf_op jit(solution)/shard_map/ppermute | solution.py:809
  266.6 3.4 %finish.1 = (bf16[4,256,512]{2,1,0:T(8,128)(2,1)}, f32[16,1024]{1,0:T(8,128)}, f32[16,1536]{1,0:T(8,128)}, f32[16,512]{1,0:T(8,128)}, f32[16,2048]{1,0:T(8,128)}...) custom-call(s32[4]{0:T(128)} %pad_add_fusion.refs_0_.info_ref, ...), custom_call_target="tpu_custom_call" | custom-call | tf_op jit(solution)/shard_map/finish/pallas_call | solution.py:737
  (128 shorter events, 36.4 us)
Async XLA Ops:
  7.2 97.2 %all-gather.3.cloned.1.call-start = ((), (), s32[]{:S(2)}) async-start(), calls=%async_computation | async-start | bytes 4866048 | tf_op jit(solution)/shard_map/all_gather | solution.py:822
  13.7 8.5 %collective-permute-start.5 = (bf16[1,336,128]{2,1,0:T(8,128)(2,1)}, bf16[1,336,128]{2,1,0:T(8,128)(2,1)S(1)}, u32[]{:S(2)}, u32[]{:S(2)}) collective-permute-start(bf16[1,336,128]{2,1,0:T(8,128)(2,1)} %bitcast.43), channel_id=1, source_target_pairs={{0,24},{1,25},{2,26},{3,27},{4,28},{5,29},{6,30},{7,31},{8,16},{9,... | collective-permute-start | bytes 258056 | tf_op jit(solution)/shard_map/ppermute | solution.py:809
  18.7 7.6 %collective-permute-start.4 = (bf16[1,336,128]{2,1,0:T(8,128)(2,1)}, bf16[1,336,128]{2,1,0:T(8,128)(2,1)S(1)}, u32[]{:S(2)}, u32[]{:S(2)}) collective-permute-start(bf16[1,336,128]{2,1,0:T(8,128)(2,1)} %bitcast.44), channel_id=1, source_target_pairs={{0,16},{1,17},{2,18},{3,19},{4,20},{5,21},{6,22},{7,23},{8,24},{9,... | collective-permute-start | bytes 258056 | tf_op jit(solution)/shard_map/ppermute | solution.py:809
  27.3 11.1 %collective-permute-start.6 = (bf16[4,336,128]{2,1,0:T(8,128)(2,1)S(1)}, bf16[4,336,128]{2,1,0:T(8,128)(2,1)S(1)}, u32[]{:S(2)}, u32[]{:S(2)}) collective-permute-start(bf16[4,336,128]{2,1,0:T(8,128)(2,1)S(1)} %pad_maximum_fusion), channel_id=1, source_target_pairs={{0,2},{1,3},{2,0},{3,1},{4,6},{5,7},{6,4},{7,5},{8,10},{9,11},{10,... | collective-permute-start | bytes 1032200 | tf_op jit(solution)/shard_map/ppermute | solution.py:809
  29.8 19.5 %collective-permute-start.8 = (bf16[4,336,128]{2,1,0:T(8,128)(2,1)S(1)}, bf16[4,336,128]{2,1,0:T(8,128)(2,1)S(1)}, u32[]{:S(2)}, u32[]{:S(2)}) collective-permute-start(bf16[4,336,128]{2,1,0:T(8,128)(2,1)S(1)} %pad_maximum_fusion), channel_id=1, source_target_pairs={{0,6},{1,7},{2,4},{3,5},{4,2},{5,3},{6,0},{7,1},{8,14},{9,15},{10,... | collective-permute-start | bytes 1032200 | tf_op jit(solution)/shard_map/ppermute | solution.py:809
  31.2 18.0 %collective-permute-start.7 = (bf16[4,336,128]{2,1,0:T(8,128)(2,1)S(1)}, bf16[4,336,128]{2,1,0:T(8,128)(2,1)S(1)}, u32[]{:S(2)}, u32[]{:S(2)}) collective-permute-start(bf16[4,336,128]{2,1,0:T(8,128)(2,1)S(1)} %pad_maximum_fusion), channel_id=1, source_target_pairs={{0,4},{1,5},{2,6},{3,7},{4,0},{5,1},{6,2},{7,3},{8,12},{9,13},{10,... | collective-permute-start | bytes 1032200 | tf_op jit(solution)/shard_map/ppermute | solution.py:809
  49.3 27.8 %collective-permute-start.9 = (bf16[16,336,128]{2,1,0:T(8,128)(2,1)S(1)}, bf16[16,336,128]{2,1,0:T(8,128)(2,1)}, u32[]{:S(2)}, u32[]{:S(2)}) collective-permute-start(bf16[16,336,128]{2,1,0:T(8,128)(2,1)S(1)} %constant_dynamic-update-slice_fusion.refs_4_), channel_id=1, source_target_pairs={{0,1},{1,0},{2,3},{3,2},{4,5},{5,4},{6,7},{7,6},{8,9},{9,8},{10,11... | collective-permute-start | bytes 4128776 | tf_op jit(solution)/shard_map/ppermute | solution.py:809
  51.8 19.1 %collective-permute-start = (bf16[256,512]{1,0:T(8,128)(2,1)}, bf16[256,512]{1,0:T(8,128)(2,1)S(1)}, u32[]{:S(2)}, u32[]{:S(2)}) collective-permute-start(bf16[256,512]{1,0:T(8,128)(2,1)} %cut_rows.9), channel_id=1, source_target_pairs={{0,1},{1,0},{2,3},{3,2},{4,5},{5,4},{6,7},{7,6},{8,9},{9,8},{10,11... | collective-permute-start | bytes 786440 | tf_op jit(solution)/shard_map/ppermute | solution.py:809
  54.6 17.8 %collective-permute-start.1 = (bf16[256,512]{1,0:T(8,128)(2,1)}, bf16[256,512]{1,0:T(8,128)(2,1)S(1)}, u32[]{:S(2)}, u32[]{:S(2)}) collective-permute-start(bf16[256,512]{1,0:T(8,128)(2,1)} %cut_rows.10), channel_id=1, source_target_pairs={{0,2},{1,3},{2,0},{3,1},{4,6},{5,7},{6,4},{7,5},{8,10},{9,11},{10,... | collective-permute-start | bytes 786440 | tf_op jit(solution)/shard_map/ppermute | solution.py:809
  58.4 18.7 %collective-permute-start.2 = (bf16[256,512]{1,0:T(8,128)(2,1)}, bf16[256,512]{1,0:T(8,128)(2,1)S(1)}, u32[]{:S(2)}, u32[]{:S(2)}) collective-permute-start(bf16[256,512]{1,0:T(8,128)(2,1)} %cut_rows.11), channel_id=1, source_target_pairs={{0,3},{1,2},{2,1},{3,0},{4,7},{5,6},{6,5},{7,4},{8,11},{9,10},{10,... | collective-permute-start | bytes 786440 | tf_op jit(solution)/shard_map/ppermute | solution.py:809
  60.8 43.5 %collective-permute-start.10 = (bf16[256,512]{1,0:T(8,128)(2,1)}, bf16[256,512]{1,0:T(8,128)(2,1)S(1)}, u32[]{:S(2)}, u32[]{:S(2)}) collective-permute-start(bf16[256,512]{1,0:T(8,128)(2,1)} %cut_rows.13), channel_id=1, source_target_pairs={{0,1},{1,0},{2,3},{3,2},{4,5},{5,4},{6,7},{7,6},{8,9},{9,8},{10,11... | collective-permute-start | bytes 786440 | tf_op jit(solution)/shard_map/ppermute | solution.py:809
  70.9 33.4 %collective-permute-start.11 = (bf16[256,512]{1,0:T(8,128)(2,1)}, bf16[256,512]{1,0:T(8,128)(2,1)S(1)}, u32[]{:S(2)}, u32[]{:S(2)}) collective-permute-start(bf16[256,512]{1,0:T(8,128)(2,1)} %cut_rows.14), channel_id=1, source_target_pairs={{0,2},{1,3},{2,0},{3,1},{4,6},{5,7},{6,4},{7,5},{8,10},{9,11},{10,... | collective-permute-start | bytes 786440 | tf_op jit(solution)/shard_map/ppermute | solution.py:809
  72.4 31.9 %collective-permute-start.12 = (bf16[256,512]{1,0:T(8,128)(2,1)S(1)}, bf16[256,512]{1,0:T(8,128)(2,1)S(1)}, u32[]{:S(2)}, u32[]{:S(2)}) collective-permute-start(bf16[256,512]{1,0:T(8,128)(2,1)S(1)} %copy-done.17), channel_id=1, source_target_pairs={{0,3},{1,2},{2,1},{3,0},{4,7},{5,6},{6,5},{7,4},{8,11},{9,10},{10,... | collective-permute-start | bytes 786440 | tf_op jit(solution)/shard_map/ppermute | solution.py:809
  142.5 39.5 %collective-permute-start.23 = (bf16[16,576,128]{2,1,0:T(8,128)(2,1)}, bf16[16,576,128]{2,1,0:T(8,128)(2,1)S(1)}, u32[]{:S(2)}, u32[]{:S(2)}) collective-permute-start(bf16[16,576,128]{2,1,0:T(8,128)(2,1)} %get-tuple-element.94), channel_id=1, source_target_pairs={{0,1},{1,0},{2,3},{3,2},{4,5},{5,4},{6,7},{7,6},{8,9},{9,8},{10,11... | collective-permute-start | bytes 7077896 | tf_op jit(solution)/shard_map/ppermute | solution.py:809
  180.0 16.7 %collective-permute-start.17 = (bf16[4,336,128]{2,1,0:T(8,128)(2,1)}, bf16[4,336,128]{2,1,0:T(8,128)(2,1)S(1)}, u32[]{:S(2)}, u32[]{:S(2)}) collective-permute-start(bf16[4,336,128]{2,1,0:T(8,128)(2,1)} %get-tuple-element.86), channel_id=1, source_target_pairs={{0,2},{1,3},{2,0},{3,1},{4,6},{5,7},{6,4},{7,5},{8,10},{9,11},{10,... | collective-permute-start | bytes 1032200 | tf_op jit(solution)/shard_map/ppermute | solution.py:809
  181.1 8.7 %collective-permute-start.13 = (bf16[256,512]{1,0:T(8,128)(2,1)}, bf16[256,512]{1,0:T(8,128)(2,1)S(1)}, u32[]{:S(2)}, u32[]{:S(2)}) collective-permute-start(bf16[256,512]{1,0:T(8,128)(2,1)} %get-tuple-element.72), channel_id=1, source_target_pairs={{0,1},{1,0},{2,3},{3,2},{4,5},{5,4},{6,7},{7,6},{8,9},{9,8},{10,11... | collective-permute-start | bytes 786440 | tf_op jit(solution)/shard_map/ppermute | solution.py:809
  181.1 15.6 %collective-permute-start.14 = (bf16[256,512]{1,0:T(8,128)(2,1)}, bf16[256,512]{1,0:T(8,128)(2,1)S(1)}, u32[]{:S(2)}, u32[]{:S(2)}) collective-permute-start(bf16[256,512]{1,0:T(8,128)(2,1)} %get-tuple-element.73), channel_id=1, source_target_pairs={{0,2},{1,3},{2,0},{3,1},{4,6},{5,7},{6,4},{7,5},{8,10},{9,11},{10,... | collective-permute-start | bytes 786440 | tf_op jit(solution)/shard_map/ppermute | solution.py:809
  187.9 44.9 %collective-permute-start.24 = (bf16[4,576,128]{2,1,0:T(8,128)(2,1)}, bf16[4,576,128]{2,1,0:T(8,128)(2,1)S(1)}, u32[]{:S(2)}, u32[]{:S(2)}) collective-permute-start(bf16[4,576,128]{2,1,0:T(8,128)(2,1)} %get-tuple-element.96), channel_id=1, source_target_pairs={{0,2},{1,3},{2,0},{3,1},{4,6},{5,7},{6,4},{7,5},{8,10},{9,11},{10,... | collective-permute-start | bytes 1769480 | tf_op jit(solution)/shard_map/ppermute | solution.py:809
  189.1 44.9 %collective-permute-start.25 = (bf16[4,576,128]{2,1,0:T(8,128)(2,1)}, bf16[4,576,128]{2,1,0:T(8,128)(2,1)S(1)}, u32[]{:S(2)}, u32[]{:S(2)}) collective-permute-start(bf16[4,576,128]{2,1,0:T(8,128)(2,1)} %get-tuple-element.97), channel_id=1, source_target_pairs={{0,4},{1,5},{2,6},{3,7},{4,0},{5,1},{6,2},{7,3},{8,12},{9,13},{10,... | collective-permute-start | bytes 1769480 | tf_op jit(solution)/shard_map/ppermute | solution.py:809
  189.9 47.5 %collective-permute-start.26 = (bf16[4,576,128]{2,1,0:T(8,128)(2,1)}, bf16[4,576,128]{2,1,0:T(8,128)(2,1)S(1)}, u32[]{:S(2)}, u32[]{:S(2)}) collective-permute-start(bf16[4,576,128]{2,1,0:T(8,128)(2,1)} %get-tuple-element.98), channel_id=1, source_target_pairs={{0,6},{1,7},{2,4},{3,5},{4,2},{5,3},{6,0},{7,1},{8,14},{9,15},{10,... | collective-permute-start | bytes 1769480 | tf_op jit(solution)/shard_map/ppermute | solution.py:809
  196.7 35.1 %collective-permute-start.18 = (bf16[4,336,128]{2,1,0:T(8,128)(2,1)}, bf16[4,336,128]{2,1,0:T(8,128)(2,1)S(1)}, u32[]{:S(2)}, u32[]{:S(2)}) collective-permute-start(bf16[4,336,128]{2,1,0:T(8,128)(2,1)} %get-tuple-element.87), channel_id=1, source_target_pairs={{0,4},{1,5},{2,6},{3,7},{4,0},{5,1},{6,2},{7,3},{8,12},{9,13},{10,... | collective-permute-start | bytes 1032200 | tf_op jit(solution)/shard_map/ppermute | solution.py:809
  197.4 34.4 %collective-permute-start.19 = (bf16[4,336,128]{2,1,0:T(8,128)(2,1)}, bf16[4,336,128]{2,1,0:T(8,128)(2,1)S(1)}, u32[]{:S(2)}, u32[]{:S(2)}) collective-permute-start(bf16[4,336,128]{2,1,0:T(8,128)(2,1)} %get-tuple-element.88), channel_id=1, source_target_pairs={{0,6},{1,7},{2,4},{3,5},{4,2},{5,3},{6,0},{7,1},{8,14},{9,15},{10,... | collective-permute-start | bytes 1032200 | tf_op jit(solution)/shard_map/ppermute | solution.py:809
  231.8 10.3 %collective-permute-start.15 = (bf16[256,512]{1,0:T(8,128)(2,1)}, bf16[256,512]{1,0:T(8,128)(2,1)}, u32[]{:S(2)}, u32[]{:S(2)}) collective-permute-start(bf16[256,512]{1,0:T(8,128)(2,1)} %get-tuple-element.74), channel_id=1, source_target_pairs={{0,3},{1,2},{2,1},{3,0},{4,7},{5,6},{6,5},{7,4},{8,11},{9,10},{10,... | collective-permute-start | bytes 786440 | tf_op jit(solution)/shard_map/ppermute | solution.py:809
  231.9 11.3 %collective-permute-start.30 = (bf16[256,512]{1,0:T(8,128)(2,1)}, bf16[256,512]{1,0:T(8,128)(2,1)}, u32[]{:S(2)}, u32[]{:S(2)}) collective-permute-start(bf16[256,512]{1,0:T(8,128)(2,1)} %get-tuple-element.104), channel_id=1, source_target_pairs={{0,1},{1,0},{2,3},{3,2},{4,5},{5,4},{6,7},{7,6},{8,9},{9,8},{10,11... | collective-permute-start | bytes 786440 | tf_op jit(solution)/shard_map/ppermute | solution.py:809
  232.8 12.4 %collective-permute-start.31 = (bf16[256,512]{1,0:T(8,128)(2,1)}, bf16[256,512]{1,0:T(8,128)(2,1)}, u32[]{:S(2)}, u32[]{:S(2)}) collective-permute-start(bf16[256,512]{1,0:T(8,128)(2,1)} %get-tuple-element.105), channel_id=1, source_target_pairs={{0,2},{1,3},{2,0},{3,1},{4,6},{5,7},{6,4},{7,5},{8,10},{9,11},{10,... | collective-permute-start | bytes 786440 | tf_op jit(solution)/shard_map/ppermute | solution.py:809
  234.0 17.4 %collective-permute-start.32 = (bf16[256,512]{1,0:T(8,128)(2,1)S(1)}, bf16[256,512]{1,0:T(8,128)(2,1)}, u32[]{:S(2)}, u32[]{:S(2)}) collective-permute-start(bf16[256,512]{1,0:T(8,128)(2,1)S(1)} %copy-done.25), channel_id=1, source_target_pairs={{0,3},{1,2},{2,1},{3,0},{4,7},{5,6},{6,5},{7,4},{8,11},{9,10},{10,... | collective-permute-start | bytes 786440 | tf_op jit(solution)/shard_map/ppermute | solution.py:809
  237.3 14.1 %collective-permute-start.20 = (bf16[1,336,128]{2,1,0:T(8,128)(2,1)}, bf16[1,336,128]{2,1,0:T(8,128)(2,1)S(1)}, u32[]{:S(2)}, u32[]{:S(2)}) collective-permute-start(bf16[1,336,128]{2,1,0:T(8,128)(2,1)} %get-tuple-element.90), channel_id=1, source_target_pairs={{0,8},{1,9},{2,10},{3,11},{4,12},{5,13},{6,14},{7,15},{8,0},{9,1},... | collective-permute-start | bytes 258056 | tf_op jit(solution)/shard_map/ppermute | solution.py:809
  242.2 23.7 %collective-permute-start.27 = (bf16[1,576,128]{2,1,0:T(8,128)(2,1)}, bf16[1,576,128]{2,1,0:T(8,128)(2,1)S(1)}, u32[]{:S(2)}, u32[]{:S(2)}) collective-permute-start(bf16[1,576,128]{2,1,0:T(8,128)(2,1)} %get-tuple-element.100), channel_id=1, source_target_pairs={{0,8},{1,9},{2,10},{3,11},{4,12},{5,13},{6,14},{7,15},{8,0},{9,1},... | collective-permute-start | bytes 442376 | tf_op jit(solution)/shard_map/ppermute | solution.py:809
  243.2 22.7 %collective-permute-start.28 = (bf16[1,576,128]{2,1,0:T(8,128)(2,1)}, bf16[1,576,128]{2,1,0:T(8,128)(2,1)S(1)}, u32[]{:S(2)}, u32[]{:S(2)}) collective-permute-start(bf16[1,576,128]{2,1,0:T(8,128)(2,1)} %get-tuple-element.101), channel_id=1, source_target_pairs={{0,16},{1,17},{2,18},{3,19},{4,20},{5,21},{6,22},{7,23},{8,24},{9,... | collective-permute-start | bytes 442376 | tf_op jit(solution)/shard_map/ppermute | solution.py:809
  245.3 20.6 %collective-permute-start.29 = (bf16[1,576,128]{2,1,0:T(8,128)(2,1)}, bf16[1,576,128]{2,1,0:T(8,128)(2,1)S(1)}, u32[]{:S(2)}, u32[]{:S(2)}) collective-permute-start(bf16[1,576,128]{2,1,0:T(8,128)(2,1)} %get-tuple-element.102), channel_id=1, source_target_pairs={{0,24},{1,25},{2,26},{3,27},{4,28},{5,29},{6,30},{7,31},{8,16},{9,... | collective-permute-start | bytes 442376 | tf_op jit(solution)/shard_map/ppermute | solution.py:809
  251.4 14.4 %collective-permute-start.21 = (bf16[1,336,128]{2,1,0:T(8,128)(2,1)S(1)}, bf16[1,336,128]{2,1,0:T(8,128)(2,1)S(1)}, u32[]{:S(2)}, u32[]{:S(2)}) collective-permute-start(bf16[1,336,128]{2,1,0:T(8,128)(2,1)S(1)} %copy-done.30), channel_id=1, source_target_pairs={{0,16},{1,17},{2,18},{3,19},{4,20},{5,21},{6,22},{7,23},{8,24},{9,... | collective-permute-start | bytes 258056 | tf_op jit(solution)/shard_map/ppermute | solution.py:809
  251.4 14.4 %collective-permute-start.22 = (bf16[1,336,128]{2,1,0:T(8,128)(2,1)S(1)}, bf16[1,336,128]{2,1,0:T(8,128)(2,1)S(1)}, u32[]{:S(2)}, u32[]{:S(2)}) collective-permute-start(bf16[1,336,128]{2,1,0:T(8,128)(2,1)S(1)} %copy-done.29), channel_id=1, source_target_pairs={{0,24},{1,25},{2,26},{3,27},{4,28},{5,29},{6,30},{7,31},{8,16},{9,... | collective-permute-start | bytes 258056 | tf_op jit(solution)/shard_map/ppermute | solution.py:809
  (33 other events, 273.5 us)
Sparse Core Ops, SparseCore 0:
  10.9 76.1 all-gather.2
where the time goes:
time: 278 us; the launch traced here: 277 us
  Pallas kernels  132 us (47%)
  waiting for transfers between devices  85.1 us (31%)
  starting transfers between devices  31.8 us (11%)
  between operations  14.3 us (5%)
  local copies, waits for them, and re-layouts  9.96 us (4%)
  other arithmetic  3.51 us (1%)
    ppermute x33, waiting for transfers between devices, swap(): lax.ppermute(value, AXES, [(d, d ^ mask) for d in range(devices)])  85.1 us
    pallas_call x1, Pallas kernels, feed(): pl.pallas_call(functools.partial(feed_kernel, plan, count), grid_spec=plt...  37.4 us
    ppermute x33, starting transfers between devices, swap(): lax.ppermute(value, AXES, [(d, d ^ mask) for d in range(devices)])  31.8 us
    pallas_call x1, Pallas kernels, attend_back(): pl.pallas_call(functools.partial(attend_back_kernel, plan, count), grid_s...  29.1 us
    pallas_call x1, Pallas kernels, attend(): pl.pallas_call(functools.partial(attend_kernel, plan, len(pieces)), grid_...  22 us
    pallas_call x8, Pallas kernels, one(): pl.pallas_call(cut_kernel, grid_spec=pltpu.PrefetchScalarGridSpec(num_sca...  18.8 us
    pallas_call x4, Pallas kernels, fold(): pl.pallas_call(functools.partial(fold_kernel, len(terms)), grid=(pieces,)...  14.8 us
    unnamed x68, local copies, waits for them, and re-layouts  9.92 us
  transfers between devices with their start and end apart: 34, of which 11 were waited for; matrix products, arithmetic and copies ran while one was open for 2% of the time, Pallas kernels for 32%

commit v1 on v0

--- a/solution.py
+++ b/solution.py
@@ -93,10 +93,15 @@
             inward_ref[piece, rows, :] = shard[at * TILE : (at + 1) * TILE, :]
         at = plan.early_pieces * TILE
         stage_ref[pl.ds(owner, 1), :, :] = shard[at : at + TILE, :].astype(F32)[None]
+    lane = lax.broadcasted_iota(jnp.int32, (1, LANE), 1)
     for vector, length in enumerate(plan.lengths):
-        group = LANE // plan.owned[vector]
+        size = plan.owned[vector]
+        group = LANE // size
         for block in range(length // LANE):
-            row = jnp.sum(stage_ref[block * group : (block + 1) * group, vector, :], axis=0, keepdims=True)
+            row = jnp.zeros((1, LANE), F32)
+            for index in range(group):
+                own = stage_ref[block * group + index, vector : vector + 1, :]
+                row = jnp.where(lane // size == index, own, row)
             at = plan.block_starts[vector] + block
             small_ref[at // plan.lanes : at // plan.lanes + 1, (at % plan.lanes) * LANE : (at % plan.lanes + 1) * LANE] = row
 
@@ -238,7 +243,7 @@
             like(inward, BF),
             like(small, F32),
         ],
-        compiler_params=params(48),
+        compiler_params=params(60),
         cost_estimate=cost(5 * 10**9, 14 * 2**20, 6 * 10**6),
         name="attend",
     )(info, *pieces, *weights)
@@ -616,40 +621,28 @@
     return values[:count], values[count:]
 
 
-def pack_early_kernel(plan, info_ref, table_ref, inward_ref, *refs):
+def pack_early_kernel(plan, table_ref, inward_ref, *refs):
     vectors, out_ref = refs[:VECTORS], refs[VECTORS]
-    me = info_ref[1]
     for piece in range(plan.table_pieces):
         out_ref[piece * TILE : (piece + 1) * TILE, :] = table_ref[:, piece * LANE : (piece + 1) * LANE]
     for piece in range(3 * plan.lanes):
         at = (plan.table_pieces + piece) * TILE
         out_ref[at : at + TILE, :] = inward_ref[:, piece * LANE : (piece + 1) * LANE]
-    lane = lax.broadcasted_iota(jnp.int32, (1, LANE), 1)
     rows = []
-    for vector, ref in zip(range(VECTORS), vectors):
-        size = plan.owned[vector]
-        wide = jnp.concatenate([ref[...].astype(F32)] * (LANE // size), axis=1)
-        slot = lax.rem(me, LANE // size)
-        rows.append(jnp.where(lane // size == slot, wide, 0.0))
+    for size, ref in zip(plan.owned, vectors):
+        rows.append(jnp.concatenate([ref[...].astype(F32)] * (LANE // size), axis=1))
     rows.append(jnp.zeros((TILE - VECTORS, LANE), F32))
     at = plan.early_pieces * TILE
     out_ref[at : at + TILE, :] = jnp.concatenate(rows, axis=0).astype(BF)
 
 
-def pack_early(plan, info, table, inward, vectors):
+def pack_early(plan, table, inward, vectors):
     values = [table, inward] + [v.reshape(1, -1) for v in vectors]
-    out = (plan.early_rows, LANE)
     return pl.pallas_call(
         functools.partial(pack_early_kernel, plan),
-        grid_spec=pltpu.PrefetchScalarGridSpec(
-            num_scalar_prefetch=1,
-            grid=(1,),
-            in_specs=[full(v.shape) for v in values],
-            out_specs=full(out),
-        ),
-        out_shape=like(out, BF),
+        out_shape=like((plan.early_rows, LANE), BF),
         name="pack_early",
-    )(info, *values)
+    )(*values)
 
 
 def pack_late_kernel(plan, outward_ref, expand_ref, contract_ref, out_ref):
@@ -767,27 +760,20 @@
     )(info, *pieces)
 
 
-def cut_kernel(*refs):
-    refs[2][...] = refs[1][0]
-
-
-def cut_rows(info, rows, count, share):
-    def one(mask):
-        return pl.pallas_call(
-            cut_kernel,
-            grid_spec=pltpu.PrefetchScalarGridSpec(
-                num_scalar_prefetch=1,
-                grid=(1,),
-                in_specs=[
-                    pl.BlockSpec((1,) + rows.shape[1:], lambda i, info: ((info[2] ^ mask) // share, 0, 0))
-                ],
-                out_specs=full(rows.shape[1:]),
-            ),
-            out_shape=like(rows.shape[1:], BF),
-            name="cut_rows",
-        )(info, rows)
-
-    return [one(mask) for mask in range(count)]
+def cut_kernel(count, share, rows_ref, *refs):
+    rank = lax.axis_index("seq")
+    for mask in range(count):
+        refs[mask][...] = rows_ref[pl.ds((rank ^ mask) // share, 1), :, :][0]
+
+
+def cut_rows(rows, count, share):
+    outs = [like(rows.shape[1:], BF)] * count
+    return pl.pallas_call(
+        functools.partial(cut_kernel, count, share),
+        out_shape=outs,
+        cost_estimate=cost(0, 4 * 2**20),
+        name="cut_rows",
+    )(rows)
 
 
 def local(tokens, first_length, cotangent, positions, inward, intake, outward, outlet, steady, offset,
@@ -811,45 +797,63 @@
     def exchange(pieces):
         return [swap(piece, mask) for mask, piece in enumerate(pieces)]
 
-    rows_in = exchange(cut_rows(info, tokens[:, 0], count, share))
-    upstreams = exchange(cut_rows(info, cotangent[:, 0], count, share))
     if plan.packed:
-        shard = pack_early(plan, info, positions.T, inward, vectors)[None]
+        shard = pack_early(plan, positions.T, inward, vectors)[None]
         late_shard = pack_late(plan, outward, expand, contract)
-        shard = jnp.concatenate([swap(shard, k << 3) for k in range(4)], axis=0)
-        shard = jnp.concatenate([swap(shard, k << 1) for k in range(4)], axis=0)
+        rows_in = cut_rows(tokens[:, 0], count, share)
+        shard, late_shard, rows_in = lax.optimization_barrier((shard, late_shard, rows_in))
+        late = [lax.all_gather(late_shard, AXES, axis=0, tiled=False)]
+        pieces = [swap(shard, k << 3) for k in range(4)]
+        pieces, rows_in = lax.optimization_barrier((pieces, exchange(rows_in)))
+        shard = jnp.concatenate(pieces, axis=0)
+        pieces = [swap(shard, k << 1) for k in range(4)]
+        upstreams = cut_rows(cotangent[:, 0], count, share)
+        pieces, upstreams = lax.optimization_barrier((pieces, upstreams))
+        shard = jnp.concatenate(pieces, axis=0)
         early = [shard, swap(shard, 1)]
-        late = lax.all_gather(late_shard, AXES, axis=0, tiled=False)
-        late = [late]
+        upstreams = exchange(upstreams)
     else:
+        rows_in = exchange(cut_rows(tokens[:, 0], count, share))
+        upstreams = exchange(cut_rows(cotangent[:, 0], count, share))
         early, late = plain_weights(plan, positions, inward, vectors, outward, expand, contract)
     lifted, query, key, value, mixed, totals, inward_all, small = attend(plan, info, rows_in, early)
     results, (mixed_back, first_back, small_grad), late_grads = feed(
         plan, info, lifted, mixed, upstreams, late, small
     )
-    output = settle_rows(info, micro_count, share, exchange(results))
+    results = exchange(results)
     if plan.packed:
         keep, send = late_grads
         terms = fold([keep, swap(send, 1)], 4)
-        terms = [swap(term, k << 1) for k, term in enumerate(terms)]
+        terms, mixed_back = lax.optimization_barrier((terms, mixed_back))
+        late_terms = [swap(term, k << 1) for k, term in enumerate(terms)]
     token_pieces, early_grads = attend_back(
         plan, info, count, lifted, (query, key, value, mixed, totals), mixed_back, inward_all,
         first_back, small_grad,
     )
-    token_pieces = exchange(token_pieces)
     if plan.packed:
+        late_terms, results, token_pieces, early_grads = lax.optimization_barrier(
+            (late_terms, results, token_pieces, early_grads)
+        )
+        keep, send = early_grads
+        send = swap(send, 1)
+        late_terms = fold(late_terms, 4)
+        output = settle_rows(info, micro_count, share, results)
+        send, late_terms, output = lax.optimization_barrier((send, late_terms, output))
+        terms = fold([keep, send], 4)
+        terms, late_terms = lax.optimization_barrier((terms, late_terms))
+        terms = [swap(term, k << 1) for k, term in enumerate(terms)]
+        late_terms = [swap(term, k << 3) for k, term in enumerate(late_terms)]
+        terms, late_terms, token_pieces = lax.optimization_barrier((terms, late_terms, token_pieces))
+        token_pieces = exchange(token_pieces)
         terms = fold(terms, 4)
-        late_terms = [swap(term, k << 3) for k, term in enumerate(terms)]
-        keep, send = early_grads
-        terms = fold([keep, swap(send, 1)], 4)
-        terms = fold([swap(term, k << 1) for k, term in enumerate(terms)], 4)
         early_terms = [swap(term, k << 3) for k, term in enumerate(terms)]
         values = finish(plan, info, micro_count, early_terms, late_terms, token_pieces)
         tokens_back, table_t, inward_own, outward_own, expand_own, contract_own = values[:6]
         own = [v.reshape(-1) for v in values[6:]]
         table_own = table_t.T
     else:
-        tokens_back = settle_rows(info, micro_count, share, token_pieces)
+        output = settle_rows(info, micro_count, share, results)
+        tokens_back = settle_rows(info, micro_count, share, exchange(token_pieces))
         table_own, inward_own, outward_own, expand_own, contract_own, own = plain_grads(
             plan, counted, early_grads, late_grads
         )

time: 278 us -> 229 us (0.82)
  waiting for transfers between devices: 85.1 us -> 53.9 us
  Pallas kernels: 132 us -> 117 us
  starting transfers between devices: 31.8 us -> 35.7 us
  local copies, waits for them, and re-layouts: 9.96 us -> 6.1 us
    ppermute x33, waiting for transfers between devices: 85.1 us -> 45.7 us  [swap(): lax.ppermute(value, AXES, [(d, d ^ mask) for d in range(devices)])]
    pallas_call x9 -> x3, Pallas kernels: 21.1 us -> 6.09 us  [the longest x2 4.52 us: cut_rows(): pl.pallas_call(functools.partial(cut_kernel, count, share), out_shape=out...]
    all_gather x1, waiting for transfers between devices: 0.02 us -> 8.12 us  [local(): late = [lax.all_gather(late_shard, AXES, axis=0, tiled=False)]]
    ppermute x33, starting transfers between devices: 31.8 us -> 35.6 us  [swap(): lax.ppermute(value, AXES, [(d, d ^ mask) for d in range(devices)])]
    unnamed x68 -> x72, local copies, waits for them, and re-layouts: 9.92 us -> 6.04 us
  transfers between devices with their start and end apart: 34 -> 34, of which waited for: 11 -> 13; matrix products, arithmetic and copies ran while one was open for 2% -> 1% of each run, Pallas kernels for 32% -> 29%
where the time goes in v1:
time: 229 us
  Pallas kernels  117 us (51%)
  waiting for transfers between devices  53.9 us (24%)
  starting transfers between devices  35.7 us (16%)
  between operations  14.5 us (6%)
  local copies, waits for them, and re-layouts  6.1 us (3%)
    ppermute x33, waiting for transfers between devices, swap(): lax.ppermute(value, AXES, [(d, d ^ mask) for d in range(devices)])  45.7 us
    pallas_call x1, Pallas kernels, feed(): pl.pallas_call(functools.partial(feed_kernel, plan, count), grid_spec=plt...  37.4 us
    ppermute x33, starting transfers between devices, swap(): lax.ppermute(value, AXES, [(d, d ^ mask) for d in range(devices)])  35.6 us
    pallas_call x1, Pallas kernels, attend_back(): pl.pallas_call(functools.partial(attend_back_kernel, plan, count), grid_s...  29.2 us
    pallas_call x1, Pallas kernels, attend(): pl.pallas_call(functools.partial(attend_kernel, plan, len(pieces)), grid_...  21.2 us
    pallas_call x4, Pallas kernels, fold(): pl.pallas_call(functools.partial(fold_kernel, len(terms)), grid=(pieces,)...  14.9 us
    all_gather x1, waiting for transfers between devices, local(): late = [lax.all_gather(late_shard, AXES, axis=0, tiled=False)]  8.12 us
    unnamed x72, local copies, waits for them, and re-layouts  6.04 us
  transfers between devices with their start and end apart: 34, of which 13 were waited for; matrix products, arithmetic and copies ran while one was open for 1% of the time, Pallas kernels for 29%

profile of v1, /device:TPU:0, one launch (start us, length us, event | category | flops | bytes accessed | tf_op | source)
XLA Modules:
  0.0 228.6 jit_solution(1569384730818212629)
XLA Ops:
  7.2 2.3 cut_rows.2
  11.0 1.6 pack_early.1
  13.2 2.6 %collective-permute-start.4 = (bf16[256,512]{1,0:T(8,128)(2,1)}, bf16[256,512]{1,0:T(8,128)(2,1)S(1)}, u32[]{:S(2)}, u32[]{:S(2)}) collective-permute-start(bf16[256,512]{1,0:T(8,128)(2,1)} %get-tuple-element.150), channel_id=1, source_target_pairs={{0,2},{1,3},{2,0},{3,1},{4,6},{5,7},{6,4},{7,5},{8,10},{9,11},{10,... | collective-permute-start | bytes 786440 | tf_op jit(solution)/shard_map/ppermute | solution.py:795
  15.8 3.9 %collective-permute-start.2 = (bf16[1,336,128]{2,1,0:T(8,128)(2,1)}, bf16[1,336,128]{2,1,0:T(8,128)(2,1)S(1)}, u32[]{:S(2)}, u32[]{:S(2)}) collective-permute-start(bf16[1,336,128]{2,1,0:T(8,128)(2,1)} %bitcast.36), channel_id=1, source_target_pairs={{0,24},{1,25},{2,26},{3,27},{4,28},{5,29},{6,30},{7,31},{8,16},{9,... | collective-permute-start | bytes 258056 | tf_op jit(solution)/shard_map/ppermute | solution.py:795
  19.7 3.6 %collective-permute-done.2 = bf16[1,336,128]{2,1,0:T(8,128)(2,1)S(1)} collective-permute-done((bf16[1,336,128]{2,1,0:T(8,128)(2,1)}, bf16[1,336,128]{2,1,0:T(8,128)(2,1)S(1)}, u32[]{:S(2)}, u32[]{:S(2)}) %collective-permute-start.2) | collective-permute-done | bytes 86048 | tf_op jit(solution)/shard_map/ppermute | solution.py:795
  23.2 3.6 %collective-permute-start = (bf16[1,336,128]{2,1,0:T(8,128)(2,1)}, bf16[1,336,128]{2,1,0:T(8,128)(2,1)S(1)}, u32[]{:S(2)}, u32[]{:S(2)}) collective-permute-start(bf16[1,336,128]{2,1,0:T(8,128)(2,1)} %bitcast.38), channel_id=1, source_target_pairs={{0,8},{1,9},{2,10},{3,11},{4,12},{5,13},{6,14},{7,15},{8,0},{9,1},... | collective-permute-start | bytes 258056 | tf_op jit(solution)/shard_map/ppermute | solution.py:795
  27.6 2.9 %collective-permute-done = bf16[1,336,128]{2,1,0:T(8,128)(2,1)S(1)} collective-permute-done((bf16[1,336,128]{2,1,0:T(8,128)(2,1)}, bf16[1,336,128]{2,1,0:T(8,128)(2,1)S(1)}, u32[]{:S(2)}, u32[]{:S(2)}) %collective-permute-start) | collective-permute-done | bytes 86048 | tf_op jit(solution)/shard_map/ppermute | solution.py:795
  31.6 2.6 %collective-permute-start.8 = (bf16[4,336,128]{2,1,0:T(8,128)(2,1)S(1)}, bf16[4,336,128]{2,1,0:T(8,128)(2,1)S(1)}, u32[]{:S(2)}, u32[]{:S(2)}) collective-permute-start(bf16[4,336,128]{2,1,0:T(8,128)(2,1)S(1)} %constant_dynamic-update-slice_fusion), channel_id=1, source_target_pairs={{0,6},{1,7},{2,4},{3,5},{4,2},{5,3},{6,0},{7,1},{8,14},{9,15},{10,... | collective-permute-start | bytes 1032200 | tf_op jit(solution)/shard_map/ppermute | solution.py:795
  35.2 2.3 cut_rows.3
  37.4 6.1 %collective-permute-done.8 = bf16[4,336,128]{2,1,0:T(8,128)(2,1)S(1)} collective-permute-done((bf16[4,336,128]{2,1,0:T(8,128)(2,1)S(1)}, bf16[4,336,128]{2,1,0:T(8,128)(2,1)S(1)}, u32[]{:S(2)}, u32[]{:S(2)}) %collective-permute-start.8) | collective-permute-done | bytes 344096 | tf_op jit(solution)/shard_map/ppermute | solution.py:795
  43.6 8.4 %collective-permute-done.7 = bf16[4,336,128]{2,1,0:T(8,128)(2,1)S(1)} collective-permute-done((bf16[4,336,128]{2,1,0:T(8,128)(2,1)S(1)}, bf16[4,336,128]{2,1,0:T(8,128)(2,1)S(1)}, u32[]{:S(2)}, u32[]{:S(2)}) %collective-permute-start.7) | collective-permute-done | bytes 344096 | tf_op jit(solution)/shard_map/ppermute | solution.py:795
  51.9 2.2 collective-permute-done.6
  59.7 21.2 %attend.1 = (f32[1024,512]{1,0:T(8,128)}, bf16[1024,512]{1,0:T(8,128)(2,1)}, bf16[1024,512]{1,0:T(8,128)(2,1)}, bf16[1024,512]{1,0:T(8,128)(2,1)}, bf16[1024,512...) custom-call(s32[4]{0:T(128)} %pad_add_fusion.info_ref, ...), custom_call_target="tpu_custom_call" | custom-call | flops 5000000000 | bytes 14680064 | tf_op jit(solution)/shard_map/attend/pallas_call | solution.py:213
  80.9 8.1 %all-gather.3.cloned.1.call-done = bf16[18432,128]{1,0:T(8,128)(2,1)} async-done(((bf16[576,128]{1,0:T(8,128)(2,1)}), bf16[18432,128]{1,0:T(8,128)(2,1)}) %all-gather.3.cloned.1.call-update) | async-done | bytes 4718608 | tf_op jit(solution)/shard_map/all_gather | solution.py:805
  89.0 37.4 %feed.1 = (bf16[256,512]{1,0:T(8,128)(2,1)}, bf16[256,512]{1,0:T(8,128)(2,1)}, bf16[256,512]{1,0:T(8,128)(2,1)}, bf16[256,512]{1,0:T(8,128)(2,1)}, bf16[1024,512...) custom-call(s32[4]{0:T(128)} %pad_add_fusion.info_ref, ...), custom_call_target="tpu_custom_call" | custom-call | flops 15000000512 | bytes 20971520 | tf_op jit(solution)/shard_map/feed/pallas_call | solution.py:418
  128.6 2.6 %collective-permute-done.13.refs_1_ = bf16[16,576,128]{2,1,0:T(8,128)(2,1)S(1)} collective-permute-done((bf16[16,576,128]{2,1,0:T(8,128)(2,1)}, bf16[16,576,128]{2,1,0:T(8,128)(2,1)S(1)}, u32[]{:S(2)}, u32[]{:S(2)}) %collective-permute-start.13) | collective-permute-done | bytes 2359328 | tf_op jit(solution)/shard_map/ppermute | solution.py:795
  132.6 4.5 %fold.4 = (bf16[4,576,128]{2,1,0:T(8,128)(2,1)}, bf16[4,576,128]{2,1,0:T(8,128)(2,1)}, bf16[4,576,128]{2,1,0:T(8,128)(2,1)}, bf16[4,576,128]{2,1,0:T(8,128)(2,1)}) custom-call(bf16[16,576,128]{2,1,0:T(8,128)(2,1)} %get-tuple-element.176.refs_0_, bf16[16,576,128]{2,1,0:T(8,128)(2,1)} %copy-done), custom_call_target="tpu_custom_call" | custom-call | flops 1000000 | bytes 9437184 | tf_op jit(solution)/shard_map/fold/pallas_call | solution.py:679
  138.7 1.9 collective-permute-start.16
  140.6 29.2 %attend_back.1 = (bf16[256,512]{1,0:T(8,128)(2,1)}, bf16[256,512]{1,0:T(8,128)(2,1)}, bf16[256,512]{1,0:T(8,128)(2,1)}, bf16[256,512]{1,0:T(8,128)(2,1)}, bf16[1...) custom-call(s32[4]{0:T(128)} %pad_add_fusion.info_ref, f32[1024,512]{1,0:T(8,128)} %get-tuple-element.168.lifted_ref, ...), custom_call_target="tpu_custom_call" | custom-call | flops 14000000000 | bytes 25165824 | tf_op jit(solution)/shard_map/attend_back/pallas_call | solution.py:587
  170.0 2.9 %settle_rows.1 = bf16[4,256,512]{2,1,0:T(8,128)(2,1)} custom-call(s32[4]{0:T(128)} %pad_add_fusion.info_ref, bf16[256,512]{1,0:T(8,128)(2,1)} %get-tuple-element.214.refs_0_, bf16[256,512]{1,0:T(8,128)(2,1)} %copy-done.8, bf16[256,512]{1,0:T(8,128)(2,1)} %collective-permute-done.18.refs_2_, bf16[256,512]{1,0:T(8,128)(2,1)} %collective-permute-done.19.refs_3_), custom_call_target="tpu_custom_call" | custom-call | tf_op jit(solution)/shard_map/settle_rows/pallas_call | solution.py:750
  172.9 3.6 %fold.5 = (bf16[1,576,128]{2,1,0:T(8,128)(2,1)}, bf16[1,576,128]{2,1,0:T(8,128)(2,1)}, bf16[1,576,128]{2,1,0:T(8,128)(2,1)}, bf16[1,576,128]{2,1,0:T(8,128)(2,1)}) custom-call(bf16[4,576,128]{2,1,0:T(8,128)(2,1)} %get-tuple-element.206.refs_0_, bf16[4,576,128]{2,1,0:T(8,128)(2,1)} %copy-done.2, bf16[4,576,128]{2,1,0:T(8,128)(2,1)} %copy-done.3, ...), custom_call_target="tpu_custom_call" | custom-call | flops 1000000 | bytes 4718592 | tf_op jit(solution)/shard_map/fold/pallas_call | solution.py:679
  177.6 3.8 %fold.6 = (bf16[4,336,128]{2,1,0:T(8,128)(2,1)}, bf16[4,336,128]{2,1,0:T(8,128)(2,1)}, bf16[4,336,128]{2,1,0:T(8,128)(2,1)}, bf16[4,336,128]{2,1,0:T(8,128)(2,1)}) custom-call(bf16[16,336,128]{2,1,0:T(8,128)(2,1)} %get-tuple-element.219.refs_0_, bf16[16,336,128]{2,1,0:T(8,128)(2,1)} %copy-done.1), custom_call_target="tpu_custom_call" | custom-call | flops 1000000 | bytes 5505024 | tf_op jit(solution)/shard_map/fold/pallas_call | solution.py:679
  183.0 1.9 collective-permute-start.23
  187.0 5.2 %collective-permute-done.24.refs_5_ = bf16[1,576,128]{2,1,0:T(8,128)(2,1)S(1)} collective-permute-done((bf16[1,576,128]{2,1,0:T(8,128)(2,1)S(1)}, bf16[1,576,128]{2,1,0:T(8,128)(2,1)S(1)}, u32[]{:S(2)}, u32[]{:S(2)}) %collective-permute-start.24) | collective-permute-done | bytes 147488 | tf_op jit(solution)/shard_map/ppermute | solution.py:795
  192.3 1.8 collective-permute-start.26
  194.0 5.7 %collective-permute-done.25.refs_6_ = bf16[1,576,128]{2,1,0:T(8,128)(2,1)S(1)} collective-permute-done((bf16[1,576,128]{2,1,0:T(8,128)(2,1)S(1)}, bf16[1,576,128]{2,1,0:T(8,128)(2,1)S(1)}, u32[]{:S(2)}, u32[]{:S(2)}) %collective-permute-start.25) | collective-permute-done | bytes 147488 | tf_op jit(solution)/shard_map/ppermute | solution.py:795
  202.2 3.0 %fold.7 = (bf16[1,336,128]{2,1,0:T(8,128)(2,1)}, bf16[1,336,128]{2,1,0:T(8,128)(2,1)}, bf16[1,336,128]{2,1,0:T(8,128)(2,1)}, bf16[1,336,128]{2,1,0:T(8,128)(2,1)}) custom-call(bf16[4,336,128]{2,1,0:T(8,128)(2,1)} %get-tuple-element.241.refs_0_, bf16[4,336,128]{2,1,0:T(8,128)(2,1)} %copy-done.5, bf16[4,336,128]{2,1,0:T(8,128)(2,1)} %copy-done.6, ...), custom_call_target="tpu_custom_call" | custom-call | flops 1000000 | bytes 2752512 | tf_op jit(solution)/shard_map/fold/pallas_call | solution.py:679
  205.1 2.3 %collective-permute-start.27 = (bf16[1,336,128]{2,1,0:T(8,128)(2,1)}, bf16[1,336,128]{2,1,0:T(8,128)(2,1)S(1)}, u32[]{:S(2)}, u32[]{:S(2)}) collective-permute-start(bf16[1,336,128]{2,1,0:T(8,128)(2,1)} %get-tuple-element.246), channel_id=1, source_target_pairs={{0,8},{1,9},{2,10},{3,11},{4,12},{5,13},{6,14},{7,15},{8,0},{9,1},... | collective-permute-start | bytes 258056 | tf_op jit(solution)/shard_map/ppermute | solution.py:795
  207.8 2.8 %collective-permute-done.27.refs_1_ = bf16[1,336,128]{2,1,0:T(8,128)(2,1)S(1)} collective-permute-done((bf16[1,336,128]{2,1,0:T(8,128)(2,1)}, bf16[1,336,128]{2,1,0:T(8,128)(2,1)S(1)}, u32[]{:S(2)}, u32[]{:S(2)}) %collective-permute-start.27) | collective-permute-done | bytes 86048 | tf_op jit(solution)/shard_map/ppermute | solution.py:795
  210.7 1.7 collective-permute-start.29
  212.4 4.9 %collective-permute-done.28.refs_2_ = bf16[1,336,128]{2,1,0:T(8,128)(2,1)S(1)} collective-permute-done((bf16[1,336,128]{2,1,0:T(8,128)(2,1)}, bf16[1,336,128]{2,1,0:T(8,128)(2,1)S(1)}, u32[]{:S(2)}, u32[]{:S(2)}) %collective-permute-start.28) | collective-permute-done | bytes 86048 | tf_op jit(solution)/shard_map/ppermute | solution.py:795
  218.3 3.4 %finish.1 = (bf16[4,256,512]{2,1,0:T(8,128)(2,1)}, f32[16,1024]{1,0:T(8,128)}, f32[16,1536]{1,0:T(8,128)}, f32[16,512]{1,0:T(8,128)}, f32[16,2048]{1,0:T(8,128)}...) custom-call(s32[4]{0:T(128)} %pad_add_fusion.info_ref, ...), custom_call_target="tpu_custom_call" | custom-call | tf_op jit(solution)/shard_map/finish/pallas_call | solution.py:730
  (126 shorter events, 24.2 us)
Async XLA Ops:
  7.2 81.8 %all-gather.3.cloned.1.call-start = ((), (), s32[]{:S(2)}) async-start(), calls=%async_computation | async-start | bytes 4866048 | tf_op jit(solution)/shard_map/all_gather | solution.py:805
  12.6 17.9 %collective-permute-start.3 = (bf16[256,512]{1,0:T(8,128)(2,1)}, bf16[256,512]{1,0:T(8,128)(2,1)S(1)}, u32[]{:S(2)}, u32[]{:S(2)}) collective-permute-start(bf16[256,512]{1,0:T(8,128)(2,1)} %get-tuple-element.149), channel_id=1, source_target_pairs={{0,1},{1,0},{2,3},{3,2},{4,5},{5,4},{6,7},{7,6},{8,9},{9,8},{10,11... | collective-permute-start | bytes 786440 | tf_op jit(solution)/shard_map/ppermute | solution.py:795
  13.2 17.4 %collective-permute-start.4 = (bf16[256,512]{1,0:T(8,128)(2,1)}, bf16[256,512]{1,0:T(8,128)(2,1)S(1)}, u32[]{:S(2)}, u32[]{:S(2)}) collective-permute-start(bf16[256,512]{1,0:T(8,128)(2,1)} %get-tuple-element.150), channel_id=1, source_target_pairs={{0,2},{1,3},{2,0},{3,1},{4,6},{5,7},{6,4},{7,5},{8,10},{9,11},{10,... | collective-permute-start | bytes 786440 | tf_op jit(solution)/shard_map/ppermute | solution.py:795
  15.7 14.8 %collective-permute-start.5 = (bf16[256,512]{1,0:T(8,128)(2,1)}, bf16[256,512]{1,0:T(8,128)(2,1)S(1)}, u32[]{:S(2)}, u32[]{:S(2)}) collective-permute-start(bf16[256,512]{1,0:T(8,128)(2,1)} %get-tuple-element.151), channel_id=1, source_target_pairs={{0,3},{1,2},{2,1},{3,0},{4,7},{5,6},{6,5},{7,4},{8,11},{9,10},{10,... | collective-permute-start | bytes 786440 | tf_op jit(solution)/shard_map/ppermute | solution.py:795
  15.8 7.4 %collective-permute-start.2 = (bf16[1,336,128]{2,1,0:T(8,128)(2,1)}, bf16[1,336,128]{2,1,0:T(8,128)(2,1)S(1)}, u32[]{:S(2)}, u32[]{:S(2)}) collective-permute-start(bf16[1,336,128]{2,1,0:T(8,128)(2,1)} %bitcast.36), channel_id=1, source_target_pairs={{0,24},{1,25},{2,26},{3,27},{4,28},{5,29},{6,30},{7,31},{8,16},{9,... | collective-permute-start | bytes 258056 | tf_op jit(solution)/shard_map/ppermute | solution.py:795
  19.6 8.0 %collective-permute-start.1 = (bf16[1,336,128]{2,1,0:T(8,128)(2,1)}, bf16[1,336,128]{2,1,0:T(8,128)(2,1)S(1)}, u32[]{:S(2)}, u32[]{:S(2)}) collective-permute-start(bf16[1,336,128]{2,1,0:T(8,128)(2,1)} %bitcast.37), channel_id=1, source_target_pairs={{0,16},{1,17},{2,18},{3,19},{4,20},{5,21},{6,22},{7,23},{8,24},{9,... | collective-permute-start | bytes 258056 | tf_op jit(solution)/shard_map/ppermute | solution.py:795
  23.2 7.3 %collective-permute-start = (bf16[1,336,128]{2,1,0:T(8,128)(2,1)}, bf16[1,336,128]{2,1,0:T(8,128)(2,1)S(1)}, u32[]{:S(2)}, u32[]{:S(2)}) collective-permute-start(bf16[1,336,128]{2,1,0:T(8,128)(2,1)} %bitcast.38), channel_id=1, source_target_pairs={{0,8},{1,9},{2,10},{3,11},{4,12},{5,13},{6,14},{7,15},{8,0},{9,1},... | collective-permute-start | bytes 258056 | tf_op jit(solution)/shard_map/ppermute | solution.py:795
  31.6 11.9 %collective-permute-start.8 = (bf16[4,336,128]{2,1,0:T(8,128)(2,1)S(1)}, bf16[4,336,128]{2,1,0:T(8,128)(2,1)S(1)}, u32[]{:S(2)}, u32[]{:S(2)}) collective-permute-start(bf16[4,336,128]{2,1,0:T(8,128)(2,1)S(1)} %constant_dynamic-update-slice_fusion), channel_id=1, source_target_pairs={{0,6},{1,7},{2,4},{3,5},{4,2},{5,3},{6,0},{7,1},{8,14},{9,15},{10,... | collective-permute-start | bytes 1032200 | tf_op jit(solution)/shard_map/ppermute | solution.py:795
  34.2 17.8 %collective-permute-start.7 = (bf16[4,336,128]{2,1,0:T(8,128)(2,1)S(1)}, bf16[4,336,128]{2,1,0:T(8,128)(2,1)S(1)}, u32[]{:S(2)}, u32[]{:S(2)}) collective-permute-start(bf16[4,336,128]{2,1,0:T(8,128)(2,1)S(1)} %constant_dynamic-update-slice_fusion), channel_id=1, source_target_pairs={{0,4},{1,5},{2,6},{3,7},{4,0},{5,1},{6,2},{7,3},{8,12},{9,13},{10,... | collective-permute-start | bytes 1032200 | tf_op jit(solution)/shard_map/ppermute | solution.py:795
  34.6 19.5 %collective-permute-start.6 = (bf16[4,336,128]{2,1,0:T(8,128)(2,1)S(1)}, bf16[4,336,128]{2,1,0:T(8,128)(2,1)S(1)}, u32[]{:S(2)}, u32[]{:S(2)}) collective-permute-start(bf16[4,336,128]{2,1,0:T(8,128)(2,1)S(1)} %constant_dynamic-update-slice_fusion), channel_id=1, source_target_pairs={{0,2},{1,3},{2,0},{3,1},{4,6},{5,7},{6,4},{7,5},{8,10},{9,11},{10,... | collective-permute-start | bytes 1032200 | tf_op jit(solution)/shard_map/ppermute | solution.py:795
  56.7 24.2 %collective-permute-start.10 = (bf16[256,512]{1,0:T(8,128)(2,1)}, bf16[256,512]{1,0:T(8,128)(2,1)S(1)}, u32[]{:S(2)}, u32[]{:S(2)}) collective-permute-start(bf16[256,512]{1,0:T(8,128)(2,1)} %get-tuple-element.171), channel_id=1, source_target_pairs={{0,1},{1,0},{2,3},{3,2},{4,5},{5,4},{6,7},{7,6},{8,9},{9,8},{10,11... | collective-permute-start | bytes 786440 | tf_op jit(solution)/shard_map/ppermute | solution.py:795
  56.8 24.0 %collective-permute-start.11 = (bf16[256,512]{1,0:T(8,128)(2,1)}, bf16[256,512]{1,0:T(8,128)(2,1)S(1)}, u32[]{:S(2)}, u32[]{:S(2)}) collective-permute-start(bf16[256,512]{1,0:T(8,128)(2,1)} %get-tuple-element.172), channel_id=1, source_target_pairs={{0,2},{1,3},{2,0},{3,1},{4,6},{5,7},{6,4},{7,5},{8,10},{9,11},{10,... | collective-permute-start | bytes 786440 | tf_op jit(solution)/shard_map/ppermute | solution.py:795
  58.3 22.6 %collective-permute-start.12 = (bf16[256,512]{1,0:T(8,128)(2,1)}, bf16[256,512]{1,0:T(8,128)(2,1)S(1)}, u32[]{:S(2)}, u32[]{:S(2)}) collective-permute-start(bf16[256,512]{1,0:T(8,128)(2,1)} %get-tuple-element.173), channel_id=1, source_target_pairs={{0,3},{1,2},{2,1},{3,0},{4,7},{5,6},{6,5},{7,4},{8,11},{9,10},{10,... | collective-permute-start | bytes 786440 | tf_op jit(solution)/shard_map/ppermute | solution.py:795
  126.7 12.0 %collective-permute-start.17 = (bf16[256,512]{1,0:T(8,128)(2,1)}, bf16[256,512]{1,0:T(8,128)(2,1)S(1)}, u32[]{:S(2)}, u32[]{:S(2)}) collective-permute-start(bf16[256,512]{1,0:T(8,128)(2,1)} %get-tuple-element.188), channel_id=1, source_target_pairs={{0,1},{1,0},{2,3},{3,2},{4,5},{5,4},{6,7},{7,6},{8,9},{9,8},{10,11... | collective-permute-start | bytes 786440 | tf_op jit(solution)/shard_map/ppermute | solution.py:795
  127.0 42.9 %collective-permute-start.18 = (bf16[256,512]{1,0:T(8,128)(2,1)}, bf16[256,512]{1,0:T(8,128)(2,1)}, u32[]{:S(2)}, u32[]{:S(2)}) collective-permute-start(bf16[256,512]{1,0:T(8,128)(2,1)} %get-tuple-element.189), channel_id=1, source_target_pairs={{0,2},{1,3},{2,0},{3,1},{4,6},{5,7},{6,4},{7,5},{8,10},{9,11},{10,... | collective-permute-start | bytes 786440 | tf_op jit(solution)/shard_map/ppermute | solution.py:795
  128.0 41.8 %collective-permute-start.19 = (bf16[256,512]{1,0:T(8,128)(2,1)}, bf16[256,512]{1,0:T(8,128)(2,1)}, u32[]{:S(2)}, u32[]{:S(2)}) collective-permute-start(bf16[256,512]{1,0:T(8,128)(2,1)} %get-tuple-element.190), channel_id=1, source_target_pairs={{0,3},{1,2},{2,1},{3,0},{4,7},{5,6},{6,5},{7,4},{8,11},{9,10},{10,... | collective-permute-start | bytes 786440 | tf_op jit(solution)/shard_map/ppermute | solution.py:795
  137.1 32.7 %collective-permute-start.14 = (bf16[4,576,128]{2,1,0:T(8,128)(2,1)}, bf16[4,576,128]{2,1,0:T(8,128)(2,1)S(1)}, u32[]{:S(2)}, u32[]{:S(2)}) collective-permute-start(bf16[4,576,128]{2,1,0:T(8,128)(2,1)} %get-tuple-element.184), channel_id=1, source_target_pairs={{0,2},{1,3},{2,0},{3,1},{4,6},{5,7},{6,4},{7,5},{8,10},{9,11},{10,... | collective-permute-start | bytes 1769480 | tf_op jit(solution)/shard_map/ppermute | solution.py:795
  138.1 31.7 %collective-permute-start.15 = (bf16[4,576,128]{2,1,0:T(8,128)(2,1)}, bf16[4,576,128]{2,1,0:T(8,128)(2,1)S(1)}, u32[]{:S(2)}, u32[]{:S(2)}) collective-permute-start(bf16[4,576,128]{2,1,0:T(8,128)(2,1)} %get-tuple-element.185), channel_id=1, source_target_pairs={{0,4},{1,5},{2,6},{3,7},{4,0},{5,1},{6,2},{7,3},{8,12},{9,13},{10,... | collective-permute-start | bytes 1769480 | tf_op jit(solution)/shard_map/ppermute | solution.py:795
  138.7 31.2 %collective-permute-start.16 = (bf16[4,576,128]{2,1,0:T(8,128)(2,1)}, bf16[4,576,128]{2,1,0:T(8,128)(2,1)S(1)}, u32[]{:S(2)}, u32[]{:S(2)}) collective-permute-start(bf16[4,576,128]{2,1,0:T(8,128)(2,1)} %get-tuple-element.186), channel_id=1, source_target_pairs={{0,6},{1,7},{2,4},{3,5},{4,2},{5,3},{6,0},{7,1},{8,14},{9,15},{10,... | collective-permute-start | bytes 1769480 | tf_op jit(solution)/shard_map/ppermute | solution.py:795
  169.9 6.6 %collective-permute-start.20 = (bf16[16,336,128]{2,1,0:T(8,128)(2,1)}, bf16[16,336,128]{2,1,0:T(8,128)(2,1)S(1)}, u32[]{:S(2)}, u32[]{:S(2)}) collective-permute-start(bf16[16,336,128]{2,1,0:T(8,128)(2,1)} %get-tuple-element.205), channel_id=1, source_target_pairs={{0,1},{1,0},{2,3},{3,2},{4,5},{5,4},{6,7},{7,6},{8,9},{9,8},{10,11... | collective-permute-start | bytes 4128776 | tf_op jit(solution)/shard_map/ppermute | solution.py:795
  181.4 18.3 %collective-permute-start.21 = (bf16[4,336,128]{2,1,0:T(8,128)(2,1)}, bf16[4,336,128]{2,1,0:T(8,128)(2,1)S(1)}, u32[]{:S(2)}, u32[]{:S(2)}) collective-permute-start(bf16[4,336,128]{2,1,0:T(8,128)(2,1)} %get-tuple-element.230), channel_id=1, source_target_pairs={{0,2},{1,3},{2,0},{3,1},{4,6},{5,7},{6,4},{7,5},{8,10},{9,11},{10,... | collective-permute-start | bytes 1032200 | tf_op jit(solution)/shard_map/ppermute | solution.py:795
  182.4 17.8 %collective-permute-start.22 = (bf16[4,336,128]{2,1,0:T(8,128)(2,1)}, bf16[4,336,128]{2,1,0:T(8,128)(2,1)S(1)}, u32[]{:S(2)}, u32[]{:S(2)}) collective-permute-start(bf16[4,336,128]{2,1,0:T(8,128)(2,1)} %get-tuple-element.231), channel_id=1, source_target_pairs={{0,4},{1,5},{2,6},{3,7},{4,0},{5,1},{6,2},{7,3},{8,12},{9,13},{10,... | collective-permute-start | bytes 1032200 | tf_op jit(solution)/shard_map/ppermute | solution.py:795
  183.0 17.2 %collective-permute-start.23 = (bf16[4,336,128]{2,1,0:T(8,128)(2,1)}, bf16[4,336,128]{2,1,0:T(8,128)(2,1)S(1)}, u32[]{:S(2)}, u32[]{:S(2)}) collective-permute-start(bf16[4,336,128]{2,1,0:T(8,128)(2,1)} %get-tuple-element.232), channel_id=1, source_target_pairs={{0,6},{1,7},{2,4},{3,5},{4,2},{5,3},{6,0},{7,1},{8,14},{9,15},{10,... | collective-permute-start | bytes 1032200 | tf_op jit(solution)/shard_map/ppermute | solution.py:795
  184.9 7.3 %collective-permute-start.24 = (bf16[1,576,128]{2,1,0:T(8,128)(2,1)S(1)}, bf16[1,576,128]{2,1,0:T(8,128)(2,1)S(1)}, u32[]{:S(2)}, u32[]{:S(2)}) collective-permute-start(bf16[1,576,128]{2,1,0:T(8,128)(2,1)S(1)} %copy-done.31), channel_id=1, source_target_pairs={{0,8},{1,9},{2,10},{3,11},{4,12},{5,13},{6,14},{7,15},{8,0},{9,1},... | collective-permute-start | bytes 442376 | tf_op jit(solution)/shard_map/ppermute | solution.py:795
  186.3 13.4 %collective-permute-start.25 = (bf16[1,576,128]{2,1,0:T(8,128)(2,1)S(1)}, bf16[1,576,128]{2,1,0:T(8,128)(2,1)S(1)}, u32[]{:S(2)}, u32[]{:S(2)}) collective-permute-start(bf16[1,576,128]{2,1,0:T(8,128)(2,1)S(1)} %copy-done.30), channel_id=1, source_target_pairs={{0,16},{1,17},{2,18},{3,19},{4,20},{5,21},{6,22},{7,23},{8,24},{9,... | collective-permute-start | bytes 442376 | tf_op jit(solution)/shard_map/ppermute | solution.py:795
  192.3 7.5 %collective-permute-start.26 = (bf16[1,576,128]{2,1,0:T(8,128)(2,1)S(1)}, bf16[1,576,128]{2,1,0:T(8,128)(2,1)S(1)}, u32[]{:S(2)}, u32[]{:S(2)}) collective-permute-start(bf16[1,576,128]{2,1,0:T(8,128)(2,1)S(1)} %copy-done.29), channel_id=1, source_target_pairs={{0,24},{1,25},{2,26},{3,27},{4,28},{5,29},{6,30},{7,31},{8,16},{9,... | collective-permute-start | bytes 442376 | tf_op jit(solution)/shard_map/ppermute | solution.py:795
  200.2 17.2 %collective-permute-start.30 = (bf16[256,512]{1,0:T(8,128)(2,1)S(1)}, bf16[256,512]{1,0:T(8,128)(2,1)S(1)}, u32[]{:S(2)}, u32[]{:S(2)}) collective-permute-start(bf16[256,512]{1,0:T(8,128)(2,1)S(1)} %copy-done.22), channel_id=1, source_target_pairs={{0,1},{1,0},{2,3},{3,2},{4,5},{5,4},{6,7},{7,6},{8,9},{9,8},{10,11... | collective-permute-start | bytes 786440 | tf_op jit(solution)/shard_map/ppermute | solution.py:795
  200.3 17.1 %collective-permute-start.31 = (bf16[256,512]{1,0:T(8,128)(2,1)S(1)}, bf16[256,512]{1,0:T(8,128)(2,1)S(1)}, u32[]{:S(2)}, u32[]{:S(2)}) collective-permute-start(bf16[256,512]{1,0:T(8,128)(2,1)S(1)} %copy-done.21), channel_id=1, source_target_pairs={{0,2},{1,3},{2,0},{3,1},{4,6},{5,7},{6,4},{7,5},{8,10},{9,11},{10,... | collective-permute-start | bytes 786440 | tf_op jit(solution)/shard_map/ppermute | solution.py:795
  201.6 15.8 %collective-permute-start.32 = (bf16[256,512]{1,0:T(8,128)(2,1)S(1)}, bf16[256,512]{1,0:T(8,128)(2,1)S(1)}, u32[]{:S(2)}, u32[]{:S(2)}) collective-permute-start(bf16[256,512]{1,0:T(8,128)(2,1)S(1)} %copy-done.20), channel_id=1, source_target_pairs={{0,3},{1,2},{2,1},{3,0},{4,7},{5,6},{6,5},{7,4},{8,11},{9,10},{10,... | collective-permute-start | bytes 786440 | tf_op jit(solution)/shard_map/ppermute | solution.py:795
  205.1 5.6 %collective-permute-start.27 = (bf16[1,336,128]{2,1,0:T(8,128)(2,1)}, bf16[1,336,128]{2,1,0:T(8,128)(2,1)S(1)}, u32[]{:S(2)}, u32[]{:S(2)}) collective-permute-start(bf16[1,336,128]{2,1,0:T(8,128)(2,1)} %get-tuple-element.246), channel_id=1, source_target_pairs={{0,8},{1,9},{2,10},{3,11},{4,12},{5,13},{6,14},{7,15},{8,0},{9,1},... | collective-permute-start | bytes 258056 | tf_op jit(solution)/shard_map/ppermute | solution.py:795
  207.4 9.9 %collective-permute-start.28 = (bf16[1,336,128]{2,1,0:T(8,128)(2,1)}, bf16[1,336,128]{2,1,0:T(8,128)(2,1)S(1)}, u32[]{:S(2)}, u32[]{:S(2)}) collective-permute-start(bf16[1,336,128]{2,1,0:T(8,128)(2,1)} %get-tuple-element.247), channel_id=1, source_target_pairs={{0,16},{1,17},{2,18},{3,19},{4,20},{5,21},{6,22},{7,23},{8,24},{9,... | collective-permute-start | bytes 258056 | tf_op jit(solution)/shard_map/ppermute | solution.py:795
  210.7 6.7 %collective-permute-start.29 = (bf16[1,336,128]{2,1,0:T(8,128)(2,1)}, bf16[1,336,128]{2,1,0:T(8,128)(2,1)S(1)}, u32[]{:S(2)}, u32[]{:S(2)}) collective-permute-start(bf16[1,336,128]{2,1,0:T(8,128)(2,1)} %get-tuple-element.248), channel_id=1, source_target_pairs={{0,24},{1,25},{2,26},{3,27},{4,28},{5,29},{6,30},{7,31},{8,16},{9,... | collective-permute-start | bytes 258056 | tf_op jit(solution)/shard_map/ppermute | solution.py:795
  (35 other events, 330.6 us)
Sparse Core Ops, SparseCore 0:
  12.8 76.2 all-gather.2

commit v2 on v1

--- a/solution.py
+++ b/solution.py
@@ -10,6 +10,7 @@
 AXES = ("batch", "seq")
 LANE = 128
 TILE = 16
+FEED_ROWS = 512
 STEP = 256
 FAR = 1e30
 BEND = 0.7978845608028654
@@ -43,7 +44,7 @@
 
 
 def full(shape):
-    return pl.BlockSpec(shape, lambda *_: (0,) * len(shape))
+    return pl.BlockSpec(shape, lambda *_: (0,) * len(shape), pipeline_mode=pl.Buffered(1))
 
 
 def params(megabytes):
@@ -172,36 +173,47 @@
 
     keep = causal()
     lower = lax.broadcasted_iota(jnp.int32, (LANE, STEP), 0) < LANE // 2
-    for block in range(total_rows // STEP):
-        spot = slice(block * STEP, (block + 1) * STEP)
+
+    value_t = value_ref[...].T
+
+    def logits_of(block, head):
         start = block * STEP
         other = half if start >= half else 0
-        query = query_ref[spot, :]
-        parts = []
-        for head in range(2):
-            mine = own_lanes(query, head)
-            near = times_t(key_ref[start : start + STEP, :], mine)
-            near = jnp.where(keep, near, -FAR)
-            peak = jnp.max(near, axis=0, keepdims=True)
-            logits = [near]
-            if start > other:
-                same = times_t(key_ref[other:start, :], mine)
-                peak = jnp.maximum(peak, jnp.max(same, axis=0, keepdims=True))
-                logits.insert(0, same)
-            if other:
-                away = times_t(key_ref[:other, :], mine)
-                peak = jnp.maximum(peak, jnp.max(away, axis=0, keepdims=True) - far)
-            raised = [jnp.exp(piece - peak) for piece in logits]
-            total = sum(jnp.sum(piece, axis=0, keepdims=True) for piece in raised)
-            low = jnp.concatenate([piece.astype(BF) for piece in raised], axis=0)
-            mixed = t_times(value_ref[other : start + STEP, :], low)
-            if other:
-                away = jnp.exp(away - (peak + far))
-                total = total + jnp.sum(away, axis=0, keepdims=True)
-                mixed = mixed + t_times(value_ref[:other, :], away.astype(BF))
-            parts.append(mixed * (1.0 / total))
-            total_ref[0, head : head + 1, spot] = peak + jnp.log(total)
-        mixed_ref[spot, :] = jnp.where(lower, parts[0], parts[1]).T.astype(BF)
+        mine = own_lanes(query_ref[start : start + STEP, :], head)
+        near = times_t(key_ref[start : start + STEP, :], mine)
+        same = times_t(key_ref[other:start, :], mine) if start > other else None
+        away = times_t(key_ref[:other, :], mine) if other else None
+        return near, same, away
+
+    def mixed_of(block, head, near, same, away):
+        start = block * STEP
+        other = half if start >= half else 0
+        near = jnp.where(keep, near, -FAR)
+        peak = jnp.max(near, axis=0, keepdims=True)
+        if same is not None:
+            peak = jnp.maximum(peak, jnp.max(same, axis=0, keepdims=True))
+        if away is not None:
+            peak = jnp.maximum(peak, jnp.max(away, axis=0, keepdims=True) - far)
+        raised = [jnp.exp(piece - peak) for piece in (same, near) if piece is not None]
+        total = sum(jnp.sum(piece, axis=0, keepdims=True) for piece in raised)
+        low = jnp.concatenate([piece.astype(BF) for piece in raised], axis=0)
+        mixed = times(value_t[:, other : start + STEP], low)
+        if away is not None:
+            away = jnp.exp(away - (peak + far))
+            total = total + jnp.sum(away, axis=0, keepdims=True)
+            mixed = mixed + times(value_t[:, :other], away.astype(BF))
+        total_ref[0, head : head + 1, start : start + STEP] = peak + jnp.log(total)
+        return mixed * (1.0 / total)
+
+    tasks = [(block, head) for block in range(total_rows // STEP) for head in range(2)]
+    ahead = logits_of(*tasks[0])
+    parts = []
+    for index, (block, head) in enumerate(tasks):
+        logits, ahead = ahead, logits_of(*tasks[index + 1]) if index + 1 < len(tasks) else None
+        parts.append(mixed_of(block, head, *logits))
+        if head:
+            mixed_ref[block * STEP : (block + 1) * STEP, :] = jnp.where(lower, *parts).T.astype(BF)
+            parts = []
 
 
 def attend(plan, info, pieces, weights):
@@ -278,8 +290,8 @@
     else:
         outward_out, expand_out, contract_out = refs[:3]
         refs = refs[3:]
-    (outward_ref, expand_ref, contract_ref, upstream_ref, active_ref, slope_ref,
-     outward_sum, expand_sum, contract_sum) = refs
+    (outward_ref, expand_ref, contract_ref, upstream_ref, result_ref, slope_ref, active_all, hidden_all, normed_all,
+     lowered_all, branch_all, mixed_all, whole_ref, expand_sum, contract_sum) = refs
     step = pl.program_id(0)
     width, parts, lanes = plan.width, plan.parts, plan.lanes
     contract_own = plan.hidden // plan.devices
@@ -304,10 +316,18 @@
             expand_ref[...] = expand_in[...]
             contract_ref[...] = contract_in[...]
 
+    size = lifted_ref.shape[0]
+    here = pl.ds(pl.multiple_of(step * size, size), size)
+    rows = plan.total_rows // count
+    group = size // rows
+
+    def spot(mask):
+        return pl.ds(pl.multiple_of(((info_ref[2] ^ mask) % group) * rows, rows), rows)
+
     for mask in range(count):
-        @pl.when(step == mask)
+        @pl.when(step == mask // group)
         def _(mask=mask):
-            upstream_ref[...] = upstreams[mask][...]
+            upstream_ref[spot(mask), :] = upstreams[mask][...]
 
     outlet, steady, offset = (small_ref[i : i + 1, :] for i in (2, 3, 4))
     settle, temper, anchor = (small_ref[i + parts : i + parts + 1, :] for i in (5, 6, 7))
@@ -316,6 +336,8 @@
     unit, root = norm(lifted_ref[...] + branch)
     normed = unit * steady + offset
     normed_low = normed.astype(BF)
+    normed_all[here, :] = normed_low
+    mixed_all[here, :] = mixed
     lowered = jnp.zeros_like(normed)
     for part in range(parts):
         cut = slice(part * width, (part + 1) * width)
@@ -324,102 +346,114 @@
         bend = jnp.tanh(hidden * (BEND + BEND * 0.044715 * square))
         half = 0.5 + 0.5 * bend
         active = (hidden * half).astype(BF)
-        active_ref[:, cut] = active
+        active_all[here, cut] = active
         slope_ref[:, cut] = half + (0.5 * hidden) * (1.0 - bend * bend) * (
             BEND + 3 * BEND * 0.044715 * square
         )
         lowered = lowered + times(active, contract_ref[cut, :])
     last_unit, last_root = norm(normed + (lowered + settle))
-    result = (last_unit * temper + anchor).astype(BF)
-    for mask in range(count):
-        @pl.when(step == mask)
-        def _(mask=mask):
-            results[mask][...] = result
-
+    result_ref[...] = (last_unit * temper + anchor).astype(BF)
     upstream = upstream_ref[...].astype(F32)
     temper_grad = column_sum(upstream * last_unit)
     anchor_grad = column_sum(upstream)
     second_back = norm_back(upstream, temper, last_unit, last_root)
     lowered_back = second_back.astype(BF)
+    lowered_all[here, :] = lowered_back
     settle_grad = column_sum(lowered_back)
     normed_back = second_back
     spread_grads = []
-    contract_terms = []
-    expand_terms = []
     for part in range(parts):
         cut = slice(part * width, (part + 1) * width)
-        contract_terms.append(t_times(active_ref[:, cut], lowered_back))
         active_back = times_t(lowered_back, contract_ref[cut, :])
         hidden_back = (active_back * slope_ref[:, cut]).astype(BF)
         spread_grads.append(column_sum(hidden_back))
-        expand_terms.append(t_times(normed_low, hidden_back))
+        hidden_all[here, cut] = hidden_back
         normed_back = normed_back + times_t(hidden_back, expand_ref[part])
     first_back = norm_back(normed_back, steady, unit, root)
     first_back_ref[...] = first_back
     branch_back = first_back.astype(BF)
     mixed_back_ref[...] = times_t(branch_back, outward_ref[...]).astype(BF)
-    outward_term = t_times(mixed, branch_back)
+    branch_all[here, :] = branch_back
     zero = jnp.zeros_like(anchor_grad)
     grads = [zero, zero, column_sum(branch_back), column_sum(normed_back * unit)]
     grads += [column_sum(normed_back)] + spread_grads + [settle_grad, temper_grad, anchor_grad]
     grads += [zero] * (plan.small_rows - len(grads))
     small_term = jnp.concatenate(grads, axis=0)
+    for mask in range(count):
+        @pl.when(step == mask // group)
+        def _(mask=mask):
+            results[mask][...] = result_ref[spot(mask), :]
 
     @pl.when(step == 0)
     def _():
         small_grad_ref[...] = small_term
-        outward_sum[...] = outward_term
-        for part in range(parts):
-            expand_sum[part] = expand_terms[part]
-            contract_sum[part * width : (part + 1) * width, :] = contract_terms[part]
 
     @pl.when(step > 0)
     def _():
         small_grad_ref[...] += small_term
-        outward_sum[...] += outward_term
-        for part in range(parts):
-            expand_sum[part] += expand_terms[part]
-            contract_sum[part * width : (part + 1) * width, :] += contract_terms[part]
-
-    @pl.when(step == count - 1)
+
+    @pl.when(step == pl.num_programs(0) - 1)
     def _():
+        outward = t_times(mixed_all[...], branch_all[...])
         if plan.packed:
+            me = info_ref[1]
+            whole_ref[...] = outward
             for mask in range(plan.devices):
                 shard = halves[mask & 1].at[plan.place(mask)]
-                owner = info_ref[1] ^ mask
-                rows = aligned(owner, TILE)
-                wide = aligned(owner, contract_own)
+                rows = aligned(me ^ mask, TILE)
                 for lane in range(lanes):
                     cut = slice(lane * LANE, (lane + 1) * LANE)
-                    shard[lane * TILE : (lane + 1) * TILE, :] = outward_sum[rows, cut].astype(BF)
-                    for part in range(parts):
-                        at = (lanes + part * lanes + lane) * TILE
-                        shard[at : at + TILE, :] = expand_sum[part, rows, cut].astype(BF)
+                    shard[lane * TILE : (lane + 1) * TILE, :] = whole_ref[rows, cut].astype(BF)
+        else:
+            outward_out[...] = outward.astype(BF)
+        per_part = plan.devices // parts
+        for mask_part in range(parts):
+            part = (me // per_part) ^ mask_part if plan.packed else mask_part
+            cut = pl.ds(pl.multiple_of(part * width, width), width)
+            expand = t_times(normed_all[...], hidden_all[:, cut])
+            contract = t_times(active_all[:, cut], lowered_all[...])
+            if not plan.packed:
+                expand_out[mask_part] = expand.astype(BF)
+                contract_out[cut, :] = contract.astype(BF)
+                continue
+            expand_sum[...] = expand
+            contract_sum[...] = contract
+            for mask in range(plan.devices):
+                shard = halves[mask & 1].at[plan.place(mask)]
+                rows = aligned(me ^ mask, TILE)
+                for lane in range(lanes):
+                    at = aligned(lanes + part * lanes + lane, TILE)
+                    shard[at, :] = expand_sum[rows, lane * LANE : (lane + 1) * LANE].astype(BF)
+            for index in range(per_part):
+                mask = mask_part * per_part + index
+                shard = halves[mask & 1].at[plan.place(mask)]
+                rows = aligned((me ^ mask) % per_part, contract_own)
+                for lane in range(lanes):
                     at = contract_at + lane * contract_own
-                    shard[at : at + contract_own, :] = contract_sum[wide, cut].astype(BF)
-        else:
-            outward_out[...] = outward_sum[...].astype(BF)
-            expand_out[...] = expand_sum[...].astype(BF)
-            contract_out[...] = contract_sum[...].astype(BF)
+                    shard[at : at + contract_own, :] = contract_sum[
+                        rows, lane * LANE : (lane + 1) * LANE
+                    ].astype(BF)
 
 
 def feed(plan, info, lifted, mixed, upstreams, weights, small):
     total_rows, width, parts = plan.total_rows, plan.width, plan.parts
     count = len(upstreams)
-    size = total_rows // count
-    rows = pl.BlockSpec((size, width), lambda i, info: (info[2] ^ i, 0))
+    piece = total_rows // count
+    size = max(piece, FEED_ROWS)
+    group = size // piece
+    rows = pl.BlockSpec((size, width), lambda i, info: ((info[2] // group) ^ i, 0))
     outward, expand, contract = (width, width), (parts, width, width), (parts * width, width)
     if plan.packed:
         grads = [like((plan.devices // 2, plan.late_rows, LANE), BF)] * 2
     else:
         grads = [like(outward, BF), like(expand, BF), like(contract, BF)]
-    ends = [like((size, width), BF)] * count
+    ends = [like((piece, width), BF)] * count
     outs = [like((total_rows, width), BF), like((total_rows, width), F32), like(small.shape, F32)]
     values = pl.pallas_call(
         functools.partial(feed_kernel, plan, count),
         grid_spec=pltpu.PrefetchScalarGridSpec(
             num_scalar_prefetch=1,
-            grid=(count,),
+            grid=(total_rows // size,),
             in_specs=[rows, rows] + [full(v.shape) for v in upstreams + weights + [small]],
             out_specs=[full(v.shape) for v in ends]
             + [rows, rows, full(small.shape)]
@@ -429,11 +463,17 @@
                 pltpu.VMEM(expand, BF),
                 pltpu.VMEM(contract, BF),
                 pltpu.VMEM((size, width), BF),
-                pltpu.VMEM((size, parts * width), BF),
+                pltpu.VMEM((size, width), BF),
                 pltpu.VMEM((size, parts * width), F32),
+                pltpu.VMEM((total_rows, parts * width), BF),
+                pltpu.VMEM((total_rows, parts * width), BF),
+                pltpu.VMEM((total_rows, width), BF),
+                pltpu.VMEM((total_rows, width), BF),
+                pltpu.VMEM((total_rows, width), BF),
+                pltpu.VMEM((total_rows, width), BF),
                 pltpu.VMEM(outward, F32),
-                pltpu.VMEM(expand, F32),
-                pltpu.VMEM(contract, F32),
+                pltpu.VMEM(outward, F32),
+                pltpu.VMEM(outward, F32),
             ],
         ),
         out_shape=ends + outs + grads,
@@ -454,7 +494,7 @@
     else:
         table_out, inward_out, small_out = refs[:3]
         refs = refs[3:]
-    low_ref, sum_ref, share_ref, score_ref, grad_ref, table_ref, joint_sums, blocks_ref = refs
+    joint_ref, sum_ref, share_ref, score_ref, grad_ref, table_ref, joint_sums, blocks_ref = refs
     pair = pl.program_id(0)
     total_rows, lanes = plan.total_rows, plan.lanes
     half = total_rows // 2
@@ -462,78 +502,80 @@
     far = jnp.where(split, FAR, 0.0)
     blocks = total_rows // STEP
 
-    @pl.when(pair == 0)
-    def _():
-        low_ref[...] = lifted_ref[...].astype(BF)
-
     keep = causal()
     lower = lax.broadcasted_iota(jnp.int32, (STEP, LANE), 1) < LANE // 2
     lower_t = lax.broadcasted_iota(jnp.int32, (LANE, STEP), 0) < LANE // 2
-    query_parts, key_parts, value_parts = [], [], []
     product = (mixed_ref[...].astype(F32) * mixed_back_ref[...].astype(F32)).T
-    scaled_key = key_ref[...] * BF(0.125)
-    for head in range(2):
-        between = jnp.sum(
-            product[head * LANE // 2 : (head + 1) * LANE // 2], axis=0, keepdims=True
-        )
-        for block in range(blocks):
-            start = block * STEP
-            spot = slice(start, start + STEP)
-            query = own_lanes(query_ref[spot, :], head)
-            back = own_lanes(mixed_back_ref[spot, :], head)
-            total = total_ref[0, head : head + 1, spot]
-            gap = between[:, spot]
-            for under in range(block + 1):
-                keys = slice(under * STEP, (under + 1) * STEP)
-                away = start >= half and under * STEP < half
-                logits = times_t(key_ref[keys, :], query)
-                share = jnp.exp(logits - (total + far if away else total))
-                if under == block:
-                    share = jnp.where(keep, share, 0.0)
-                share_back = times_t(value_ref[keys, :], back)
-                score = share * (share_back - gap)
-                share_ref[head, keys, spot] = share.astype(BF)
-                score_ref[head, keys, spot] = score.astype(BF)
-        queries, keys_, values = [], [], []
-        for block in range(blocks):
-            start = block * STEP
-            spot = slice(start, start + STEP)
-            end = start + STEP
-            queries.append(t_times(scaled_key[:end], score_ref[head, :end, spot]))
-            keys_.append(times(score_ref[head, spot, start:], query_ref[start:, :]))
-            values.append(times(share_ref[head, spot, start:], mixed_back_ref[start:, :]))
-        query_parts.append(queries)
-        key_parts.append(keys_)
-        value_parts.append(values)
-    weights = jnp.concatenate([inward_ref[pair + i * lanes] for i in range(3)], axis=1)
-    joints = []
-    for block in range(blocks):
+    scaled_key = (key_ref[...] * BF(0.125)).T
+    betweens = [
+        jnp.sum(product[head * LANE // 2 : (head + 1) * LANE // 2], axis=0, keepdims=True)
+        for head in range(2)
+    ]
+
+    def logits_of(block, head):
         spot = slice(block * STEP, (block + 1) * STEP)
-        query_back = jnp.where(lower_t, query_parts[0][block], query_parts[1][block]).T
-        key_back = jnp.where(lower, key_parts[0][block], key_parts[1][block])
-        value_back = jnp.where(lower, value_parts[0][block], value_parts[1][block])
-        joint = jnp.concatenate([query_back, key_back, value_back], axis=1).astype(BF)
-        joints.append(joint)
-        term = times_t(joint, weights)
-
-        @pl.when(pair == 0)
-        def _():
-            sum_ref[spot, :] = term + first_back_ref[spot, :]
-
-        @pl.when(pair > 0)
-        def _():
-            sum_ref[spot, :] += term
-
-    joint = jnp.concatenate(joints, axis=0)
-    grads = t_times(low_ref[...], joint)
-    for part in range(3):
-        grad_ref[pair + part * lanes] = grads[:, part * LANE : (part + 1) * LANE]
-    sums = column_sum(joint)
-    joint_sums[pl.ds(pair, 1), :] = sums[:, :LANE]
-    joint_sums[pl.ds(pair + lanes, 1), :] = sums[:, 2 * LANE :]
+        keys = slice(0, (block + 1) * STEP)
+        query = own_lanes(query_ref[spot, :], head)
+        back = own_lanes(mixed_back_ref[spot, :], head)
+        return times_t(key_ref[keys, :], query), times_t(value_ref[keys, :], back)
+
+    def scores_of(block, head, logits, share_back):
+        start = block * STEP
+        spot = slice(start, start + STEP)
+        total = total_ref[0, head : head + 1, spot]
+        gap = betweens[head][:, spot]
+        for under in range(block + 1):
+            keys = slice(under * STEP, (under + 1) * STEP)
+            away = start >= half and under * STEP < half
+            share = jnp.exp(logits[keys] - (total + far if away else total))
+            if under == block:
+                share = jnp.where(keep, share, 0.0)
+            score = share * (share_back[keys] - gap)
+            share_ref[head, keys, spot] = share.astype(BF)
+            score_ref[head, keys, spot] = score.astype(BF)
+
+    def backs_of(block, head):
+        start = block * STEP
+        spot = slice(start, start + STEP)
+        end = start + STEP
+        query_back = times(scaled_key[:, :end], score_ref[head, :end, spot])
+        key_back = times(score_ref[head, spot, start:], query_ref[start:, :])
+        value_back = times(share_ref[head, spot, start:], mixed_back_ref[start:, :])
+        return query_back, key_back, value_back
+
+    tasks = [(block, head) for block in reversed(range(blocks)) for head in range(2)]
+    ahead = logits_of(*tasks[0])
+    parts = []
+    for index, (block, head) in enumerate(tasks):
+        logits, ahead = ahead, logits_of(*tasks[index + 1]) if index + 1 < len(tasks) else None
+        scores_of(block, head, *logits)
+        parts.append(backs_of(block, head))
+        if head:
+            spot = slice(block * STEP, (block + 1) * STEP)
+            query_back = jnp.where(lower_t, parts[0][0], parts[1][0]).T
+            key_back = jnp.where(lower, parts[0][1], parts[1][1])
+            value_back = jnp.where(lower, parts[0][2], parts[1][2])
+            for part, back in enumerate((query_back, key_back, value_back)):
+                joint_ref[spot, aligned(pair + part * lanes, LANE)] = back.astype(BF)
+            parts = []
 
     @pl.when(pair == lanes - 1)
     def _():
+        low = lifted_ref[...].astype(BF).T
+        weights = jnp.concatenate([inward_ref[i] for i in range(3 * lanes)], axis=1)
+        for block in range(blocks):
+            spot = slice(block * STEP, (block + 1) * STEP)
+            sum_ref[spot, :] = first_back_ref[spot, :] + times_t(joint_ref[spot, :], weights)
+        for part in range(3):
+            joint = joint_ref[:, part * plan.width : (part + 1) * plan.width]
+            grads = times(low, joint)
+            for lane in range(lanes):
+                grad_ref[part * lanes + lane] = grads[:, lane * LANE : (lane + 1) * LANE]
+            if part != 1:
+                sums = column_sum(joint)
+                for lane in range(lanes):
+                    at = lane if part == 0 else lane + lanes
+                    joint_sums[at : at + 1, :] = sums[:, lane * LANE : (lane + 1) * LANE]
         rows = total_rows // count
         for mask in range(count):
             spot = pl.ds(pl.multiple_of((info_ref[2] ^ mask) * rows, rows), rows)
@@ -603,7 +645,7 @@
             ],
             out_specs=[full(v.shape) for v in tokens + grads],
             scratch_shapes=[
-                pltpu.VMEM((total_rows, width), BF),
+                pltpu.VMEM((total_rows, 3 * width), BF),
                 pltpu.VMEM((total_rows, width), F32),
                 pltpu.VMEM((2, total_rows, total_rows), BF),
                 pltpu.VMEM((2, total_rows, total_rows), BF),

time: 229 us -> 217 us (0.948)
  Pallas kernels: 117 us -> 96.6 us
  waiting for transfers between devices: 53.9 us -> 60.4 us
    pallas_call x1, Pallas kernels: 37.4 us -> 27.9 us  [feed(): pl.pallas_call(functools.partial(feed_kernel, plan, count), grid_spec=plt...]
    pallas_call x1, Pallas kernels: 29.2 us -> 23.4 us  [attend_back(): pl.pallas_call(functools.partial(attend_back_kernel, plan, count), grid_s...]
    pallas_call x1, Pallas kernels: 21.2 us -> 16.5 us  [attend(): pl.pallas_call(functools.partial(attend_kernel, plan, len(pieces)), grid_...]
    ppermute x33, waiting for transfers between devices: 45.7 us -> 49.7 us  [swap(): lax.ppermute(value, AXES, [(d, d ^ mask) for d in range(devices)])]
    all_gather x1, waiting for transfers between devices: 8.12 us -> 10.8 us  [local(): late = [lax.all_gather(late_shard, AXES, axis=0, tiled=False)]]
  transfers between devices with their start and end apart: 34 -> 34, of which waited for: 13 -> 15; matrix products, arithmetic and copies ran while one was open for 1% -> 1% of each run, Pallas kernels for 29% -> 26%
where the time goes in v2:
time: 217 us; the launch traced here: 216 us
  Pallas kernels  96.6 us (45%)
  waiting for transfers between devices  60.4 us (28%)
  starting transfers between devices  36.7 us (17%)
  between operations  14.4 us (7%)
  local copies, waits for them, and re-layouts  6.1 us (3%)
    ppermute x33, waiting for transfers between devices, swap(): lax.ppermute(value, AXES, [(d, d ^ mask) for d in range(devices)])  49.7 us
    ppermute x33, starting transfers between devices, swap(): lax.ppermute(value, AXES, [(d, d ^ mask) for d in range(devices)])  36.7 us
    pallas_call x1, Pallas kernels, feed(): pl.pallas_call(functools.partial(feed_kernel, plan, count), grid_spec=plt...  27.9 us
    pallas_call x1, Pallas kernels, attend_back(): pl.pallas_call(functools.partial(attend_back_kernel, plan, count), grid_s...  23.4 us
    pallas_call x1, Pallas kernels, attend(): pl.pallas_call(functools.partial(attend_kernel, plan, len(pieces)), grid_...  16.5 us
    pallas_call x4, Pallas kernels, fold(): pl.pallas_call(functools.partial(fold_kernel, len(terms)), grid=(pieces,)...  14.9 us
    all_gather x1, waiting for transfers between devices, local(): late = [lax.all_gather(late_shard, AXES, axis=0, tiled=False)]  10.8 us
    unnamed x72, local copies, waits for them, and re-layouts  6.04 us
  transfers between devices with their start and end apart: 34, of which 15 were waited for; matrix products, arithmetic and copies ran while one was open for 1% of the time, Pallas kernels for 26%

profile of v2, /device:TPU:0, one launch (start us, length us, event | category | flops | bytes accessed | tf_op | source)
XLA Modules:
  0.0 216.2 jit_solution(12650891597501004220)
XLA Ops:
  7.2 2.3 %cut_rows.2 = (bf16[256,512]{1,0:T(8,128)(2,1)}, bf16[256,512]{1,0:T(8,128)(2,1)}, bf16[256,512]{1,0:T(8,128)(2,1)}, bf16[256,512]{1,0:T(8,128)(2,1)}) custom-call(bf16[4,256,512]{2,1,0:T(8,128)(2,1)} %bitcast.34), custom_call_target="tpu_custom_call" | custom-call | bytes 4194304 | tf_op jit(solution)/shard_map/cut_rows/pallas_call | solution.py:813
  13.2 2.6 %collective-permute-start.4 = (bf16[256,512]{1,0:T(8,128)(2,1)}, bf16[256,512]{1,0:T(8,128)(2,1)S(1)}, u32[]{:S(2)}, u32[]{:S(2)}) collective-permute-start(bf16[256,512]{1,0:T(8,128)(2,1)} %get-tuple-element.150), channel_id=1, source_target_pairs={{0,2},{1,3},{2,0},{3,1},{4,6},{5,7},{6,4},{7,5},{8,10},{9,11},{10,... | collective-permute-start | bytes 786440 | tf_op jit(solution)/shard_map/ppermute | solution.py:837
  15.8 3.9 %collective-permute-start.2 = (bf16[1,336,128]{2,1,0:T(8,128)(2,1)}, bf16[1,336,128]{2,1,0:T(8,128)(2,1)S(1)}, u32[]{:S(2)}, u32[]{:S(2)}) collective-permute-start(bf16[1,336,128]{2,1,0:T(8,128)(2,1)} %bitcast.36), channel_id=1, source_target_pairs={{0,24},{1,25},{2,26},{3,27},{4,28},{5,29},{6,30},{7,31},{8,16},{9,... | collective-permute-start | bytes 258056 | tf_op jit(solution)/shard_map/ppermute | solution.py:837
  19.7 3.6 %collective-permute-done.2 = bf16[1,336,128]{2,1,0:T(8,128)(2,1)S(1)} collective-permute-done((bf16[1,336,128]{2,1,0:T(8,128)(2,1)}, bf16[1,336,128]{2,1,0:T(8,128)(2,1)S(1)}, u32[]{:S(2)}, u32[]{:S(2)}) %collective-permute-start.2) | collective-permute-done | bytes 86048 | tf_op jit(solution)/shard_map/ppermute | solution.py:837
  23.2 3.6 %collective-permute-start = (bf16[1,336,128]{2,1,0:T(8,128)(2,1)}, bf16[1,336,128]{2,1,0:T(8,128)(2,1)S(1)}, u32[]{:S(2)}, u32[]{:S(2)}) collective-permute-start(bf16[1,336,128]{2,1,0:T(8,128)(2,1)} %bitcast.38), channel_id=1, source_target_pairs={{0,8},{1,9},{2,10},{3,11},{4,12},{5,13},{6,14},{7,15},{8,0},{9,1},... | collective-permute-start | bytes 258056 | tf_op jit(solution)/shard_map/ppermute | solution.py:837
  27.6 2.9 %collective-permute-done = bf16[1,336,128]{2,1,0:T(8,128)(2,1)S(1)} collective-permute-done((bf16[1,336,128]{2,1,0:T(8,128)(2,1)}, bf16[1,336,128]{2,1,0:T(8,128)(2,1)S(1)}, u32[]{:S(2)}, u32[]{:S(2)}) %collective-permute-start) | collective-permute-done | bytes 86048 | tf_op jit(solution)/shard_map/ppermute | solution.py:837
  31.6 2.6 %collective-permute-start.8 = (bf16[4,336,128]{2,1,0:T(8,128)(2,1)S(1)}, bf16[4,336,128]{2,1,0:T(8,128)(2,1)S(1)}, u32[]{:S(2)}, u32[]{:S(2)}) collective-permute-start(bf16[4,336,128]{2,1,0:T(8,128)(2,1)S(1)} %constant_dynamic-update-slice_fusion), channel_id=1, source_target_pairs={{0,6},{1,7},{2,4},{3,5},{4,2},{5,3},{6,0},{7,1},{8,14},{9,15},{10,... | collective-permute-start | bytes 1032200 | tf_op jit(solution)/shard_map/ppermute | solution.py:837
  35.2 2.3 %cut_rows.3 = (bf16[256,512]{1,0:T(8,128)(2,1)}, bf16[256,512]{1,0:T(8,128)(2,1)}, bf16[256,512]{1,0:T(8,128)(2,1)}, bf16[256,512]{1,0:T(8,128)(2,1)}) custom-call(bf16[4,256,512]{2,1,0:T(8,128)(2,1)} %bitcast.35), custom_call_target="tpu_custom_call" | custom-call | bytes 4194304 | tf_op jit(solution)/shard_map/cut_rows/pallas_call | solution.py:813
  37.4 6.1 %collective-permute-done.8 = bf16[4,336,128]{2,1,0:T(8,128)(2,1)S(1)} collective-permute-done((bf16[4,336,128]{2,1,0:T(8,128)(2,1)S(1)}, bf16[4,336,128]{2,1,0:T(8,128)(2,1)S(1)}, u32[]{:S(2)}, u32[]{:S(2)}) %collective-permute-start.8) | collective-permute-done | bytes 344096 | tf_op jit(solution)/shard_map/ppermute | solution.py:837
  43.6 8.4 %collective-permute-done.7 = bf16[4,336,128]{2,1,0:T(8,128)(2,1)S(1)} collective-permute-done((bf16[4,336,128]{2,1,0:T(8,128)(2,1)S(1)}, bf16[4,336,128]{2,1,0:T(8,128)(2,1)S(1)}, u32[]{:S(2)}, u32[]{:S(2)}) %collective-permute-start.7) | collective-permute-done | bytes 344096 | tf_op jit(solution)/shard_map/ppermute | solution.py:837
  51.9 2.2 %collective-permute-done.6 = bf16[4,336,128]{2,1,0:T(8,128)(2,1)S(1)} collective-permute-done((bf16[4,336,128]{2,1,0:T(8,128)(2,1)S(1)}, bf16[4,336,128]{2,1,0:T(8,128)(2,1)S(1)}, u32[]{:S(2)}, u32[]{:S(2)}) %collective-permute-start.6) | collective-permute-done | bytes 344096 | tf_op jit(solution)/shard_map/ppermute | solution.py:837
  59.7 16.5 %attend.1 = (f32[1024,512]{1,0:T(8,128)}, bf16[1024,512]{1,0:T(8,128)(2,1)}, bf16[1024,512]{1,0:T(8,128)(2,1)}, bf16[1024,512]{1,0:T(8,128)(2,1)}, bf16[1024,512...) custom-call(s32[4]{0:T(128)} %pad_add_fusion.info_ref, ...), custom_call_target="tpu_custom_call" | custom-call | flops 5000000000 | bytes 14680064 | tf_op jit(solution)/shard_map/attend/pallas_call | solution.py:225
  76.2 1.7 collective-permute-done.12.refs_3_
  77.8 10.8 %all-gather.3.cloned.1.call-done = bf16[18432,128]{1,0:T(8,128)(2,1)} async-done(((bf16[576,128]{1,0:T(8,128)(2,1)}), bf16[18432,128]{1,0:T(8,128)(2,1)}) %all-gather.3.cloned.1.call-update) | async-done | bytes 4718608 | tf_op jit(solution)/shard_map/all_gather | solution.py:847
  88.6 27.9 %feed.1 = (bf16[256,512]{1,0:T(8,128)(2,1)}, bf16[256,512]{1,0:T(8,128)(2,1)}, bf16[256,512]{1,0:T(8,128)(2,1)}, bf16[256,512]{1,0:T(8,128)(2,1)}, bf16[1024,512...) custom-call(s32[4]{0:T(128)} %pad_add_fusion.info_ref, ...), custom_call_target="tpu_custom_call" | custom-call | flops 15000000512 | bytes 20971520 | tf_op jit(solution)/shard_map/feed/pallas_call | solution.py:452
  118.8 2.6 %collective-permute-done.13.refs_1_ = bf16[16,576,128]{2,1,0:T(8,128)(2,1)S(1)} collective-permute-done((bf16[16,576,128]{2,1,0:T(8,128)(2,1)}, bf16[16,576,128]{2,1,0:T(8,128)(2,1)S(1)}, u32[]{:S(2)}, u32[]{:S(2)}) %collective-permute-start.13) | collective-permute-done | bytes 2359328 | tf_op jit(solution)/shard_map/ppermute | solution.py:837
  122.8 4.5 %fold.4 = (bf16[4,576,128]{2,1,0:T(8,128)(2,1)}, bf16[4,576,128]{2,1,0:T(8,128)(2,1)}, bf16[4,576,128]{2,1,0:T(8,128)(2,1)}, bf16[4,576,128]{2,1,0:T(8,128)(2,1)}) custom-call(bf16[16,576,128]{2,1,0:T(8,128)(2,1)} %get-tuple-element.176.refs_0_, bf16[16,576,128]{2,1,0:T(8,128)(2,1)} %copy-done), custom_call_target="tpu_custom_call" | custom-call | flops 1000000 | bytes 9437184 | tf_op jit(solution)/shard_map/fold/pallas_call | solution.py:721
  130.8 23.4 %attend_back.1 = (bf16[256,512]{1,0:T(8,128)(2,1)}, bf16[256,512]{1,0:T(8,128)(2,1)}, bf16[256,512]{1,0:T(8,128)(2,1)}, bf16[256,512]{1,0:T(8,128)(2,1)}, bf16[1...) custom-call(s32[4]{0:T(128)} %pad_add_fusion.info_ref, f32[1024,512]{1,0:T(8,128)} %get-tuple-element.168.lifted_ref, ...), custom_call_target="tpu_custom_call" | custom-call | flops 14000000000 | bytes 25165824 | tf_op jit(solution)/shard_map/attend_back/pallas_call | solution.py:629
  154.2 2.7 %collective-permute-done.15.refs_2_ = bf16[4,576,128]{2,1,0:T(8,128)(2,1)S(1)} collective-permute-done((bf16[4,576,128]{2,1,0:T(8,128)(2,1)}, bf16[4,576,128]{2,1,0:T(8,128)(2,1)S(1)}, u32[]{:S(2)}, u32[]{:S(2)}) %collective-permute-start.15) | collective-permute-done | bytes 589856 | tf_op jit(solution)/shard_map/ppermute | solution.py:837
  157.0 2.9 %settle_rows.1 = bf16[4,256,512]{2,1,0:T(8,128)(2,1)} custom-call(s32[4]{0:T(128)} %pad_add_fusion.info_ref, bf16[256,512]{1,0:T(8,128)(2,1)} %get-tuple-element.214.refs_0_, bf16[256,512]{1,0:T(8,128)(2,1)} %copy-done.8, bf16[256,512]{1,0:T(8,128)(2,1)} %collective-permute-done.18.refs_2_, bf16[256,512]{1,0:T(8,128)(2,1)} %collective-permute-done.19.refs_3_), custom_call_target="tpu_custom_call" | custom-call | tf_op jit(solution)/shard_map/settle_rows/pallas_call | solution.py:792
  159.9 3.6 %fold.5 = (bf16[1,576,128]{2,1,0:T(8,128)(2,1)}, bf16[1,576,128]{2,1,0:T(8,128)(2,1)}, bf16[1,576,128]{2,1,0:T(8,128)(2,1)}, bf16[1,576,128]{2,1,0:T(8,128)(2,1)}) custom-call(bf16[4,576,128]{2,1,0:T(8,128)(2,1)} %get-tuple-element.206.refs_0_, bf16[4,576,128]{2,1,0:T(8,128)(2,1)} %copy-done.2, bf16[4,576,128]{2,1,0:T(8,128)(2,1)} %copy-done.3, ...), custom_call_target="tpu_custom_call" | custom-call | flops 1000000 | bytes 4718592 | tf_op jit(solution)/shard_map/fold/pallas_call | solution.py:721
  164.6 3.8 %fold.6 = (bf16[4,336,128]{2,1,0:T(8,128)(2,1)}, bf16[4,336,128]{2,1,0:T(8,128)(2,1)}, bf16[4,336,128]{2,1,0:T(8,128)(2,1)}, bf16[4,336,128]{2,1,0:T(8,128)(2,1)}) custom-call(bf16[16,336,128]{2,1,0:T(8,128)(2,1)} %get-tuple-element.219.refs_0_, bf16[16,336,128]{2,1,0:T(8,128)(2,1)} %copy-done.1), custom_call_target="tpu_custom_call" | custom-call | flops 1000000 | bytes 5505024 | tf_op jit(solution)/shard_map/fold/pallas_call | solution.py:721
  171.9 2.1 collective-permute-start.24
  174.5 4.8 %collective-permute-done.24.refs_5_ = bf16[1,576,128]{2,1,0:T(8,128)(2,1)S(1)} collective-permute-done((bf16[1,576,128]{2,1,0:T(8,128)(2,1)S(1)}, bf16[1,576,128]{2,1,0:T(8,128)(2,1)S(1)}, u32[]{:S(2)}, u32[]{:S(2)}) %collective-permute-start.24) | collective-permute-done | bytes 147488 | tf_op jit(solution)/shard_map/ppermute | solution.py:837
  179.3 2.0 collective-permute-start.26
  181.3 6.0 %collective-permute-done.25.refs_6_ = bf16[1,576,128]{2,1,0:T(8,128)(2,1)S(1)} collective-permute-done((bf16[1,576,128]{2,1,0:T(8,128)(2,1)S(1)}, bf16[1,576,128]{2,1,0:T(8,128)(2,1)S(1)}, u32[]{:S(2)}, u32[]{:S(2)}) %collective-permute-start.25) | collective-permute-done | bytes 147488 | tf_op jit(solution)/shard_map/ppermute | solution.py:837
  189.4 3.0 %fold.7 = (bf16[1,336,128]{2,1,0:T(8,128)(2,1)}, bf16[1,336,128]{2,1,0:T(8,128)(2,1)}, bf16[1,336,128]{2,1,0:T(8,128)(2,1)}, bf16[1,336,128]{2,1,0:T(8,128)(2,1)}) custom-call(bf16[4,336,128]{2,1,0:T(8,128)(2,1)} %get-tuple-element.241.refs_0_, bf16[4,336,128]{2,1,0:T(8,128)(2,1)} %copy-done.5, bf16[4,336,128]{2,1,0:T(8,128)(2,1)} %copy-done.6, ...), custom_call_target="tpu_custom_call" | custom-call | flops 1000000 | bytes 2752512 | tf_op jit(solution)/shard_map/fold/pallas_call | solution.py:721
  192.4 2.7 %collective-permute-start.27 = (bf16[1,336,128]{2,1,0:T(8,128)(2,1)}, bf16[1,336,128]{2,1,0:T(8,128)(2,1)S(1)}, u32[]{:S(2)}, u32[]{:S(2)}) collective-permute-start(bf16[1,336,128]{2,1,0:T(8,128)(2,1)} %get-tuple-element.246), channel_id=1, source_target_pairs={{0,8},{1,9},{2,10},{3,11},{4,12},{5,13},{6,14},{7,15},{8,0},{9,1},... | collective-permute-start | bytes 258056 | tf_op jit(solution)/shard_map/ppermute | solution.py:837
  195.4 2.9 %collective-permute-done.27.refs_1_ = bf16[1,336,128]{2,1,0:T(8,128)(2,1)S(1)} collective-permute-done((bf16[1,336,128]{2,1,0:T(8,128)(2,1)}, bf16[1,336,128]{2,1,0:T(8,128)(2,1)S(1)}, u32[]{:S(2)}, u32[]{:S(2)}) %collective-permute-start.27) | collective-permute-done | bytes 86048 | tf_op jit(solution)/shard_map/ppermute | solution.py:837
  198.3 1.7 collective-permute-start.29
  200.1 4.9 %collective-permute-done.28.refs_2_ = bf16[1,336,128]{2,1,0:T(8,128)(2,1)S(1)} collective-permute-done((bf16[1,336,128]{2,1,0:T(8,128)(2,1)}, bf16[1,336,128]{2,1,0:T(8,128)(2,1)S(1)}, u32[]{:S(2)}, u32[]{:S(2)}) %collective-permute-start.28) | collective-permute-done | bytes 86048 | tf_op jit(solution)/shard_map/ppermute | solution.py:837
  206.0 3.4 %finish.1 = (bf16[4,256,512]{2,1,0:T(8,128)(2,1)}, f32[16,1024]{1,0:T(8,128)}, f32[16,1536]{1,0:T(8,128)}, f32[16,512]{1,0:T(8,128)}, f32[16,2048]{1,0:T(8,128)}...) custom-call(s32[4]{0:T(128)} %pad_add_fusion.info_ref, ...), custom_call_target="tpu_custom_call" | custom-call | tf_op jit(solution)/shard_map/finish/pallas_call | solution.py:772
  (126 shorter events, 27.7 us)
Async XLA Ops:
  7.2 81.4 %all-gather.3.cloned.1.call-start = ((), (), s32[]{:S(2)}) async-start(), calls=%async_computation | async-start | bytes 4866048 | tf_op jit(solution)/shard_map/all_gather | solution.py:847
  12.6 17.9 %collective-permute-start.3 = (bf16[256,512]{1,0:T(8,128)(2,1)}, bf16[256,512]{1,0:T(8,128)(2,1)S(1)}, u32[]{:S(2)}, u32[]{:S(2)}) collective-permute-start(bf16[256,512]{1,0:T(8,128)(2,1)} %get-tuple-element.149), channel_id=1, source_target_pairs={{0,1},{1,0},{2,3},{3,2},{4,5},{5,4},{6,7},{7,6},{8,9},{9,8},{10,11... | collective-permute-start | bytes 786440 | tf_op jit(solution)/shard_map/ppermute | solution.py:837
  13.2 17.4 %collective-permute-start.4 = (bf16[256,512]{1,0:T(8,128)(2,1)}, bf16[256,512]{1,0:T(8,128)(2,1)S(1)}, u32[]{:S(2)}, u32[]{:S(2)}) collective-permute-start(bf16[256,512]{1,0:T(8,128)(2,1)} %get-tuple-element.150), channel_id=1, source_target_pairs={{0,2},{1,3},{2,0},{3,1},{4,6},{5,7},{6,4},{7,5},{8,10},{9,11},{10,... | collective-permute-start | bytes 786440 | tf_op jit(solution)/shard_map/ppermute | solution.py:837
  15.7 14.8 %collective-permute-start.5 = (bf16[256,512]{1,0:T(8,128)(2,1)}, bf16[256,512]{1,0:T(8,128)(2,1)S(1)}, u32[]{:S(2)}, u32[]{:S(2)}) collective-permute-start(bf16[256,512]{1,0:T(8,128)(2,1)} %get-tuple-element.151), channel_id=1, source_target_pairs={{0,3},{1,2},{2,1},{3,0},{4,7},{5,6},{6,5},{7,4},{8,11},{9,10},{10,... | collective-permute-start | bytes 786440 | tf_op jit(solution)/shard_map/ppermute | solution.py:837
  15.8 7.4 %collective-permute-start.2 = (bf16[1,336,128]{2,1,0:T(8,128)(2,1)}, bf16[1,336,128]{2,1,0:T(8,128)(2,1)S(1)}, u32[]{:S(2)}, u32[]{:S(2)}) collective-permute-start(bf16[1,336,128]{2,1,0:T(8,128)(2,1)} %bitcast.36), channel_id=1, source_target_pairs={{0,24},{1,25},{2,26},{3,27},{4,28},{5,29},{6,30},{7,31},{8,16},{9,... | collective-permute-start | bytes 258056 | tf_op jit(solution)/shard_map/ppermute | solution.py:837
  19.6 8.0 %collective-permute-start.1 = (bf16[1,336,128]{2,1,0:T(8,128)(2,1)}, bf16[1,336,128]{2,1,0:T(8,128)(2,1)S(1)}, u32[]{:S(2)}, u32[]{:S(2)}) collective-permute-start(bf16[1,336,128]{2,1,0:T(8,128)(2,1)} %bitcast.37), channel_id=1, source_target_pairs={{0,16},{1,17},{2,18},{3,19},{4,20},{5,21},{6,22},{7,23},{8,24},{9,... | collective-permute-start | bytes 258056 | tf_op jit(solution)/shard_map/ppermute | solution.py:837
  23.2 7.3 %collective-permute-start = (bf16[1,336,128]{2,1,0:T(8,128)(2,1)}, bf16[1,336,128]{2,1,0:T(8,128)(2,1)S(1)}, u32[]{:S(2)}, u32[]{:S(2)}) collective-permute-start(bf16[1,336,128]{2,1,0:T(8,128)(2,1)} %bitcast.38), channel_id=1, source_target_pairs={{0,8},{1,9},{2,10},{3,11},{4,12},{5,13},{6,14},{7,15},{8,0},{9,1},... | collective-permute-start | bytes 258056 | tf_op jit(solution)/shard_map/ppermute | solution.py:837
  31.6 11.9 %collective-permute-start.8 = (bf16[4,336,128]{2,1,0:T(8,128)(2,1)S(1)}, bf16[4,336,128]{2,1,0:T(8,128)(2,1)S(1)}, u32[]{:S(2)}, u32[]{:S(2)}) collective-permute-start(bf16[4,336,128]{2,1,0:T(8,128)(2,1)S(1)} %constant_dynamic-update-slice_fusion), channel_id=1, source_target_pairs={{0,6},{1,7},{2,4},{3,5},{4,2},{5,3},{6,0},{7,1},{8,14},{9,15},{10,... | collective-permute-start | bytes 1032200 | tf_op jit(solution)/shard_map/ppermute | solution.py:837
  34.2 17.8 %collective-permute-start.7 = (bf16[4,336,128]{2,1,0:T(8,128)(2,1)S(1)}, bf16[4,336,128]{2,1,0:T(8,128)(2,1)S(1)}, u32[]{:S(2)}, u32[]{:S(2)}) collective-permute-start(bf16[4,336,128]{2,1,0:T(8,128)(2,1)S(1)} %constant_dynamic-update-slice_fusion), channel_id=1, source_target_pairs={{0,4},{1,5},{2,6},{3,7},{4,0},{5,1},{6,2},{7,3},{8,12},{9,13},{10,... | collective-permute-start | bytes 1032200 | tf_op jit(solution)/shard_map/ppermute | solution.py:837
  34.6 19.5 %collective-permute-start.6 = (bf16[4,336,128]{2,1,0:T(8,128)(2,1)S(1)}, bf16[4,336,128]{2,1,0:T(8,128)(2,1)S(1)}, u32[]{:S(2)}, u32[]{:S(2)}) collective-permute-start(bf16[4,336,128]{2,1,0:T(8,128)(2,1)S(1)} %constant_dynamic-update-slice_fusion), channel_id=1, source_target_pairs={{0,2},{1,3},{2,0},{3,1},{4,6},{5,7},{6,4},{7,5},{8,10},{9,11},{10,... | collective-permute-start | bytes 1032200 | tf_op jit(solution)/shard_map/ppermute | solution.py:837
  56.7 19.5 %collective-permute-start.10 = (bf16[256,512]{1,0:T(8,128)(2,1)}, bf16[256,512]{1,0:T(8,128)(2,1)S(1)}, u32[]{:S(2)}, u32[]{:S(2)}) collective-permute-start(bf16[256,512]{1,0:T(8,128)(2,1)} %get-tuple-element.171), channel_id=1, source_target_pairs={{0,1},{1,0},{2,3},{3,2},{4,5},{5,4},{6,7},{7,6},{8,9},{9,8},{10,11... | collective-permute-start | bytes 786440 | tf_op jit(solution)/shard_map/ppermute | solution.py:837
  56.8 19.3 %collective-permute-start.11 = (bf16[256,512]{1,0:T(8,128)(2,1)}, bf16[256,512]{1,0:T(8,128)(2,1)S(1)}, u32[]{:S(2)}, u32[]{:S(2)}) collective-permute-start(bf16[256,512]{1,0:T(8,128)(2,1)} %get-tuple-element.172), channel_id=1, source_target_pairs={{0,2},{1,3},{2,0},{3,1},{4,6},{5,7},{6,4},{7,5},{8,10},{9,11},{10,... | collective-permute-start | bytes 786440 | tf_op jit(solution)/shard_map/ppermute | solution.py:837
  58.3 19.5 %collective-permute-start.12 = (bf16[256,512]{1,0:T(8,128)(2,1)}, bf16[256,512]{1,0:T(8,128)(2,1)S(1)}, u32[]{:S(2)}, u32[]{:S(2)}) collective-permute-start(bf16[256,512]{1,0:T(8,128)(2,1)} %get-tuple-element.173), channel_id=1, source_target_pairs={{0,3},{1,2},{2,1},{3,0},{4,7},{5,6},{6,5},{7,4},{8,11},{9,10},{10,... | collective-permute-start | bytes 786440 | tf_op jit(solution)/shard_map/ppermute | solution.py:837
  116.9 12.5 %collective-permute-start.17 = (bf16[256,512]{1,0:T(8,128)(2,1)}, bf16[256,512]{1,0:T(8,128)(2,1)S(1)}, u32[]{:S(2)}, u32[]{:S(2)}) collective-permute-start(bf16[256,512]{1,0:T(8,128)(2,1)} %get-tuple-element.188), channel_id=1, source_target_pairs={{0,1},{1,0},{2,3},{3,2},{4,5},{5,4},{6,7},{7,6},{8,9},{9,8},{10,11... | collective-permute-start | bytes 786440 | tf_op jit(solution)/shard_map/ppermute | solution.py:837
  117.2 37.0 %collective-permute-start.18 = (bf16[256,512]{1,0:T(8,128)(2,1)}, bf16[256,512]{1,0:T(8,128)(2,1)}, u32[]{:S(2)}, u32[]{:S(2)}) collective-permute-start(bf16[256,512]{1,0:T(8,128)(2,1)} %get-tuple-element.189), channel_id=1, source_target_pairs={{0,2},{1,3},{2,0},{3,1},{4,6},{5,7},{6,4},{7,5},{8,10},{9,11},{10,... | collective-permute-start | bytes 786440 | tf_op jit(solution)/shard_map/ppermute | solution.py:837
  118.7 35.5 %collective-permute-start.19 = (bf16[256,512]{1,0:T(8,128)(2,1)}, bf16[256,512]{1,0:T(8,128)(2,1)}, u32[]{:S(2)}, u32[]{:S(2)}) collective-permute-start(bf16[256,512]{1,0:T(8,128)(2,1)} %get-tuple-element.190), channel_id=1, source_target_pairs={{0,3},{1,2},{2,1},{3,0},{4,7},{5,6},{6,5},{7,4},{8,11},{9,10},{10,... | collective-permute-start | bytes 786440 | tf_op jit(solution)/shard_map/ppermute | solution.py:837
  127.3 26.9 %collective-permute-start.14 = (bf16[4,576,128]{2,1,0:T(8,128)(2,1)}, bf16[4,576,128]{2,1,0:T(8,128)(2,1)S(1)}, u32[]{:S(2)}, u32[]{:S(2)}) collective-permute-start(bf16[4,576,128]{2,1,0:T(8,128)(2,1)} %get-tuple-element.184), channel_id=1, source_target_pairs={{0,2},{1,3},{2,0},{3,1},{4,6},{5,7},{6,4},{7,5},{8,10},{9,11},{10,... | collective-permute-start | bytes 1769480 | tf_op jit(solution)/shard_map/ppermute | solution.py:837
  128.8 28.1 %collective-permute-start.15 = (bf16[4,576,128]{2,1,0:T(8,128)(2,1)}, bf16[4,576,128]{2,1,0:T(8,128)(2,1)S(1)}, u32[]{:S(2)}, u32[]{:S(2)}) collective-permute-start(bf16[4,576,128]{2,1,0:T(8,128)(2,1)} %get-tuple-element.185), channel_id=1, source_target_pairs={{0,4},{1,5},{2,6},{3,7},{4,0},{5,1},{6,2},{7,3},{8,12},{9,13},{10,... | collective-permute-start | bytes 1769480 | tf_op jit(solution)/shard_map/ppermute | solution.py:837
  129.4 27.5 %collective-permute-start.16 = (bf16[4,576,128]{2,1,0:T(8,128)(2,1)}, bf16[4,576,128]{2,1,0:T(8,128)(2,1)S(1)}, u32[]{:S(2)}, u32[]{:S(2)}) collective-permute-start(bf16[4,576,128]{2,1,0:T(8,128)(2,1)} %get-tuple-element.186), channel_id=1, source_target_pairs={{0,6},{1,7},{2,4},{3,5},{4,2},{5,3},{6,0},{7,1},{8,14},{9,15},{10,... | collective-permute-start | bytes 1769480 | tf_op jit(solution)/shard_map/ppermute | solution.py:837
  156.9 6.6 %collective-permute-start.20 = (bf16[16,336,128]{2,1,0:T(8,128)(2,1)}, bf16[16,336,128]{2,1,0:T(8,128)(2,1)S(1)}, u32[]{:S(2)}, u32[]{:S(2)}) collective-permute-start(bf16[16,336,128]{2,1,0:T(8,128)(2,1)} %get-tuple-element.205), channel_id=1, source_target_pairs={{0,1},{1,0},{2,3},{3,2},{4,5},{5,4},{6,7},{7,6},{8,9},{9,8},{10,11... | collective-permute-start | bytes 4128776 | tf_op jit(solution)/shard_map/ppermute | solution.py:837
  168.4 18.9 %collective-permute-start.21 = (bf16[4,336,128]{2,1,0:T(8,128)(2,1)}, bf16[4,336,128]{2,1,0:T(8,128)(2,1)S(1)}, u32[]{:S(2)}, u32[]{:S(2)}) collective-permute-start(bf16[4,336,128]{2,1,0:T(8,128)(2,1)} %get-tuple-element.230), channel_id=1, source_target_pairs={{0,2},{1,3},{2,0},{3,1},{4,6},{5,7},{6,4},{7,5},{8,10},{9,11},{10,... | collective-permute-start | bytes 1032200 | tf_op jit(solution)/shard_map/ppermute | solution.py:837
  169.7 17.8 %collective-permute-start.22 = (bf16[4,336,128]{2,1,0:T(8,128)(2,1)}, bf16[4,336,128]{2,1,0:T(8,128)(2,1)S(1)}, u32[]{:S(2)}, u32[]{:S(2)}) collective-permute-start(bf16[4,336,128]{2,1,0:T(8,128)(2,1)} %get-tuple-element.231), channel_id=1, source_target_pairs={{0,4},{1,5},{2,6},{3,7},{4,0},{5,1},{6,2},{7,3},{8,12},{9,13},{10,... | collective-permute-start | bytes 1032200 | tf_op jit(solution)/shard_map/ppermute | solution.py:837
  171.2 16.3 %collective-permute-start.23 = (bf16[4,336,128]{2,1,0:T(8,128)(2,1)}, bf16[4,336,128]{2,1,0:T(8,128)(2,1)S(1)}, u32[]{:S(2)}, u32[]{:S(2)}) collective-permute-start(bf16[4,336,128]{2,1,0:T(8,128)(2,1)} %get-tuple-element.232), channel_id=1, source_target_pairs={{0,6},{1,7},{2,4},{3,5},{4,2},{5,3},{6,0},{7,1},{8,14},{9,15},{10,... | collective-permute-start | bytes 1032200 | tf_op jit(solution)/shard_map/ppermute | solution.py:837
  171.9 7.4 %collective-permute-start.24 = (bf16[1,576,128]{2,1,0:T(8,128)(2,1)S(1)}, bf16[1,576,128]{2,1,0:T(8,128)(2,1)S(1)}, u32[]{:S(2)}, u32[]{:S(2)}) collective-permute-start(bf16[1,576,128]{2,1,0:T(8,128)(2,1)S(1)} %copy-done.31), channel_id=1, source_target_pairs={{0,8},{1,9},{2,10},{3,11},{4,12},{5,13},{6,14},{7,15},{8,0},{9,1},... | collective-permute-start | bytes 442376 | tf_op jit(solution)/shard_map/ppermute | solution.py:837
  174.0 13.3 %collective-permute-start.25 = (bf16[1,576,128]{2,1,0:T(8,128)(2,1)S(1)}, bf16[1,576,128]{2,1,0:T(8,128)(2,1)S(1)}, u32[]{:S(2)}, u32[]{:S(2)}) collective-permute-start(bf16[1,576,128]{2,1,0:T(8,128)(2,1)S(1)} %copy-done.30), channel_id=1, source_target_pairs={{0,16},{1,17},{2,18},{3,19},{4,20},{5,21},{6,22},{7,23},{8,24},{9,... | collective-permute-start | bytes 442376 | tf_op jit(solution)/shard_map/ppermute | solution.py:837
  179.3 8.0 %collective-permute-start.26 = (bf16[1,576,128]{2,1,0:T(8,128)(2,1)S(1)}, bf16[1,576,128]{2,1,0:T(8,128)(2,1)S(1)}, u32[]{:S(2)}, u32[]{:S(2)}) collective-permute-start(bf16[1,576,128]{2,1,0:T(8,128)(2,1)S(1)} %copy-done.29), channel_id=1, source_target_pairs={{0,24},{1,25},{2,26},{3,27},{4,28},{5,29},{6,30},{7,31},{8,16},{9,... | collective-permute-start | bytes 442376 | tf_op jit(solution)/shard_map/ppermute | solution.py:837
  187.5 17.5 %collective-permute-start.30 = (bf16[256,512]{1,0:T(8,128)(2,1)S(1)}, bf16[256,512]{1,0:T(8,128)(2,1)S(1)}, u32[]{:S(2)}, u32[]{:S(2)}) collective-permute-start(bf16[256,512]{1,0:T(8,128)(2,1)S(1)} %copy-done.22), channel_id=1, source_target_pairs={{0,1},{1,0},{2,3},{3,2},{4,5},{5,4},{6,7},{7,6},{8,9},{9,8},{10,11... | collective-permute-start | bytes 786440 | tf_op jit(solution)/shard_map/ppermute | solution.py:837
  187.6 17.4 %collective-permute-start.31 = (bf16[256,512]{1,0:T(8,128)(2,1)S(1)}, bf16[256,512]{1,0:T(8,128)(2,1)S(1)}, u32[]{:S(2)}, u32[]{:S(2)}) collective-permute-start(bf16[256,512]{1,0:T(8,128)(2,1)S(1)} %copy-done.21), channel_id=1, source_target_pairs={{0,2},{1,3},{2,0},{3,1},{4,6},{5,7},{6,4},{7,5},{8,10},{9,11},{10,... | collective-permute-start | bytes 786440 | tf_op jit(solution)/shard_map/ppermute | solution.py:837
  188.7 16.3 %collective-permute-start.32 = (bf16[256,512]{1,0:T(8,128)(2,1)S(1)}, bf16[256,512]{1,0:T(8,128)(2,1)S(1)}, u32[]{:S(2)}, u32[]{:S(2)}) collective-permute-start(bf16[256,512]{1,0:T(8,128)(2,1)S(1)} %copy-done.20), channel_id=1, source_target_pairs={{0,3},{1,2},{2,1},{3,0},{4,7},{5,6},{6,5},{7,4},{8,11},{9,10},{10,... | collective-permute-start | bytes 786440 | tf_op jit(solution)/shard_map/ppermute | solution.py:837
  192.4 5.9 %collective-permute-start.27 = (bf16[1,336,128]{2,1,0:T(8,128)(2,1)}, bf16[1,336,128]{2,1,0:T(8,128)(2,1)S(1)}, u32[]{:S(2)}, u32[]{:S(2)}) collective-permute-start(bf16[1,336,128]{2,1,0:T(8,128)(2,1)} %get-tuple-element.246), channel_id=1, source_target_pairs={{0,8},{1,9},{2,10},{3,11},{4,12},{5,13},{6,14},{7,15},{8,0},{9,1},... | collective-permute-start | bytes 258056 | tf_op jit(solution)/shard_map/ppermute | solution.py:837
  195.1 9.9 %collective-permute-start.28 = (bf16[1,336,128]{2,1,0:T(8,128)(2,1)}, bf16[1,336,128]{2,1,0:T(8,128)(2,1)S(1)}, u32[]{:S(2)}, u32[]{:S(2)}) collective-permute-start(bf16[1,336,128]{2,1,0:T(8,128)(2,1)} %get-tuple-element.247), channel_id=1, source_target_pairs={{0,16},{1,17},{2,18},{3,19},{4,20},{5,21},{6,22},{7,23},{8,24},{9,... | collective-permute-start | bytes 258056 | tf_op jit(solution)/shard_map/ppermute | solution.py:837
  198.3 6.7 %collective-permute-start.29 = (bf16[1,336,128]{2,1,0:T(8,128)(2,1)}, bf16[1,336,128]{2,1,0:T(8,128)(2,1)S(1)}, u32[]{:S(2)}, u32[]{:S(2)}) collective-permute-start(bf16[1,336,128]{2,1,0:T(8,128)(2,1)} %get-tuple-element.248), channel_id=1, source_target_pairs={{0,24},{1,25},{2,26},{3,27},{4,28},{5,29},{6,30},{7,31},{8,16},{9,... | collective-permute-start | bytes 258056 | tf_op jit(solution)/shard_map/ppermute | solution.py:837
  (35 other events, 339.7 us)
Sparse Core Ops, SparseCore 0:
  12.8 75.8 all-gather.2

commit v3 on v2

--- a/solution.py
+++ b/solution.py
@@ -73,13 +73,22 @@
         self.lengths = lengths
         self.owned = [n // devices for n in lengths]
         self.small_rows = 16
+        self.z_order = (0, 16, 8, 24)
         starts = [0]
         for n in lengths:
             starts.append(starts[-1] + n // LANE)
         self.block_starts = starts
 
     def place(self, mask):
-        return ((mask >> 1) & 3) * 4 + ((mask >> 3) & 3)
+        return ((mask >> 1) & 3) * 4 + self.z_order.index(mask & 24)
+
+    def grad_piece(self, half, mask, at, rows):
+        cut = self.late_rows // 2
+        if at < cut:
+            assert at + rows <= cut
+            return half.at[self.place(mask), at : at + rows, :]
+        swapped = (mask & ~6) | ((mask >> 1) & 2) | ((mask & 2) << 1)
+        return half.at[16 + self.place(swapped), at - cut : at - cut + rows, :]
 
 
 def fill_early(plan, me, halves, table_ref, inward_ref, small_ref, stage_ref):
@@ -216,14 +225,14 @@
             parts = []
 
 
-def attend(plan, info, pieces, weights):
+def attend(plan, info, count, pieces, weights):
     total_rows, width = plan.total_rows, plan.width
     block = pl.BlockSpec((total_rows, LANE), lambda p, *_: (0, p))
-    low = like((total_rows, width), BF)
+    low = pltpu.HBM((total_rows, width), BF)
     inward = (3 * plan.lanes, width, LANE)
     small = (plan.small_rows, width)
     return pl.pallas_call(
-        functools.partial(attend_kernel, plan, len(pieces)),
+        functools.partial(attend_kernel, plan, count),
         grid_spec=pltpu.PrefetchScalarGridSpec(
             num_scalar_prefetch=1,
             grid=(plan.lanes,),
@@ -246,16 +255,16 @@
             ],
         ),
         out_shape=[
-            like((total_rows, width), F32),
+            pltpu.HBM((total_rows, width), F32),
             low,
             low,
             low,
             low,
-            like((plan.lanes, 8, total_rows), F32),
-            like(inward, BF),
-            like(small, F32),
+            pltpu.HBM((plan.lanes, 8, total_rows), F32),
+            pltpu.HBM(inward, BF),
+            pltpu.HBM(small, F32),
         ],
-        compiler_params=params(60),
+        compiler_params=params(36),
         cost_estimate=cost(5 * 10**9, 14 * 2**20, 6 * 10**6),
         name="attend",
     )(info, *pieces, *weights)
@@ -277,8 +286,8 @@
 def feed_kernel(plan, count, info_ref, lifted_ref, mixed_ref, *refs):
     upstreams, refs = refs[:count], refs[count:]
     if plan.packed:
-        late_in, small_ref = refs[:2]
-        refs = refs[2:]
+        late_halves, small_ref = refs[:2], refs[2]
+        refs = refs[3:]
     else:
         outward_in, expand_in, contract_in, small_ref = refs[:4]
         refs = refs[4:]
@@ -300,9 +309,10 @@
     @pl.when(step == 0)
     def _():
         if plan.packed:
-            for device in range(plan.devices):
-                rows = slice(device * TILE, (device + 1) * TILE)
-                shard = late_in.at[device]
+            for mask in range(plan.devices):
+                shard = late_halves[mask & 1].at[plan.place(mask)]
+                owner = info_ref[1] ^ mask
+                rows, wide = aligned(owner, TILE), aligned(owner, contract_own)
                 for lane in range(lanes):
                     cut = slice(lane * LANE, (lane + 1) * LANE)
                     outward_ref[rows, cut] = shard[lane * TILE : (lane + 1) * TILE, :]
@@ -310,7 +320,7 @@
                         at = (lanes + part * lanes + lane) * TILE
                         expand_ref[part, rows, cut] = shard[at : at + TILE, :]
                     at = contract_at + lane * contract_own
-                    contract_ref[device * contract_own : (device + 1) * contract_own, cut] = shard[at : at + contract_own, :]
+                    contract_ref[wide, cut] = shard[at : at + contract_own, :]
         else:
             outward_ref[...] = outward_in[...]
             expand_ref[...] = expand_in[...]
@@ -399,52 +409,55 @@
             me = info_ref[1]
             whole_ref[...] = outward
             for mask in range(plan.devices):
-                shard = halves[mask & 1].at[plan.place(mask)]
+                half = halves[mask & 1]
                 rows = aligned(me ^ mask, TILE)
                 for lane in range(lanes):
                     cut = slice(lane * LANE, (lane + 1) * LANE)
-                    shard[lane * TILE : (lane + 1) * TILE, :] = whole_ref[rows, cut].astype(BF)
+                    plan.grad_piece(half, mask, lane * TILE, TILE)[...] = whole_ref[rows, cut].astype(BF)
         else:
             outward_out[...] = outward.astype(BF)
         per_part = plan.devices // parts
+        for part in range(parts):
+            cut = slice(part * width, (part + 1) * width)
+            expand = t_times(normed_all[...], hidden_all[:, cut])
+            if not plan.packed:
+                expand_out[part] = expand.astype(BF)
+                continue
+            expand_sum[...] = expand
+            for mask in range(plan.devices):
+                rows = aligned(me ^ mask, TILE)
+                for lane in range(lanes):
+                    at = (lanes + part * lanes + lane) * TILE
+                    plan.grad_piece(halves[mask & 1], mask, at, TILE)[...] = expand_sum[
+                        rows, lane * LANE : (lane + 1) * LANE
+                    ].astype(BF)
         for mask_part in range(parts):
             part = (me // per_part) ^ mask_part if plan.packed else mask_part
             cut = pl.ds(pl.multiple_of(part * width, width), width)
-            expand = t_times(normed_all[...], hidden_all[:, cut])
             contract = t_times(active_all[:, cut], lowered_all[...])
             if not plan.packed:
-                expand_out[mask_part] = expand.astype(BF)
                 contract_out[cut, :] = contract.astype(BF)
                 continue
-            expand_sum[...] = expand
             contract_sum[...] = contract
-            for mask in range(plan.devices):
-                shard = halves[mask & 1].at[plan.place(mask)]
-                rows = aligned(me ^ mask, TILE)
-                for lane in range(lanes):
-                    at = aligned(lanes + part * lanes + lane, TILE)
-                    shard[at, :] = expand_sum[rows, lane * LANE : (lane + 1) * LANE].astype(BF)
             for index in range(per_part):
                 mask = mask_part * per_part + index
-                shard = halves[mask & 1].at[plan.place(mask)]
                 rows = aligned((me ^ mask) % per_part, contract_own)
                 for lane in range(lanes):
                     at = contract_at + lane * contract_own
-                    shard[at : at + contract_own, :] = contract_sum[
+                    plan.grad_piece(halves[mask & 1], mask, at, contract_own)[...] = contract_sum[
                         rows, lane * LANE : (lane + 1) * LANE
                     ].astype(BF)
 
 
-def feed(plan, info, lifted, mixed, upstreams, weights, small):
+def feed(plan, info, count, lifted, mixed, upstreams, weights, small):
     total_rows, width, parts = plan.total_rows, plan.width, plan.parts
-    count = len(upstreams)
     piece = total_rows // count
     size = max(piece, FEED_ROWS)
     group = size // piece
     rows = pl.BlockSpec((size, width), lambda i, info: ((info[2] // group) ^ i, 0))
     outward, expand, contract = (width, width), (parts, width, width), (parts * width, width)
     if plan.packed:
-        grads = [like((plan.devices // 2, plan.late_rows, LANE), BF)] * 2
+        grads = [like((plan.devices, plan.late_rows // 2, LANE), BF)] * 2
     else:
         grads = [like(outward, BF), like(expand, BF), like(contract, BF)]
     ends = [like((piece, width), BF)] * count
@@ -656,7 +669,7 @@
             ],
         ),
         out_shape=tokens + grads,
-        compiler_params=params(60),
+        compiler_params=params(44),
         cost_estimate=cost(14 * 10**9, 24 * 2**20, 6 * 10**6),
         name="attend_back",
     )(info, lifted, query, key, value, mixed, mixed_back, totals, inward, first_back, small_grad)
@@ -704,39 +717,20 @@
     )(outward, expand, contract)
 
 
-def fold_kernel(count, *refs):
-    total = refs[0][...].astype(F32)
-    for ref in refs[1:count]:
-        total = total + ref[...].astype(F32)
-    size = total.shape[0] // len(refs[count:])
-    for index, ref in enumerate(refs[count:]):
-        ref[...] = total[index * size : (index + 1) * size].astype(ref.dtype)
-
-
 def fold(terms, cuts):
-    entries, rows, _ = terms[0].shape
-    pieces = 4 if rows % 64 == 0 else 3
-    size = rows // pieces
-    out = like((entries // cuts, rows, LANE), BF)
-    return pl.pallas_call(
-        functools.partial(fold_kernel, len(terms)),
-        grid=(pieces,),
-        in_specs=[pl.BlockSpec((entries, size, LANE), lambda i: (0, i, 0))] * len(terms),
-        out_specs=[pl.BlockSpec((entries // cuts, size, LANE), lambda i: (0, i, 0))] * cuts,
-        out_shape=[out] * cuts,
-        cost_estimate=cost(10**6, len(terms) * entries * rows * LANE * 4),
-        name="fold",
-    )(*terms)
-
-
-def finish_kernel(plan, count, info_ref, *refs):
-    early, late, tokens = refs[:4], refs[4:8], refs[8 : 8 + count]
-    (tokens_ref, table_ref, inward_ref, outward_ref, expand_ref, contract_ref) = refs[8 + count : 14 + count]
-    vectors = refs[14 + count :]
+    size = terms[0].shape[0] // cuts
+    return [
+        sum(term[index * size : (index + 1) * size].astype(F32) for term in terms).astype(BF)
+        for index in range(cuts)
+    ]
+
+
+def finish_kernel(plan, info_ref, *refs):
+    early, late, refs = refs[:4], refs[4:8], refs[8:]
+    table_ref, inward_ref, outward_ref, expand_ref, contract_ref = refs[:5]
+    vectors = refs[5:]
     early = sum(ref[0].astype(F32) for ref in early)
     late = sum(ref[0].astype(F32) for ref in late)
-    for mask in range(count):
-        tokens_ref[pl.ds(info_ref[2] ^ mask, 1), :, :] = tokens[mask][...][None]
     for piece in range(plan.table_pieces):
         table_ref[:, piece * LANE : (piece + 1) * LANE] = early[piece * TILE : (piece + 1) * TILE]
     for piece in range(3 * plan.lanes):
@@ -757,20 +751,18 @@
         ref[...] = row[vector : vector + 1, :size]
 
 
-def finish(plan, info, micro_count, early, late, tokens):
-    rows, width = tokens[0].shape
-    own = plan.own_rows
+def finish(plan, info, early, late):
+    own, width = plan.own_rows, plan.width
     outs = [
-        like((micro_count, rows, width), BF),
         like((own, plan.total_rows), F32),
         like((own, 3 * width), F32),
         like((own, width), F32),
         like((own, plan.hidden), F32),
         like((plan.hidden // plan.devices, width), F32),
     ] + [like((1, n), F32) for n in plan.owned]
-    values = early + late + tokens
+    values = early + late
     return pl.pallas_call(
-        functools.partial(finish_kernel, plan, len(tokens)),
+        functools.partial(finish_kernel, plan),
         grid_spec=pltpu.PrefetchScalarGridSpec(
             num_scalar_prefetch=1,
             grid=(1,),
@@ -780,6 +772,13 @@
         out_shape=outs,
         name="finish",
     )(info, *values)
+
+
+def ordered(rank, pieces):
+    for bit in (1, 2):
+        flip = (rank & bit) > 0
+        pieces = [jnp.where(flip, pieces[i ^ bit], pieces[i]) for i in range(4)]
+    return jnp.stack(pieces)
 
 
 def settle_kernel(count, share, info_ref, *refs):
@@ -839,63 +838,92 @@
     def exchange(pieces):
         return [swap(piece, mask) for mask, piece in enumerate(pieces)]
 
+    def in_order(pieces):
+        if count != 4 or share != 1:
+            return settle_rows(info, micro_count, share, pieces)
+        return ordered(rank, pieces)
+
     if plan.packed:
+        rows_in = cut_rows(tokens[:, 0], count, share)
+        rows_in, inward = lax.optimization_barrier((rows_in, inward))
+        rows_in = exchange(rows_in)
         shard = pack_early(plan, positions.T, inward, vectors)[None]
-        late_shard = pack_late(plan, outward, expand, contract)
-        rows_in = cut_rows(tokens[:, 0], count, share)
-        shard, late_shard, rows_in = lax.optimization_barrier((shard, late_shard, rows_in))
-        late = [lax.all_gather(late_shard, AXES, axis=0, tiled=False)]
-        pieces = [swap(shard, k << 3) for k in range(4)]
-        pieces, rows_in = lax.optimization_barrier((pieces, exchange(rows_in)))
+        shard, rows_in[1], outward = lax.optimization_barrier((shard, rows_in[1], outward))
+        pieces = [swap(shard, mask) for mask in plan.z_order]
+        late = pack_late(plan, outward, expand, contract)[None]
+        pieces, rows_in, info, late, cotangent = lax.optimization_barrier(
+            (pieces, rows_in, info, late, cotangent)
+        )
         shard = jnp.concatenate(pieces, axis=0)
         pieces = [swap(shard, k << 1) for k in range(4)]
+        late = [swap(late, mask) for mask in plan.z_order]
         upstreams = cut_rows(cotangent[:, 0], count, share)
-        pieces, upstreams = lax.optimization_barrier((pieces, upstreams))
+        pieces, upstreams, late = lax.optimization_barrier((pieces, list(upstreams), late))
+        late = jnp.concatenate(late, axis=0)
+        late_x, late_y = swap(late, 2), swap(late, 4)
         shard = jnp.concatenate(pieces, axis=0)
         early = [shard, swap(shard, 1)]
-        upstreams = exchange(upstreams)
+        upstreams[1] = swap(upstreams[1], 1)
+        early, late_x, late_y, upstreams = lax.optimization_barrier((early, late_x, late_y, upstreams))
+        late_xy = swap(late_x, 4)
+        upstreams[2:] = [swap(upstreams[mask], mask) for mask in (2, 3)]
     else:
         rows_in = exchange(cut_rows(tokens[:, 0], count, share))
         upstreams = exchange(cut_rows(cotangent[:, 0], count, share))
         early, late = plain_weights(plan, positions, inward, vectors, outward, expand, contract)
-    lifted, query, key, value, mixed, totals, inward_all, small = attend(plan, info, rows_in, early)
+    lifted, query, key, value, mixed, totals, inward_all, small = attend(plan, info, count, rows_in, early)
+    if plan.packed:
+        late_xy, upstreams, mixed = lax.optimization_barrier((late_xy, upstreams, mixed))
+        late = jnp.concatenate([late, late_x, late_y, late_xy], axis=0)
+        late = [late, swap(late, 1)]
     results, (mixed_back, first_back, small_grad), late_grads = feed(
-        plan, info, lifted, mixed, upstreams, late, small
+        plan, info, count, lifted, mixed, upstreams, late, small
     )
     results = exchange(results)
     if plan.packed:
         keep, send = late_grads
-        terms = fold([keep, swap(send, 1)], 4)
-        terms, mixed_back = lax.optimization_barrier((terms, mixed_back))
-        late_terms = [swap(term, k << 1) for k, term in enumerate(terms)]
+        one, one_send, two, two_send = fold([keep, swap(send, 1)], 4)
+        one, one_send, two, two_send, mixed_back = lax.optimization_barrier(
+            (one, one_send, two, two_send, mixed_back)
+        )
+        one_other, two_other = swap(one_send, 4), swap(two_send, 2)
     token_pieces, early_grads = attend_back(
         plan, info, count, lifted, (query, key, value, mixed, totals), mixed_back, inward_all,
         first_back, small_grad,
     )
     if plan.packed:
-        late_terms, results, token_pieces, early_grads = lax.optimization_barrier(
-            (late_terms, results, token_pieces, early_grads)
+        one_other, two_other, results, token_pieces, early_grads = lax.optimization_barrier(
+            (one_other, two_other, results, token_pieces, early_grads)
         )
         keep, send = early_grads
         send = swap(send, 1)
-        late_terms = fold(late_terms, 4)
-        output = settle_rows(info, micro_count, share, results)
-        send, late_terms, output = lax.optimization_barrier((send, late_terms, output))
+        one, one_send = fold([one, one_other], 2)
+        two, two_send = fold([two, two_other], 2)
+        one, one_send, two, two_send, keep = lax.optimization_barrier((one, one_send, two, two_send, keep))
+        one_other, two_other = swap(one_send, 2), swap(two_send, 4)
         terms = fold([keep, send], 4)
-        terms, late_terms = lax.optimization_barrier((terms, late_terms))
+        terms, results, token_pieces = lax.optimization_barrier((terms, results, token_pieces))
         terms = [swap(term, k << 1) for k, term in enumerate(terms)]
-        late_terms = [swap(term, k << 3) for k, term in enumerate(late_terms)]
-        terms, late_terms, token_pieces = lax.optimization_barrier((terms, late_terms, token_pieces))
-        token_pieces = exchange(token_pieces)
+        one_other, two_other, terms[2], results = lax.optimization_barrier(
+            (one_other, two_other, terms[2], results)
+        )
+        ones, twos = fold([one, one_other], 4), fold([two, two_other], 4)
+        late_terms = [jnp.concatenate(pair, axis=1) for pair in zip(ones, twos)]
+        late_terms = [swap(term, mask) for term, mask in zip(late_terms, plan.z_order)]
+        output = in_order(results)
+        terms, late_terms, output, token_pieces = lax.optimization_barrier(
+            (terms, late_terms, output, token_pieces)
+        )
         terms = fold(terms, 4)
-        early_terms = [swap(term, k << 3) for k, term in enumerate(terms)]
-        values = finish(plan, info, micro_count, early_terms, late_terms, token_pieces)
-        tokens_back, table_t, inward_own, outward_own, expand_own, contract_own = values[:6]
-        own = [v.reshape(-1) for v in values[6:]]
+        early_terms = [swap(term, mask) for term, mask in zip(terms, plan.z_order)]
+        tokens_back = in_order(exchange(token_pieces))
+        values = finish(plan, info, early_terms, late_terms)
+        table_t, inward_own, outward_own, expand_own, contract_own = values[:5]
+        own = [v.reshape(-1) for v in values[5:]]
         table_own = table_t.T
     else:
-        output = settle_rows(info, micro_count, share, results)
-        tokens_back = settle_rows(info, micro_count, share, exchange(token_pieces))
+        output = in_order(results)
+        tokens_back = in_order(exchange(token_pieces))
         table_own, inward_own, outward_own, expand_own, contract_own, own = plain_grads(
             plan, counted, early_grads, late_grads
         )

time: 217 us -> 201 us (0.926)
  Pallas kernels: 96.6 us -> 74.1 us
  between operations: 14.4 us -> 1.15 us
  starting transfers between devices: 36.7 us -> 48.3 us
  other arithmetic: 1.87 us -> 12 us
    pallas_call x7 -> x2, Pallas kernels: 37.7 us -> 17.1 us  [the longest x1 14.3 us: attend(): pl.pallas_call(functools.partial(attend_kernel, plan, count), grid_spec=p...]
    ppermute x33 -> x41, starting transfers between devices: 36.7 us -> 48.3 us  [swap(): lax.ppermute(value, AXES, [(d, d ^ mask) for d in range(devices)])]
    all_gather x1 -> x0, waiting for transfers between devices: 10.8 us -> none  [local(): late = [lax.all_gather(late_shard, AXES, axis=0, tiled=False)]]
    ppermute x33 -> x41, waiting for transfers between devices: 49.7 us -> 58.9 us  [swap(): lax.ppermute(value, AXES, [(d, d ^ mask) for d in range(devices)])]
    convert_element_type x0 -> x6, other arithmetic: none -> 6.84 us  [fold(): sum((term[index * size:(index + 1) * size].astype(F32) for term in terms))]
    unnamed x72 -> x76, local copies, waits for them, and re-layouts: 6.04 us -> 5.54 us
  transfers between devices with their start and end apart: 34 -> 41, of which waited for: 15 -> 18; matrix products, arithmetic and copies ran while one was open for 1% -> 5% of each run, Pallas kernels for 26% -> 22%
where the time goes in v3:
time: 201 us; the launch traced here: 200 us
  Pallas kernels  74.1 us (37%)
  waiting for transfers between devices  58.9 us (29%)
  starting transfers between devices  48.3 us (24%)
  other arithmetic  12 us (6%)
  local copies, waits for them, and re-layouts  5.68 us (3%)
    ppermute x41, waiting for transfers between devices, swap(): lax.ppermute(value, AXES, [(d, d ^ mask) for d in range(devices)])  58.9 us
    ppermute x41, starting transfers between devices, swap(): lax.ppermute(value, AXES, [(d, d ^ mask) for d in range(devices)])  48.3 us
    pallas_call x1, Pallas kernels, feed(): pl.pallas_call(functools.partial(feed_kernel, plan, count), grid_spec=plt...  28 us
    pallas_call x1, Pallas kernels, attend_back(): pl.pallas_call(functools.partial(attend_back_kernel, plan, count), grid_s...  21.4 us
    pallas_call x1, Pallas kernels, attend(): pl.pallas_call(functools.partial(attend_kernel, plan, count), grid_spec=p...  14.3 us
    convert_element_type x6, other arithmetic, fold(): sum((term[index * size:(index + 1) * size].astype(F32) for term in terms))  6.84 us
    unnamed x76, local copies, waits for them, and re-layouts  5.54 us
    pallas_call x2, Pallas kernels, cut_rows(): pl.pallas_call(functools.partial(cut_kernel, count, share), out_shape=out...  4.49 us
  transfers between devices with their start and end apart: 41, of which 18 were waited for; matrix products, arithmetic and copies ran while one was open for 5% of the time, Pallas kernels for 22%

profile of v3, /device:TPU:0, one launch (start us, length us, event | category | flops | bytes accessed | tf_op | source)
XLA Modules:
  0.0 200.1 jit_solution(4220473743360927984)
XLA Ops:
  0.6 2.2 %cut_rows.2 = (bf16[256,512]{1,0:T(8,128)(2,1)}, bf16[256,512]{1,0:T(8,128)(2,1)}, bf16[256,512]{1,0:T(8,128)(2,1)}, bf16[256,512]{1,0:T(8,128)(2,1)}) custom-call(bf16[4,256,512]{2,1,0:T(8,128)(2,1)} %bitcast.50), custom_call_target="tpu_custom_call" | custom-call | bytes 4194304 | tf_op jit(solution)/shard_map/cut_rows/pallas_call | solution.py:812
  3.3 2.5 %collective-permute-start.4 = (bf16[256,512]{1,0:T(8,128)(2,1)}, bf16[256,512]{1,0:T(8,128)(2,1)S(1)}, u32[]{:S(2)}, u32[]{:S(2)}) collective-permute-start(bf16[256,512]{1,0:T(8,128)(2,1)} %get-tuple-element.167), channel_id=1, source_target_pairs={{0,2},{1,3},{2,0},{3,1},{4,6},{5,7},{6,4},{7,5},{8,10},{9,11},{10,... | collective-permute-start | bytes 786440 | tf_op jit(solution)/shard_map/ppermute | solution.py:836
  6.0 1.6 pack_early.1
  8.8 2.8 %collective-permute-start.1 = (bf16[1,336,128]{2,1,0:T(8,128)(2,1)}, bf16[1,336,128]{2,1,0:T(8,128)(2,1)S(1)}, u32[]{:S(2)}, u32[]{:S(2)}) collective-permute-start(bf16[1,336,128]{2,1,0:T(8,128)(2,1)} %bitcast.57), channel_id=1, source_target_pairs={{0,16},{1,17},{2,18},{3,19},{4,20},{5,21},{6,22},{7,23},{8,24},{9,... | collective-permute-start | bytes 258056 | tf_op jit(solution)/shard_map/ppermute | solution.py:836
  11.7 1.6 collective-permute-start.2
  15.5 2.9 %collective-permute-done.5.refs_3_ = bf16[256,512]{1,0:T(8,128)(2,1)S(1)} collective-permute-done((bf16[256,512]{1,0:T(8,128)(2,1)}, bf16[256,512]{1,0:T(8,128)(2,1)S(1)}, u32[]{:S(2)}, u32[]{:S(2)}) %collective-permute-start.5) | collective-permute-done | bytes 262176 | tf_op jit(solution)/shard_map/ppermute | solution.py:836
  25.7 3.3 %collective-permute-start.11 = (bf16[1,576,128]{2,1,0:T(8,128)(2,1)}, bf16[1,576,128]{2,1,0:T(8,128)(2,1)S(1)}, u32[]{:S(2)}, u32[]{:S(2)}) collective-permute-start(bf16[1,576,128]{2,1,0:T(8,128)(2,1)} %bitcast.54), channel_id=1, source_target_pairs={{0,24},{1,25},{2,26},{3,27},{4,28},{5,29},{6,30},{7,31},{8,16},{9,... | collective-permute-start | bytes 442376 | tf_op jit(solution)/shard_map/ppermute | solution.py:836
  29.7 4.9 %collective-permute-start.9 = (bf16[1,576,128]{2,1,0:T(8,128)(2,1)}, bf16[1,576,128]{2,1,0:T(8,128)(2,1)S(1)}, u32[]{:S(2)}, u32[]{:S(2)}) collective-permute-start(bf16[1,576,128]{2,1,0:T(8,128)(2,1)} %bitcast.55), channel_id=1, source_target_pairs={{0,16},{1,17},{2,18},{3,19},{4,20},{5,21},{6,22},{7,23},{8,24},{9,... | collective-permute-start | bytes 442376 | tf_op jit(solution)/shard_map/ppermute | solution.py:836
  34.5 2.2 %cut_rows.3 = (bf16[256,512]{1,0:T(8,128)(2,1)}, bf16[256,512]{1,0:T(8,128)(2,1)}, bf16[256,512]{1,0:T(8,128)(2,1)}, bf16[256,512]{1,0:T(8,128)(2,1)}) custom-call(bf16[4,256,512]{2,1,0:T(8,128)(2,1)} %bitcast.51), custom_call_target="tpu_custom_call" | custom-call | bytes 4194304 | tf_op jit(solution)/shard_map/cut_rows/pallas_call | solution.py:812
  36.9 3.9 %collective-permute-done.9 = bf16[1,576,128]{2,1,0:T(8,128)(2,1)S(1)} collective-permute-done((bf16[1,576,128]{2,1,0:T(8,128)(2,1)}, bf16[1,576,128]{2,1,0:T(8,128)(2,1)S(1)}, u32[]{:S(2)}, u32[]{:S(2)}) %collective-permute-start.9) | collective-permute-done | bytes 147488 | tf_op jit(solution)/shard_map/ppermute | solution.py:836
  45.9 11.2 %collective-permute-done.13 = bf16[4,576,128]{2,1,0:T(8,128)(2,1)S(1)} collective-permute-done((bf16[4,576,128]{2,1,0:T(8,128)(2,1)S(1)}, bf16[4,576,128]{2,1,0:T(8,128)(2,1)S(1)}, u32[]{:S(2)}, u32[]{:S(2)}) %collective-permute-start.13) | collective-permute-done | bytes 589856 | tf_op jit(solution)/shard_map/ppermute | solution.py:836
  60.4 14.3 %attend.1 = (f32[1024,512]{1,0:T(8,128)}, bf16[1024,512]{1,0:T(8,128)(2,1)}, bf16[1024,512]{1,0:T(8,128)(2,1)}, bf16[1024,512]{1,0:T(8,128)(2,1)}, bf16[1024,512...) custom-call(s32[4]{0:T(128)S(1)} %pad_add_fusion.info_ref, ...), custom_call_target="tpu_custom_call" | custom-call | flops 5000000000 | bytes 14680064 | tf_op jit(solution)/shard_map/attend/pallas_call | solution.py:234
  76.4 1.6 collective-permute-start.19
  78.0 4.2 %collective-permute-done.19.refs_5_ = bf16[16,576,128]{2,1,0:T(8,128)(2,1)S(1)} collective-permute-done((bf16[16,576,128]{2,1,0:T(8,128)(2,1)S(1)}, bf16[16,576,128]{2,1,0:T(8,128)(2,1)S(1)}, u32[]{:S(2)}, u32[]{:S(2)}) %collective-permute-start.19) | collective-permute-done | bytes 2359328 | tf_op jit(solution)/shard_map/ppermute | solution.py:836
  83.6 28.0 %feed.1 = (bf16[256,512]{1,0:T(8,128)(2,1)}, bf16[256,512]{1,0:T(8,128)(2,1)}, bf16[256,512]{1,0:T(8,128)(2,1)}, bf16[256,512]{1,0:T(8,128)(2,1)}, bf16[1024,512...) custom-call(s32[4]{0:T(128)} %copy-done, ...), custom_call_target="tpu_custom_call" | custom-call | flops 15000000512 | bytes 20971520 | tf_op jit(solution)/shard_map/feed/pallas_call | solution.py:465
  113.9 2.5 %collective-permute-done.20 = bf16[32,288,128]{2,1,0:T(8,128)(2,1)S(1)} collective-permute-done((bf16[32,288,128]{2,1,0:T(8,128)(2,1)}, bf16[32,288,128]{2,1,0:T(8,128)(2,1)S(1)}, u32[]{:S(2)}, u32[]{:S(2)}) %collective-permute-start.20) | collective-permute-done | bytes 2359328 | tf_op jit(solution)/shard_map/ppermute | solution.py:836
  116.5 2.4 %add_convert_fusion = (bf16[8,288,128]{2,1,0:T(8,128)(2,1)S(1)}, bf16[8,288,128]{2,1,0:T(8,128)(2,1)S(1)}, bf16[8,288,128]{2,1,0:T(8,128)(2,1)S(1)}, bf16[8,288,128]{2,1,0:T(8,128)(2,1)S(1)}) fusion(bf16[32,288,128]{2,1,0:T(8,128)(2,1)S(1)} %collective-permute-done.20, bf16[32,288,128]{2,1,0:T(8,128)(2,1)} %get-tuple-element.214), kind=kLoop, calls=%fused_computation | loop fusion | flops 4718592 | bytes 7077888 | tf_op jit(solution)/shard_map/convert_element_type | solution.py:723
  120.1 21.4 %attend_back.1 = (bf16[256,512]{1,0:T(8,128)(2,1)S(1)}, bf16[256,512]{1,0:T(8,128)(2,1)S(1)}, bf16[256,512]{1,0:T(8,128)(2,1)S(1)}, bf16[256,512]{1,0:T(8,128)(2...) custom-call(s32[4]{0:T(128)S(1)} %copy-done.1, f32[1024,512]{1,0:T(8,128)} %get-tuple-element.199.lifted_ref, ...), custom_call_target="tpu_custom_call" | custom-call | flops 14000000000 | bytes 25165824 | tf_op jit(solution)/shard_map/attend_back/pallas_call | solution.py:642
  143.3 2.0 %collective-permute-done.26 = bf16[16,336,128]{2,1,0:T(8,128)(2,1)S(1)} collective-permute-done((bf16[16,336,128]{2,1,0:T(8,128)(2,1)S(1)}, bf16[16,336,128]{2,1,0:T(8,128)(2,1)S(1)}, u32[]{:S(2)}, u32[]{:S(2)}) %collective-permute-start.26) | collective-permute-done | bytes 1376288 | tf_op jit(solution)/shard_map/ppermute | solution.py:836
  145.7 1.6 collective-permute-start.30
  149.9 2.4 %collective-permute-start.31 = (bf16[4,336,128]{2,1,0:T(8,128)(2,1)S(1)}, bf16[4,336,128]{2,1,0:T(8,128)(2,1)S(1)}, u32[]{:S(2)}, u32[]{:S(2)}) collective-permute-start(bf16[4,336,128]{2,1,0:T(8,128)(2,1)S(1)} %get-tuple-element.262), channel_id=1, source_target_pairs={{0,6},{1,7},{2,4},{3,5},{4,2},{5,3},{6,0},{7,1},{8,14},{9,15},{10,... | collective-permute-start | bytes 1032200 | tf_op jit(solution)/shard_map/ppermute | solution.py:836
  152.3 5.2 %collective-permute-done.28 = bf16[4,288,128]{2,1,0:T(8,128)(2,1)} collective-permute-done((bf16[4,288,128]{2,1,0:T(8,128)(2,1)}, bf16[4,288,128]{2,1,0:T(8,128)(2,1)}, u32[]{:S(2)}, u32[]{:S(2)}) %collective-permute-start.28) | collective-permute-done | bytes 294944 | tf_op jit(solution)/shard_map/ppermute | solution.py:836
  157.5 4.8 %collective-permute-done.29 = bf16[4,288,128]{2,1,0:T(8,128)(2,1)} collective-permute-done((bf16[4,288,128]{2,1,0:T(8,128)(2,1)}, bf16[4,288,128]{2,1,0:T(8,128)(2,1)}, u32[]{:S(2)}, u32[]{:S(2)}) %collective-permute-start.29) | collective-permute-done | bytes 294944 | tf_op jit(solution)/shard_map/ppermute | solution.py:836
  164.5 2.5 %collective-permute-start.34 = (bf16[1,576,128]{2,1,0:T(8,128)(2,1)S(1)}, bf16[1,576,128]{2,1,0:T(8,128)(2,1)S(1)}, u32[]{:S(2)}, u32[]{:S(2)}) collective-permute-start(bf16[1,576,128]{2,1,0:T(8,128)(2,1)S(1)} %pad_maximum_fusion.4), channel_id=1, source_target_pairs={{0,24},{1,25},{2,26},{3,27},{4,28},{5,29},{6,30},{7,31},{8,16},{9,... | collective-permute-start | bytes 442376 | tf_op jit(solution)/shard_map/ppermute | solution.py:836
  167.1 1.9 collective-permute-start.32
  171.0 2.1 %collective-permute-done.34.refs_7_ = bf16[1,576,128]{2,1,0:T(8,128)(2,1)S(1)} collective-permute-done((bf16[1,576,128]{2,1,0:T(8,128)(2,1)S(1)}, bf16[1,576,128]{2,1,0:T(8,128)(2,1)S(1)}, u32[]{:S(2)}, u32[]{:S(2)}) %collective-permute-start.34) | collective-permute-done | bytes 147488 | tf_op jit(solution)/shard_map/ppermute | solution.py:836
  173.1 3.3 %collective-permute-done.33.refs_6_ = bf16[1,576,128]{2,1,0:T(8,128)(2,1)S(1)} collective-permute-done((bf16[1,576,128]{2,1,0:T(8,128)(2,1)S(1)}, bf16[1,576,128]{2,1,0:T(8,128)(2,1)S(1)}, u32[]{:S(2)}, u32[]{:S(2)}) %collective-permute-start.33) | collective-permute-done | bytes 147488 | tf_op jit(solution)/shard_map/ppermute | solution.py:836
  176.4 2.8 %collective-permute-done.32.refs_5_ = bf16[1,576,128]{2,1,0:T(8,128)(2,1)S(1)} collective-permute-done((bf16[1,576,128]{2,1,0:T(8,128)(2,1)S(1)}, bf16[1,576,128]{2,1,0:T(8,128)(2,1)S(1)}, u32[]{:S(2)}, u32[]{:S(2)}) %collective-permute-start.32) | collective-permute-done | bytes 147488 | tf_op jit(solution)/shard_map/ppermute | solution.py:836
  182.0 3.0 %collective-permute-start.39 = (bf16[1,336,128]{2,1,0:T(8,128)(2,1)S(1)}, bf16[1,336,128]{2,1,0:T(8,128)(2,1)S(1)}, u32[]{:S(2)}, u32[]{:S(2)}) collective-permute-start(bf16[1,336,128]{2,1,0:T(8,128)(2,1)S(1)} %get-tuple-element.325), channel_id=1, source_target_pairs={{0,8},{1,9},{2,10},{3,11},{4,12},{5,13},{6,14},{7,15},{8,0},{9,1},... | collective-permute-start | bytes 258056 | tf_op jit(solution)/shard_map/ppermute | solution.py:836
  185.1 4.1 %collective-permute-done.38.refs_1_ = bf16[1,336,128]{2,1,0:T(8,128)(2,1)S(1)} collective-permute-done((bf16[1,336,128]{2,1,0:T(8,128)(2,1)S(1)}, bf16[1,336,128]{2,1,0:T(8,128)(2,1)S(1)}, u32[]{:S(2)}, u32[]{:S(2)}) %collective-permute-start.38) | collective-permute-done | bytes 86048 | tf_op jit(solution)/shard_map/ppermute | solution.py:836
  190.4 5.1 %collective-permute-done.40.refs_3_ = bf16[1,336,128]{2,1,0:T(8,128)(2,1)S(1)} collective-permute-done((bf16[1,336,128]{2,1,0:T(8,128)(2,1)S(1)}, bf16[1,336,128]{2,1,0:T(8,128)(2,1)S(1)}, u32[]{:S(2)}, u32[]{:S(2)}) %collective-permute-start.40) | collective-permute-done | bytes 86048 | tf_op jit(solution)/shard_map/ppermute | solution.py:836
  196.1 2.8 %finish.1 = (f32[16,1024]{1,0:T(8,128)}, f32[16,1536]{1,0:T(8,128)}, f32[16,512]{1,0:T(8,128)}, f32[16,2048]{1,0:T(8,128)}, f32[64,512]{1,0:T(8,128)}, /*index=5...) custom-call(s32[4]{0:T(128)} %copy-done, ...), custom_call_target="tpu_custom_call" | custom-call | tf_op jit(solution)/shard_map/finish/pallas_call | solution.py:764
  (153 shorter events, 41.9 us)
Async XLA Ops:
  3.3 12.2 %collective-permute-start.4 = (bf16[256,512]{1,0:T(8,128)(2,1)}, bf16[256,512]{1,0:T(8,128)(2,1)S(1)}, u32[]{:S(2)}, u32[]{:S(2)}) collective-permute-start(bf16[256,512]{1,0:T(8,128)(2,1)} %get-tuple-element.167), channel_id=1, source_target_pairs={{0,2},{1,3},{2,0},{3,1},{4,6},{5,7},{6,4},{7,5},{8,10},{9,11},{10,... | collective-permute-start | bytes 786440 | tf_op jit(solution)/shard_map/ppermute | solution.py:836
  5.8 12.6 %collective-permute-start.5 = (bf16[256,512]{1,0:T(8,128)(2,1)}, bf16[256,512]{1,0:T(8,128)(2,1)S(1)}, u32[]{:S(2)}, u32[]{:S(2)}) collective-permute-start(bf16[256,512]{1,0:T(8,128)(2,1)} %get-tuple-element.168), channel_id=1, source_target_pairs={{0,3},{1,2},{2,1},{3,0},{4,7},{5,6},{6,5},{7,4},{8,11},{9,10},{10,... | collective-permute-start | bytes 786440 | tf_op jit(solution)/shard_map/ppermute | solution.py:836
  8.8 9.6 %collective-permute-start.1 = (bf16[1,336,128]{2,1,0:T(8,128)(2,1)}, bf16[1,336,128]{2,1,0:T(8,128)(2,1)S(1)}, u32[]{:S(2)}, u32[]{:S(2)}) collective-permute-start(bf16[1,336,128]{2,1,0:T(8,128)(2,1)} %bitcast.57), channel_id=1, source_target_pairs={{0,16},{1,17},{2,18},{3,19},{4,20},{5,21},{6,22},{7,23},{8,24},{9,... | collective-permute-start | bytes 258056 | tf_op jit(solution)/shard_map/ppermute | solution.py:836
  20.7 20.0 %collective-permute-start.6 = (bf16[4,336,128]{2,1,0:T(8,128)(2,1)S(1)}, bf16[4,336,128]{2,1,0:T(8,128)(2,1)S(1)}, u32[]{:S(2)}, u32[]{:S(2)}) collective-permute-start(bf16[4,336,128]{2,1,0:T(8,128)(2,1)S(1)} %constant_dynamic-update-slice_fusion), channel_id=1, source_target_pairs={{0,2},{1,3},{2,0},{3,1},{4,6},{5,7},{6,4},{7,5},{8,10},{9,11},{10,... | collective-permute-start | bytes 1032200 | tf_op jit(solution)/shard_map/ppermute | solution.py:836
  22.3 18.5 %collective-permute-start.7 = (bf16[4,336,128]{2,1,0:T(8,128)(2,1)S(1)}, bf16[4,336,128]{2,1,0:T(8,128)(2,1)S(1)}, u32[]{:S(2)}, u32[]{:S(2)}) collective-permute-start(bf16[4,336,128]{2,1,0:T(8,128)(2,1)S(1)} %constant_dynamic-update-slice_fusion), channel_id=1, source_target_pairs={{0,4},{1,5},{2,6},{3,7},{4,0},{5,1},{6,2},{7,3},{8,12},{9,13},{10,... | collective-permute-start | bytes 1032200 | tf_op jit(solution)/shard_map/ppermute | solution.py:836
  23.8 17.0 %collective-permute-start.8 = (bf16[4,336,128]{2,1,0:T(8,128)(2,1)S(1)}, bf16[4,336,128]{2,1,0:T(8,128)(2,1)S(1)}, u32[]{:S(2)}, u32[]{:S(2)}) collective-permute-start(bf16[4,336,128]{2,1,0:T(8,128)(2,1)S(1)} %constant_dynamic-update-slice_fusion), channel_id=1, source_target_pairs={{0,6},{1,7},{2,4},{3,5},{4,2},{5,3},{6,0},{7,1},{8,14},{9,15},{10,... | collective-permute-start | bytes 1032200 | tf_op jit(solution)/shard_map/ppermute | solution.py:836
  25.7 11.2 %collective-permute-start.11 = (bf16[1,576,128]{2,1,0:T(8,128)(2,1)}, bf16[1,576,128]{2,1,0:T(8,128)(2,1)S(1)}, u32[]{:S(2)}, u32[]{:S(2)}) collective-permute-start(bf16[1,576,128]{2,1,0:T(8,128)(2,1)} %bitcast.54), channel_id=1, source_target_pairs={{0,24},{1,25},{2,26},{3,27},{4,28},{5,29},{6,30},{7,31},{8,16},{9,... | collective-permute-start | bytes 442376 | tf_op jit(solution)/shard_map/ppermute | solution.py:836
  29.7 11.1 %collective-permute-start.9 = (bf16[1,576,128]{2,1,0:T(8,128)(2,1)}, bf16[1,576,128]{2,1,0:T(8,128)(2,1)S(1)}, u32[]{:S(2)}, u32[]{:S(2)}) collective-permute-start(bf16[1,576,128]{2,1,0:T(8,128)(2,1)} %bitcast.55), channel_id=1, source_target_pairs={{0,16},{1,17},{2,18},{3,19},{4,20},{5,21},{6,22},{7,23},{8,24},{9,... | collective-permute-start | bytes 442376 | tf_op jit(solution)/shard_map/ppermute | solution.py:836
  41.0 17.3 %collective-permute-start.12 = (bf16[16,336,128]{2,1,0:T(8,128)(2,1)S(1)}, bf16[16,336,128]{2,1,0:T(8,128)(2,1)S(1)}, u32[]{:S(2)}, u32[]{:S(2)}) collective-permute-start(bf16[16,336,128]{2,1,0:T(8,128)(2,1)S(1)} %constant_dynamic-update-slice_fusion.4.refs_4_), channel_id=1, source_target_pairs={{0,1},{1,0},{2,3},{3,2},{4,5},{5,4},{6,7},{7,6},{8,9},{9,8},{10,11... | collective-permute-start | bytes 4128776 | tf_op jit(solution)/shard_map/ppermute | solution.py:836
  41.3 15.8 %collective-permute-start.13 = (bf16[4,576,128]{2,1,0:T(8,128)(2,1)S(1)}, bf16[4,576,128]{2,1,0:T(8,128)(2,1)S(1)}, u32[]{:S(2)}, u32[]{:S(2)}) collective-permute-start(bf16[4,576,128]{2,1,0:T(8,128)(2,1)S(1)} %get-tuple-element.349), channel_id=1, source_target_pairs={{0,2},{1,3},{2,0},{3,1},{4,6},{5,7},{6,4},{7,5},{8,10},{9,11},{10,... | collective-permute-start | bytes 1769480 | tf_op jit(solution)/shard_map/ppermute | solution.py:836
  42.9 15.4 %collective-permute-start.14 = (bf16[4,576,128]{2,1,0:T(8,128)(2,1)S(1)}, bf16[4,576,128]{2,1,0:T(8,128)(2,1)S(1)}, u32[]{:S(2)}, u32[]{:S(2)}) collective-permute-start(bf16[4,576,128]{2,1,0:T(8,128)(2,1)S(1)} %get-tuple-element.349), channel_id=1, source_target_pairs={{0,4},{1,5},{2,6},{3,7},{4,0},{5,1},{6,2},{7,3},{8,12},{9,13},{10,... | collective-permute-start | bytes 1769480 | tf_op jit(solution)/shard_map/ppermute | solution.py:836
  58.3 16.6 %collective-permute-start.16 = (bf16[4,576,128]{2,1,0:T(8,128)(2,1)S(1)}, bf16[4,576,128]{2,1,0:T(8,128)(2,1)S(1)}, u32[]{:S(2)}, u32[]{:S(2)}) collective-permute-start(bf16[4,576,128]{2,1,0:T(8,128)(2,1)S(1)} %collective-permute-done.13), channel_id=1, source_target_pairs={{0,4},{1,5},{2,6},{3,7},{4,0},{5,1},{6,2},{7,3},{8,12},{9,13},{10,... | collective-permute-start | bytes 1769480 | tf_op jit(solution)/shard_map/ppermute | solution.py:836
  59.8 15.0 %collective-permute-start.17 = (bf16[256,512]{1,0:T(8,128)(2,1)S(1)}, bf16[256,512]{1,0:T(8,128)(2,1)S(1)}, u32[]{:S(2)}, u32[]{:S(2)}) collective-permute-start(bf16[256,512]{1,0:T(8,128)(2,1)S(1)} %copy-done.27), channel_id=1, source_target_pairs={{0,2},{1,3},{2,0},{3,1},{4,6},{5,7},{6,4},{7,5},{8,10},{9,11},{10,... | collective-permute-start | bytes 786440 | tf_op jit(solution)/shard_map/ppermute | solution.py:836
  60.4 14.5 %collective-permute-start.18 = (bf16[256,512]{1,0:T(8,128)(2,1)S(1)}, bf16[256,512]{1,0:T(8,128)(2,1)S(1)}, u32[]{:S(2)}, u32[]{:S(2)}) collective-permute-start(bf16[256,512]{1,0:T(8,128)(2,1)S(1)} %copy-done.26), channel_id=1, source_target_pairs={{0,3},{1,2},{2,1},{3,0},{4,7},{5,6},{6,5},{7,4},{8,11},{9,10},{10,... | collective-permute-start | bytes 786440 | tf_op jit(solution)/shard_map/ppermute | solution.py:836
  112.0 29.4 %collective-permute-start.23 = (bf16[256,512]{1,0:T(8,128)(2,1)}, bf16[256,512]{1,0:T(8,128)(2,1)S(1)}, u32[]{:S(2)}, u32[]{:S(2)}) collective-permute-start(bf16[256,512]{1,0:T(8,128)(2,1)} %get-tuple-element.221), channel_id=1, source_target_pairs={{0,1},{1,0},{2,3},{3,2},{4,5},{5,4},{6,7},{7,6},{8,9},{9,8},{10,11... | collective-permute-start | bytes 786440 | tf_op jit(solution)/shard_map/ppermute | solution.py:836
  112.2 29.3 %collective-permute-start.24 = (bf16[256,512]{1,0:T(8,128)(2,1)}, bf16[256,512]{1,0:T(8,128)(2,1)S(1)}, u32[]{:S(2)}, u32[]{:S(2)}) collective-permute-start(bf16[256,512]{1,0:T(8,128)(2,1)} %get-tuple-element.222), channel_id=1, source_target_pairs={{0,2},{1,3},{2,0},{3,1},{4,6},{5,7},{6,4},{7,5},{8,10},{9,11},{10,... | collective-permute-start | bytes 786440 | tf_op jit(solution)/shard_map/ppermute | solution.py:836
  112.8 28.7 %collective-permute-start.25 = (bf16[256,512]{1,0:T(8,128)(2,1)}, bf16[256,512]{1,0:T(8,128)(2,1)S(1)}, u32[]{:S(2)}, u32[]{:S(2)}) collective-permute-start(bf16[256,512]{1,0:T(8,128)(2,1)} %get-tuple-element.223), channel_id=1, source_target_pairs={{0,3},{1,2},{2,1},{3,0},{4,7},{5,6},{6,5},{7,4},{8,11},{9,10},{10,... | collective-permute-start | bytes 786440 | tf_op jit(solution)/shard_map/ppermute | solution.py:836
  118.8 22.7 %collective-permute-start.21 = (bf16[8,288,128]{2,1,0:T(8,128)(2,1)S(1)}, bf16[8,288,128]{2,1,0:T(8,128)(2,1)S(1)}, u32[]{:S(2)}, u32[]{:S(2)}) collective-permute-start(bf16[8,288,128]{2,1,0:T(8,128)(2,1)S(1)} %get-tuple-element.218), channel_id=1, source_target_pairs={{0,4},{1,5},{2,6},{3,7},{4,0},{5,1},{6,2},{7,3},{8,12},{9,13},{10,... | collective-permute-start | bytes 1769480 | tf_op jit(solution)/shard_map/ppermute | solution.py:836
  119.4 22.1 %collective-permute-start.22 = (bf16[8,288,128]{2,1,0:T(8,128)(2,1)S(1)}, bf16[8,288,128]{2,1,0:T(8,128)(2,1)S(1)}, u32[]{:S(2)}, u32[]{:S(2)}) collective-permute-start(bf16[8,288,128]{2,1,0:T(8,128)(2,1)S(1)} %get-tuple-element.219), channel_id=1, source_target_pairs={{0,2},{1,3},{2,0},{3,1},{4,6},{5,7},{6,4},{7,5},{8,10},{9,11},{10,... | collective-permute-start | bytes 1769480 | tf_op jit(solution)/shard_map/ppermute | solution.py:836
  145.7 16.6 %collective-permute-start.30 = (bf16[4,336,128]{2,1,0:T(8,128)(2,1)S(1)}, bf16[4,336,128]{2,1,0:T(8,128)(2,1)S(1)}, u32[]{:S(2)}, u32[]{:S(2)}) collective-permute-start(bf16[4,336,128]{2,1,0:T(8,128)(2,1)S(1)} %get-tuple-element.256), channel_id=1, source_target_pairs={{0,4},{1,5},{2,6},{3,7},{4,0},{5,1},{6,2},{7,3},{8,12},{9,13},{10,... | collective-permute-start | bytes 1032200 | tf_op jit(solution)/shard_map/ppermute | solution.py:836
  147.3 10.2 %collective-permute-start.28 = (bf16[4,288,128]{2,1,0:T(8,128)(2,1)}, bf16[4,288,128]{2,1,0:T(8,128)(2,1)}, u32[]{:S(2)}, u32[]{:S(2)}) collective-permute-start(bf16[4,288,128]{2,1,0:T(8,128)(2,1)} %get-tuple-element.254), channel_id=1, source_target_pairs={{0,2},{1,3},{2,0},{3,1},{4,6},{5,7},{6,4},{7,5},{8,10},{9,11},{10,... | collective-permute-start | bytes 884744 | tf_op jit(solution)/shard_map/ppermute | solution.py:836
  148.7 13.6 %collective-permute-start.29 = (bf16[4,288,128]{2,1,0:T(8,128)(2,1)}, bf16[4,288,128]{2,1,0:T(8,128)(2,1)}, u32[]{:S(2)}, u32[]{:S(2)}) collective-permute-start(bf16[4,288,128]{2,1,0:T(8,128)(2,1)} %get-tuple-element.255), channel_id=1, source_target_pairs={{0,4},{1,5},{2,6},{3,7},{4,0},{5,1},{6,2},{7,3},{8,12},{9,13},{10,... | collective-permute-start | bytes 884744 | tf_op jit(solution)/shard_map/ppermute | solution.py:836
  149.2 21.7 %collective-permute-start.27 = (bf16[4,336,128]{2,1,0:T(8,128)(2,1)S(1)}, bf16[4,336,128]{2,1,0:T(8,128)(2,1)S(1)}, u32[]{:S(2)}, u32[]{:S(2)}) collective-permute-start(bf16[4,336,128]{2,1,0:T(8,128)(2,1)S(1)} %get-tuple-element.253), channel_id=1, source_target_pairs={{0,2},{1,3},{2,0},{3,1},{4,6},{5,7},{6,4},{7,5},{8,10},{9,11},{10,... | collective-permute-start | bytes 1032200 | tf_op jit(solution)/shard_map/ppermute | solution.py:836
  149.9 21.1 %collective-permute-start.31 = (bf16[4,336,128]{2,1,0:T(8,128)(2,1)S(1)}, bf16[4,336,128]{2,1,0:T(8,128)(2,1)S(1)}, u32[]{:S(2)}, u32[]{:S(2)}) collective-permute-start(bf16[4,336,128]{2,1,0:T(8,128)(2,1)S(1)} %get-tuple-element.262), channel_id=1, source_target_pairs={{0,6},{1,7},{2,4},{3,5},{4,2},{5,3},{6,0},{7,1},{8,14},{9,15},{10,... | collective-permute-start | bytes 1032200 | tf_op jit(solution)/shard_map/ppermute | solution.py:836
  164.5 8.7 %collective-permute-start.34 = (bf16[1,576,128]{2,1,0:T(8,128)(2,1)S(1)}, bf16[1,576,128]{2,1,0:T(8,128)(2,1)S(1)}, u32[]{:S(2)}, u32[]{:S(2)}) collective-permute-start(bf16[1,576,128]{2,1,0:T(8,128)(2,1)S(1)} %pad_maximum_fusion.4), channel_id=1, source_target_pairs={{0,24},{1,25},{2,26},{3,27},{4,28},{5,29},{6,30},{7,31},{8,16},{9,... | collective-permute-start | bytes 442376 | tf_op jit(solution)/shard_map/ppermute | solution.py:836
  167.0 9.4 %collective-permute-start.33 = (bf16[1,576,128]{2,1,0:T(8,128)(2,1)S(1)}, bf16[1,576,128]{2,1,0:T(8,128)(2,1)S(1)}, u32[]{:S(2)}, u32[]{:S(2)}) collective-permute-start(bf16[1,576,128]{2,1,0:T(8,128)(2,1)S(1)} %pad_maximum_fusion.3), channel_id=1, source_target_pairs={{0,8},{1,9},{2,10},{3,11},{4,12},{5,13},{6,14},{7,15},{8,0},{9,1},... | collective-permute-start | bytes 442376 | tf_op jit(solution)/shard_map/ppermute | solution.py:836
  167.1 12.0 %collective-permute-start.32 = (bf16[1,576,128]{2,1,0:T(8,128)(2,1)S(1)}, bf16[1,576,128]{2,1,0:T(8,128)(2,1)S(1)}, u32[]{:S(2)}, u32[]{:S(2)}) collective-permute-start(bf16[1,576,128]{2,1,0:T(8,128)(2,1)S(1)} %pad_maximum_fusion.2), channel_id=1, source_target_pairs={{0,16},{1,17},{2,18},{3,19},{4,20},{5,21},{6,22},{7,23},{8,24},{9,... | collective-permute-start | bytes 442376 | tf_op jit(solution)/shard_map/ppermute | solution.py:836
  179.2 19.7 %collective-permute-start.35 = (bf16[256,512]{1,0:T(8,128)(2,1)S(1)}, bf16[256,512]{1,0:T(8,128)(2,1)S(1)}, u32[]{:S(2)}, u32[]{:S(2)}) collective-permute-start(bf16[256,512]{1,0:T(8,128)(2,1)S(1)} %get-tuple-element.276), channel_id=1, source_target_pairs={{0,3},{1,2},{2,1},{3,0},{4,7},{5,6},{6,5},{7,4},{8,11},{9,10},{10,... | collective-permute-start | bytes 786440 | tf_op jit(solution)/shard_map/ppermute | solution.py:836
  179.2 19.7 %collective-permute-start.36 = (bf16[256,512]{1,0:T(8,128)(2,1)S(1)}, bf16[256,512]{1,0:T(8,128)(2,1)S(1)}, u32[]{:S(2)}, u32[]{:S(2)}) collective-permute-start(bf16[256,512]{1,0:T(8,128)(2,1)S(1)} %get-tuple-element.277), channel_id=1, source_target_pairs={{0,2},{1,3},{2,0},{3,1},{4,6},{5,7},{6,4},{7,5},{8,10},{9,11},{10,... | collective-permute-start | bytes 786440 | tf_op jit(solution)/shard_map/ppermute | solution.py:836
  180.4 18.5 %collective-permute-start.37 = (bf16[256,512]{1,0:T(8,128)(2,1)S(1)}, bf16[256,512]{1,0:T(8,128)(2,1)S(1)}, u32[]{:S(2)}, u32[]{:S(2)}) collective-permute-start(bf16[256,512]{1,0:T(8,128)(2,1)S(1)} %get-tuple-element.278), channel_id=1, source_target_pairs={{0,1},{1,0},{2,3},{3,2},{4,5},{5,4},{6,7},{7,6},{8,9},{9,8},{10,11... | collective-permute-start | bytes 786440 | tf_op jit(solution)/shard_map/ppermute | solution.py:836
  181.9 7.3 %collective-permute-start.38 = (bf16[1,336,128]{2,1,0:T(8,128)(2,1)S(1)}, bf16[1,336,128]{2,1,0:T(8,128)(2,1)S(1)}, u32[]{:S(2)}, u32[]{:S(2)}) collective-permute-start(bf16[1,336,128]{2,1,0:T(8,128)(2,1)S(1)} %get-tuple-element.326), channel_id=1, source_target_pairs={{0,16},{1,17},{2,18},{3,19},{4,20},{5,21},{6,22},{7,23},{8,24},{9,... | collective-permute-start | bytes 258056 | tf_op jit(solution)/shard_map/ppermute | solution.py:836
  182.0 8.3 %collective-permute-start.39 = (bf16[1,336,128]{2,1,0:T(8,128)(2,1)S(1)}, bf16[1,336,128]{2,1,0:T(8,128)(2,1)S(1)}, u32[]{:S(2)}, u32[]{:S(2)}) collective-permute-start(bf16[1,336,128]{2,1,0:T(8,128)(2,1)S(1)} %get-tuple-element.325), channel_id=1, source_target_pairs={{0,8},{1,9},{2,10},{3,11},{4,12},{5,13},{6,14},{7,15},{8,0},{9,1},... | collective-permute-start | bytes 258056 | tf_op jit(solution)/shard_map/ppermute | solution.py:836
  (41 other events, 386.8 us)

commit v4 on v3

--- a/solution.py
+++ b/solution.py
@@ -84,11 +84,12 @@
 
     def grad_piece(self, half, mask, at, rows):
         cut = self.late_rows // 2
-        if at < cut:
-            assert at + rows <= cut
-            return half.at[self.place(mask), at : at + rows, :]
-        swapped = (mask & ~6) | ((mask >> 1) & 2) | ((mask & 2) << 1)
-        return half.at[16 + self.place(swapped), at - cut : at - cut + rows, :]
+        first = at < cut
+        assert not first or at + rows <= cut
+        swapped = mask if first else (mask & ~6) | ((mask >> 1) & 2) | ((mask & 2) << 1)
+        place = self.place(swapped)
+        start = at if first else at - cut
+        return half[place // 8].at[place % 8 + (0 if first else 8), start : start + rows, :]
 
 
 def fill_early(plan, me, halves, table_ref, inward_ref, small_ref, stage_ref):
@@ -286,8 +287,8 @@
 def feed_kernel(plan, count, info_ref, lifted_ref, mixed_ref, *refs):
     upstreams, refs = refs[:count], refs[count:]
     if plan.packed:
-        late_halves, small_ref = refs[:2], refs[2]
-        refs = refs[3:]
+        late_quarters, small_ref = refs[:8], refs[8]
+        refs = refs[9:]
     else:
         outward_in, expand_in, contract_in, small_ref = refs[:4]
         refs = refs[4:]
@@ -295,7 +296,7 @@
     mixed_back_ref, first_back_ref, small_grad_ref = refs[:3]
     refs = refs[3:]
     if plan.packed:
-        halves, refs = refs[:2], refs[2:]
+        halves, refs = (refs[:2], refs[2:4]), refs[4:]
     else:
         outward_out, expand_out, contract_out = refs[:3]
         refs = refs[3:]
@@ -310,7 +311,8 @@
     def _():
         if plan.packed:
             for mask in range(plan.devices):
-                shard = late_halves[mask & 1].at[plan.place(mask)]
+                at = plan.place(mask)
+                shard = late_quarters[(mask & 1) * 4 + at // 4].at[at % 4]
                 owner = info_ref[1] ^ mask
                 rows, wide = aligned(owner, TILE), aligned(owner, contract_own)
                 for lane in range(lanes):
@@ -457,7 +459,7 @@
     rows = pl.BlockSpec((size, width), lambda i, info: ((info[2] // group) ^ i, 0))
     outward, expand, contract = (width, width), (parts, width, width), (parts * width, width)
     if plan.packed:
-        grads = [like((plan.devices, plan.late_rows // 2, LANE), BF)] * 2
+        grads = [like((plan.devices // 2, plan.late_rows // 2, LANE), BF)] * 4
     else:
         grads = [like(outward, BF), like(expand, BF), like(contract, BF)]
     ends = [like((piece, width), BF)] * count
@@ -669,52 +671,49 @@
             ],
         ),
         out_shape=tokens + grads,
-        compiler_params=params(44),
+        compiler_params=params(56),
         cost_estimate=cost(14 * 10**9, 24 * 2**20, 6 * 10**6),
         name="attend_back",
     )(info, lifted, query, key, value, mixed, mixed_back, totals, inward, first_back, small_grad)
     return values[:count], values[count:]
 
 
-def pack_early_kernel(plan, table_ref, inward_ref, *refs):
-    vectors, out_ref = refs[:VECTORS], refs[VECTORS]
-    for piece in range(plan.table_pieces):
-        out_ref[piece * TILE : (piece + 1) * TILE, :] = table_ref[:, piece * LANE : (piece + 1) * LANE]
-    for piece in range(3 * plan.lanes):
-        at = (plan.table_pieces + piece) * TILE
-        out_ref[at : at + TILE, :] = inward_ref[:, piece * LANE : (piece + 1) * LANE]
+def pack_kernel(plan, count, share, rows_ref, table_ref, inward_ref, *refs):
+    vectors, refs = refs[:VECTORS], refs[VECTORS:]
+    outward_ref, expand_ref, contract_ref = refs[:3]
+    pieces, early_ref, late_ref = refs[3 : 3 + count], refs[3 + count], refs[4 + count]
+    rank = lax.axis_index("seq")
+    for mask in range(count):
+        pieces[mask][...] = rows_ref[pl.ds((rank ^ mask) // share, 1), :, :][0]
+    at = 0
+    for ref in (table_ref, inward_ref):
+        for lane in range(ref.shape[1] // LANE):
+            early_ref[0, at : at + TILE, :] = ref[:, lane * LANE : (lane + 1) * LANE]
+            at += TILE
     rows = []
     for size, ref in zip(plan.owned, vectors):
         rows.append(jnp.concatenate([ref[...].astype(F32)] * (LANE // size), axis=1))
     rows.append(jnp.zeros((TILE - VECTORS, LANE), F32))
-    at = plan.early_pieces * TILE
-    out_ref[at : at + TILE, :] = jnp.concatenate(rows, axis=0).astype(BF)
-
-
-def pack_early(plan, table, inward, vectors):
-    values = [table, inward] + [v.reshape(1, -1) for v in vectors]
-    return pl.pallas_call(
-        functools.partial(pack_early_kernel, plan),
-        out_shape=like((plan.early_rows, LANE), BF),
-        name="pack_early",
-    )(*values)
-
-
-def pack_late_kernel(plan, outward_ref, expand_ref, contract_ref, out_ref):
+    early_ref[0, at : at + TILE, :] = jnp.concatenate(rows, axis=0).astype(BF)
     at = 0
     for ref in (outward_ref, expand_ref, contract_ref):
         rows = ref.shape[0]
         for lane in range(ref.shape[1] // LANE):
-            out_ref[at : at + rows, :] = ref[:, lane * LANE : (lane + 1) * LANE]
+            late_ref[0, at : at + rows, :] = ref[:, lane * LANE : (lane + 1) * LANE]
             at += rows
 
 
-def pack_late(plan, outward, expand, contract):
-    return pl.pallas_call(
-        functools.partial(pack_late_kernel, plan),
-        out_shape=like((plan.late_rows, LANE), BF),
-        name="pack_late",
-    )(outward, expand, contract)
+def pack(plan, count, share, rows, table, inward, vectors, outward, expand, contract):
+    vectors = [v.reshape(1, -1) for v in vectors]
+    outs = [like(rows.shape[1:], BF)] * count
+    outs += [like((1, plan.early_rows, LANE), BF), like((1, plan.late_rows, LANE), BF)]
+    values = pl.pallas_call(
+        functools.partial(pack_kernel, plan, count, share),
+        out_shape=outs,
+        cost_estimate=cost(0, 4 * 2**20),
+        name="pack",
+    )(rows, table, inward, *vectors, outward, expand, contract)
+    return values[:count], values[count], values[count + 1]
 
 
 def fold(terms, cuts):
@@ -827,9 +826,12 @@
     assert share * micro_count == count
     plan = Plan(devices, width, contract.shape[0] * devices, block_rows * count)
     micro = rank // share
-    firsts = jnp.where(jnp.arange(micro_count) == micro, first_length[:, 0], 0)
     counted = (rank % share == 0).astype(jnp.int32)
-    info = jnp.stack([jnp.sum(firsts), me, rank, counted]).astype(jnp.int32)
+
+    def info_of(lengths):
+        first = jnp.sum(jnp.where(jnp.arange(micro_count) == micro, lengths[:, 0], 0))
+        return jnp.stack([first, me, rank, counted]).astype(jnp.int32)
+
     vectors = (intake, outlet, steady, offset, spread, settle, temper, anchor)
 
     def swap(value, mask):
@@ -844,79 +846,86 @@
         return ordered(rank, pieces)
 
     if plan.packed:
-        rows_in = cut_rows(tokens[:, 0], count, share)
-        rows_in, inward = lax.optimization_barrier((rows_in, inward))
+        rows_in, shard, late = pack(
+            plan, count, share, tokens[:, 0], positions.T, inward, vectors, outward, expand, contract
+        )
         rows_in = exchange(rows_in)
-        shard = pack_early(plan, positions.T, inward, vectors)[None]
-        shard, rows_in[1], outward = lax.optimization_barrier((shard, rows_in[1], outward))
+        shard, rows_in[1] = lax.optimization_barrier((shard, rows_in[1]))
         pieces = [swap(shard, mask) for mask in plan.z_order]
-        late = pack_late(plan, outward, expand, contract)[None]
-        pieces, rows_in, info, late, cotangent = lax.optimization_barrier(
-            (pieces, rows_in, info, late, cotangent)
+        pieces, rows_in, late, cotangent, first_length = lax.optimization_barrier(
+            (pieces, rows_in, late, cotangent, first_length)
         )
+        info = info_of(first_length)
         shard = jnp.concatenate(pieces, axis=0)
         pieces = [swap(shard, k << 1) for k in range(4)]
         late = [swap(late, mask) for mask in plan.z_order]
         upstreams = cut_rows(cotangent[:, 0], count, share)
-        pieces, upstreams, late = lax.optimization_barrier((pieces, list(upstreams), late))
+        pieces, upstreams, late, info = lax.optimization_barrier((pieces, list(upstreams), late, info))
         late = jnp.concatenate(late, axis=0)
         late_x, late_y = swap(late, 2), swap(late, 4)
         shard = jnp.concatenate(pieces, axis=0)
         early = [shard, swap(shard, 1)]
         upstreams[1] = swap(upstreams[1], 1)
-        early, late_x, late_y, upstreams = lax.optimization_barrier((early, late_x, late_y, upstreams))
+        late_core = swap(late, 1)
+        early, late_core, late_x, late_y, upstreams = lax.optimization_barrier(
+            (early, late_core, late_x, late_y, upstreams)
+        )
         late_xy = swap(late_x, 4)
         upstreams[2:] = [swap(upstreams[mask], mask) for mask in (2, 3)]
+        late_cores = [late_core, swap(late_x, 1), swap(late_y, 1)]
     else:
+        info = info_of(first_length)
         rows_in = exchange(cut_rows(tokens[:, 0], count, share))
         upstreams = exchange(cut_rows(cotangent[:, 0], count, share))
         early, late = plain_weights(plan, positions, inward, vectors, outward, expand, contract)
     lifted, query, key, value, mixed, totals, inward_all, small = attend(plan, info, count, rows_in, early)
     if plan.packed:
-        late_xy, upstreams, mixed = lax.optimization_barrier((late_xy, upstreams, mixed))
-        late = jnp.concatenate([late, late_x, late_y, late_xy], axis=0)
-        late = [late, swap(late, 1)]
+        late_xy, late_cores, upstreams, mixed = lax.optimization_barrier(
+            (late_xy, late_cores, upstreams, mixed)
+        )
+        late = [late, late_x, late_y, late_xy] + late_cores + [swap(late_xy, 1)]
     results, (mixed_back, first_back, small_grad), late_grads = feed(
         plan, info, count, lifted, mixed, upstreams, late, small
     )
     results = exchange(results)
     if plan.packed:
-        keep, send = late_grads
-        one, one_send, two, two_send = fold([keep, swap(send, 1)], 4)
-        one, one_send, two, two_send, mixed_back = lax.optimization_barrier(
-            (one, one_send, two, two_send, mixed_back)
-        )
+        stay_keep, go_keep, stay_send, go_send = late_grads
+        one_send, two_send = fold([go_keep, swap(go_send, 1)], 2)
+        stay_other = swap(stay_send, 1)
+        one_send, two_send, mixed_back = lax.optimization_barrier((one_send, two_send, mixed_back))
         one_other, two_other = swap(one_send, 4), swap(two_send, 2)
     token_pieces, early_grads = attend_back(
         plan, info, count, lifted, (query, key, value, mixed, totals), mixed_back, inward_all,
         first_back, small_grad,
     )
     if plan.packed:
-        one_other, two_other, results, token_pieces, early_grads = lax.optimization_barrier(
-            (one_other, two_other, results, token_pieces, early_grads)
+        one_other, two_other, stay_other, results, token_pieces, early_grads = lax.optimization_barrier(
+            (one_other, two_other, stay_other, results, token_pieces, early_grads)
         )
         keep, send = early_grads
         send = swap(send, 1)
-        one, one_send = fold([one, one_other], 2)
-        two, two_send = fold([two, two_other], 2)
+        one, one_send = fold([stay_keep[:8], stay_other[:8], one_other], 2)
+        two, two_send = fold([stay_keep[8:], stay_other[8:], two_other], 2)
         one, one_send, two, two_send, keep = lax.optimization_barrier((one, one_send, two, two_send, keep))
         one_other, two_other = swap(one_send, 2), swap(two_send, 4)
         terms = fold([keep, send], 4)
-        terms, results, token_pieces = lax.optimization_barrier((terms, results, token_pieces))
+        terms, results, token_pieces, one_other, two_other = lax.optimization_barrier(
+            (terms, results, token_pieces, one_other, two_other)
+        )
         terms = [swap(term, k << 1) for k, term in enumerate(terms)]
-        one_other, two_other, terms[2], results = lax.optimization_barrier(
-            (one_other, two_other, terms[2], results)
-        )
         ones, twos = fold([one, one_other], 4), fold([two, two_other], 4)
         late_terms = [jnp.concatenate(pair, axis=1) for pair in zip(ones, twos)]
         late_terms = [swap(term, mask) for term, mask in zip(late_terms, plan.z_order)]
         output = in_order(results)
+        token_pieces = list(token_pieces)
+        token_pieces[1] = swap(token_pieces[1], 1)
         terms, late_terms, output, token_pieces = lax.optimization_barrier(
             (terms, late_terms, output, token_pieces)
         )
         terms = fold(terms, 4)
         early_terms = [swap(term, mask) for term, mask in zip(terms, plan.z_order)]
-        tokens_back = in_order(exchange(token_pieces))
+        token_pieces[2:] = [swap(token_pieces[mask], mask) for mask in (2, 3)]
+        tokens_back = in_order(token_pieces)
         values = finish(plan, info, early_terms, late_terms)
         table_t, inward_own, outward_own, expand_own, contract_own = values[:5]
         own = [v.reshape(-1) for v in values[5:]]

time: 201 us -> 189 us (0.940)
  starting transfers between devices: 48.3 us -> 42.5 us
  waiting for transfers between devices: 58.9 us -> 55.9 us
    ppermute x41 -> x45, starting transfers between devices: 48.3 us -> 42.5 us  [swap(): lax.ppermute(value, AXES, [(d, d ^ mask) for d in range(devices)])]
    ppermute x41 -> x45, waiting for transfers between devices: 58.9 us -> 55.9 us  [swap(): lax.ppermute(value, AXES, [(d, d ^ mask) for d in range(devices)])]
    pallas_call x2 -> x1, Pallas kernels: 4.49 us -> 2.25 us  [cut_rows(): pl.pallas_call(functools.partial(cut_kernel, count, share), out_shape=out...]
    pallas_call x1, Pallas kernels: 21.4 us -> 23.4 us  [attend_back(): pl.pallas_call(functools.partial(attend_back_kernel, plan, count), grid_s...]
    convert_element_type x6 -> x5, other arithmetic: 6.84 us -> 5.29 us  [fold(): sum((term[index * size:(index + 1) * size].astype(F32) for term in terms))]
    unnamed x76 -> x79, local copies, waits for them, and re-layouts: 5.54 us -> 4.68 us
  transfers between devices with their start and end apart: 41 -> 45, of which waited for: 18 -> 17; matrix products, arithmetic and copies ran while one was open for 5% -> 4% of each run, Pallas kernels for 22% -> 23%
where the time goes in v4:
time: 189 us; the launch traced here: 188 us
  Pallas kernels  73.1 us (39%)
  waiting for transfers between devices  55.9 us (30%)
  starting transfers between devices  42.5 us (22%)
  other arithmetic  10.7 us (6%)
  local copies, waits for them, and re-layouts  4.76 us (3%)
    ppermute x45, waiting for transfers between devices, swap(): lax.ppermute(value, AXES, [(d, d ^ mask) for d in range(devices)])  55.9 us
    ppermute x45, starting transfers between devices, swap(): lax.ppermute(value, AXES, [(d, d ^ mask) for d in range(devices)])  42.5 us
    pallas_call x1, Pallas kernels, feed(): pl.pallas_call(functools.partial(feed_kernel, plan, count), grid_spec=plt...  27.9 us
    pallas_call x1, Pallas kernels, attend_back(): pl.pallas_call(functools.partial(attend_back_kernel, plan, count), grid_s...  23.4 us
    pallas_call x1, Pallas kernels, attend(): pl.pallas_call(functools.partial(attend_kernel, plan, count), grid_spec=p...  14.3 us
    convert_element_type x5, other arithmetic, fold(): sum((term[index * size:(index + 1) * size].astype(F32) for term in terms))  5.29 us
    unnamed x79, local copies, waits for them, and re-layouts  4.68 us
  transfers between devices with their start and end apart: 45, of which 17 were waited for; matrix products, arithmetic and copies ran while one was open for 4% of the time, Pallas kernels for 23%

profile of v4, /device:TPU:0, one launch (start us, length us, event | category | flops | bytes accessed | tf_op | source)
XLA Modules:
  0.0 188.2 jit_solution(3584564351029231613)
XLA Ops:
  0.7 2.4 %pack.1 = (bf16[256,512]{1,0:T(8,128)(2,1)}, bf16[256,512]{1,0:T(8,128)(2,1)}, bf16[256,512]{1,0:T(8,128)(2,1)}, bf16[256,512]{1,0:T(8,128)(2,1)}, bf16[1,336,12...) custom-call(bf16[4,256,512]{2,1,0:T(8,128)(2,1)} %bitcast.48, bf16[16,1024]{1,0:T(8,128)(2,1)} %bitcast.51, ...), custom_call_target="tpu_custom_call" | custom-call | bytes 4194304 | tf_op jit(solution)/shard_map/pack/pallas_call | solution.py:710
  3.6 2.6 %collective-permute-start.4 = (bf16[256,512]{1,0:T(8,128)(2,1)}, bf16[256,512]{1,0:T(8,128)(2,1)S(1)}, u32[]{:S(2)}, u32[]{:S(2)}) collective-permute-start(bf16[256,512]{1,0:T(8,128)(2,1)} %get-tuple-element.160), channel_id=1, source_target_pairs={{0,2},{1,3},{2,0},{3,1},{4,6},{5,7},{6,4},{7,5},{8,10},{9,11},{10,... | collective-permute-start | bytes 786440 | tf_op jit(solution)/shard_map/ppermute | solution.py:838
  6.2 2.8 %collective-permute-start.1 = (bf16[1,336,128]{2,1,0:T(8,128)(2,1)}, bf16[1,336,128]{2,1,0:T(8,128)(2,1)S(1)}, u32[]{:S(2)}, u32[]{:S(2)}) collective-permute-start(bf16[1,336,128]{2,1,0:T(8,128)(2,1)} %get-tuple-element.163), channel_id=1, source_target_pairs={{0,16},{1,17},{2,18},{3,19},{4,20},{5,21},{6,22},{7,23},{8,24},{9,... | collective-permute-start | bytes 258056 | tf_op jit(solution)/shard_map/ppermute | solution.py:838
  9.0 1.6 collective-permute-start.2
  10.6 2.9 %collective-permute-done.4.refs_2_ = bf16[256,512]{1,0:T(8,128)(2,1)S(1)} collective-permute-done((bf16[256,512]{1,0:T(8,128)(2,1)}, bf16[256,512]{1,0:T(8,128)(2,1)S(1)}, u32[]{:S(2)}, u32[]{:S(2)}) %collective-permute-start.4) | collective-permute-done | bytes 262176 | tf_op jit(solution)/shard_map/ppermute | solution.py:838
  13.5 5.1 %collective-permute-done.5.refs_3_ = bf16[256,512]{1,0:T(8,128)(2,1)S(1)} collective-permute-done((bf16[256,512]{1,0:T(8,128)(2,1)}, bf16[256,512]{1,0:T(8,128)(2,1)S(1)}, u32[]{:S(2)}, u32[]{:S(2)}) %collective-permute-start.5) | collective-permute-done | bytes 262176 | tf_op jit(solution)/shard_map/ppermute | solution.py:838
  19.5 1.7 collective-permute-start.10
  21.2 1.6 collective-permute-start.6
  22.8 1.5 collective-permute-start.7
  24.8 2.5 %collective-permute-start.11 = (bf16[1,576,128]{2,1,0:T(8,128)(2,1)}, bf16[1,576,128]{2,1,0:T(8,128)(2,1)S(1)}, u32[]{:S(2)}, u32[]{:S(2)}) collective-permute-start(bf16[1,576,128]{2,1,0:T(8,128)(2,1)} %get-tuple-element.183), channel_id=1, source_target_pairs={{0,24},{1,25},{2,26},{3,27},{4,28},{5,29},{6,30},{7,31},{8,16},{9,... | collective-permute-start | bytes 442376 | tf_op jit(solution)/shard_map/ppermute | solution.py:838
  29.1 2.3 %cut_rows.1 = (bf16[256,512]{1,0:T(8,128)(2,1)}, bf16[256,512]{1,0:T(8,128)(2,1)}, bf16[256,512]{1,0:T(8,128)(2,1)}, bf16[256,512]{1,0:T(8,128)(2,1)}) custom-call(bf16[4,256,512]{2,1,0:T(8,128)(2,1)} %bitcast.49), custom_call_target="tpu_custom_call" | custom-call | bytes 4194304 | tf_op jit(solution)/shard_map/cut_rows/pallas_call | solution.py:811
  33.4 6.8 %collective-permute-done.9 = bf16[1,576,128]{2,1,0:T(8,128)(2,1)S(1)} collective-permute-done((bf16[1,576,128]{2,1,0:T(8,128)(2,1)}, bf16[1,576,128]{2,1,0:T(8,128)(2,1)S(1)}, u32[]{:S(2)}, u32[]{:S(2)}) %collective-permute-start.9) | collective-permute-done | bytes 147488 | tf_op jit(solution)/shard_map/ppermute | solution.py:838
  41.4 1.6 collective-permute-start.14
  42.9 1.5 collective-permute-start.15
  44.4 1.5 collective-permute-done.16.refs_1_
  46.0 11.1 %collective-permute-done.14.refs_5_ = bf16[4,576,128]{2,1,0:T(8,128)(2,1)S(1)} collective-permute-done((bf16[4,576,128]{2,1,0:T(8,128)(2,1)S(1)}, bf16[4,576,128]{2,1,0:T(8,128)(2,1)S(1)}, u32[]{:S(2)}, u32[]{:S(2)}) %collective-permute-start.14) | collective-permute-done | bytes 589856 | tf_op jit(solution)/shard_map/ppermute | solution.py:838
  58.3 1.5 collective-permute-start.17
  61.7 14.3 %attend.1 = (f32[1024,512]{1,0:T(8,128)}, bf16[1024,512]{1,0:T(8,128)(2,1)}, bf16[1024,512]{1,0:T(8,128)(2,1)}, bf16[1024,512]{1,0:T(8,128)(2,1)}, bf16[1024,512...) custom-call(s32[4]{0:T(128)S(1)} %pad_add_fusion.info_ref, ...), custom_call_target="tpu_custom_call" | custom-call | flops 5000000000 | bytes 14680064 | tf_op jit(solution)/shard_map/attend/pallas_call | solution.py:235
  77.7 1.6 collective-permute-done.22.refs_11_
  80.2 27.9 %feed.1 = (bf16[256,512]{1,0:T(8,128)(2,1)}, bf16[256,512]{1,0:T(8,128)(2,1)}, bf16[256,512]{1,0:T(8,128)(2,1)}, bf16[256,512]{1,0:T(8,128)(2,1)}, bf16[1024,512...) custom-call(s32[4]{0:T(128)} %copy-done, ...), custom_call_target="tpu_custom_call" | custom-call | flops 15000000512 | bytes 20971520 | tf_op jit(solution)/shard_map/feed/pallas_call | solution.py:467
  111.2 1.5 add_convert_fusion
  113.9 23.4 %attend_back.1 = (bf16[256,512]{1,0:T(8,128)(2,1)}, bf16[256,512]{1,0:T(8,128)(2,1)}, bf16[256,512]{1,0:T(8,128)(2,1)}, bf16[256,512]{1,0:T(8,128)(2,1)}, bf16[1...) custom-call(s32[4]{0:T(128)} %copy-done, f32[1024,512]{1,0:T(8,128)} %get-tuple-element.193.lifted_ref, ...), custom_call_target="tpu_custom_call" | custom-call | flops 14000000000 | bytes 25165824 | tf_op jit(solution)/shard_map/attend_back/pallas_call | solution.py:644
  139.4 1.5 collective-permute-start.31
  140.9 1.5 collective-permute-start.32
  142.8 5.7 %collective-permute-done.31 = bf16[4,288,128]{2,1,0:T(8,128)(2,1)} collective-permute-done((bf16[4,288,128]{2,1,0:T(8,128)(2,1)}, bf16[4,288,128]{2,1,0:T(8,128)(2,1)}, u32[]{:S(2)}, u32[]{:S(2)}) %collective-permute-start.31) | collective-permute-done | bytes 294944 | tf_op jit(solution)/shard_map/ppermute | solution.py:838
  151.1 2.7 %collective-permute-start.38 = (bf16[1,576,128]{2,1,0:T(8,128)(2,1)S(1)}, bf16[1,576,128]{2,1,0:T(8,128)(2,1)S(1)}, u32[]{:S(2)}, u32[]{:S(2)}) collective-permute-start(bf16[1,576,128]{2,1,0:T(8,128)(2,1)S(1)} %pad_maximum_fusion.4), channel_id=1, source_target_pairs={{0,24},{1,25},{2,26},{3,27},{4,28},{5,29},{6,30},{7,31},{8,16},{9,... | collective-permute-start | bytes 442376 | tf_op jit(solution)/shard_map/ppermute | solution.py:838
  154.5 1.5 collective-permute-start.34
  162.8 6.6 %collective-permute-done.36.refs_5_ = bf16[1,576,128]{2,1,0:T(8,128)(2,1)S(1)} collective-permute-done((bf16[1,576,128]{2,1,0:T(8,128)(2,1)S(1)}, bf16[1,576,128]{2,1,0:T(8,128)(2,1)S(1)}, u32[]{:S(2)}, u32[]{:S(2)}) %collective-permute-start.36) | collective-permute-done | bytes 147488 | tf_op jit(solution)/shard_map/ppermute | solution.py:838
  174.7 2.0 %collective-permute-start.44 = (bf16[1,336,128]{2,1,0:T(8,128)(2,1)S(1)}, bf16[1,336,128]{2,1,0:T(8,128)(2,1)S(1)}, u32[]{:S(2)}, u32[]{:S(2)}) collective-permute-start(bf16[1,336,128]{2,1,0:T(8,128)(2,1)S(1)} %get-tuple-element.322), channel_id=1, source_target_pairs={{0,24},{1,25},{2,26},{3,27},{4,28},{5,29},{6,30},{7,31},{8,16},{9,... | collective-permute-start | bytes 258056 | tf_op jit(solution)/shard_map/ppermute | solution.py:838
  176.7 3.7 %collective-permute-done.42.refs_1_ = bf16[1,336,128]{2,1,0:T(8,128)(2,1)S(1)} collective-permute-done((bf16[1,336,128]{2,1,0:T(8,128)(2,1)S(1)}, bf16[1,336,128]{2,1,0:T(8,128)(2,1)S(1)}, u32[]{:S(2)}, u32[]{:S(2)}) %collective-permute-start.42) | collective-permute-done | bytes 86048 | tf_op jit(solution)/shard_map/ppermute | solution.py:838
  180.4 3.1 %collective-permute-done.44.refs_3_ = bf16[1,336,128]{2,1,0:T(8,128)(2,1)S(1)} collective-permute-done((bf16[1,336,128]{2,1,0:T(8,128)(2,1)S(1)}, bf16[1,336,128]{2,1,0:T(8,128)(2,1)S(1)}, u32[]{:S(2)}, u32[]{:S(2)}) %collective-permute-start.44) | collective-permute-done | bytes 86048 | tf_op jit(solution)/shard_map/ppermute | solution.py:838
  184.2 2.8 %finish.1 = (f32[16,1024]{1,0:T(8,128)}, f32[16,1536]{1,0:T(8,128)}, f32[16,512]{1,0:T(8,128)}, f32[16,2048]{1,0:T(8,128)}, f32[64,512]{1,0:T(8,128)}, /*index=5...) custom-call(s32[4]{0:T(128)} %copy-done, ...), custom_call_target="tpu_custom_call" | custom-call | tf_op jit(solution)/shard_map/finish/pallas_call | solution.py:763
  (161 shorter events, 36.1 us)
Async XLA Ops:
  3.6 9.9 %collective-permute-start.4 = (bf16[256,512]{1,0:T(8,128)(2,1)}, bf16[256,512]{1,0:T(8,128)(2,1)S(1)}, u32[]{:S(2)}, u32[]{:S(2)}) collective-permute-start(bf16[256,512]{1,0:T(8,128)(2,1)} %get-tuple-element.160), channel_id=1, source_target_pairs={{0,2},{1,3},{2,0},{3,1},{4,6},{5,7},{6,4},{7,5},{8,10},{9,11},{10,... | collective-permute-start | bytes 786440 | tf_op jit(solution)/shard_map/ppermute | solution.py:838
  6.2 12.5 %collective-permute-start.5 = (bf16[256,512]{1,0:T(8,128)(2,1)}, bf16[256,512]{1,0:T(8,128)(2,1)S(1)}, u32[]{:S(2)}, u32[]{:S(2)}) collective-permute-start(bf16[256,512]{1,0:T(8,128)(2,1)} %get-tuple-element.161), channel_id=1, source_target_pairs={{0,3},{1,2},{2,1},{3,0},{4,7},{5,6},{6,5},{7,4},{8,11},{9,10},{10,... | collective-permute-start | bytes 786440 | tf_op jit(solution)/shard_map/ppermute | solution.py:838
  6.2 12.4 %collective-permute-start.1 = (bf16[1,336,128]{2,1,0:T(8,128)(2,1)}, bf16[1,336,128]{2,1,0:T(8,128)(2,1)S(1)}, u32[]{:S(2)}, u32[]{:S(2)}) collective-permute-start(bf16[1,336,128]{2,1,0:T(8,128)(2,1)} %get-tuple-element.163), channel_id=1, source_target_pairs={{0,16},{1,17},{2,18},{3,19},{4,20},{5,21},{6,22},{7,23},{8,24},{9,... | collective-permute-start | bytes 258056 | tf_op jit(solution)/shard_map/ppermute | solution.py:838
  9.0 9.6 %collective-permute-start.2 = (bf16[1,336,128]{2,1,0:T(8,128)(2,1)}, bf16[1,336,128]{2,1,0:T(8,128)(2,1)S(1)}, u32[]{:S(2)}, u32[]{:S(2)}) collective-permute-start(bf16[1,336,128]{2,1,0:T(8,128)(2,1)} %get-tuple-element.163), channel_id=1, source_target_pairs={{0,8},{1,9},{2,10},{3,11},{4,12},{5,13},{6,14},{7,15},{8,0},{9,1},... | collective-permute-start | bytes 258056 | tf_op jit(solution)/shard_map/ppermute | solution.py:838
  21.2 19.0 %collective-permute-start.6 = (bf16[4,336,128]{2,1,0:T(8,128)(2,1)S(1)}, bf16[4,336,128]{2,1,0:T(8,128)(2,1)S(1)}, u32[]{:S(2)}, u32[]{:S(2)}) collective-permute-start(bf16[4,336,128]{2,1,0:T(8,128)(2,1)S(1)} %constant_dynamic-update-slice_fusion), channel_id=1, source_target_pairs={{0,2},{1,3},{2,0},{3,1},{4,6},{5,7},{6,4},{7,5},{8,10},{9,11},{10,... | collective-permute-start | bytes 1032200 | tf_op jit(solution)/shard_map/ppermute | solution.py:838
  22.8 17.4 %collective-permute-start.7 = (bf16[4,336,128]{2,1,0:T(8,128)(2,1)S(1)}, bf16[4,336,128]{2,1,0:T(8,128)(2,1)S(1)}, u32[]{:S(2)}, u32[]{:S(2)}) collective-permute-start(bf16[4,336,128]{2,1,0:T(8,128)(2,1)S(1)} %constant_dynamic-update-slice_fusion), channel_id=1, source_target_pairs={{0,4},{1,5},{2,6},{3,7},{4,0},{5,1},{6,2},{7,3},{8,12},{9,13},{10,... | collective-permute-start | bytes 1032200 | tf_op jit(solution)/shard_map/ppermute | solution.py:838
  24.3 15.9 %collective-permute-start.8 = (bf16[4,336,128]{2,1,0:T(8,128)(2,1)S(1)}, bf16[4,336,128]{2,1,0:T(8,128)(2,1)S(1)}, u32[]{:S(2)}, u32[]{:S(2)}) collective-permute-start(bf16[4,336,128]{2,1,0:T(8,128)(2,1)S(1)} %constant_dynamic-update-slice_fusion), channel_id=1, source_target_pairs={{0,6},{1,7},{2,4},{3,5},{4,2},{5,3},{6,0},{7,1},{8,14},{9,15},{10,... | collective-permute-start | bytes 1032200 | tf_op jit(solution)/shard_map/ppermute | solution.py:838
  24.8 8.6 %collective-permute-start.11 = (bf16[1,576,128]{2,1,0:T(8,128)(2,1)}, bf16[1,576,128]{2,1,0:T(8,128)(2,1)S(1)}, u32[]{:S(2)}, u32[]{:S(2)}) collective-permute-start(bf16[1,576,128]{2,1,0:T(8,128)(2,1)} %get-tuple-element.183), channel_id=1, source_target_pairs={{0,24},{1,25},{2,26},{3,27},{4,28},{5,29},{6,30},{7,31},{8,16},{9,... | collective-permute-start | bytes 442376 | tf_op jit(solution)/shard_map/ppermute | solution.py:838
  27.3 13.0 %collective-permute-start.9 = (bf16[1,576,128]{2,1,0:T(8,128)(2,1)}, bf16[1,576,128]{2,1,0:T(8,128)(2,1)S(1)}, u32[]{:S(2)}, u32[]{:S(2)}) collective-permute-start(bf16[1,576,128]{2,1,0:T(8,128)(2,1)} %get-tuple-element.183), channel_id=1, source_target_pairs={{0,16},{1,17},{2,18},{3,19},{4,20},{5,21},{6,22},{7,23},{8,24},{9,... | collective-permute-start | bytes 442376 | tf_op jit(solution)/shard_map/ppermute | solution.py:838
  40.5 17.8 %collective-permute-start.12 = (bf16[16,336,128]{2,1,0:T(8,128)(2,1)S(1)}, bf16[16,336,128]{2,1,0:T(8,128)(2,1)S(1)}, u32[]{:S(2)}, u32[]{:S(2)}) collective-permute-start(bf16[16,336,128]{2,1,0:T(8,128)(2,1)S(1)} %constant_dynamic-update-slice_fusion.4.refs_4_), channel_id=1, source_target_pairs={{0,1},{1,0},{2,3},{3,2},{4,5},{5,4},{6,7},{7,6},{8,9},{9,8},{10,11... | collective-permute-start | bytes 4128776 | tf_op jit(solution)/shard_map/ppermute | solution.py:838
  41.4 15.7 %collective-permute-start.14 = (bf16[4,576,128]{2,1,0:T(8,128)(2,1)S(1)}, bf16[4,576,128]{2,1,0:T(8,128)(2,1)S(1)}, u32[]{:S(2)}, u32[]{:S(2)}) collective-permute-start(bf16[4,576,128]{2,1,0:T(8,128)(2,1)S(1)} %constant_dynamic-update-slice_fusion.8.refs_4_), channel_id=1, source_target_pairs={{0,2},{1,3},{2,0},{3,1},{4,6},{5,7},{6,4},{7,5},{8,10},{9,11},{10,... | collective-permute-start | bytes 1769480 | tf_op jit(solution)/shard_map/ppermute | solution.py:838
  42.9 15.4 %collective-permute-start.15 = (bf16[4,576,128]{2,1,0:T(8,128)(2,1)S(1)}, bf16[4,576,128]{2,1,0:T(8,128)(2,1)S(1)}, u32[]{:S(2)}, u32[]{:S(2)}) collective-permute-start(bf16[4,576,128]{2,1,0:T(8,128)(2,1)S(1)} %constant_dynamic-update-slice_fusion.8.refs_4_), channel_id=1, source_target_pairs={{0,4},{1,5},{2,6},{3,7},{4,0},{5,1},{6,2},{7,3},{8,12},{9,13},{10,... | collective-permute-start | bytes 1769480 | tf_op jit(solution)/shard_map/ppermute | solution.py:838
  58.3 17.7 %collective-permute-start.17 = (bf16[4,576,128]{2,1,0:T(8,128)(2,1)S(1)}, bf16[4,576,128]{2,1,0:T(8,128)(2,1)S(1)}, u32[]{:S(2)}, u32[]{:S(2)}) collective-permute-start(bf16[4,576,128]{2,1,0:T(8,128)(2,1)S(1)} %collective-permute-done.14.refs_5_), channel_id=1, source_target_pairs={{0,4},{1,5},{2,6},{3,7},{4,0},{5,1},{6,2},{7,3},{8,12},{9,13},{10,... | collective-permute-start | bytes 1769480 | tf_op jit(solution)/shard_map/ppermute | solution.py:838
  59.8 16.2 %collective-permute-start.18 = (bf16[4,576,128]{2,1,0:T(8,128)(2,1)S(1)}, bf16[4,576,128]{2,1,0:T(8,128)(2,1)S(1)}, u32[]{:S(2)}, u32[]{:S(2)}) collective-permute-start(bf16[4,576,128]{2,1,0:T(8,128)(2,1)S(1)} %collective-permute-done.14.refs_5_), channel_id=1, source_target_pairs={{0,1},{1,0},{2,3},{3,2},{4,5},{5,4},{6,7},{7,6},{8,9},{9,8},{10,11... | collective-permute-start | bytes 1769480 | tf_op jit(solution)/shard_map/ppermute | solution.py:838
  59.8 16.3 %collective-permute-start.19 = (bf16[4,576,128]{2,1,0:T(8,128)(2,1)S(1)}, bf16[4,576,128]{2,1,0:T(8,128)(2,1)S(1)}, u32[]{:S(2)}, u32[]{:S(2)}) collective-permute-start(bf16[4,576,128]{2,1,0:T(8,128)(2,1)S(1)} %collective-permute-done.15.refs_6_), channel_id=1, source_target_pairs={{0,1},{1,0},{2,3},{3,2},{4,5},{5,4},{6,7},{7,6},{8,9},{9,8},{10,11... | collective-permute-start | bytes 1769480 | tf_op jit(solution)/shard_map/ppermute | solution.py:838
  60.3 15.7 %collective-permute-start.20 = (bf16[256,512]{1,0:T(8,128)(2,1)S(1)}, bf16[256,512]{1,0:T(8,128)(2,1)S(1)}, u32[]{:S(2)}, u32[]{:S(2)}) collective-permute-start(bf16[256,512]{1,0:T(8,128)(2,1)S(1)} %copy-done.29), channel_id=1, source_target_pairs={{0,2},{1,3},{2,0},{3,1},{4,6},{5,7},{6,4},{7,5},{8,10},{9,11},{10,... | collective-permute-start | bytes 786440 | tf_op jit(solution)/shard_map/ppermute | solution.py:838
  60.9 15.1 %collective-permute-start.21 = (bf16[256,512]{1,0:T(8,128)(2,1)S(1)}, bf16[256,512]{1,0:T(8,128)(2,1)S(1)}, u32[]{:S(2)}, u32[]{:S(2)}) collective-permute-start(bf16[256,512]{1,0:T(8,128)(2,1)S(1)} %copy-done.28), channel_id=1, source_target_pairs={{0,3},{1,2},{2,1},{3,0},{4,7},{5,6},{6,5},{7,4},{8,11},{9,10},{10,... | collective-permute-start | bytes 786440 | tf_op jit(solution)/shard_map/ppermute | solution.py:838
  108.6 28.8 %collective-permute-start.26 = (bf16[16,288,128]{2,1,0:T(8,128)(2,1)}, bf16[16,288,128]{2,1,0:T(8,128)(2,1)S(1)}, u32[]{:S(2)}, u32[]{:S(2)}) collective-permute-start(bf16[16,288,128]{2,1,0:T(8,128)(2,1)} %get-tuple-element.218), channel_id=1, source_target_pairs={{0,1},{1,0},{2,3},{3,2},{4,5},{5,4},{6,7},{7,6},{8,9},{9,8},{10,11... | collective-permute-start | bytes 3538952 | tf_op jit(solution)/shard_map/ppermute | solution.py:838
  109.1 28.3 %collective-permute-start.28 = (bf16[256,512]{1,0:T(8,128)(2,1)}, bf16[256,512]{1,0:T(8,128)(2,1)S(1)}, u32[]{:S(2)}, u32[]{:S(2)}) collective-permute-start(bf16[256,512]{1,0:T(8,128)(2,1)} %get-tuple-element.221), channel_id=1, source_target_pairs={{0,2},{1,3},{2,0},{3,1},{4,6},{5,7},{6,4},{7,5},{8,10},{9,11},{10,... | collective-permute-start | bytes 786440 | tf_op jit(solution)/shard_map/ppermute | solution.py:838
  109.6 27.8 %collective-permute-start.29 = (bf16[256,512]{1,0:T(8,128)(2,1)}, bf16[256,512]{1,0:T(8,128)(2,1)S(1)}, u32[]{:S(2)}, u32[]{:S(2)}) collective-permute-start(bf16[256,512]{1,0:T(8,128)(2,1)} %get-tuple-element.222), channel_id=1, source_target_pairs={{0,3},{1,2},{2,1},{3,0},{4,7},{5,6},{6,5},{7,4},{8,11},{9,10},{10,... | collective-permute-start | bytes 786440 | tf_op jit(solution)/shard_map/ppermute | solution.py:838
  112.8 24.6 %collective-permute-start.24 = (bf16[8,288,128]{2,1,0:T(8,128)(2,1)S(1)}, bf16[8,288,128]{2,1,0:T(8,128)(2,1)S(1)}, u32[]{:S(2)}, u32[]{:S(2)}) collective-permute-start(bf16[8,288,128]{2,1,0:T(8,128)(2,1)S(1)} %get-tuple-element.216), channel_id=1, source_target_pairs={{0,4},{1,5},{2,6},{3,7},{4,0},{5,1},{6,2},{7,3},{8,12},{9,13},{10,... | collective-permute-start | bytes 1769480 | tf_op jit(solution)/shard_map/ppermute | solution.py:838
  113.4 24.0 %collective-permute-start.25 = (bf16[8,288,128]{2,1,0:T(8,128)(2,1)S(1)}, bf16[8,288,128]{2,1,0:T(8,128)(2,1)S(1)}, u32[]{:S(2)}, u32[]{:S(2)}) collective-permute-start(bf16[8,288,128]{2,1,0:T(8,128)(2,1)S(1)} %get-tuple-element.217), channel_id=1, source_target_pairs={{0,2},{1,3},{2,0},{3,1},{4,6},{5,7},{6,4},{7,5},{8,10},{9,11},{10,... | collective-permute-start | bytes 1769480 | tf_op jit(solution)/shard_map/ppermute | solution.py:838
  139.4 9.1 %collective-permute-start.31 = (bf16[4,288,128]{2,1,0:T(8,128)(2,1)}, bf16[4,288,128]{2,1,0:T(8,128)(2,1)}, u32[]{:S(2)}, u32[]{:S(2)}) collective-permute-start(bf16[4,288,128]{2,1,0:T(8,128)(2,1)} %get-tuple-element.251), channel_id=1, source_target_pairs={{0,2},{1,3},{2,0},{3,1},{4,6},{5,7},{6,4},{7,5},{8,10},{9,11},{10,... | collective-permute-start | bytes 884744 | tf_op jit(solution)/shard_map/ppermute | solution.py:838
  140.9 8.8 %collective-permute-start.32 = (bf16[4,288,128]{2,1,0:T(8,128)(2,1)}, bf16[4,288,128]{2,1,0:T(8,128)(2,1)}, u32[]{:S(2)}, u32[]{:S(2)}) collective-permute-start(bf16[4,288,128]{2,1,0:T(8,128)(2,1)} %get-tuple-element.252), channel_id=1, source_target_pairs={{0,4},{1,5},{2,6},{3,7},{4,0},{5,1},{6,2},{7,3},{8,12},{9,13},{10,... | collective-permute-start | bytes 884744 | tf_op jit(solution)/shard_map/ppermute | solution.py:838
  153.8 15.6 %collective-permute-start.33 = (bf16[4,336,128]{2,1,0:T(8,128)(2,1)S(1)}, bf16[4,336,128]{2,1,0:T(8,128)(2,1)S(1)}, u32[]{:S(2)}, u32[]{:S(2)}) collective-permute-start(bf16[4,336,128]{2,1,0:T(8,128)(2,1)S(1)} %get-tuple-element.254), channel_id=1, source_target_pairs={{0,2},{1,3},{2,0},{3,1},{4,6},{5,7},{6,4},{7,5},{8,10},{9,11},{10,... | collective-permute-start | bytes 1032200 | tf_op jit(solution)/shard_map/ppermute | solution.py:838
  154.5 15.0 %collective-permute-start.34 = (bf16[4,336,128]{2,1,0:T(8,128)(2,1)S(1)}, bf16[4,336,128]{2,1,0:T(8,128)(2,1)S(1)}, u32[]{:S(2)}, u32[]{:S(2)}) collective-permute-start(bf16[4,336,128]{2,1,0:T(8,128)(2,1)S(1)} %get-tuple-element.255), channel_id=1, source_target_pairs={{0,4},{1,5},{2,6},{3,7},{4,0},{5,1},{6,2},{7,3},{8,12},{9,13},{10,... | collective-permute-start | bytes 1032200 | tf_op jit(solution)/shard_map/ppermute | solution.py:838
  156.0 14.6 %collective-permute-start.35 = (bf16[4,336,128]{2,1,0:T(8,128)(2,1)S(1)}, bf16[4,336,128]{2,1,0:T(8,128)(2,1)S(1)}, u32[]{:S(2)}, u32[]{:S(2)}) collective-permute-start(bf16[4,336,128]{2,1,0:T(8,128)(2,1)S(1)} %get-tuple-element.256), channel_id=1, source_target_pairs={{0,6},{1,7},{2,4},{3,5},{4,2},{5,3},{6,0},{7,1},{8,14},{9,15},{10,... | collective-permute-start | bytes 1032200 | tf_op jit(solution)/shard_map/ppermute | solution.py:838
  159.0 10.4 %collective-permute-start.39 = (bf16[256,512]{1,0:T(8,128)(2,1)S(1)}, bf16[256,512]{1,0:T(8,128)(2,1)S(1)}, u32[]{:S(2)}, u32[]{:S(2)}) collective-permute-start(bf16[256,512]{1,0:T(8,128)(2,1)S(1)} %copy-done.27), channel_id=1, source_target_pairs={{0,1},{1,0},{2,3},{3,2},{4,5},{5,4},{6,7},{7,6},{8,9},{9,8},{10,11... | collective-permute-start | bytes 786440 | tf_op jit(solution)/shard_map/ppermute | solution.py:838
  160.5 8.9 %collective-permute-start.36 = (bf16[1,576,128]{2,1,0:T(8,128)(2,1)S(1)}, bf16[1,576,128]{2,1,0:T(8,128)(2,1)S(1)}, u32[]{:S(2)}, u32[]{:S(2)}) collective-permute-start(bf16[1,576,128]{2,1,0:T(8,128)(2,1)S(1)} %pad_maximum_fusion.2), channel_id=1, source_target_pairs={{0,16},{1,17},{2,18},{3,19},{4,20},{5,21},{6,22},{7,23},{8,24},{9,... | collective-permute-start | bytes 442376 | tf_op jit(solution)/shard_map/ppermute | solution.py:838
  170.6 16.3 %collective-permute-start.40 = (bf16[256,512]{1,0:T(8,128)(2,1)S(1)}, bf16[256,512]{1,0:T(8,128)(2,1)S(1)}, u32[]{:S(2)}, u32[]{:S(2)}) collective-permute-start(bf16[256,512]{1,0:T(8,128)(2,1)S(1)} %copy-done.26), channel_id=1, source_target_pairs={{0,3},{1,2},{2,1},{3,0},{4,7},{5,6},{6,5},{7,4},{8,11},{9,10},{10,... | collective-permute-start | bytes 786440 | tf_op jit(solution)/shard_map/ppermute | solution.py:838
  170.6 16.3 %collective-permute-start.41 = (bf16[256,512]{1,0:T(8,128)(2,1)S(1)}, bf16[256,512]{1,0:T(8,128)(2,1)S(1)}, u32[]{:S(2)}, u32[]{:S(2)}) collective-permute-start(bf16[256,512]{1,0:T(8,128)(2,1)S(1)} %copy-done.25), channel_id=1, source_target_pairs={{0,2},{1,3},{2,0},{3,1},{4,6},{5,7},{6,4},{7,5},{8,10},{9,11},{10,... | collective-permute-start | bytes 786440 | tf_op jit(solution)/shard_map/ppermute | solution.py:838
  174.7 8.8 %collective-permute-start.44 = (bf16[1,336,128]{2,1,0:T(8,128)(2,1)S(1)}, bf16[1,336,128]{2,1,0:T(8,128)(2,1)S(1)}, u32[]{:S(2)}, u32[]{:S(2)}) collective-permute-start(bf16[1,336,128]{2,1,0:T(8,128)(2,1)S(1)} %get-tuple-element.322), channel_id=1, source_target_pairs={{0,24},{1,25},{2,26},{3,27},{4,28},{5,29},{6,30},{7,31},{8,16},{9,... | collective-permute-start | bytes 258056 | tf_op jit(solution)/shard_map/ppermute | solution.py:838
  (48 other events, 516.6 us)

commit v5 on v4

--- a/solution.py
+++ b/solution.py
@@ -45,6 +45,13 @@
 
 def full(shape):
     return pl.BlockSpec(shape, lambda *_: (0,) * len(shape), pipeline_mode=pl.Buffered(1))
+
+
+HELD = pl.BlockSpec(memory_space=pltpu.VMEM)
+
+
+def hold(values):
+    return [pltpu.with_memory_space_constraint(v, pltpu.VMEM) for v in values]
 
 
 def params(megabytes):
@@ -135,9 +142,13 @@
     else:
         table_in, inward_in, small_in = refs[:3]
         refs = refs[3:]
-    (lifted_ref, query_ref, key_ref, value_ref, mixed_ref, total_ref, inward_ref, small_ref) = refs[:8]
-    low_ref, table_ref, place_ref, stage_ref = refs[8:]
+    (lifted_out, query_ref, key_ref, value_ref, mixed_ref, total_ref, inward_out, small_ref) = refs[:8]
+    low_ref, table_ref, place_ref, stage_ref, lifted_ref, inward_ref, copied = refs[8:]
     pair = pl.program_id(0)
+    copies = [
+        pltpu.make_async_copy(lifted_ref, lifted_out, copied.at[0]),
+        pltpu.make_async_copy(inward_ref, inward_out, copied.at[1]),
+    ]
     total_rows, width = plan.total_rows, plan.width
     half = total_rows // 2
     split = info_ref[0] < total_rows
@@ -169,6 +180,8 @@
             spot = pl.ds(pl.multiple_of(start, rows), rows)
             lifted_ref[spot, :] = lifted
             low_ref[spot, :] = lifted.astype(BF)
+        for copy in copies:
+            copy.start()
 
     weights = jnp.concatenate([inward_ref[pair + i * plan.lanes] for i in range(3)], axis=1)
     lanes = aligned(pair, LANE)
@@ -225,6 +238,11 @@
             mixed_ref[block * STEP : (block + 1) * STEP, :] = jnp.where(lower, *parts).T.astype(BF)
             parts = []
 
+    @pl.when(pair == pl.num_programs(0) - 1)
+    def _():
+        for copy in copies:
+            copy.wait()
+
 
 def attend(plan, info, count, pieces, weights):
     total_rows, width = plan.total_rows, plan.width
@@ -237,15 +255,15 @@
         grid_spec=pltpu.PrefetchScalarGridSpec(
             num_scalar_prefetch=1,
             grid=(plan.lanes,),
-            in_specs=[full(v.shape) for v in pieces + weights],
+            in_specs=[HELD for v in pieces + weights],
             out_specs=[
-                full((total_rows, width)),
+                pl.BlockSpec(memory_space=pl.ANY),
                 block,
                 block,
                 block,
                 block,
                 pl.BlockSpec((1, 8, total_rows), lambda p, *_: (p, 0, 0)),
-                full(inward),
+                pl.BlockSpec(memory_space=pl.ANY),
                 full(small),
             ],
             scratch_shapes=[
@@ -253,6 +271,9 @@
                 pltpu.VMEM((plan.table_pieces, width, LANE), BF),
                 pltpu.VMEM((total_rows, width), F32),
                 pltpu.VMEM((plan.devices, TILE, LANE), F32),
+                pltpu.VMEM((total_rows, width), F32),
+                pltpu.VMEM(inward, BF),
+                pltpu.SemaphoreType.DMA((2,)),
             ],
         ),
         out_shape=[
@@ -268,7 +289,7 @@
         compiler_params=params(36),
         cost_estimate=cost(5 * 10**9, 14 * 2**20, 6 * 10**6),
         name="attend",
-    )(info, *pieces, *weights)
+    )(info, *hold(pieces), *hold(weights))
 
 
 def norm(rows):
@@ -459,9 +480,9 @@
     rows = pl.BlockSpec((size, width), lambda i, info: ((info[2] // group) ^ i, 0))
     outward, expand, contract = (width, width), (parts, width, width), (parts * width, width)
     if plan.packed:
-        grads = [like((plan.devices // 2, plan.late_rows // 2, LANE), BF)] * 4
+        grads = [pltpu.VMEM((plan.devices // 2, plan.late_rows // 2, LANE), BF)] * 4
     else:
-        grads = [like(outward, BF), like(expand, BF), like(contract, BF)]
+        grads = [pltpu.VMEM(outward, BF), pltpu.VMEM(expand, BF), pltpu.VMEM(contract, BF)]
     ends = [like((piece, width), BF)] * count
     outs = [like((total_rows, width), BF), like((total_rows, width), F32), like(small.shape, F32)]
     values = pl.pallas_call(
@@ -469,10 +490,13 @@
         grid_spec=pltpu.PrefetchScalarGridSpec(
             num_scalar_prefetch=1,
             grid=(total_rows // size,),
-            in_specs=[rows, rows] + [full(v.shape) for v in upstreams + weights + [small]],
+            in_specs=[rows, rows]
+            + [full(v.shape) for v in upstreams]
+            + [HELD for v in weights]
+            + [full(small.shape)],
             out_specs=[full(v.shape) for v in ends]
             + [rows, rows, full(small.shape)]
-            + [full(v.shape) for v in grads],
+            + [HELD for v in grads],
             scratch_shapes=[
                 pltpu.VMEM(outward, BF),
                 pltpu.VMEM(expand, BF),
@@ -492,10 +516,10 @@
             ],
         ),
         out_shape=ends + outs + grads,
-        compiler_params=params(60),
+        compiler_params=params(51),
         cost_estimate=cost(15 * 10**9, 20 * 2**20, 2 * 10**6),
         name="feed",
-    )(info, lifted, mixed, *upstreams, *weights, small)
+    )(info, lifted, mixed, *upstreams, *hold(weights), small)
     return values[:count], values[count : count + 3], values[count + 3 :]
 
 
@@ -509,8 +533,21 @@
     else:
         table_out, inward_out, small_out = refs[:3]
         refs = refs[3:]
-    joint_ref, sum_ref, share_ref, score_ref, grad_ref, table_ref, joint_sums, blocks_ref = refs
+    (joint_ref, sum_ref, share_ref, score_ref, grad_ref, table_ref, joint_sums, blocks_ref,
+     lifted_here, inward_here, copied) = refs
     pair = pl.program_id(0)
+    copies = [
+        pltpu.make_async_copy(source, target, copied.at[index])
+        for index, (source, target) in enumerate(
+            ((lifted_ref, lifted_here), (inward_ref, inward_here), (first_back_ref, sum_ref))
+        )
+    ]
+
+    @pl.when(pair == 0)
+    def _():
+        for copy in copies:
+            copy.start()
+
     total_rows, lanes = plan.total_rows, plan.lanes
     half = total_rows // 2
     split = info_ref[0] < total_rows
@@ -576,11 +613,13 @@
 
     @pl.when(pair == lanes - 1)
     def _():
-        low = lifted_ref[...].astype(BF).T
-        weights = jnp.concatenate([inward_ref[i] for i in range(3 * lanes)], axis=1)
+        for copy in copies:
+            copy.wait()
+        low = lifted_here[...].astype(BF).T
+        weights = jnp.concatenate([inward_here[i] for i in range(3 * lanes)], axis=1)
         for block in range(blocks):
             spot = slice(block * STEP, (block + 1) * STEP)
-            sum_ref[spot, :] = first_back_ref[spot, :] + times_t(joint_ref[spot, :], weights)
+            sum_ref[spot, :] += times_t(joint_ref[spot, :], weights)
         for part in range(3):
             joint = joint_ref[:, part * plan.width : (part + 1) * plan.width]
             grads = times(low, joint)
@@ -637,28 +676,28 @@
     block = pl.BlockSpec((total_rows, LANE), lambda p, *_: (0, p))
     blocks = (plan.block_starts[-1], LANE)
     if plan.packed:
-        grads = [like((plan.devices // 2, plan.early_rows, LANE), BF)] * 2
+        grads = [pltpu.VMEM((plan.devices // 2, plan.early_rows, LANE), BF)] * 2
     else:
-        grads = [like((width, total_rows), BF), like(inward.shape, BF), like(blocks, F32)]
-    tokens = [like((total_rows // count, width), BF)] * count
+        grads = [pltpu.VMEM((width, total_rows), BF), pltpu.VMEM(inward.shape, BF), pltpu.VMEM(blocks, F32)]
+    tokens = [pltpu.VMEM((total_rows // count, width), BF)] * count
     values = pl.pallas_call(
         functools.partial(attend_back_kernel, plan, count),
         grid_spec=pltpu.PrefetchScalarGridSpec(
             num_scalar_prefetch=1,
             grid=(lanes,),
             in_specs=[
-                full(lifted.shape),
+                pl.BlockSpec(memory_space=pl.ANY),
                 block,
                 block,
                 block,
                 block,
                 block,
                 pl.BlockSpec((1, 8, total_rows), lambda p, *_: (p, 0, 0)),
-                full(inward.shape),
-                full(first_back.shape),
+                pl.BlockSpec(memory_space=pl.ANY),
+                pl.BlockSpec(memory_space=pl.ANY),
                 full(small_grad.shape),
             ],
-            out_specs=[full(v.shape) for v in tokens + grads],
+            out_specs=[HELD for v in tokens + grads],
             scratch_shapes=[
                 pltpu.VMEM((total_rows, 3 * width), BF),
                 pltpu.VMEM((total_rows, width), F32),
@@ -668,6 +707,9 @@
                 pltpu.VMEM((width, total_rows), F32),
                 pltpu.VMEM((8, LANE), F32),
                 pltpu.VMEM(blocks, F32),
+                pltpu.VMEM(lifted.shape, F32),
+                pltpu.VMEM(inward.shape, BF),
+                pltpu.SemaphoreType.DMA((3,)),
             ],
         ),
         out_shape=tokens + grads,
@@ -765,12 +807,12 @@
         grid_spec=pltpu.PrefetchScalarGridSpec(
             num_scalar_prefetch=1,
             grid=(1,),
-            in_specs=[full(v.shape) for v in values],
+            in_specs=[HELD for v in values],
             out_specs=[full(v.shape) for v in outs],
         ),
         out_shape=outs,
         name="finish",
-    )(info, *values)
+    )(info, *hold(values))
 
 
 def ordered(rank, pieces):

time: 189 us -> 182 us (0.963)
  Pallas kernels: 73.1 us -> 66.6 us
  waiting for transfers between devices: 55.9 us -> 58.7 us
  local copies, waits for them, and re-layouts: 4.76 us -> 2.22 us
  starting transfers between devices: 42.5 us -> 40.6 us
    pallas_call x1, Pallas kernels: 23.4 us -> 20.4 us  [attend_back(): pl.pallas_call(functools.partial(attend_back_kernel, plan, count), grid_s...]
    ppermute x45, waiting for transfers between devices: 55.9 us -> 58.7 us  [swap(): lax.ppermute(value, AXES, [(d, d ^ mask) for d in range(devices)])]
    pallas_call x1, Pallas kernels: 27.9 us -> 25.3 us  [feed(): pl.pallas_call(functools.partial(feed_kernel, plan, count), grid_spec=plt...]
    unnamed x79 -> x43, local copies, waits for them, and re-layouts: 4.68 us -> 2.13 us
    ppermute x45, starting transfers between devices: 42.5 us -> 40.6 us  [swap(): lax.ppermute(value, AXES, [(d, d ^ mask) for d in range(devices)])]
  transfers between devices with their start and end apart: 45 -> 45, of which waited for: 17 -> 18; matrix products, arithmetic and copies ran while one was open for 4% -> 5% of each run, Pallas kernels for 23% -> 21%
where the time goes in v5:
time: 182 us; the launch traced here: 181 us
  Pallas kernels  66.6 us (37%)
  waiting for transfers between devices  58.7 us (32%)
  starting transfers between devices  40.6 us (22%)
  other arithmetic  11.9 us (7%)
  local copies, waits for them, and re-layouts  2.22 us (1%)
    ppermute x45, waiting for transfers between devices, swap(): lax.ppermute(value, AXES, [(d, d ^ mask) for d in range(devices)])  58.7 us
    ppermute x45, starting transfers between devices, swap(): lax.ppermute(value, AXES, [(d, d ^ mask) for d in range(devices)])  40.6 us
    pallas_call x1, Pallas kernels, feed(): pl.pallas_call(functools.partial(feed_kernel, plan, count), grid_spec=plt...  25.3 us
    pallas_call x1, Pallas kernels, attend_back(): pl.pallas_call(functools.partial(attend_back_kernel, plan, count), grid_s...  20.4 us
    pallas_call x1, Pallas kernels, attend(): pl.pallas_call(functools.partial(attend_kernel, plan, count), grid_spec=p...  14.7 us
    convert_element_type x5, other arithmetic, fold(): sum((term[index * size:(index + 1) * size].astype(F32) for term in terms))  7.14 us
  transfers between devices with their start and end apart: 45, of which 18 were waited for; matrix products, arithmetic and copies ran while one was open for 5% of the time, Pallas kernels for 21%

profile of v5, /device:TPU:0, one launch (start us, length us, event | category | flops | bytes accessed | tf_op | source)
XLA Modules:
  0.0 181.1 jit_solution(10662946638243239280)
XLA Ops:
  0.7 2.4 %pack.1 = (bf16[256,512]{1,0:T(8,128)(2,1)}, bf16[256,512]{1,0:T(8,128)(2,1)}, bf16[256,512]{1,0:T(8,128)(2,1)}, bf16[256,512]{1,0:T(8,128)(2,1)}, bf16[1,336,12...) custom-call(bf16[4,256,512]{2,1,0:T(8,128)(2,1)} %bitcast.48, bf16[16,1024]{1,0:T(8,128)(2,1)} %bitcast.51, ...), custom_call_target="tpu_custom_call" | custom-call | bytes 4194304 | tf_op jit(solution)/shard_map/pack/pallas_call | solution.py:752
  3.6 2.6 %collective-permute-start.4 = (bf16[256,512]{1,0:T(8,128)(2,1)}, bf16[256,512]{1,0:T(8,128)(2,1)S(1)}, u32[]{:S(2)}, u32[]{:S(2)}) collective-permute-start(bf16[256,512]{1,0:T(8,128)(2,1)} %get-tuple-element.160), channel_id=1, source_target_pairs={{0,2},{1,3},{2,0},{3,1},{4,6},{5,7},{6,4},{7,5},{8,10},{9,11},{10,... | collective-permute-start | bytes 786440 | tf_op jit(solution)/shard_map/ppermute | solution.py:880
  6.2 2.8 %collective-permute-start.1 = (bf16[1,336,128]{2,1,0:T(8,128)(2,1)}, bf16[1,336,128]{2,1,0:T(8,128)(2,1)S(1)}, u32[]{:S(2)}, u32[]{:S(2)}) collective-permute-start(bf16[1,336,128]{2,1,0:T(8,128)(2,1)} %get-tuple-element.163), channel_id=1, source_target_pairs={{0,16},{1,17},{2,18},{3,19},{4,20},{5,21},{6,22},{7,23},{8,24},{9,... | collective-permute-start | bytes 258056 | tf_op jit(solution)/shard_map/ppermute | solution.py:880
  9.1 1.6 collective-permute-start.2
  10.6 2.9 %collective-permute-done.4.refs_2_ = bf16[256,512]{1,0:T(8,128)(2,1)S(1)} collective-permute-done((bf16[256,512]{1,0:T(8,128)(2,1)}, bf16[256,512]{1,0:T(8,128)(2,1)S(1)}, u32[]{:S(2)}, u32[]{:S(2)}) %collective-permute-start.4) | collective-permute-done | bytes 262176 | tf_op jit(solution)/shard_map/ppermute | solution.py:880
  13.5 5.1 %collective-permute-done.5.refs_3_ = bf16[256,512]{1,0:T(8,128)(2,1)S(1)} collective-permute-done((bf16[256,512]{1,0:T(8,128)(2,1)}, bf16[256,512]{1,0:T(8,128)(2,1)S(1)}, u32[]{:S(2)}, u32[]{:S(2)}) %collective-permute-start.5) | collective-permute-done | bytes 262176 | tf_op jit(solution)/shard_map/ppermute | solution.py:880
  19.5 1.7 collective-permute-start.10
  21.2 1.6 collective-permute-start.6
  22.8 1.5 collective-permute-start.7
  24.8 2.5 %collective-permute-start.11 = (bf16[1,576,128]{2,1,0:T(8,128)(2,1)}, bf16[1,576,128]{2,1,0:T(8,128)(2,1)S(1)}, u32[]{:S(2)}, u32[]{:S(2)}) collective-permute-start(bf16[1,576,128]{2,1,0:T(8,128)(2,1)} %get-tuple-element.183), channel_id=1, source_target_pairs={{0,24},{1,25},{2,26},{3,27},{4,28},{5,29},{6,30},{7,31},{8,16},{9,... | collective-permute-start | bytes 442376 | tf_op jit(solution)/shard_map/ppermute | solution.py:880
  29.1 2.3 %cut_rows.1 = (bf16[256,512]{1,0:T(8,128)(2,1)}, bf16[256,512]{1,0:T(8,128)(2,1)}, bf16[256,512]{1,0:T(8,128)(2,1)}, bf16[256,512]{1,0:T(8,128)(2,1)}) custom-call(bf16[4,256,512]{2,1,0:T(8,128)(2,1)} %bitcast.49), custom_call_target="tpu_custom_call" | custom-call | bytes 4194304 | tf_op jit(solution)/shard_map/cut_rows/pallas_call | solution.py:853
  33.4 6.8 %collective-permute-done.9 = bf16[1,576,128]{2,1,0:T(8,128)(2,1)S(1)} collective-permute-done((bf16[1,576,128]{2,1,0:T(8,128)(2,1)}, bf16[1,576,128]{2,1,0:T(8,128)(2,1)S(1)}, u32[]{:S(2)}, u32[]{:S(2)}) %collective-permute-start.9) | collective-permute-done | bytes 147488 | tf_op jit(solution)/shard_map/ppermute | solution.py:880
  41.3 1.6 collective-permute-start.14
  42.9 1.5 collective-permute-start.15
  44.4 1.5 collective-permute-done.16.refs_1_
  46.0 11.1 %collective-permute-done.14.refs_5_ = bf16[4,576,128]{2,1,0:T(8,128)(2,1)S(1)} collective-permute-done((bf16[4,576,128]{2,1,0:T(8,128)(2,1)S(1)}, bf16[4,576,128]{2,1,0:T(8,128)(2,1)S(1)}, u32[]{:S(2)}, u32[]{:S(2)}) %collective-permute-start.14) | collective-permute-done | bytes 589856 | tf_op jit(solution)/shard_map/ppermute | solution.py:880
  58.3 1.5 collective-permute-start.17
  61.7 14.7 %attend.1 = (f32[1024,512]{1,0:T(8,128)}, bf16[1024,512]{1,0:T(8,128)(2,1)}, bf16[1024,512]{1,0:T(8,128)(2,1)}, bf16[1024,512]{1,0:T(8,128)(2,1)}, bf16[1024,512...) custom-call(s32[4]{0:T(128)S(1)} %pad_add_fusion.info_ref, ...), custom_call_target="tpu_custom_call" | custom-call | flops 5000000000 | bytes 14680064 | tf_op jit(solution)/shard_map/attend/pallas_call | solution.py:253
  77.3 1.6 collective-permute-done.22.refs_11_
  79.0 25.3 %feed.1 = (bf16[256,512]{1,0:T(8,128)(2,1)}, bf16[256,512]{1,0:T(8,128)(2,1)}, bf16[256,512]{1,0:T(8,128)(2,1)}, bf16[256,512]{1,0:T(8,128)(2,1)}, bf16[1024,512...) custom-call(s32[4]{0:T(128)} %copy-done, ...), custom_call_target="tpu_custom_call" | custom-call | flops 15000000512 | bytes 20971520 | tf_op jit(solution)/shard_map/feed/pallas_call | solution.py:488
  110.1 20.4 %attend_back.1 = (bf16[256,512]{1,0:T(8,128)(2,1)S(1)}, bf16[256,512]{1,0:T(8,128)(2,1)S(1)}, bf16[256,512]{1,0:T(8,128)(2,1)S(1)}, bf16[256,512]{1,0:T(8,128)(2...) custom-call(s32[4]{0:T(128)} %copy-done, f32[1024,512]{1,0:T(8,128)} %get-tuple-element.193.lifted_ref, ...), custom_call_target="tpu_custom_call" | custom-call | flops 14000000000 | bytes 25165824 | tf_op jit(solution)/shard_map/attend_back/pallas_call | solution.py:683
  132.0 2.6 %add_convert_fusion.6 = (bf16[4,288,128]{2,1,0:T(8,128)(2,1)}, bf16[4,288,128]{2,1,0:T(8,128)(2,1)}, bf16[4,288,128]{2,1,0:T(8,128)(2,1)}, bf16[4,288,128]{2,1,0:T(8,128)(2,1)}) fusion(bf16[8,288,128]{2,1,0:T(8,128)(2,1)S(1)} %collective-permute-done.25, bf16[16,288,128]{2,1,0:T(8,128)(2,1)} %collective-permute-done.26, ...), kind=kLoop, calls=%fused_computation.8 | loop fusion | flops 3538944 | bytes 4718592 | tf_op jit(solution)/shard_map/convert_element_type | solution.py:764
  135.9 1.7 add_convert_fusion.2
  137.7 6.7 %collective-permute-done.31 = bf16[4,288,128]{2,1,0:T(8,128)(2,1)} collective-permute-done((bf16[4,288,128]{2,1,0:T(8,128)(2,1)}, bf16[4,288,128]{2,1,0:T(8,128)(2,1)}, u32[]{:S(2)}, u32[]{:S(2)}) %collective-permute-start.31) | collective-permute-done | bytes 294944 | tf_op jit(solution)/shard_map/ppermute | solution.py:880
  146.0 2.7 %collective-permute-start.38 = (bf16[1,576,128]{2,1,0:T(8,128)(2,1)S(1)}, bf16[1,576,128]{2,1,0:T(8,128)(2,1)S(1)}, u32[]{:S(2)}, u32[]{:S(2)}) collective-permute-start(bf16[1,576,128]{2,1,0:T(8,128)(2,1)S(1)} %pad_maximum_fusion.4), channel_id=1, source_target_pairs={{0,24},{1,25},{2,26},{3,27},{4,28},{5,29},{6,30},{7,31},{8,16},{9,... | collective-permute-start | bytes 442376 | tf_op jit(solution)/shard_map/ppermute | solution.py:880
  150.8 1.5 collective-permute-start.35
  154.6 1.7 collective-permute-done.37.refs_6_
  157.9 7.4 %collective-permute-done.36.refs_5_ = bf16[1,576,128]{2,1,0:T(8,128)(2,1)S(1)} collective-permute-done((bf16[1,576,128]{2,1,0:T(8,128)(2,1)S(1)}, bf16[1,576,128]{2,1,0:T(8,128)(2,1)S(1)}, u32[]{:S(2)}, u32[]{:S(2)}) %collective-permute-start.36) | collective-permute-done | bytes 147488 | tf_op jit(solution)/shard_map/ppermute | solution.py:880
  170.0 1.7 collective-permute-start.44
  171.8 3.5 %collective-permute-done.42.refs_1_ = bf16[1,336,128]{2,1,0:T(8,128)(2,1)S(1)} collective-permute-done((bf16[1,336,128]{2,1,0:T(8,128)(2,1)S(1)}, bf16[1,336,128]{2,1,0:T(8,128)(2,1)S(1)}, u32[]{:S(2)}, u32[]{:S(2)}) %collective-permute-start.42) | collective-permute-done | bytes 86048 | tf_op jit(solution)/shard_map/ppermute | solution.py:880
  175.3 3.1 %collective-permute-done.44.refs_3_ = bf16[1,336,128]{2,1,0:T(8,128)(2,1)S(1)} collective-permute-done((bf16[1,336,128]{2,1,0:T(8,128)(2,1)S(1)}, bf16[1,336,128]{2,1,0:T(8,128)(2,1)S(1)}, u32[]{:S(2)}, u32[]{:S(2)}) %collective-permute-start.44) | collective-permute-done | bytes 86048 | tf_op jit(solution)/shard_map/ppermute | solution.py:880
  178.4 1.5 finish.1
  (125 shorter events, 32.9 us)
Async XLA Ops:
  3.6 9.9 %collective-permute-start.4 = (bf16[256,512]{1,0:T(8,128)(2,1)}, bf16[256,512]{1,0:T(8,128)(2,1)S(1)}, u32[]{:S(2)}, u32[]{:S(2)}) collective-permute-start(bf16[256,512]{1,0:T(8,128)(2,1)} %get-tuple-element.160), channel_id=1, source_target_pairs={{0,2},{1,3},{2,0},{3,1},{4,6},{5,7},{6,4},{7,5},{8,10},{9,11},{10,... | collective-permute-start | bytes 786440 | tf_op jit(solution)/shard_map/ppermute | solution.py:880
  6.2 12.5 %collective-permute-start.5 = (bf16[256,512]{1,0:T(8,128)(2,1)}, bf16[256,512]{1,0:T(8,128)(2,1)S(1)}, u32[]{:S(2)}, u32[]{:S(2)}) collective-permute-start(bf16[256,512]{1,0:T(8,128)(2,1)} %get-tuple-element.161), channel_id=1, source_target_pairs={{0,3},{1,2},{2,1},{3,0},{4,7},{5,6},{6,5},{7,4},{8,11},{9,10},{10,... | collective-permute-start | bytes 786440 | tf_op jit(solution)/shard_map/ppermute | solution.py:880
  6.2 12.4 %collective-permute-start.1 = (bf16[1,336,128]{2,1,0:T(8,128)(2,1)}, bf16[1,336,128]{2,1,0:T(8,128)(2,1)S(1)}, u32[]{:S(2)}, u32[]{:S(2)}) collective-permute-start(bf16[1,336,128]{2,1,0:T(8,128)(2,1)} %get-tuple-element.163), channel_id=1, source_target_pairs={{0,16},{1,17},{2,18},{3,19},{4,20},{5,21},{6,22},{7,23},{8,24},{9,... | collective-permute-start | bytes 258056 | tf_op jit(solution)/shard_map/ppermute | solution.py:880
  9.1 9.6 %collective-permute-start.2 = (bf16[1,336,128]{2,1,0:T(8,128)(2,1)}, bf16[1,336,128]{2,1,0:T(8,128)(2,1)S(1)}, u32[]{:S(2)}, u32[]{:S(2)}) collective-permute-start(bf16[1,336,128]{2,1,0:T(8,128)(2,1)} %get-tuple-element.163), channel_id=1, source_target_pairs={{0,8},{1,9},{2,10},{3,11},{4,12},{5,13},{6,14},{7,15},{8,0},{9,1},... | collective-permute-start | bytes 258056 | tf_op jit(solution)/shard_map/ppermute | solution.py:880
  21.2 19.0 %collective-permute-start.6 = (bf16[4,336,128]{2,1,0:T(8,128)(2,1)S(1)}, bf16[4,336,128]{2,1,0:T(8,128)(2,1)S(1)}, u32[]{:S(2)}, u32[]{:S(2)}) collective-permute-start(bf16[4,336,128]{2,1,0:T(8,128)(2,1)S(1)} %constant_dynamic-update-slice_fusion), channel_id=1, source_target_pairs={{0,2},{1,3},{2,0},{3,1},{4,6},{5,7},{6,4},{7,5},{8,10},{9,11},{10,... | collective-permute-start | bytes 1032200 | tf_op jit(solution)/shard_map/ppermute | solution.py:880
  22.8 17.4 %collective-permute-start.7 = (bf16[4,336,128]{2,1,0:T(8,128)(2,1)S(1)}, bf16[4,336,128]{2,1,0:T(8,128)(2,1)S(1)}, u32[]{:S(2)}, u32[]{:S(2)}) collective-permute-start(bf16[4,336,128]{2,1,0:T(8,128)(2,1)S(1)} %constant_dynamic-update-slice_fusion), channel_id=1, source_target_pairs={{0,4},{1,5},{2,6},{3,7},{4,0},{5,1},{6,2},{7,3},{8,12},{9,13},{10,... | collective-permute-start | bytes 1032200 | tf_op jit(solution)/shard_map/ppermute | solution.py:880
  24.3 15.9 %collective-permute-start.8 = (bf16[4,336,128]{2,1,0:T(8,128)(2,1)S(1)}, bf16[4,336,128]{2,1,0:T(8,128)(2,1)S(1)}, u32[]{:S(2)}, u32[]{:S(2)}) collective-permute-start(bf16[4,336,128]{2,1,0:T(8,128)(2,1)S(1)} %constant_dynamic-update-slice_fusion), channel_id=1, source_target_pairs={{0,6},{1,7},{2,4},{3,5},{4,2},{5,3},{6,0},{7,1},{8,14},{9,15},{10,... | collective-permute-start | bytes 1032200 | tf_op jit(solution)/shard_map/ppermute | solution.py:880
  24.8 8.6 %collective-permute-start.11 = (bf16[1,576,128]{2,1,0:T(8,128)(2,1)}, bf16[1,576,128]{2,1,0:T(8,128)(2,1)S(1)}, u32[]{:S(2)}, u32[]{:S(2)}) collective-permute-start(bf16[1,576,128]{2,1,0:T(8,128)(2,1)} %get-tuple-element.183), channel_id=1, source_target_pairs={{0,24},{1,25},{2,26},{3,27},{4,28},{5,29},{6,30},{7,31},{8,16},{9,... | collective-permute-start | bytes 442376 | tf_op jit(solution)/shard_map/ppermute | solution.py:880
  27.3 13.0 %collective-permute-start.9 = (bf16[1,576,128]{2,1,0:T(8,128)(2,1)}, bf16[1,576,128]{2,1,0:T(8,128)(2,1)S(1)}, u32[]{:S(2)}, u32[]{:S(2)}) collective-permute-start(bf16[1,576,128]{2,1,0:T(8,128)(2,1)} %get-tuple-element.183), channel_id=1, source_target_pairs={{0,16},{1,17},{2,18},{3,19},{4,20},{5,21},{6,22},{7,23},{8,24},{9,... | collective-permute-start | bytes 442376 | tf_op jit(solution)/shard_map/ppermute | solution.py:880
  40.5 17.8 %collective-permute-start.12 = (bf16[16,336,128]{2,1,0:T(8,128)(2,1)S(1)}, bf16[16,336,128]{2,1,0:T(8,128)(2,1)S(1)}, u32[]{:S(2)}, u32[]{:S(2)}) collective-permute-start(bf16[16,336,128]{2,1,0:T(8,128)(2,1)S(1)} %constant_dynamic-update-slice_fusion.4.refs_4_), channel_id=1, source_target_pairs={{0,1},{1,0},{2,3},{3,2},{4,5},{5,4},{6,7},{7,6},{8,9},{9,8},{10,11... | collective-permute-start | bytes 4128776 | tf_op jit(solution)/shard_map/ppermute | solution.py:880
  41.3 15.7 %collective-permute-start.14 = (bf16[4,576,128]{2,1,0:T(8,128)(2,1)S(1)}, bf16[4,576,128]{2,1,0:T(8,128)(2,1)S(1)}, u32[]{:S(2)}, u32[]{:S(2)}) collective-permute-start(bf16[4,576,128]{2,1,0:T(8,128)(2,1)S(1)} %constant_dynamic-update-slice_fusion.8.refs_4_), channel_id=1, source_target_pairs={{0,2},{1,3},{2,0},{3,1},{4,6},{5,7},{6,4},{7,5},{8,10},{9,11},{10,... | collective-permute-start | bytes 1769480 | tf_op jit(solution)/shard_map/ppermute | solution.py:880
  42.9 15.4 %collective-permute-start.15 = (bf16[4,576,128]{2,1,0:T(8,128)(2,1)S(1)}, bf16[4,576,128]{2,1,0:T(8,128)(2,1)S(1)}, u32[]{:S(2)}, u32[]{:S(2)}) collective-permute-start(bf16[4,576,128]{2,1,0:T(8,128)(2,1)S(1)} %constant_dynamic-update-slice_fusion.8.refs_4_), channel_id=1, source_target_pairs={{0,4},{1,5},{2,6},{3,7},{4,0},{5,1},{6,2},{7,3},{8,12},{9,13},{10,... | collective-permute-start | bytes 1769480 | tf_op jit(solution)/shard_map/ppermute | solution.py:880
  58.3 18.1 %collective-permute-start.17 = (bf16[4,576,128]{2,1,0:T(8,128)(2,1)S(1)}, bf16[4,576,128]{2,1,0:T(8,128)(2,1)S(1)}, u32[]{:S(2)}, u32[]{:S(2)}) collective-permute-start(bf16[4,576,128]{2,1,0:T(8,128)(2,1)S(1)} %collective-permute-done.14.refs_5_), channel_id=1, source_target_pairs={{0,4},{1,5},{2,6},{3,7},{4,0},{5,1},{6,2},{7,3},{8,12},{9,13},{10,... | collective-permute-start | bytes 1769480 | tf_op jit(solution)/shard_map/ppermute | solution.py:880
  59.8 16.6 %collective-permute-start.18 = (bf16[4,576,128]{2,1,0:T(8,128)(2,1)S(1)}, bf16[4,576,128]{2,1,0:T(8,128)(2,1)S(1)}, u32[]{:S(2)}, u32[]{:S(2)}) collective-permute-start(bf16[4,576,128]{2,1,0:T(8,128)(2,1)S(1)} %collective-permute-done.14.refs_5_), channel_id=1, source_target_pairs={{0,1},{1,0},{2,3},{3,2},{4,5},{5,4},{6,7},{7,6},{8,9},{9,8},{10,11... | collective-permute-start | bytes 1769480 | tf_op jit(solution)/shard_map/ppermute | solution.py:880
  59.8 16.6 %collective-permute-start.19 = (bf16[4,576,128]{2,1,0:T(8,128)(2,1)S(1)}, bf16[4,576,128]{2,1,0:T(8,128)(2,1)S(1)}, u32[]{:S(2)}, u32[]{:S(2)}) collective-permute-start(bf16[4,576,128]{2,1,0:T(8,128)(2,1)S(1)} %collective-permute-done.15.refs_6_), channel_id=1, source_target_pairs={{0,1},{1,0},{2,3},{3,2},{4,5},{5,4},{6,7},{7,6},{8,9},{9,8},{10,11... | collective-permute-start | bytes 1769480 | tf_op jit(solution)/shard_map/ppermute | solution.py:880
  60.3 16.1 %collective-permute-start.20 = (bf16[256,512]{1,0:T(8,128)(2,1)S(1)}, bf16[256,512]{1,0:T(8,128)(2,1)S(1)}, u32[]{:S(2)}, u32[]{:S(2)}) collective-permute-start(bf16[256,512]{1,0:T(8,128)(2,1)S(1)} %copy-done.11), channel_id=1, source_target_pairs={{0,2},{1,3},{2,0},{3,1},{4,6},{5,7},{6,4},{7,5},{8,10},{9,11},{10,... | collective-permute-start | bytes 786440 | tf_op jit(solution)/shard_map/ppermute | solution.py:880
  60.9 15.5 %collective-permute-start.21 = (bf16[256,512]{1,0:T(8,128)(2,1)S(1)}, bf16[256,512]{1,0:T(8,128)(2,1)S(1)}, u32[]{:S(2)}, u32[]{:S(2)}) collective-permute-start(bf16[256,512]{1,0:T(8,128)(2,1)S(1)} %copy-done.10), channel_id=1, source_target_pairs={{0,3},{1,2},{2,1},{3,0},{4,7},{5,6},{6,5},{7,4},{8,11},{9,10},{10,... | collective-permute-start | bytes 786440 | tf_op jit(solution)/shard_map/ppermute | solution.py:880
  104.7 25.9 %collective-permute-start.26 = (bf16[16,288,128]{2,1,0:T(8,128)(2,1)}, bf16[16,288,128]{2,1,0:T(8,128)(2,1)}, u32[]{:S(2)}, u32[]{:S(2)}) collective-permute-start(bf16[16,288,128]{2,1,0:T(8,128)(2,1)} %get-tuple-element.218), channel_id=1, source_target_pairs={{0,1},{1,0},{2,3},{3,2},{4,5},{5,4},{6,7},{7,6},{8,9},{9,8},{10,11... | collective-permute-start | bytes 3538952 | tf_op jit(solution)/shard_map/ppermute | solution.py:880
  105.2 25.4 %collective-permute-start.28 = (bf16[256,512]{1,0:T(8,128)(2,1)}, bf16[256,512]{1,0:T(8,128)(2,1)}, u32[]{:S(2)}, u32[]{:S(2)}) collective-permute-start(bf16[256,512]{1,0:T(8,128)(2,1)} %get-tuple-element.221), channel_id=1, source_target_pairs={{0,2},{1,3},{2,0},{3,1},{4,6},{5,7},{6,4},{7,5},{8,10},{9,11},{10,... | collective-permute-start | bytes 786440 | tf_op jit(solution)/shard_map/ppermute | solution.py:880
  105.7 24.9 %collective-permute-start.29 = (bf16[256,512]{1,0:T(8,128)(2,1)}, bf16[256,512]{1,0:T(8,128)(2,1)}, u32[]{:S(2)}, u32[]{:S(2)}) collective-permute-start(bf16[256,512]{1,0:T(8,128)(2,1)} %get-tuple-element.222), channel_id=1, source_target_pairs={{0,3},{1,2},{2,1},{3,0},{4,7},{5,6},{6,5},{7,4},{8,11},{9,10},{10,... | collective-permute-start | bytes 786440 | tf_op jit(solution)/shard_map/ppermute | solution.py:880
  108.6 22.0 %collective-permute-start.24 = (bf16[8,288,128]{2,1,0:T(8,128)(2,1)}, bf16[8,288,128]{2,1,0:T(8,128)(2,1)S(1)}, u32[]{:S(2)}, u32[]{:S(2)}) collective-permute-start(bf16[8,288,128]{2,1,0:T(8,128)(2,1)} %get-tuple-element.216), channel_id=1, source_target_pairs={{0,4},{1,5},{2,6},{3,7},{4,0},{5,1},{6,2},{7,3},{8,12},{9,13},{10,... | collective-permute-start | bytes 1769480 | tf_op jit(solution)/shard_map/ppermute | solution.py:880
  109.4 22.6 %collective-permute-start.25 = (bf16[8,288,128]{2,1,0:T(8,128)(2,1)}, bf16[8,288,128]{2,1,0:T(8,128)(2,1)S(1)}, u32[]{:S(2)}, u32[]{:S(2)}) collective-permute-start(bf16[8,288,128]{2,1,0:T(8,128)(2,1)} %get-tuple-element.217), channel_id=1, source_target_pairs={{0,2},{1,3},{2,0},{3,1},{4,6},{5,7},{6,4},{7,5},{8,10},{9,11},{10,... | collective-permute-start | bytes 1769480 | tf_op jit(solution)/shard_map/ppermute | solution.py:880
  134.6 9.7 %collective-permute-start.31 = (bf16[4,288,128]{2,1,0:T(8,128)(2,1)}, bf16[4,288,128]{2,1,0:T(8,128)(2,1)}, u32[]{:S(2)}, u32[]{:S(2)}) collective-permute-start(bf16[4,288,128]{2,1,0:T(8,128)(2,1)} %get-tuple-element.251), channel_id=1, source_target_pairs={{0,2},{1,3},{2,0},{3,1},{4,6},{5,7},{6,4},{7,5},{8,10},{9,11},{10,... | collective-permute-start | bytes 884744 | tf_op jit(solution)/shard_map/ppermute | solution.py:880
  135.2 9.5 %collective-permute-start.32 = (bf16[4,288,128]{2,1,0:T(8,128)(2,1)}, bf16[4,288,128]{2,1,0:T(8,128)(2,1)}, u32[]{:S(2)}, u32[]{:S(2)}) collective-permute-start(bf16[4,288,128]{2,1,0:T(8,128)(2,1)} %get-tuple-element.252), channel_id=1, source_target_pairs={{0,4},{1,5},{2,6},{3,7},{4,0},{5,1},{6,2},{7,3},{8,12},{9,13},{10,... | collective-permute-start | bytes 884744 | tf_op jit(solution)/shard_map/ppermute | solution.py:880
  146.0 8.6 %collective-permute-start.38 = (bf16[1,576,128]{2,1,0:T(8,128)(2,1)S(1)}, bf16[1,576,128]{2,1,0:T(8,128)(2,1)S(1)}, u32[]{:S(2)}, u32[]{:S(2)}) collective-permute-start(bf16[1,576,128]{2,1,0:T(8,128)(2,1)S(1)} %pad_maximum_fusion.4), channel_id=1, source_target_pairs={{0,24},{1,25},{2,26},{3,27},{4,28},{5,29},{6,30},{7,31},{8,16},{9,... | collective-permute-start | bytes 442376 | tf_op jit(solution)/shard_map/ppermute | solution.py:880
  148.9 16.5 %collective-permute-start.33 = (bf16[4,336,128]{2,1,0:T(8,128)(2,1)S(1)}, bf16[4,336,128]{2,1,0:T(8,128)(2,1)S(1)}, u32[]{:S(2)}, u32[]{:S(2)}) collective-permute-start(bf16[4,336,128]{2,1,0:T(8,128)(2,1)S(1)} %get-tuple-element.254), channel_id=1, source_target_pairs={{0,2},{1,3},{2,0},{3,1},{4,6},{5,7},{6,4},{7,5},{8,10},{9,11},{10,... | collective-permute-start | bytes 1032200 | tf_op jit(solution)/shard_map/ppermute | solution.py:880
  150.3 16.2 %collective-permute-start.34 = (bf16[4,336,128]{2,1,0:T(8,128)(2,1)S(1)}, bf16[4,336,128]{2,1,0:T(8,128)(2,1)S(1)}, u32[]{:S(2)}, u32[]{:S(2)}) collective-permute-start(bf16[4,336,128]{2,1,0:T(8,128)(2,1)S(1)} %get-tuple-element.255), channel_id=1, source_target_pairs={{0,4},{1,5},{2,6},{3,7},{4,0},{5,1},{6,2},{7,3},{8,12},{9,13},{10,... | collective-permute-start | bytes 1032200 | tf_op jit(solution)/shard_map/ppermute | solution.py:880
  150.8 15.7 %collective-permute-start.35 = (bf16[4,336,128]{2,1,0:T(8,128)(2,1)S(1)}, bf16[4,336,128]{2,1,0:T(8,128)(2,1)S(1)}, u32[]{:S(2)}, u32[]{:S(2)}) collective-permute-start(bf16[4,336,128]{2,1,0:T(8,128)(2,1)S(1)} %get-tuple-element.256), channel_id=1, source_target_pairs={{0,6},{1,7},{2,4},{3,5},{4,2},{5,3},{6,0},{7,1},{8,14},{9,15},{10,... | collective-permute-start | bytes 1032200 | tf_op jit(solution)/shard_map/ppermute | solution.py:880
  154.6 10.7 %collective-permute-start.39 = (bf16[256,512]{1,0:T(8,128)(2,1)S(1)}, bf16[256,512]{1,0:T(8,128)(2,1)S(1)}, u32[]{:S(2)}, u32[]{:S(2)}) collective-permute-start(bf16[256,512]{1,0:T(8,128)(2,1)S(1)} %copy-done.3), channel_id=1, source_target_pairs={{0,1},{1,0},{2,3},{3,2},{4,5},{5,4},{6,7},{7,6},{8,9},{9,8},{10,11... | collective-permute-start | bytes 786440 | tf_op jit(solution)/shard_map/ppermute | solution.py:880
  156.3 9.0 %collective-permute-start.36 = (bf16[1,576,128]{2,1,0:T(8,128)(2,1)S(1)}, bf16[1,576,128]{2,1,0:T(8,128)(2,1)S(1)}, u32[]{:S(2)}, u32[]{:S(2)}) collective-permute-start(bf16[1,576,128]{2,1,0:T(8,128)(2,1)S(1)} %pad_maximum_fusion.2), channel_id=1, source_target_pairs={{0,16},{1,17},{2,18},{3,19},{4,20},{5,21},{6,22},{7,23},{8,24},{9,... | collective-permute-start | bytes 442376 | tf_op jit(solution)/shard_map/ppermute | solution.py:880
  166.5 13.4 %collective-permute-start.40 = (bf16[256,512]{1,0:T(8,128)(2,1)S(1)}, bf16[256,512]{1,0:T(8,128)(2,1)S(1)}, u32[]{:S(2)}, u32[]{:S(2)}) collective-permute-start(bf16[256,512]{1,0:T(8,128)(2,1)S(1)} %get-tuple-element.270), channel_id=1, source_target_pairs={{0,3},{1,2},{2,1},{3,0},{4,7},{5,6},{6,5},{7,4},{8,11},{9,10},{10,... | collective-permute-start | bytes 786440 | tf_op jit(solution)/shard_map/ppermute | solution.py:880
  166.5 13.4 %collective-permute-start.41 = (bf16[256,512]{1,0:T(8,128)(2,1)S(1)}, bf16[256,512]{1,0:T(8,128)(2,1)S(1)}, u32[]{:S(2)}, u32[]{:S(2)}) collective-permute-start(bf16[256,512]{1,0:T(8,128)(2,1)S(1)} %get-tuple-element.271), channel_id=1, source_target_pairs={{0,2},{1,3},{2,0},{3,1},{4,6},{5,7},{6,4},{7,5},{8,10},{9,11},{10,... | collective-permute-start | bytes 786440 | tf_op jit(solution)/shard_map/ppermute | solution.py:880
  (30 other events, 289.6 us)

commit v6 on v5

--- a/solution.py
+++ b/solution.py
@@ -52,6 +52,10 @@
 
 def hold(values):
     return [pltpu.with_memory_space_constraint(v, pltpu.VMEM) for v in values]
+
+
+def stay(values):
+    return [pltpu.with_memory_space_constraint(v, pltpu.HBM) for v in values]
 
 
 def params(megabytes):
@@ -76,6 +80,7 @@
         self.early_pieces = self.table_pieces + 3 * self.lanes
         self.early_rows = (self.early_pieces + 1) * TILE
         self.late_rows = (self.lanes + hidden // LANE) * TILE + self.lanes * (hidden // devices)
+        self.late_cut = (self.lanes + hidden // LANE) * TILE + hidden // devices
         lengths = [2 * width, width, width, width, hidden, width, width, width]
         self.lengths = lengths
         self.owned = [n // devices for n in lengths]
@@ -90,13 +95,16 @@
         return ((mask >> 1) & 3) * 4 + self.z_order.index(mask & 24)
 
     def grad_piece(self, half, mask, at, rows):
-        cut = self.late_rows // 2
-        first = at < cut
-        assert not first or at + rows <= cut
+        first = at < self.late_cut
+        assert not first or at + rows <= self.late_cut
         swapped = mask if first else (mask & ~6) | ((mask >> 1) & 2) | ((mask & 2) << 1)
         place = self.place(swapped)
-        start = at if first else at - cut
-        return half[place // 8].at[place % 8 + (0 if first else 8), start : start + rows, :]
+        last_rows = self.late_rows - self.late_cut
+        if first:
+            start = (place % 8) * self.late_cut + at
+        else:
+            start = 8 * self.late_cut + (place % 8) * last_rows + at - self.late_cut
+        return half[place // 8].at[start : start + rows, :]
 
 
 def fill_early(plan, me, halves, table_ref, inward_ref, small_ref, stage_ref):
@@ -142,13 +150,9 @@
     else:
         table_in, inward_in, small_in = refs[:3]
         refs = refs[3:]
-    (lifted_out, query_ref, key_ref, value_ref, mixed_ref, total_ref, inward_out, small_ref) = refs[:8]
-    low_ref, table_ref, place_ref, stage_ref, lifted_ref, inward_ref, copied = refs[8:]
+    (lifted_ref, query_ref, key_ref, value_ref, mixed_ref, total_ref, inward_ref, small_ref) = refs[:8]
+    low_ref, table_ref, place_ref, stage_ref = refs[8:]
     pair = pl.program_id(0)
-    copies = [
-        pltpu.make_async_copy(lifted_ref, lifted_out, copied.at[0]),
-        pltpu.make_async_copy(inward_ref, inward_out, copied.at[1]),
-    ]
     total_rows, width = plan.total_rows, plan.width
     half = total_rows // 2
     split = info_ref[0] < total_rows
@@ -180,8 +184,6 @@
             spot = pl.ds(pl.multiple_of(start, rows), rows)
             lifted_ref[spot, :] = lifted
             low_ref[spot, :] = lifted.astype(BF)
-        for copy in copies:
-            copy.start()
 
     weights = jnp.concatenate([inward_ref[pair + i * plan.lanes] for i in range(3)], axis=1)
     lanes = aligned(pair, LANE)
@@ -238,11 +240,6 @@
             mixed_ref[block * STEP : (block + 1) * STEP, :] = jnp.where(lower, *parts).T.astype(BF)
             parts = []
 
-    @pl.when(pair == pl.num_programs(0) - 1)
-    def _():
-        for copy in copies:
-            copy.wait()
-
 
 def attend(plan, info, count, pieces, weights):
     total_rows, width = plan.total_rows, plan.width
@@ -257,13 +254,13 @@
             grid=(plan.lanes,),
             in_specs=[HELD for v in pieces + weights],
             out_specs=[
-                pl.BlockSpec(memory_space=pl.ANY),
+                full((total_rows, width)),
                 block,
                 block,
                 block,
                 block,
                 pl.BlockSpec((1, 8, total_rows), lambda p, *_: (p, 0, 0)),
-                pl.BlockSpec(memory_space=pl.ANY),
+                full(inward),
                 full(small),
             ],
             scratch_shapes=[
@@ -271,9 +268,6 @@
                 pltpu.VMEM((plan.table_pieces, width, LANE), BF),
                 pltpu.VMEM((total_rows, width), F32),
                 pltpu.VMEM((plan.devices, TILE, LANE), F32),
-                pltpu.VMEM((total_rows, width), F32),
-                pltpu.VMEM(inward, BF),
-                pltpu.SemaphoreType.DMA((2,)),
             ],
         ),
         out_shape=[
@@ -480,7 +474,7 @@
     rows = pl.BlockSpec((size, width), lambda i, info: ((info[2] // group) ^ i, 0))
     outward, expand, contract = (width, width), (parts, width, width), (parts * width, width)
     if plan.packed:
-        grads = [pltpu.VMEM((plan.devices // 2, plan.late_rows // 2, LANE), BF)] * 4
+        grads = [pltpu.VMEM((8 * plan.late_rows, LANE), BF)] * 4
     else:
         grads = [pltpu.VMEM(outward, BF), pltpu.VMEM(expand, BF), pltpu.VMEM(contract, BF)]
     ends = [like((piece, width), BF)] * count
@@ -713,10 +707,10 @@
             ],
         ),
         out_shape=tokens + grads,
-        compiler_params=params(56),
+        compiler_params=params(40),
         cost_estimate=cost(14 * 10**9, 24 * 2**20, 6 * 10**6),
         name="attend_back",
-    )(info, lifted, query, key, value, mixed, mixed_back, totals, inward, first_back, small_grad)
+    )(info, *stay([lifted, query, key, value, mixed, mixed_back, totals, inward, first_back]), small_grad)
     return values[:count], values[count:]
 
 
@@ -771,7 +765,7 @@
     table_ref, inward_ref, outward_ref, expand_ref, contract_ref = refs[:5]
     vectors = refs[5:]
     early = sum(ref[0].astype(F32) for ref in early)
-    late = sum(ref[0].astype(F32) for ref in late)
+    late = sum(ref[...].astype(F32) for ref in late)
     for piece in range(plan.table_pieces):
         table_ref[:, piece * LANE : (piece + 1) * LANE] = early[piece * TILE : (piece + 1) * TILE]
     for piece in range(3 * plan.lanes):
@@ -838,6 +832,7 @@
             out_specs=full(out),
         ),
         out_shape=like(out, BF),
+        cost_estimate=cost(0, 48 * 2**20),
         name="settle_rows",
     )(info, *pieces)
 
@@ -932,7 +927,9 @@
     results = exchange(results)
     if plan.packed:
         stay_keep, go_keep, stay_send, go_send = late_grads
-        one_send, two_send = fold([go_keep, swap(go_send, 1)], 2)
+        cut = 8 * plan.late_cut
+        go = [go_keep, swap(go_send, 1)]
+        one_send, two_send = fold([v[:cut] for v in go], 1) + fold([v[cut:] for v in go], 1)
         stay_other = swap(stay_send, 1)
         one_send, two_send, mixed_back = lax.optimization_barrier((one_send, two_send, mixed_back))
         one_other, two_other = swap(one_send, 4), swap(two_send, 2)
@@ -946,19 +943,18 @@
         )
         keep, send = early_grads
         send = swap(send, 1)
-        one, one_send = fold([stay_keep[:8], stay_other[:8], one_other], 2)
-        two, two_send = fold([stay_keep[8:], stay_other[8:], two_other], 2)
+        one, one_send = fold([stay_keep[:cut], stay_other[:cut], one_other], 2)
+        two, two_send = fold([stay_keep[cut:], stay_other[cut:], two_other], 2)
         one, one_send, two, two_send, keep = lax.optimization_barrier((one, one_send, two, two_send, keep))
         one_other, two_other = swap(one_send, 2), swap(two_send, 4)
         terms = fold([keep, send], 4)
-        terms, results, token_pieces, one_other, two_other = lax.optimization_barrier(
-            (terms, results, token_pieces, one_other, two_other)
-        )
+        terms, results, token_pieces = lax.optimization_barrier((terms, results, token_pieces))
         terms = [swap(term, k << 1) for k, term in enumerate(terms)]
+        output = settle_rows(info, micro_count, share, results)
+        one_other, two_other, output = lax.optimization_barrier((one_other, two_other, output))
         ones, twos = fold([one, one_other], 4), fold([two, two_other], 4)
-        late_terms = [jnp.concatenate(pair, axis=1) for pair in zip(ones, twos)]
+        late_terms = [jnp.concatenate(pair, axis=0) for pair in zip(ones, twos)]
         late_terms = [swap(term, mask) for term, mask in zip(late_terms, plan.z_order)]
-        output = in_order(results)
         token_pieces = list(token_pieces)
         token_pieces[1] = swap(token_pieces[1], 1)
         terms, late_terms, output, token_pieces = lax.optimization_barrier(

time: 182 us -> 175 us (0.962)
  other arithmetic: 11.9 us -> 5.55 us
  waiting for transfers between devices: 58.7 us -> 56.5 us
    convert_element_type x5 -> x8, other arithmetic: 7.14 us -> 2.96 us  [fold(): sum((term[index * size:(index + 1) * size].astype(F32) for term in terms))]
    pallas_call x0 -> x1, Pallas kernels: none -> 2.89 us  [settle_rows(): pl.pallas_call(functools.partial(settle_kernel, len(pieces), share), grid...]
    another operation x3 -> x1, other arithmetic: 2.31 us -> 0.09 us  [ordered(): return jnp.stack(pieces)]
    ppermute x45, waiting for transfers between devices: 58.7 us -> 56.5 us  [swap(): lax.ppermute(value, AXES, [(d, d ^ mask) for d in range(devices)])]
  transfers between devices with their start and end apart: 45 -> 45, of which waited for: 18 -> 19; matrix products, arithmetic and copies ran while one was open for 5% -> 2% of each run, Pallas kernels for 21% -> 23%
where the time goes in v6:
time: 175 us
  Pallas kernels  67.3 us (38%)
  waiting for transfers between devices  56.5 us (32%)
  starting transfers between devices  42.4 us (24%)
  other arithmetic  5.55 us (3%)
  local copies, waits for them, and re-layouts  1.97 us (1%)
    ppermute x45, waiting for transfers between devices, swap(): lax.ppermute(value, AXES, [(d, d ^ mask) for d in range(devices)])  56.5 us
    ppermute x45, starting transfers between devices, swap(): lax.ppermute(value, AXES, [(d, d ^ mask) for d in range(devices)])  42.4 us
    pallas_call x1, Pallas kernels, feed(): pl.pallas_call(functools.partial(feed_kernel, plan, count), grid_spec=plt...  24.9 us
    pallas_call x1, Pallas kernels, attend_back(): pl.pallas_call(functools.partial(attend_back_kernel, plan, count), grid_s...  19.1 us
    pallas_call x1, Pallas kernels, attend(): pl.pallas_call(functools.partial(attend_kernel, plan, count), grid_spec=p...  14.3 us
  transfers between devices with their start and end apart: 45, of which 19 were waited for; matrix products, arithmetic and copies ran while one was open for 2% of the time, Pallas kernels for 23%

profile of v6, /device:TPU:0, one launch (start us, length us, event | category | flops | bytes accessed | tf_op | source)
XLA Modules:
  0.0 174.8 jit_solution(4514231794999426836)
XLA Ops:
  0.7 2.4 %pack.1 = (bf16[256,512]{1,0:T(8,128)(2,1)}, bf16[256,512]{1,0:T(8,128)(2,1)}, bf16[256,512]{1,0:T(8,128)(2,1)}, bf16[256,512]{1,0:T(8,128)(2,1)}, bf16[1,336,12...) custom-call(bf16[4,256,512]{2,1,0:T(8,128)(2,1)} %bitcast.41, bf16[16,1024]{1,0:T(8,128)(2,1)} %bitcast.43, ...), custom_call_target="tpu_custom_call" | custom-call | bytes 4194304 | tf_op jit(solution)/shard_map/pack/pallas_call | solution.py:746
  3.6 2.6 %collective-permute-start.4 = (bf16[256,512]{1,0:T(8,128)(2,1)}, bf16[256,512]{1,0:T(8,128)(2,1)S(1)}, u32[]{:S(2)}, u32[]{:S(2)}) collective-permute-start(bf16[256,512]{1,0:T(8,128)(2,1)} %get-tuple-element.161), channel_id=1, source_target_pairs={{0,2},{1,3},{2,0},{3,1},{4,6},{5,7},{6,4},{7,5},{8,10},{9,11},{10,... | collective-permute-start | bytes 786440 | tf_op jit(solution)/shard_map/ppermute | solution.py:875
  6.2 2.8 %collective-permute-start.1 = (bf16[1,336,128]{2,1,0:T(8,128)(2,1)}, bf16[1,336,128]{2,1,0:T(8,128)(2,1)S(1)}, u32[]{:S(2)}, u32[]{:S(2)}) collective-permute-start(bf16[1,336,128]{2,1,0:T(8,128)(2,1)} %get-tuple-element.164), channel_id=1, source_target_pairs={{0,16},{1,17},{2,18},{3,19},{4,20},{5,21},{6,22},{7,23},{8,24},{9,... | collective-permute-start | bytes 258056 | tf_op jit(solution)/shard_map/ppermute | solution.py:875
  9.0 1.6 collective-permute-start.2
  10.6 2.9 %collective-permute-done.4.refs_2_ = bf16[256,512]{1,0:T(8,128)(2,1)S(1)} collective-permute-done((bf16[256,512]{1,0:T(8,128)(2,1)}, bf16[256,512]{1,0:T(8,128)(2,1)S(1)}, u32[]{:S(2)}, u32[]{:S(2)}) %collective-permute-start.4) | collective-permute-done | bytes 262176 | tf_op jit(solution)/shard_map/ppermute | solution.py:875
  13.5 5.1 %collective-permute-done.5.refs_3_ = bf16[256,512]{1,0:T(8,128)(2,1)S(1)} collective-permute-done((bf16[256,512]{1,0:T(8,128)(2,1)}, bf16[256,512]{1,0:T(8,128)(2,1)S(1)}, u32[]{:S(2)}, u32[]{:S(2)}) %collective-permute-start.5) | collective-permute-done | bytes 262176 | tf_op jit(solution)/shard_map/ppermute | solution.py:875
  19.5 1.7 collective-permute-start.10
  21.2 1.6 collective-permute-start.6
  22.8 1.5 collective-permute-start.7
  24.8 2.5 %collective-permute-start.11 = (bf16[1,576,128]{2,1,0:T(8,128)(2,1)}, bf16[1,576,128]{2,1,0:T(8,128)(2,1)S(1)}, u32[]{:S(2)}, u32[]{:S(2)}) collective-permute-start(bf16[1,576,128]{2,1,0:T(8,128)(2,1)} %get-tuple-element.184), channel_id=1, source_target_pairs={{0,24},{1,25},{2,26},{3,27},{4,28},{5,29},{6,30},{7,31},{8,16},{9,... | collective-permute-start | bytes 442376 | tf_op jit(solution)/shard_map/ppermute | solution.py:875
  29.1 2.2 %cut_rows.1 = (bf16[256,512]{1,0:T(8,128)(2,1)}, bf16[256,512]{1,0:T(8,128)(2,1)}, bf16[256,512]{1,0:T(8,128)(2,1)}, bf16[256,512]{1,0:T(8,128)(2,1)}) custom-call(bf16[4,256,512]{2,1,0:T(8,128)(2,1)} %bitcast.42), custom_call_target="tpu_custom_call" | custom-call | bytes 4194304 | tf_op jit(solution)/shard_map/cut_rows/pallas_call | solution.py:848
  33.4 6.8 %collective-permute-done.9 = bf16[1,576,128]{2,1,0:T(8,128)(2,1)S(1)} collective-permute-done((bf16[1,576,128]{2,1,0:T(8,128)(2,1)}, bf16[1,576,128]{2,1,0:T(8,128)(2,1)S(1)}, u32[]{:S(2)}, u32[]{:S(2)}) %collective-permute-start.9) | collective-permute-done | bytes 147488 | tf_op jit(solution)/shard_map/ppermute | solution.py:875
  41.3 1.6 collective-permute-start.14
  42.9 1.5 collective-permute-start.15
  44.4 1.5 collective-permute-done.16.refs_1_
  46.0 11.1 %collective-permute-done.14.refs_5_ = bf16[4,576,128]{2,1,0:T(8,128)(2,1)S(1)} collective-permute-done((bf16[4,576,128]{2,1,0:T(8,128)(2,1)S(1)}, bf16[4,576,128]{2,1,0:T(8,128)(2,1)S(1)}, u32[]{:S(2)}, u32[]{:S(2)}) %collective-permute-start.14) | collective-permute-done | bytes 589856 | tf_op jit(solution)/shard_map/ppermute | solution.py:875
  58.3 1.5 collective-permute-start.17
  61.7 14.3 %attend.1 = (f32[1024,512]{1,0:T(8,128)}, bf16[1024,512]{1,0:T(8,128)(2,1)}, bf16[1024,512]{1,0:T(8,128)(2,1)}, bf16[1024,512]{1,0:T(8,128)(2,1)}, bf16[1024,512...) custom-call(s32[4]{0:T(128)S(1)} %pad_add_fusion.info_ref, ...), custom_call_target="tpu_custom_call" | custom-call | flops 5000000000 | bytes 14680064 | tf_op jit(solution)/shard_map/attend/pallas_call | solution.py:250
  76.9 1.6 collective-permute-done.22.refs_11_
  78.6 24.9 %feed.1 = (bf16[256,512]{1,0:T(8,128)(2,1)}, bf16[256,512]{1,0:T(8,128)(2,1)}, bf16[256,512]{1,0:T(8,128)(2,1)}, bf16[256,512]{1,0:T(8,128)(2,1)}, bf16[1024,512...) custom-call(s32[4]{0:T(128)} %copy-done, ...), custom_call_target="tpu_custom_call" | custom-call | flops 15000000512 | bytes 20971520 | tf_op jit(solution)/shard_map/feed/pallas_call | solution.py:482
  107.8 19.1 %attend_back.1 = (bf16[256,512]{1,0:T(8,128)(2,1)S(1)}, bf16[256,512]{1,0:T(8,128)(2,1)S(1)}, bf16[256,512]{1,0:T(8,128)(2,1)S(1)}, bf16[256,512]{1,0:T(8,128)(2...) custom-call(s32[4]{0:T(128)S(1)} %copy-done.1, f32[1024,512]{1,0:T(8,128)} %get-tuple-element.194.lifted_ref, ...), custom_call_target="tpu_custom_call" | custom-call | flops 14000000000 | bytes 25165824 | tf_op jit(solution)/shard_map/attend_back/pallas_call | solution.py:677
  127.8 1.5 collective-permute-start.34
  131.9 2.9 %settle_rows.1 = bf16[4,256,512]{2,1,0:T(8,128)(2,1)} custom-call(s32[4]{0:T(128)} %copy-done, bf16[256,512]{1,0:T(8,128)(2,1)} %get-tuple-element.259.refs_0_, bf16[256,512]{1,0:T(8,128)(2,1)} %copy-done.7, bf16[256,512]{1,0:T(8,128)(2,1)} %copy-done.8, bf16[256,512]{1,0:T(8,128)(2,1)} %copy-done.9), custom_call_target="tpu_custom_call" | custom-call | bytes 50331648 | tf_op jit(solution)/shard_map/settle_rows/pallas_call | solution.py:826
  136.1 3.0 %collective-permute-done.34 = bf16[1536,128]{1,0:T(8,128)(2,1)S(1)} collective-permute-done((bf16[1536,128]{1,0:T(8,128)(2,1)S(1)}, bf16[1536,128]{1,0:T(8,128)(2,1)S(1)}, u32[]{:S(2)}, u32[]{:S(2)}) %collective-permute-start.34) | collective-permute-done | bytes 393248 | tf_op jit(solution)/shard_map/ppermute | solution.py:875
  139.4 2.7 %collective-permute-start.38 = (bf16[576,128]{1,0:T(8,128)(2,1)S(1)}, bf16[576,128]{1,0:T(8,128)(2,1)S(1)}, u32[]{:S(2)}, u32[]{:S(2)}) collective-permute-start(bf16[576,128]{1,0:T(8,128)(2,1)S(1)} %pad_maximum_fusion.3), channel_id=1, source_target_pairs={{0,24},{1,25},{2,26},{3,27},{4,28},{5,29},{6,30},{7,31},{8,16},{9,... | collective-permute-start | bytes 442376 | tf_op jit(solution)/shard_map/ppermute | solution.py:875
  147.0 3.8 %collective-permute-done.37.refs_6_ = bf16[576,128]{1,0:T(8,128)(2,1)S(1)} collective-permute-done((bf16[576,128]{1,0:T(8,128)(2,1)S(1)}, bf16[576,128]{1,0:T(8,128)(2,1)S(1)}, u32[]{:S(2)}, u32[]{:S(2)}) %collective-permute-start.37) | collective-permute-done | bytes 147488 | tf_op jit(solution)/shard_map/ppermute | solution.py:875
  150.8 7.5 %collective-permute-done.36.refs_5_ = bf16[576,128]{1,0:T(8,128)(2,1)S(1)} collective-permute-done((bf16[576,128]{1,0:T(8,128)(2,1)S(1)}, bf16[576,128]{1,0:T(8,128)(2,1)S(1)}, u32[]{:S(2)}, u32[]{:S(2)}) %collective-permute-start.36) | collective-permute-done | bytes 147488 | tf_op jit(solution)/shard_map/ppermute | solution.py:875
  158.3 1.5 collective-permute-done.32
  161.9 2.2 %collective-permute-start.43 = (bf16[1,336,128]{2,1,0:T(8,128)(2,1)S(1)}, bf16[1,336,128]{2,1,0:T(8,128)(2,1)S(1)}, u32[]{:S(2)}, u32[]{:S(2)}) collective-permute-start(bf16[1,336,128]{2,1,0:T(8,128)(2,1)S(1)} %get-tuple-element.321), channel_id=1, source_target_pairs={{0,8},{1,9},{2,10},{3,11},{4,12},{5,13},{6,14},{7,15},{8,0},{9,1},... | collective-permute-start | bytes 258056 | tf_op jit(solution)/shard_map/ppermute | solution.py:875
  164.1 2.2 %collective-permute-start.44 = (bf16[1,336,128]{2,1,0:T(8,128)(2,1)S(1)}, bf16[1,336,128]{2,1,0:T(8,128)(2,1)S(1)}, u32[]{:S(2)}, u32[]{:S(2)}) collective-permute-start(bf16[1,336,128]{2,1,0:T(8,128)(2,1)S(1)} %get-tuple-element.320), channel_id=1, source_target_pairs={{0,24},{1,25},{2,26},{3,27},{4,28},{5,29},{6,30},{7,31},{8,16},{9,... | collective-permute-start | bytes 258056 | tf_op jit(solution)/shard_map/ppermute | solution.py:875
  166.3 3.5 %collective-permute-done.42.refs_1_ = bf16[1,336,128]{2,1,0:T(8,128)(2,1)S(1)} collective-permute-done((bf16[1,336,128]{2,1,0:T(8,128)(2,1)}, bf16[1,336,128]{2,1,0:T(8,128)(2,1)S(1)}, u32[]{:S(2)}, u32[]{:S(2)}) %collective-permute-start.42) | collective-permute-done | bytes 86048 | tf_op jit(solution)/shard_map/ppermute | solution.py:875
  171.1 1.5 finish.1
  (129 shorter events, 30.6 us)
Async XLA Ops:
  3.6 9.9 %collective-permute-start.4 = (bf16[256,512]{1,0:T(8,128)(2,1)}, bf16[256,512]{1,0:T(8,128)(2,1)S(1)}, u32[]{:S(2)}, u32[]{:S(2)}) collective-permute-start(bf16[256,512]{1,0:T(8,128)(2,1)} %get-tuple-element.161), channel_id=1, source_target_pairs={{0,2},{1,3},{2,0},{3,1},{4,6},{5,7},{6,4},{7,5},{8,10},{9,11},{10,... | collective-permute-start | bytes 786440 | tf_op jit(solution)/shard_map/ppermute | solution.py:875
  6.1 12.5 %collective-permute-start.5 = (bf16[256,512]{1,0:T(8,128)(2,1)}, bf16[256,512]{1,0:T(8,128)(2,1)S(1)}, u32[]{:S(2)}, u32[]{:S(2)}) collective-permute-start(bf16[256,512]{1,0:T(8,128)(2,1)} %get-tuple-element.162), channel_id=1, source_target_pairs={{0,3},{1,2},{2,1},{3,0},{4,7},{5,6},{6,5},{7,4},{8,11},{9,10},{10,... | collective-permute-start | bytes 786440 | tf_op jit(solution)/shard_map/ppermute | solution.py:875
  6.2 12.4 %collective-permute-start.1 = (bf16[1,336,128]{2,1,0:T(8,128)(2,1)}, bf16[1,336,128]{2,1,0:T(8,128)(2,1)S(1)}, u32[]{:S(2)}, u32[]{:S(2)}) collective-permute-start(bf16[1,336,128]{2,1,0:T(8,128)(2,1)} %get-tuple-element.164), channel_id=1, source_target_pairs={{0,16},{1,17},{2,18},{3,19},{4,20},{5,21},{6,22},{7,23},{8,24},{9,... | collective-permute-start | bytes 258056 | tf_op jit(solution)/shard_map/ppermute | solution.py:875
  9.0 9.6 %collective-permute-start.2 = (bf16[1,336,128]{2,1,0:T(8,128)(2,1)}, bf16[1,336,128]{2,1,0:T(8,128)(2,1)S(1)}, u32[]{:S(2)}, u32[]{:S(2)}) collective-permute-start(bf16[1,336,128]{2,1,0:T(8,128)(2,1)} %get-tuple-element.164), channel_id=1, source_target_pairs={{0,8},{1,9},{2,10},{3,11},{4,12},{5,13},{6,14},{7,15},{8,0},{9,1},... | collective-permute-start | bytes 258056 | tf_op jit(solution)/shard_map/ppermute | solution.py:875
  10.6 8.0 %collective-permute-start.3 = (bf16[1,336,128]{2,1,0:T(8,128)(2,1)}, bf16[1,336,128]{2,1,0:T(8,128)(2,1)S(1)}, u32[]{:S(2)}, u32[]{:S(2)}) collective-permute-start(bf16[1,336,128]{2,1,0:T(8,128)(2,1)} %get-tuple-element.164), channel_id=1, source_target_pairs={{0,24},{1,25},{2,26},{3,27},{4,28},{5,29},{6,30},{7,31},{8,16},{9,... | collective-permute-start | bytes 258056 | tf_op jit(solution)/shard_map/ppermute | solution.py:875
  21.2 19.0 %collective-permute-start.6 = (bf16[4,336,128]{2,1,0:T(8,128)(2,1)S(1)}, bf16[4,336,128]{2,1,0:T(8,128)(2,1)S(1)}, u32[]{:S(2)}, u32[]{:S(2)}) collective-permute-start(bf16[4,336,128]{2,1,0:T(8,128)(2,1)S(1)} %constant_dynamic-update-slice_fusion), channel_id=1, source_target_pairs={{0,2},{1,3},{2,0},{3,1},{4,6},{5,7},{6,4},{7,5},{8,10},{9,11},{10,... | collective-permute-start | bytes 1032200 | tf_op jit(solution)/shard_map/ppermute | solution.py:875
  22.8 17.4 %collective-permute-start.7 = (bf16[4,336,128]{2,1,0:T(8,128)(2,1)S(1)}, bf16[4,336,128]{2,1,0:T(8,128)(2,1)S(1)}, u32[]{:S(2)}, u32[]{:S(2)}) collective-permute-start(bf16[4,336,128]{2,1,0:T(8,128)(2,1)S(1)} %constant_dynamic-update-slice_fusion), channel_id=1, source_target_pairs={{0,4},{1,5},{2,6},{3,7},{4,0},{5,1},{6,2},{7,3},{8,12},{9,13},{10,... | collective-permute-start | bytes 1032200 | tf_op jit(solution)/shard_map/ppermute | solution.py:875
  24.3 15.9 %collective-permute-start.8 = (bf16[4,336,128]{2,1,0:T(8,128)(2,1)S(1)}, bf16[4,336,128]{2,1,0:T(8,128)(2,1)S(1)}, u32[]{:S(2)}, u32[]{:S(2)}) collective-permute-start(bf16[4,336,128]{2,1,0:T(8,128)(2,1)S(1)} %constant_dynamic-update-slice_fusion), channel_id=1, source_target_pairs={{0,6},{1,7},{2,4},{3,5},{4,2},{5,3},{6,0},{7,1},{8,14},{9,15},{10,... | collective-permute-start | bytes 1032200 | tf_op jit(solution)/shard_map/ppermute | solution.py:875
  24.8 8.6 %collective-permute-start.11 = (bf16[1,576,128]{2,1,0:T(8,128)(2,1)}, bf16[1,576,128]{2,1,0:T(8,128)(2,1)S(1)}, u32[]{:S(2)}, u32[]{:S(2)}) collective-permute-start(bf16[1,576,128]{2,1,0:T(8,128)(2,1)} %get-tuple-element.184), channel_id=1, source_target_pairs={{0,24},{1,25},{2,26},{3,27},{4,28},{5,29},{6,30},{7,31},{8,16},{9,... | collective-permute-start | bytes 442376 | tf_op jit(solution)/shard_map/ppermute | solution.py:875
  27.3 13.0 %collective-permute-start.9 = (bf16[1,576,128]{2,1,0:T(8,128)(2,1)}, bf16[1,576,128]{2,1,0:T(8,128)(2,1)S(1)}, u32[]{:S(2)}, u32[]{:S(2)}) collective-permute-start(bf16[1,576,128]{2,1,0:T(8,128)(2,1)} %get-tuple-element.184), channel_id=1, source_target_pairs={{0,16},{1,17},{2,18},{3,19},{4,20},{5,21},{6,22},{7,23},{8,24},{9,... | collective-permute-start | bytes 442376 | tf_op jit(solution)/shard_map/ppermute | solution.py:875
  40.5 17.8 %collective-permute-start.12 = (bf16[16,336,128]{2,1,0:T(8,128)(2,1)S(1)}, bf16[16,336,128]{2,1,0:T(8,128)(2,1)S(1)}, u32[]{:S(2)}, u32[]{:S(2)}) collective-permute-start(bf16[16,336,128]{2,1,0:T(8,128)(2,1)S(1)} %constant_dynamic-update-slice_fusion.4.refs_4_), channel_id=1, source_target_pairs={{0,1},{1,0},{2,3},{3,2},{4,5},{5,4},{6,7},{7,6},{8,9},{9,8},{10,11... | collective-permute-start | bytes 4128776 | tf_op jit(solution)/shard_map/ppermute | solution.py:875
  41.3 15.7 %collective-permute-start.14 = (bf16[4,576,128]{2,1,0:T(8,128)(2,1)S(1)}, bf16[4,576,128]{2,1,0:T(8,128)(2,1)S(1)}, u32[]{:S(2)}, u32[]{:S(2)}) collective-permute-start(bf16[4,576,128]{2,1,0:T(8,128)(2,1)S(1)} %constant_dynamic-update-slice_fusion.8.refs_4_), channel_id=1, source_target_pairs={{0,2},{1,3},{2,0},{3,1},{4,6},{5,7},{6,4},{7,5},{8,10},{9,11},{10,... | collective-permute-start | bytes 1769480 | tf_op jit(solution)/shard_map/ppermute | solution.py:875
  42.9 15.4 %collective-permute-start.15 = (bf16[4,576,128]{2,1,0:T(8,128)(2,1)S(1)}, bf16[4,576,128]{2,1,0:T(8,128)(2,1)S(1)}, u32[]{:S(2)}, u32[]{:S(2)}) collective-permute-start(bf16[4,576,128]{2,1,0:T(8,128)(2,1)S(1)} %constant_dynamic-update-slice_fusion.8.refs_4_), channel_id=1, source_target_pairs={{0,4},{1,5},{2,6},{3,7},{4,0},{5,1},{6,2},{7,3},{8,12},{9,13},{10,... | collective-permute-start | bytes 1769480 | tf_op jit(solution)/shard_map/ppermute | solution.py:875
  58.3 17.7 %collective-permute-start.17 = (bf16[4,576,128]{2,1,0:T(8,128)(2,1)S(1)}, bf16[4,576,128]{2,1,0:T(8,128)(2,1)S(1)}, u32[]{:S(2)}, u32[]{:S(2)}) collective-permute-start(bf16[4,576,128]{2,1,0:T(8,128)(2,1)S(1)} %collective-permute-done.14.refs_5_), channel_id=1, source_target_pairs={{0,4},{1,5},{2,6},{3,7},{4,0},{5,1},{6,2},{7,3},{8,12},{9,13},{10,... | collective-permute-start | bytes 1769480 | tf_op jit(solution)/shard_map/ppermute | solution.py:875
  59.8 16.2 %collective-permute-start.18 = (bf16[4,576,128]{2,1,0:T(8,128)(2,1)S(1)}, bf16[4,576,128]{2,1,0:T(8,128)(2,1)S(1)}, u32[]{:S(2)}, u32[]{:S(2)}) collective-permute-start(bf16[4,576,128]{2,1,0:T(8,128)(2,1)S(1)} %collective-permute-done.14.refs_5_), channel_id=1, source_target_pairs={{0,1},{1,0},{2,3},{3,2},{4,5},{5,4},{6,7},{7,6},{8,9},{9,8},{10,11... | collective-permute-start | bytes 1769480 | tf_op jit(solution)/shard_map/ppermute | solution.py:875
  59.8 16.2 %collective-permute-start.19 = (bf16[4,576,128]{2,1,0:T(8,128)(2,1)S(1)}, bf16[4,576,128]{2,1,0:T(8,128)(2,1)S(1)}, u32[]{:S(2)}, u32[]{:S(2)}) collective-permute-start(bf16[4,576,128]{2,1,0:T(8,128)(2,1)S(1)} %collective-permute-done.15.refs_6_), channel_id=1, source_target_pairs={{0,1},{1,0},{2,3},{3,2},{4,5},{5,4},{6,7},{7,6},{8,9},{9,8},{10,11... | collective-permute-start | bytes 1769480 | tf_op jit(solution)/shard_map/ppermute | solution.py:875
  60.3 15.7 %collective-permute-start.20 = (bf16[256,512]{1,0:T(8,128)(2,1)S(1)}, bf16[256,512]{1,0:T(8,128)(2,1)S(1)}, u32[]{:S(2)}, u32[]{:S(2)}) collective-permute-start(bf16[256,512]{1,0:T(8,128)(2,1)S(1)} %copy-done.12), channel_id=1, source_target_pairs={{0,2},{1,3},{2,0},{3,1},{4,6},{5,7},{6,4},{7,5},{8,10},{9,11},{10,... | collective-permute-start | bytes 786440 | tf_op jit(solution)/shard_map/ppermute | solution.py:875
  60.9 15.1 %collective-permute-start.21 = (bf16[256,512]{1,0:T(8,128)(2,1)S(1)}, bf16[256,512]{1,0:T(8,128)(2,1)S(1)}, u32[]{:S(2)}, u32[]{:S(2)}) collective-permute-start(bf16[256,512]{1,0:T(8,128)(2,1)S(1)} %copy-done.11), channel_id=1, source_target_pairs={{0,3},{1,2},{2,1},{3,0},{4,7},{5,6},{6,5},{7,4},{8,11},{9,10},{10,... | collective-permute-start | bytes 786440 | tf_op jit(solution)/shard_map/ppermute | solution.py:875
  103.8 23.1 %collective-permute-start.26 = (bf16[4608,128]{1,0:T(8,128)(2,1)S(1)}, bf16[4608,128]{1,0:T(8,128)(2,1)S(1)}, u32[]{:S(2)}, u32[]{:S(2)}) collective-permute-start(bf16[4608,128]{1,0:T(8,128)(2,1)S(1)} %get-tuple-element.219), channel_id=1, source_target_pairs={{0,1},{1,0},{2,3},{3,2},{4,5},{5,4},{6,7},{7,6},{8,9},{9,8},{10,11... | collective-permute-start | bytes 3538952 | tf_op jit(solution)/shard_map/ppermute | solution.py:875
  104.3 22.6 %collective-permute-start.28 = (bf16[256,512]{1,0:T(8,128)(2,1)}, bf16[256,512]{1,0:T(8,128)(2,1)S(1)}, u32[]{:S(2)}, u32[]{:S(2)}) collective-permute-start(bf16[256,512]{1,0:T(8,128)(2,1)} %get-tuple-element.222), channel_id=1, source_target_pairs={{0,2},{1,3},{2,0},{3,1},{4,6},{5,7},{6,4},{7,5},{8,10},{9,11},{10,... | collective-permute-start | bytes 786440 | tf_op jit(solution)/shard_map/ppermute | solution.py:875
  104.9 22.1 %collective-permute-start.29 = (bf16[256,512]{1,0:T(8,128)(2,1)}, bf16[256,512]{1,0:T(8,128)(2,1)S(1)}, u32[]{:S(2)}, u32[]{:S(2)}) collective-permute-start(bf16[256,512]{1,0:T(8,128)(2,1)} %get-tuple-element.223), channel_id=1, source_target_pairs={{0,3},{1,2},{2,1},{3,0},{4,7},{5,6},{6,5},{7,4},{8,11},{9,10},{10,... | collective-permute-start | bytes 786440 | tf_op jit(solution)/shard_map/ppermute | solution.py:875
  106.6 20.4 %collective-permute-start.24 = (bf16[3072,128]{1,0:T(8,128)(2,1)S(1)}, bf16[3072,128]{1,0:T(8,128)(2,1)S(1)}, u32[]{:S(2)}, u32[]{:S(2)}) collective-permute-start(bf16[3072,128]{1,0:T(8,128)(2,1)S(1)} %add_convert_fusion), channel_id=1, source_target_pairs={{0,4},{1,5},{2,6},{3,7},{4,0},{5,1},{6,2},{7,3},{8,12},{9,13},{10,... | collective-permute-start | bytes 2359304 | tf_op jit(solution)/shard_map/ppermute | solution.py:875
  107.3 19.7 %collective-permute-start.25 = (bf16[1536,128]{1,0:T(8,128)(2,1)S(1)}, bf16[1536,128]{1,0:T(8,128)(2,1)S(1)}, u32[]{:S(2)}, u32[]{:S(2)}) collective-permute-start(bf16[1536,128]{1,0:T(8,128)(2,1)S(1)} %add_convert_fusion.3), channel_id=1, source_target_pairs={{0,2},{1,3},{2,0},{3,1},{4,6},{5,7},{6,4},{7,5},{8,10},{9,11},{10,... | collective-permute-start | bytes 1179656 | tf_op jit(solution)/shard_map/ppermute | solution.py:875
  127.8 11.4 %collective-permute-start.34 = (bf16[1536,128]{1,0:T(8,128)(2,1)S(1)}, bf16[1536,128]{1,0:T(8,128)(2,1)S(1)}, u32[]{:S(2)}, u32[]{:S(2)}) collective-permute-start(bf16[1536,128]{1,0:T(8,128)(2,1)S(1)} %get-tuple-element.257), channel_id=1, source_target_pairs={{0,2},{1,3},{2,0},{3,1},{4,6},{5,7},{6,4},{7,5},{8,10},{9,11},{10,... | collective-permute-start | bytes 1179656 | tf_op jit(solution)/shard_map/ppermute | solution.py:875
  142.1 16.3 %collective-permute-start.31 = (bf16[4,336,128]{2,1,0:T(8,128)(2,1)S(1)}, bf16[4,336,128]{2,1,0:T(8,128)(2,1)S(1)}, u32[]{:S(2)}, u32[]{:S(2)}) collective-permute-start(bf16[4,336,128]{2,1,0:T(8,128)(2,1)S(1)} %copy-done.6), channel_id=1, source_target_pairs={{0,2},{1,3},{2,0},{3,1},{4,6},{5,7},{6,4},{7,5},{8,10},{9,11},{10,... | collective-permute-start | bytes 1032200 | tf_op jit(solution)/shard_map/ppermute | solution.py:875
  143.5 16.3 %collective-permute-start.32 = (bf16[4,336,128]{2,1,0:T(8,128)(2,1)S(1)}, bf16[4,336,128]{2,1,0:T(8,128)(2,1)S(1)}, u32[]{:S(2)}, u32[]{:S(2)}) collective-permute-start(bf16[4,336,128]{2,1,0:T(8,128)(2,1)S(1)} %copy-done.5), channel_id=1, source_target_pairs={{0,4},{1,5},{2,6},{3,7},{4,0},{5,1},{6,2},{7,3},{8,12},{9,13},{10,... | collective-permute-start | bytes 1032200 | tf_op jit(solution)/shard_map/ppermute | solution.py:875
  145.0 14.9 %collective-permute-start.33 = (bf16[4,336,128]{2,1,0:T(8,128)(2,1)S(1)}, bf16[4,336,128]{2,1,0:T(8,128)(2,1)S(1)}, u32[]{:S(2)}, u32[]{:S(2)}) collective-permute-start(bf16[4,336,128]{2,1,0:T(8,128)(2,1)S(1)} %copy-done.4), channel_id=1, source_target_pairs={{0,6},{1,7},{2,4},{3,5},{4,2},{5,3},{6,0},{7,1},{8,14},{9,15},{10,... | collective-permute-start | bytes 1032200 | tf_op jit(solution)/shard_map/ppermute | solution.py:875
  147.0 11.3 %collective-permute-start.39 = (bf16[256,512]{1,0:T(8,128)(2,1)S(1)}, bf16[256,512]{1,0:T(8,128)(2,1)S(1)}, u32[]{:S(2)}, u32[]{:S(2)}) collective-permute-start(bf16[256,512]{1,0:T(8,128)(2,1)S(1)} %get-tuple-element.268), channel_id=1, source_target_pairs={{0,1},{1,0},{2,3},{3,2},{4,5},{5,4},{6,7},{7,6},{8,9},{9,8},{10,11... | collective-permute-start | bytes 786440 | tf_op jit(solution)/shard_map/ppermute | solution.py:875
  159.9 12.8 %collective-permute-start.40 = (bf16[256,512]{1,0:T(8,128)(2,1)S(1)}, bf16[256,512]{1,0:T(8,128)(2,1)S(1)}, u32[]{:S(2)}, u32[]{:S(2)}) collective-permute-start(bf16[256,512]{1,0:T(8,128)(2,1)S(1)} %get-tuple-element.272), channel_id=1, source_target_pairs={{0,3},{1,2},{2,1},{3,0},{4,7},{5,6},{6,5},{7,4},{8,11},{9,10},{10,... | collective-permute-start | bytes 786440 | tf_op jit(solution)/shard_map/ppermute | solution.py:875
  159.9 13.7 %collective-permute-start.41 = (bf16[256,512]{1,0:T(8,128)(2,1)S(1)}, bf16[256,512]{1,0:T(8,128)(2,1)S(1)}, u32[]{:S(2)}, u32[]{:S(2)}) collective-permute-start(bf16[256,512]{1,0:T(8,128)(2,1)S(1)} %get-tuple-element.273), channel_id=1, source_target_pairs={{0,2},{1,3},{2,0},{3,1},{4,6},{5,7},{6,4},{7,5},{8,10},{9,11},{10,... | collective-permute-start | bytes 786440 | tf_op jit(solution)/shard_map/ppermute | solution.py:875
  161.9 7.9 %collective-permute-start.42 = (bf16[1,336,128]{2,1,0:T(8,128)(2,1)}, bf16[1,336,128]{2,1,0:T(8,128)(2,1)S(1)}, u32[]{:S(2)}, u32[]{:S(2)}) collective-permute-start(bf16[1,336,128]{2,1,0:T(8,128)(2,1)} %get-tuple-element.322), channel_id=1, source_target_pairs={{0,16},{1,17},{2,18},{3,19},{4,20},{5,21},{6,22},{7,23},{8,24},{9,... | collective-permute-start | bytes 258056 | tf_op jit(solution)/shard_map/ppermute | solution.py:875
  161.9 7.9 %collective-permute-start.43 = (bf16[1,336,128]{2,1,0:T(8,128)(2,1)S(1)}, bf16[1,336,128]{2,1,0:T(8,128)(2,1)S(1)}, u32[]{:S(2)}, u32[]{:S(2)}) collective-permute-start(bf16[1,336,128]{2,1,0:T(8,128)(2,1)S(1)} %get-tuple-element.321), channel_id=1, source_target_pairs={{0,8},{1,9},{2,10},{3,11},{4,12},{5,13},{6,14},{7,15},{8,0},{9,1},... | collective-permute-start | bytes 258056 | tf_op jit(solution)/shard_map/ppermute | solution.py:875
  (31 other events, 273.6 us)

commit v7 on v6

--- a/solution.py
+++ b/solution.py
@@ -477,7 +477,7 @@
         grads = [pltpu.VMEM((8 * plan.late_rows, LANE), BF)] * 4
     else:
         grads = [pltpu.VMEM(outward, BF), pltpu.VMEM(expand, BF), pltpu.VMEM(contract, BF)]
-    ends = [like((piece, width), BF)] * count
+    ends = [pltpu.VMEM((piece, width), BF)] * count
     outs = [like((total_rows, width), BF), like((total_rows, width), F32), like(small.shape, F32)]
     values = pl.pallas_call(
         functools.partial(feed_kernel, plan, count),
@@ -485,10 +485,9 @@
             num_scalar_prefetch=1,
             grid=(total_rows // size,),
             in_specs=[rows, rows]
-            + [full(v.shape) for v in upstreams]
-            + [HELD for v in weights]
+            + [HELD for v in upstreams + weights]
             + [full(small.shape)],
-            out_specs=[full(v.shape) for v in ends]
+            out_specs=[HELD for v in ends]
             + [rows, rows, full(small.shape)]
             + [HELD for v in grads],
             scratch_shapes=[
@@ -510,10 +509,10 @@
             ],
         ),
         out_shape=ends + outs + grads,
-        compiler_params=params(51),
+        compiler_params=params(50),
         cost_estimate=cost(15 * 10**9, 20 * 2**20, 2 * 10**6),
         name="feed",
-    )(info, lifted, mixed, *upstreams, *hold(weights), small)
+    )(info, lifted, mixed, *hold(upstreams), *hold(weights), small)
     return values[:count], values[count : count + 3], values[count + 3 :]
 
 
@@ -963,6 +962,7 @@
         terms = fold(terms, 4)
         early_terms = [swap(term, mask) for term, mask in zip(terms, plan.z_order)]
         token_pieces[2:] = [swap(token_pieces[mask], mask) for mask in (2, 3)]
+        early_terms, token_pieces = lax.optimization_barrier((early_terms, token_pieces))
         tokens_back = in_order(token_pieces)
         values = finish(plan, info, early_terms, late_terms)
         table_t, inward_own, outward_own, expand_own, contract_own = values[:5]

time: 175 us -> 174 us (level)
  transfers between devices with their start and end apart: 45 -> 45, of which waited for: 19 -> 18; matrix products, arithmetic and copies ran while one was open for 2% -> 2% of each run, Pallas kernels for 23% -> 22%
where the time goes in v7:
time: 174 us; the launch traced here: 173 us
  Pallas kernels  66.6 us (38%)
  waiting for transfers between devices  55.2 us (32%)
  starting transfers between devices  42.2 us (24%)
  other arithmetic  5.82 us (3%)
  local copies, waits for them, and re-layouts  2.39 us (1%)
    ppermute x45, waiting for transfers between devices, swap(): lax.ppermute(value, AXES, [(d, d ^ mask) for d in range(devices)])  55.2 us
    ppermute x45, starting transfers between devices, swap(): lax.ppermute(value, AXES, [(d, d ^ mask) for d in range(devices)])  42.2 us
    pallas_call x1, Pallas kernels, feed(): pl.pallas_call(functools.partial(feed_kernel, plan, count), grid_spec=plt...  24.2 us
    pallas_call x1, Pallas kernels, attend_back(): pl.pallas_call(functools.partial(attend_back_kernel, plan, count), grid_s...  19.1 us
    pallas_call x1, Pallas kernels, attend(): pl.pallas_call(functools.partial(attend_kernel, plan, count), grid_spec=p...  14.3 us
  transfers between devices with their start and end apart: 45, of which 18 were waited for; matrix products, arithmetic and copies ran while one was open for 2% of the time, Pallas kernels for 22%

profile of v7, /device:TPU:0, one launch (start us, length us, event | category | flops | bytes accessed | tf_op | source)
XLA Modules:
  0.0 173.5 jit_solution(2845852293484335286)
XLA Ops:
  0.7 2.4 %pack.1 = (bf16[256,512]{1,0:T(8,128)(2,1)}, bf16[256,512]{1,0:T(8,128)(2,1)}, bf16[256,512]{1,0:T(8,128)(2,1)}, bf16[256,512]{1,0:T(8,128)(2,1)}, bf16[1,336,12...) custom-call(bf16[4,256,512]{2,1,0:T(8,128)(2,1)} %bitcast.41, bf16[16,1024]{1,0:T(8,128)(2,1)} %bitcast.43, ...), custom_call_target="tpu_custom_call" | custom-call | bytes 4194304 | tf_op jit(solution)/shard_map/pack/pallas_call | solution.py:745
  3.6 2.6 %collective-permute-start.4 = (bf16[256,512]{1,0:T(8,128)(2,1)}, bf16[256,512]{1,0:T(8,128)(2,1)S(1)}, u32[]{:S(2)}, u32[]{:S(2)}) collective-permute-start(bf16[256,512]{1,0:T(8,128)(2,1)} %get-tuple-element.169), channel_id=1, source_target_pairs={{0,2},{1,3},{2,0},{3,1},{4,6},{5,7},{6,4},{7,5},{8,10},{9,11},{10,... | collective-permute-start | bytes 786440 | tf_op jit(solution)/shard_map/ppermute | solution.py:874
  6.2 2.8 %collective-permute-start.1 = (bf16[1,336,128]{2,1,0:T(8,128)(2,1)}, bf16[1,336,128]{2,1,0:T(8,128)(2,1)S(1)}, u32[]{:S(2)}, u32[]{:S(2)}) collective-permute-start(bf16[1,336,128]{2,1,0:T(8,128)(2,1)} %get-tuple-element.172), channel_id=1, source_target_pairs={{0,16},{1,17},{2,18},{3,19},{4,20},{5,21},{6,22},{7,23},{8,24},{9,... | collective-permute-start | bytes 258056 | tf_op jit(solution)/shard_map/ppermute | solution.py:874
  9.0 1.6 collective-permute-start.2
  10.6 2.9 %collective-permute-done.4.refs_2_ = bf16[256,512]{1,0:T(8,128)(2,1)S(1)} collective-permute-done((bf16[256,512]{1,0:T(8,128)(2,1)}, bf16[256,512]{1,0:T(8,128)(2,1)S(1)}, u32[]{:S(2)}, u32[]{:S(2)}) %collective-permute-start.4) | collective-permute-done | bytes 262176 | tf_op jit(solution)/shard_map/ppermute | solution.py:874
  13.5 5.1 %collective-permute-done.5.refs_3_ = bf16[256,512]{1,0:T(8,128)(2,1)S(1)} collective-permute-done((bf16[256,512]{1,0:T(8,128)(2,1)}, bf16[256,512]{1,0:T(8,128)(2,1)S(1)}, u32[]{:S(2)}, u32[]{:S(2)}) %collective-permute-start.5) | collective-permute-done | bytes 262176 | tf_op jit(solution)/shard_map/ppermute | solution.py:874
  19.5 1.7 collective-permute-start.10
  21.2 1.6 collective-permute-start.6
  22.8 1.5 collective-permute-start.7
  24.8 2.5 %collective-permute-start.11 = (bf16[1,576,128]{2,1,0:T(8,128)(2,1)}, bf16[1,576,128]{2,1,0:T(8,128)(2,1)S(1)}, u32[]{:S(2)}, u32[]{:S(2)}) collective-permute-start(bf16[1,576,128]{2,1,0:T(8,128)(2,1)} %get-tuple-element.192), channel_id=1, source_target_pairs={{0,24},{1,25},{2,26},{3,27},{4,28},{5,29},{6,30},{7,31},{8,16},{9,... | collective-permute-start | bytes 442376 | tf_op jit(solution)/shard_map/ppermute | solution.py:874
  29.1 2.2 %cut_rows.1 = (bf16[256,512]{1,0:T(8,128)(2,1)}, bf16[256,512]{1,0:T(8,128)(2,1)}, bf16[256,512]{1,0:T(8,128)(2,1)}, bf16[256,512]{1,0:T(8,128)(2,1)}) custom-call(bf16[4,256,512]{2,1,0:T(8,128)(2,1)} %bitcast.42), custom_call_target="tpu_custom_call" | custom-call | bytes 4194304 | tf_op jit(solution)/shard_map/cut_rows/pallas_call | solution.py:847
  33.4 6.8 %collective-permute-done.9 = bf16[1,576,128]{2,1,0:T(8,128)(2,1)S(1)} collective-permute-done((bf16[1,576,128]{2,1,0:T(8,128)(2,1)}, bf16[1,576,128]{2,1,0:T(8,128)(2,1)S(1)}, u32[]{:S(2)}, u32[]{:S(2)}) %collective-permute-start.9) | collective-permute-done | bytes 147488 | tf_op jit(solution)/shard_map/ppermute | solution.py:874
  41.3 1.6 collective-permute-start.14
  42.9 1.5 collective-permute-start.15
  44.4 1.5 collective-permute-done.16.refs_1_
  46.0 11.1 %collective-permute-done.14.refs_5_ = bf16[4,576,128]{2,1,0:T(8,128)(2,1)S(1)} collective-permute-done((bf16[4,576,128]{2,1,0:T(8,128)(2,1)S(1)}, bf16[4,576,128]{2,1,0:T(8,128)(2,1)S(1)}, u32[]{:S(2)}, u32[]{:S(2)}) %collective-permute-start.14) | collective-permute-done | bytes 589856 | tf_op jit(solution)/shard_map/ppermute | solution.py:874
  58.3 1.5 collective-permute-start.17
  61.7 14.3 %attend.1 = (f32[1024,512]{1,0:T(8,128)}, bf16[1024,512]{1,0:T(8,128)(2,1)}, bf16[1024,512]{1,0:T(8,128)(2,1)}, bf16[1024,512]{1,0:T(8,128)(2,1)}, bf16[1024,512...) custom-call(s32[4]{0:T(128)S(1)} %pad_add_fusion.info_ref, ...), custom_call_target="tpu_custom_call" | custom-call | flops 5000000000 | bytes 14680064 | tf_op jit(solution)/shard_map/attend/pallas_call | solution.py:250
  76.9 1.6 collective-permute-done.22.refs_11_
  78.5 24.2 %feed.1 = (bf16[256,512]{1,0:T(8,128)(2,1)S(1)}, bf16[256,512]{1,0:T(8,128)(2,1)S(1)}, bf16[256,512]{1,0:T(8,128)(2,1)S(1)}, bf16[256,512]{1,0:T(8,128)(2,1)S(1)...) custom-call(s32[4]{0:T(128)} %copy-done.1, ...), custom_call_target="tpu_custom_call" | custom-call | flops 15000000512 | bytes 20971520 | tf_op jit(solution)/shard_map/feed/pallas_call | solution.py:482
  107.1 19.1 %attend_back.1 = (bf16[256,512]{1,0:T(8,128)(2,1)S(1)}, bf16[256,512]{1,0:T(8,128)(2,1)S(1)}, bf16[256,512]{1,0:T(8,128)(2,1)S(1)}, bf16[256,512]{1,0:T(8,128)(2...) custom-call(s32[4]{0:T(128)S(1)} %copy-done.2, f32[1024,512]{1,0:T(8,128)} %get-tuple-element.202.lifted_ref, ...), custom_call_target="tpu_custom_call" | custom-call | flops 14000000000 | bytes 25165824 | tf_op jit(solution)/shard_map/attend_back/pallas_call | solution.py:676
  127.4 1.5 collective-permute-start.34
  128.9 1.5 collective-permute-start.35
  131.7 2.9 %settle_rows.1 = bf16[4,256,512]{2,1,0:T(8,128)(2,1)} custom-call(s32[4]{0:T(128)} %copy-done.1, bf16[256,512]{1,0:T(8,128)(2,1)} %copy-done, bf16[256,512]{1,0:T(8,128)(2,1)} %collective-permute-done.27.refs_1_, bf16[256,512]{1,0:T(8,128)(2,1)} %copy-done.8, bf16[256,512]{1,0:T(8,128)(2,1)} %copy-done.9), custom_call_target="tpu_custom_call" | custom-call | bytes 50331648 | tf_op jit(solution)/shard_map/settle_rows/pallas_call | solution.py:825
  135.6 2.9 %collective-permute-done.34 = bf16[1536,128]{1,0:T(8,128)(2,1)S(1)} collective-permute-done((bf16[1536,128]{1,0:T(8,128)(2,1)S(1)}, bf16[1536,128]{1,0:T(8,128)(2,1)S(1)}, u32[]{:S(2)}, u32[]{:S(2)}) %collective-permute-start.34) | collective-permute-done | bytes 393248 | tf_op jit(solution)/shard_map/ppermute | solution.py:874
  139.6 2.7 %collective-permute-start.38 = (bf16[576,128]{1,0:T(8,128)(2,1)S(1)}, bf16[576,128]{1,0:T(8,128)(2,1)S(1)}, u32[]{:S(2)}, u32[]{:S(2)}) collective-permute-start(bf16[576,128]{1,0:T(8,128)(2,1)S(1)} %pad_maximum_fusion.3), channel_id=1, source_target_pairs={{0,24},{1,25},{2,26},{3,27},{4,28},{5,29},{6,30},{7,31},{8,16},{9,... | collective-permute-start | bytes 442376 | tf_op jit(solution)/shard_map/ppermute | solution.py:874
  147.2 3.8 %collective-permute-done.37.refs_6_ = bf16[576,128]{1,0:T(8,128)(2,1)S(1)} collective-permute-done((bf16[576,128]{1,0:T(8,128)(2,1)S(1)}, bf16[576,128]{1,0:T(8,128)(2,1)S(1)}, u32[]{:S(2)}, u32[]{:S(2)}) %collective-permute-start.37) | collective-permute-done | bytes 147488 | tf_op jit(solution)/shard_map/ppermute | solution.py:874
  151.0 7.3 %collective-permute-done.36.refs_5_ = bf16[576,128]{1,0:T(8,128)(2,1)S(1)} collective-permute-done((bf16[576,128]{1,0:T(8,128)(2,1)S(1)}, bf16[576,128]{1,0:T(8,128)(2,1)S(1)}, u32[]{:S(2)}, u32[]{:S(2)}) %collective-permute-start.36) | collective-permute-done | bytes 147488 | tf_op jit(solution)/shard_map/ppermute | solution.py:874
  160.9 2.4 %collective-permute-start.41 = (bf16[1,336,128]{2,1,0:T(8,128)(2,1)S(1)}, bf16[1,336,128]{2,1,0:T(8,128)(2,1)S(1)}, u32[]{:S(2)}, u32[]{:S(2)}) collective-permute-start(bf16[1,336,128]{2,1,0:T(8,128)(2,1)S(1)} %get-tuple-element.337), channel_id=1, source_target_pairs={{0,8},{1,9},{2,10},{3,11},{4,12},{5,13},{6,14},{7,15},{8,0},{9,1},... | collective-permute-start | bytes 258056 | tf_op jit(solution)/shard_map/ppermute | solution.py:874
  163.3 2.0 %collective-permute-start.42 = (bf16[1,336,128]{2,1,0:T(8,128)(2,1)S(1)}, bf16[1,336,128]{2,1,0:T(8,128)(2,1)S(1)}, u32[]{:S(2)}, u32[]{:S(2)}) collective-permute-start(bf16[1,336,128]{2,1,0:T(8,128)(2,1)S(1)} %get-tuple-element.336), channel_id=1, source_target_pairs={{0,24},{1,25},{2,26},{3,27},{4,28},{5,29},{6,30},{7,31},{8,16},{9,... | collective-permute-start | bytes 258056 | tf_op jit(solution)/shard_map/ppermute | solution.py:874
  165.3 3.0 %collective-permute-done.40.refs_1_ = bf16[1,336,128]{2,1,0:T(8,128)(2,1)S(1)} collective-permute-done((bf16[1,336,128]{2,1,0:T(8,128)(2,1)S(1)}, bf16[1,336,128]{2,1,0:T(8,128)(2,1)S(1)}, u32[]{:S(2)}, u32[]{:S(2)}) %collective-permute-start.40) | collective-permute-done | bytes 86048 | tf_op jit(solution)/shard_map/ppermute | solution.py:874
  168.5 2.1 %collective-permute-done.42.refs_3_ = bf16[1,336,128]{2,1,0:T(8,128)(2,1)S(1)} collective-permute-done((bf16[1,336,128]{2,1,0:T(8,128)(2,1)S(1)}, bf16[1,336,128]{2,1,0:T(8,128)(2,1)S(1)}, u32[]{:S(2)}, u32[]{:S(2)}) %collective-permute-start.42) | collective-permute-done | bytes 86048 | tf_op jit(solution)/shard_map/ppermute | solution.py:874
  (123 shorter events, 29.9 us)
Async XLA Ops:
  3.6 9.9 %collective-permute-start.4 = (bf16[256,512]{1,0:T(8,128)(2,1)}, bf16[256,512]{1,0:T(8,128)(2,1)S(1)}, u32[]{:S(2)}, u32[]{:S(2)}) collective-permute-start(bf16[256,512]{1,0:T(8,128)(2,1)} %get-tuple-element.169), channel_id=1, source_target_pairs={{0,2},{1,3},{2,0},{3,1},{4,6},{5,7},{6,4},{7,5},{8,10},{9,11},{10,... | collective-permute-start | bytes 786440 | tf_op jit(solution)/shard_map/ppermute | solution.py:874
  6.1 12.5 %collective-permute-start.5 = (bf16[256,512]{1,0:T(8,128)(2,1)}, bf16[256,512]{1,0:T(8,128)(2,1)S(1)}, u32[]{:S(2)}, u32[]{:S(2)}) collective-permute-start(bf16[256,512]{1,0:T(8,128)(2,1)} %get-tuple-element.170), channel_id=1, source_target_pairs={{0,3},{1,2},{2,1},{3,0},{4,7},{5,6},{6,5},{7,4},{8,11},{9,10},{10,... | collective-permute-start | bytes 786440 | tf_op jit(solution)/shard_map/ppermute | solution.py:874
  6.2 12.4 %collective-permute-start.1 = (bf16[1,336,128]{2,1,0:T(8,128)(2,1)}, bf16[1,336,128]{2,1,0:T(8,128)(2,1)S(1)}, u32[]{:S(2)}, u32[]{:S(2)}) collective-permute-start(bf16[1,336,128]{2,1,0:T(8,128)(2,1)} %get-tuple-element.172), channel_id=1, source_target_pairs={{0,16},{1,17},{2,18},{3,19},{4,20},{5,21},{6,22},{7,23},{8,24},{9,... | collective-permute-start | bytes 258056 | tf_op jit(solution)/shard_map/ppermute | solution.py:874
  9.0 9.6 %collective-permute-start.2 = (bf16[1,336,128]{2,1,0:T(8,128)(2,1)}, bf16[1,336,128]{2,1,0:T(8,128)(2,1)S(1)}, u32[]{:S(2)}, u32[]{:S(2)}) collective-permute-start(bf16[1,336,128]{2,1,0:T(8,128)(2,1)} %get-tuple-element.172), channel_id=1, source_target_pairs={{0,8},{1,9},{2,10},{3,11},{4,12},{5,13},{6,14},{7,15},{8,0},{9,1},... | collective-permute-start | bytes 258056 | tf_op jit(solution)/shard_map/ppermute | solution.py:874
  10.6 8.0 %collective-permute-start.3 = (bf16[1,336,128]{2,1,0:T(8,128)(2,1)}, bf16[1,336,128]{2,1,0:T(8,128)(2,1)S(1)}, u32[]{:S(2)}, u32[]{:S(2)}) collective-permute-start(bf16[1,336,128]{2,1,0:T(8,128)(2,1)} %get-tuple-element.172), channel_id=1, source_target_pairs={{0,24},{1,25},{2,26},{3,27},{4,28},{5,29},{6,30},{7,31},{8,16},{9,... | collective-permute-start | bytes 258056 | tf_op jit(solution)/shard_map/ppermute | solution.py:874
  19.5 7.7 %collective-permute-start.10 = (bf16[1,576,128]{2,1,0:T(8,128)(2,1)}, bf16[1,576,128]{2,1,0:T(8,128)(2,1)S(1)}, u32[]{:S(2)}, u32[]{:S(2)}) collective-permute-start(bf16[1,576,128]{2,1,0:T(8,128)(2,1)} %get-tuple-element.192), channel_id=1, source_target_pairs={{0,8},{1,9},{2,10},{3,11},{4,12},{5,13},{6,14},{7,15},{8,0},{9,1},... | collective-permute-start | bytes 442376 | tf_op jit(solution)/shard_map/ppermute | solution.py:874
  21.2 19.0 %collective-permute-start.6 = (bf16[4,336,128]{2,1,0:T(8,128)(2,1)S(1)}, bf16[4,336,128]{2,1,0:T(8,128)(2,1)S(1)}, u32[]{:S(2)}, u32[]{:S(2)}) collective-permute-start(bf16[4,336,128]{2,1,0:T(8,128)(2,1)S(1)} %constant_dynamic-update-slice_fusion), channel_id=1, source_target_pairs={{0,2},{1,3},{2,0},{3,1},{4,6},{5,7},{6,4},{7,5},{8,10},{9,11},{10,... | collective-permute-start | bytes 1032200 | tf_op jit(solution)/shard_map/ppermute | solution.py:874
  22.8 17.4 %collective-permute-start.7 = (bf16[4,336,128]{2,1,0:T(8,128)(2,1)S(1)}, bf16[4,336,128]{2,1,0:T(8,128)(2,1)S(1)}, u32[]{:S(2)}, u32[]{:S(2)}) collective-permute-start(bf16[4,336,128]{2,1,0:T(8,128)(2,1)S(1)} %constant_dynamic-update-slice_fusion), channel_id=1, source_target_pairs={{0,4},{1,5},{2,6},{3,7},{4,0},{5,1},{6,2},{7,3},{8,12},{9,13},{10,... | collective-permute-start | bytes 1032200 | tf_op jit(solution)/shard_map/ppermute | solution.py:874
  24.3 15.9 %collective-permute-start.8 = (bf16[4,336,128]{2,1,0:T(8,128)(2,1)S(1)}, bf16[4,336,128]{2,1,0:T(8,128)(2,1)S(1)}, u32[]{:S(2)}, u32[]{:S(2)}) collective-permute-start(bf16[4,336,128]{2,1,0:T(8,128)(2,1)S(1)} %constant_dynamic-update-slice_fusion), channel_id=1, source_target_pairs={{0,6},{1,7},{2,4},{3,5},{4,2},{5,3},{6,0},{7,1},{8,14},{9,15},{10,... | collective-permute-start | bytes 1032200 | tf_op jit(solution)/shard_map/ppermute | solution.py:874
  24.8 8.6 %collective-permute-start.11 = (bf16[1,576,128]{2,1,0:T(8,128)(2,1)}, bf16[1,576,128]{2,1,0:T(8,128)(2,1)S(1)}, u32[]{:S(2)}, u32[]{:S(2)}) collective-permute-start(bf16[1,576,128]{2,1,0:T(8,128)(2,1)} %get-tuple-element.192), channel_id=1, source_target_pairs={{0,24},{1,25},{2,26},{3,27},{4,28},{5,29},{6,30},{7,31},{8,16},{9,... | collective-permute-start | bytes 442376 | tf_op jit(solution)/shard_map/ppermute | solution.py:874
  27.3 13.0 %collective-permute-start.9 = (bf16[1,576,128]{2,1,0:T(8,128)(2,1)}, bf16[1,576,128]{2,1,0:T(8,128)(2,1)S(1)}, u32[]{:S(2)}, u32[]{:S(2)}) collective-permute-start(bf16[1,576,128]{2,1,0:T(8,128)(2,1)} %get-tuple-element.192), channel_id=1, source_target_pairs={{0,16},{1,17},{2,18},{3,19},{4,20},{5,21},{6,22},{7,23},{8,24},{9,... | collective-permute-start | bytes 442376 | tf_op jit(solution)/shard_map/ppermute | solution.py:874
  40.5 17.8 %collective-permute-start.12 = (bf16[16,336,128]{2,1,0:T(8,128)(2,1)S(1)}, bf16[16,336,128]{2,1,0:T(8,128)(2,1)S(1)}, u32[]{:S(2)}, u32[]{:S(2)}) collective-permute-start(bf16[16,336,128]{2,1,0:T(8,128)(2,1)S(1)} %constant_dynamic-update-slice_fusion.4.refs_4_), channel_id=1, source_target_pairs={{0,1},{1,0},{2,3},{3,2},{4,5},{5,4},{6,7},{7,6},{8,9},{9,8},{10,11... | collective-permute-start | bytes 4128776 | tf_op jit(solution)/shard_map/ppermute | solution.py:874
  41.3 15.7 %collective-permute-start.14 = (bf16[4,576,128]{2,1,0:T(8,128)(2,1)S(1)}, bf16[4,576,128]{2,1,0:T(8,128)(2,1)S(1)}, u32[]{:S(2)}, u32[]{:S(2)}) collective-permute-start(bf16[4,576,128]{2,1,0:T(8,128)(2,1)S(1)} %constant_dynamic-update-slice_fusion.8.refs_4_), channel_id=1, source_target_pairs={{0,2},{1,3},{2,0},{3,1},{4,6},{5,7},{6,4},{7,5},{8,10},{9,11},{10,... | collective-permute-start | bytes 1769480 | tf_op jit(solution)/shard_map/ppermute | solution.py:874
  42.9 15.4 %collective-permute-start.15 = (bf16[4,576,128]{2,1,0:T(8,128)(2,1)S(1)}, bf16[4,576,128]{2,1,0:T(8,128)(2,1)S(1)}, u32[]{:S(2)}, u32[]{:S(2)}) collective-permute-start(bf16[4,576,128]{2,1,0:T(8,128)(2,1)S(1)} %constant_dynamic-update-slice_fusion.8.refs_4_), channel_id=1, source_target_pairs={{0,4},{1,5},{2,6},{3,7},{4,0},{5,1},{6,2},{7,3},{8,12},{9,13},{10,... | collective-permute-start | bytes 1769480 | tf_op jit(solution)/shard_map/ppermute | solution.py:874
  58.3 17.7 %collective-permute-start.17 = (bf16[4,576,128]{2,1,0:T(8,128)(2,1)S(1)}, bf16[4,576,128]{2,1,0:T(8,128)(2,1)S(1)}, u32[]{:S(2)}, u32[]{:S(2)}) collective-permute-start(bf16[4,576,128]{2,1,0:T(8,128)(2,1)S(1)} %collective-permute-done.14.refs_5_), channel_id=1, source_target_pairs={{0,4},{1,5},{2,6},{3,7},{4,0},{5,1},{6,2},{7,3},{8,12},{9,13},{10,... | collective-permute-start | bytes 1769480 | tf_op jit(solution)/shard_map/ppermute | solution.py:874
  59.8 16.2 %collective-permute-start.18 = (bf16[4,576,128]{2,1,0:T(8,128)(2,1)S(1)}, bf16[4,576,128]{2,1,0:T(8,128)(2,1)S(1)}, u32[]{:S(2)}, u32[]{:S(2)}) collective-permute-start(bf16[4,576,128]{2,1,0:T(8,128)(2,1)S(1)} %collective-permute-done.14.refs_5_), channel_id=1, source_target_pairs={{0,1},{1,0},{2,3},{3,2},{4,5},{5,4},{6,7},{7,6},{8,9},{9,8},{10,11... | collective-permute-start | bytes 1769480 | tf_op jit(solution)/shard_map/ppermute | solution.py:874
  59.8 16.2 %collective-permute-start.19 = (bf16[4,576,128]{2,1,0:T(8,128)(2,1)S(1)}, bf16[4,576,128]{2,1,0:T(8,128)(2,1)S(1)}, u32[]{:S(2)}, u32[]{:S(2)}) collective-permute-start(bf16[4,576,128]{2,1,0:T(8,128)(2,1)S(1)} %collective-permute-done.15.refs_6_), channel_id=1, source_target_pairs={{0,1},{1,0},{2,3},{3,2},{4,5},{5,4},{6,7},{7,6},{8,9},{9,8},{10,11... | collective-permute-start | bytes 1769480 | tf_op jit(solution)/shard_map/ppermute | solution.py:874
  60.3 15.7 %collective-permute-start.20 = (bf16[256,512]{1,0:T(8,128)(2,1)S(1)}, bf16[256,512]{1,0:T(8,128)(2,1)S(1)}, u32[]{:S(2)}, u32[]{:S(2)}) collective-permute-start(bf16[256,512]{1,0:T(8,128)(2,1)S(1)} %copy-done.12), channel_id=1, source_target_pairs={{0,2},{1,3},{2,0},{3,1},{4,6},{5,7},{6,4},{7,5},{8,10},{9,11},{10,... | collective-permute-start | bytes 786440 | tf_op jit(solution)/shard_map/ppermute | solution.py:874
  60.9 15.1 %collective-permute-start.21 = (bf16[256,512]{1,0:T(8,128)(2,1)S(1)}, bf16[256,512]{1,0:T(8,128)(2,1)S(1)}, u32[]{:S(2)}, u32[]{:S(2)}) collective-permute-start(bf16[256,512]{1,0:T(8,128)(2,1)S(1)} %copy-done.11), channel_id=1, source_target_pairs={{0,3},{1,2},{2,1},{3,0},{4,7},{5,6},{6,5},{7,4},{8,11},{9,10},{10,... | collective-permute-start | bytes 786440 | tf_op jit(solution)/shard_map/ppermute | solution.py:874
  103.1 23.1 %collective-permute-start.26 = (bf16[4608,128]{1,0:T(8,128)(2,1)S(1)}, bf16[4608,128]{1,0:T(8,128)(2,1)S(1)}, u32[]{:S(2)}, u32[]{:S(2)}) collective-permute-start(bf16[4608,128]{1,0:T(8,128)(2,1)S(1)} %get-tuple-element.227), channel_id=1, source_target_pairs={{0,1},{1,0},{2,3},{3,2},{4,5},{5,4},{6,7},{7,6},{8,9},{9,8},{10,11... | collective-permute-start | bytes 3538952 | tf_op jit(solution)/shard_map/ppermute | solution.py:874
  103.6 22.5 %collective-permute-start.28 = (bf16[256,512]{1,0:T(8,128)(2,1)S(1)}, bf16[256,512]{1,0:T(8,128)(2,1)S(1)}, u32[]{:S(2)}, u32[]{:S(2)}) collective-permute-start(bf16[256,512]{1,0:T(8,128)(2,1)S(1)} %get-tuple-element.230), channel_id=1, source_target_pairs={{0,2},{1,3},{2,0},{3,1},{4,6},{5,7},{6,4},{7,5},{8,10},{9,11},{10,... | collective-permute-start | bytes 786440 | tf_op jit(solution)/shard_map/ppermute | solution.py:874
  104.2 22.0 %collective-permute-start.29 = (bf16[256,512]{1,0:T(8,128)(2,1)S(1)}, bf16[256,512]{1,0:T(8,128)(2,1)S(1)}, u32[]{:S(2)}, u32[]{:S(2)}) collective-permute-start(bf16[256,512]{1,0:T(8,128)(2,1)S(1)} %get-tuple-element.231), channel_id=1, source_target_pairs={{0,3},{1,2},{2,1},{3,0},{4,7},{5,6},{6,5},{7,4},{8,11},{9,10},{10,... | collective-permute-start | bytes 786440 | tf_op jit(solution)/shard_map/ppermute | solution.py:874
  105.9 20.3 %collective-permute-start.24 = (bf16[3072,128]{1,0:T(8,128)(2,1)S(1)}, bf16[3072,128]{1,0:T(8,128)(2,1)S(1)}, u32[]{:S(2)}, u32[]{:S(2)}) collective-permute-start(bf16[3072,128]{1,0:T(8,128)(2,1)S(1)} %add_convert_fusion), channel_id=1, source_target_pairs={{0,4},{1,5},{2,6},{3,7},{4,0},{5,1},{6,2},{7,3},{8,12},{9,13},{10,... | collective-permute-start | bytes 2359304 | tf_op jit(solution)/shard_map/ppermute | solution.py:874
  106.5 19.7 %collective-permute-start.25 = (bf16[1536,128]{1,0:T(8,128)(2,1)S(1)}, bf16[1536,128]{1,0:T(8,128)(2,1)S(1)}, u32[]{:S(2)}, u32[]{:S(2)}) collective-permute-start(bf16[1536,128]{1,0:T(8,128)(2,1)S(1)} %add_convert_fusion.3), channel_id=1, source_target_pairs={{0,2},{1,3},{2,0},{3,1},{4,6},{5,7},{6,4},{7,5},{8,10},{9,11},{10,... | collective-permute-start | bytes 1179656 | tf_op jit(solution)/shard_map/ppermute | solution.py:874
  127.4 11.1 %collective-permute-start.34 = (bf16[1536,128]{1,0:T(8,128)(2,1)S(1)}, bf16[1536,128]{1,0:T(8,128)(2,1)S(1)}, u32[]{:S(2)}, u32[]{:S(2)}) collective-permute-start(bf16[1536,128]{1,0:T(8,128)(2,1)S(1)} %get-tuple-element.265), channel_id=1, source_target_pairs={{0,2},{1,3},{2,0},{3,1},{4,6},{5,7},{6,4},{7,5},{8,10},{9,11},{10,... | collective-permute-start | bytes 1179656 | tf_op jit(solution)/shard_map/ppermute | solution.py:874
  139.6 7.6 %collective-permute-start.38 = (bf16[576,128]{1,0:T(8,128)(2,1)S(1)}, bf16[576,128]{1,0:T(8,128)(2,1)S(1)}, u32[]{:S(2)}, u32[]{:S(2)}) collective-permute-start(bf16[576,128]{1,0:T(8,128)(2,1)S(1)} %pad_maximum_fusion.3), channel_id=1, source_target_pairs={{0,24},{1,25},{2,26},{3,27},{4,28},{5,29},{6,30},{7,31},{8,16},{9,... | collective-permute-start | bytes 442376 | tf_op jit(solution)/shard_map/ppermute | solution.py:874
  142.3 16.1 %collective-permute-start.31 = (bf16[4,336,128]{2,1,0:T(8,128)(2,1)S(1)}, bf16[4,336,128]{2,1,0:T(8,128)(2,1)S(1)}, u32[]{:S(2)}, u32[]{:S(2)}) collective-permute-start(bf16[4,336,128]{2,1,0:T(8,128)(2,1)S(1)} %copy-done.7), channel_id=1, source_target_pairs={{0,2},{1,3},{2,0},{3,1},{4,6},{5,7},{6,4},{7,5},{8,10},{9,11},{10,... | collective-permute-start | bytes 1032200 | tf_op jit(solution)/shard_map/ppermute | solution.py:874
  143.8 16.0 %collective-permute-start.32 = (bf16[4,336,128]{2,1,0:T(8,128)(2,1)S(1)}, bf16[4,336,128]{2,1,0:T(8,128)(2,1)S(1)}, u32[]{:S(2)}, u32[]{:S(2)}) collective-permute-start(bf16[4,336,128]{2,1,0:T(8,128)(2,1)S(1)} %copy-done.6), channel_id=1, source_target_pairs={{0,4},{1,5},{2,6},{3,7},{4,0},{5,1},{6,2},{7,3},{8,12},{9,13},{10,... | collective-permute-start | bytes 1032200 | tf_op jit(solution)/shard_map/ppermute | solution.py:874
  145.1 14.6 %collective-permute-start.33 = (bf16[4,336,128]{2,1,0:T(8,128)(2,1)S(1)}, bf16[4,336,128]{2,1,0:T(8,128)(2,1)S(1)}, u32[]{:S(2)}, u32[]{:S(2)}) collective-permute-start(bf16[4,336,128]{2,1,0:T(8,128)(2,1)S(1)} %get-tuple-element.263), channel_id=1, source_target_pairs={{0,6},{1,7},{2,4},{3,5},{4,2},{5,3},{6,0},{7,1},{8,14},{9,15},{10,... | collective-permute-start | bytes 1032200 | tf_op jit(solution)/shard_map/ppermute | solution.py:874
  147.2 11.2 %collective-permute-start.39 = (bf16[256,512]{1,0:T(8,128)(2,1)S(1)}, bf16[256,512]{1,0:T(8,128)(2,1)S(1)}, u32[]{:S(2)}, u32[]{:S(2)}) collective-permute-start(bf16[256,512]{1,0:T(8,128)(2,1)S(1)} %get-tuple-element.276), channel_id=1, source_target_pairs={{0,1},{1,0},{2,3},{3,2},{4,5},{5,4},{6,7},{7,6},{8,9},{9,8},{10,11... | collective-permute-start | bytes 786440 | tf_op jit(solution)/shard_map/ppermute | solution.py:874
  159.8 10.9 %collective-permute-start.43 = (bf16[256,512]{1,0:T(8,128)(2,1)S(1)}, bf16[256,512]{1,0:T(8,128)(2,1)S(1)}, u32[]{:S(2)}, u32[]{:S(2)}) collective-permute-start(bf16[256,512]{1,0:T(8,128)(2,1)S(1)} %get-tuple-element.286), channel_id=1, source_target_pairs={{0,2},{1,3},{2,0},{3,1},{4,6},{5,7},{6,4},{7,5},{8,10},{9,11},{10,... | collective-permute-start | bytes 786440 | tf_op jit(solution)/shard_map/ppermute | solution.py:874
  160.7 10.0 %collective-permute-start.44 = (bf16[256,512]{1,0:T(8,128)(2,1)S(1)}, bf16[256,512]{1,0:T(8,128)(2,1)S(1)}, u32[]{:S(2)}, u32[]{:S(2)}) collective-permute-start(bf16[256,512]{1,0:T(8,128)(2,1)S(1)} %get-tuple-element.287), channel_id=1, source_target_pairs={{0,3},{1,2},{2,1},{3,0},{4,7},{5,6},{6,5},{7,4},{8,11},{9,10},{10,... | collective-permute-start | bytes 786440 | tf_op jit(solution)/shard_map/ppermute | solution.py:874
  (28 other events, 250.3 us)

commit v8 on v7

--- a/solution.py
+++ b/solution.py
@@ -716,10 +716,14 @@
 def pack_kernel(plan, count, share, rows_ref, table_ref, inward_ref, *refs):
     vectors, refs = refs[:VECTORS], refs[VECTORS:]
     outward_ref, expand_ref, contract_ref = refs[:3]
-    pieces, early_ref, late_ref = refs[3 : 3 + count], refs[3 + count], refs[4 + count]
+    pieces, early_ref, late_ref, copied = refs[3 : 3 + count], refs[3 + count], refs[4 + count], refs[5 + count]
     rank = lax.axis_index("seq")
-    for mask in range(count):
-        pieces[mask][...] = rows_ref[pl.ds((rank ^ mask) // share, 1), :, :][0]
+    copies = [
+        pltpu.make_async_copy(rows_ref.at[(rank ^ mask) // share], pieces[mask], copied.at[mask])
+        for mask in range(count)
+    ]
+    for copy in copies:
+        copy.start()
     at = 0
     for ref in (table_ref, inward_ref):
         for lane in range(ref.shape[1] // LANE):
@@ -736,15 +740,20 @@
         for lane in range(ref.shape[1] // LANE):
             late_ref[0, at : at + rows, :] = ref[:, lane * LANE : (lane + 1) * LANE]
             at += rows
+    for copy in copies:
+        copy.wait()
 
 
 def pack(plan, count, share, rows, table, inward, vectors, outward, expand, contract):
     vectors = [v.reshape(1, -1) for v in vectors]
-    outs = [like(rows.shape[1:], BF)] * count
-    outs += [like((1, plan.early_rows, LANE), BF), like((1, plan.late_rows, LANE), BF)]
+    outs = [pltpu.VMEM(rows.shape[1:], BF)] * count
+    outs += [pltpu.VMEM((1, plan.early_rows, LANE), BF), pltpu.VMEM((1, plan.late_rows, LANE), BF)]
     values = pl.pallas_call(
         functools.partial(pack_kernel, plan, count, share),
         out_shape=outs,
+        in_specs=[pl.BlockSpec(memory_space=pl.ANY)] + [HELD] * (5 + len(vectors)),
+        out_specs=[HELD] * len(outs),
+        scratch_shapes=[pltpu.SemaphoreType.DMA((count,))],
         cost_estimate=cost(0, 4 * 2**20),
         name="pack",
     )(rows, table, inward, *vectors, outward, expand, contract)

time: 174 us -> 172 us (0.989)
  transfers between devices with their start and end apart: 45 -> 45, of which waited for: 18 -> 17; matrix products, arithmetic and copies ran while one was open for 2% -> 2% of each run, Pallas kernels for 22% -> 22%
where the time goes in v8:
time: 172 us
  Pallas kernels  66.5 us (39%)
  waiting for transfers between devices  54.4 us (32%)
  starting transfers between devices  42.7 us (25%)
  other arithmetic  5.8 us (3%)
    ppermute x45, waiting for transfers between devices, swap(): lax.ppermute(value, AXES, [(d, d ^ mask) for d in range(devices)])  54.4 us
    ppermute x45, starting transfers between devices, swap(): lax.ppermute(value, AXES, [(d, d ^ mask) for d in range(devices)])  42.7 us
    pallas_call x1, Pallas kernels, feed(): pl.pallas_call(functools.partial(feed_kernel, plan, count), grid_spec=plt...  24.2 us
    pallas_call x1, Pallas kernels, attend_back(): pl.pallas_call(functools.partial(attend_back_kernel, plan, count), grid_s...  19.1 us
    pallas_call x1, Pallas kernels, attend(): pl.pallas_call(functools.partial(attend_kernel, plan, count), grid_spec=p...  14.3 us
  transfers between devices with their start and end apart: 45, of which 17 were waited for; matrix products, arithmetic and copies ran while one was open for 2% of the time, Pallas kernels for 22%

profile of v8, /device:TPU:0, one launch (start us, length us, event | category | flops | bytes accessed | tf_op | source)
XLA Modules:
  0.0 171.6 jit_solution(12930502696763200809)
XLA Ops:
  0.7 2.3 %pack.1 = (bf16[256,512]{1,0:T(8,128)(2,1)S(1)}, bf16[256,512]{1,0:T(8,128)(2,1)S(1)}, bf16[256,512]{1,0:T(8,128)(2,1)S(1)}, bf16[256,512]{1,0:T(8,128)(2,1)S(1)...) custom-call(bf16[4,256,512]{2,1,0:T(8,128)(2,1)} %bitcast.41, bf16[16,1024]{1,0:T(8,128)(2,1)} %bitcast.43, ...), custom_call_target="tpu_custom_call" | custom-call | bytes 4194304 | tf_op jit(solution)/shard_map/pack/pallas_call | solution.py:751
  3.5 2.6 %collective-permute-start.4 = (bf16[256,512]{1,0:T(8,128)(2,1)S(1)}, bf16[256,512]{1,0:T(8,128)(2,1)S(1)}, u32[]{:S(2)}, u32[]{:S(2)}) collective-permute-start(bf16[256,512]{1,0:T(8,128)(2,1)S(1)} %get-tuple-element.169), channel_id=1, source_target_pairs={{0,2},{1,3},{2,0},{3,1},{4,6},{5,7},{6,4},{7,5},{8,10},{9,11},{10,... | collective-permute-start | bytes 786440 | tf_op jit(solution)/shard_map/ppermute | solution.py:883
  6.1 2.8 %collective-permute-start.1 = (bf16[1,336,128]{2,1,0:T(8,128)(2,1)S(1)}, bf16[1,336,128]{2,1,0:T(8,128)(2,1)S(1)}, u32[]{:S(2)}, u32[]{:S(2)}) collective-permute-start(bf16[1,336,128]{2,1,0:T(8,128)(2,1)S(1)} %get-tuple-element.172), channel_id=1, source_target_pairs={{0,16},{1,17},{2,18},{3,19},{4,20},{5,21},{6,22},{7,23},{8,24},{9,... | collective-permute-start | bytes 258056 | tf_op jit(solution)/shard_map/ppermute | solution.py:883
  9.0 1.6 collective-permute-start.2
  10.5 2.7 %collective-permute-done.4.refs_2_ = bf16[256,512]{1,0:T(8,128)(2,1)S(1)} collective-permute-done((bf16[256,512]{1,0:T(8,128)(2,1)S(1)}, bf16[256,512]{1,0:T(8,128)(2,1)S(1)}, u32[]{:S(2)}, u32[]{:S(2)}) %collective-permute-start.4) | collective-permute-done | bytes 262176 | tf_op jit(solution)/shard_map/ppermute | solution.py:883
  13.2 5.1 %collective-permute-done.5.refs_3_ = bf16[256,512]{1,0:T(8,128)(2,1)S(1)} collective-permute-done((bf16[256,512]{1,0:T(8,128)(2,1)S(1)}, bf16[256,512]{1,0:T(8,128)(2,1)S(1)}, u32[]{:S(2)}, u32[]{:S(2)}) %collective-permute-start.5) | collective-permute-done | bytes 262176 | tf_op jit(solution)/shard_map/ppermute | solution.py:883
  18.3 1.7 %collective-permute-start.10 = (bf16[1,576,128]{2,1,0:T(8,128)(2,1)S(1)}, bf16[1,576,128]{2,1,0:T(8,128)(2,1)S(1)}, u32[]{:S(2)}, u32[]{:S(2)}) collective-permute-start(bf16[1,576,128]{2,1,0:T(8,128)(2,1)S(1)} %get-tuple-element.192), channel_id=1, source_target_pairs={{0,8},{1,9},{2,10},{3,11},{4,12},{5,13},{6,14},{7,15},{8,0},{9,1},... | collective-permute-start | bytes 442376 | tf_op jit(solution)/shard_map/ppermute | solution.py:883
  20.1 1.6 collective-permute-start.6
  21.7 1.5 collective-permute-start.7
  23.7 2.5 %collective-permute-start.11 = (bf16[1,576,128]{2,1,0:T(8,128)(2,1)S(1)}, bf16[1,576,128]{2,1,0:T(8,128)(2,1)S(1)}, u32[]{:S(2)}, u32[]{:S(2)}) collective-permute-start(bf16[1,576,128]{2,1,0:T(8,128)(2,1)S(1)} %get-tuple-element.192), channel_id=1, source_target_pairs={{0,24},{1,25},{2,26},{3,27},{4,28},{5,29},{6,30},{7,31},{8,16},{9,... | collective-permute-start | bytes 442376 | tf_op jit(solution)/shard_map/ppermute | solution.py:883
  27.7 2.2 %cut_rows.1 = (bf16[256,512]{1,0:T(8,128)(2,1)}, bf16[256,512]{1,0:T(8,128)(2,1)}, bf16[256,512]{1,0:T(8,128)(2,1)}, bf16[256,512]{1,0:T(8,128)(2,1)}) custom-call(bf16[4,256,512]{2,1,0:T(8,128)(2,1)} %bitcast.42), custom_call_target="tpu_custom_call" | custom-call | bytes 4194304 | tf_op jit(solution)/shard_map/cut_rows/pallas_call | solution.py:856
  32.1 6.8 %collective-permute-done.9 = bf16[1,576,128]{2,1,0:T(8,128)(2,1)S(1)} collective-permute-done((bf16[1,576,128]{2,1,0:T(8,128)(2,1)S(1)}, bf16[1,576,128]{2,1,0:T(8,128)(2,1)S(1)}, u32[]{:S(2)}, u32[]{:S(2)}) %collective-permute-start.9) | collective-permute-done | bytes 147488 | tf_op jit(solution)/shard_map/ppermute | solution.py:883
  41.4 1.5 collective-permute-start.15
  42.9 1.5 collective-permute-done.16.refs_1_
  44.5 10.8 %collective-permute-done.14.refs_5_ = bf16[4,576,128]{2,1,0:T(8,128)(2,1)S(1)} collective-permute-done((bf16[4,576,128]{2,1,0:T(8,128)(2,1)S(1)}, bf16[4,576,128]{2,1,0:T(8,128)(2,1)S(1)}, u32[]{:S(2)}, u32[]{:S(2)}) %collective-permute-start.14) | collective-permute-done | bytes 589856 | tf_op jit(solution)/shard_map/ppermute | solution.py:883
  56.4 1.5 collective-permute-start.17
  59.8 14.3 %attend.1 = (f32[1024,512]{1,0:T(8,128)}, bf16[1024,512]{1,0:T(8,128)(2,1)}, bf16[1024,512]{1,0:T(8,128)(2,1)}, bf16[1024,512]{1,0:T(8,128)(2,1)}, bf16[1024,512...) custom-call(s32[4]{0:T(128)S(1)} %pad_add_fusion.info_ref, ...), custom_call_target="tpu_custom_call" | custom-call | flops 5000000000 | bytes 14680064 | tf_op jit(solution)/shard_map/attend/pallas_call | solution.py:250
  75.0 1.6 collective-permute-done.22.refs_11_
  76.7 24.2 %feed.1 = (bf16[256,512]{1,0:T(8,128)(2,1)S(1)}, bf16[256,512]{1,0:T(8,128)(2,1)S(1)}, bf16[256,512]{1,0:T(8,128)(2,1)S(1)}, bf16[256,512]{1,0:T(8,128)(2,1)S(1)...) custom-call(s32[4]{0:T(128)} %copy-done.1, ...), custom_call_target="tpu_custom_call" | custom-call | flops 15000000512 | bytes 20971520 | tf_op jit(solution)/shard_map/feed/pallas_call | solution.py:482
  105.2 19.1 %attend_back.1 = (bf16[256,512]{1,0:T(8,128)(2,1)S(1)}, bf16[256,512]{1,0:T(8,128)(2,1)S(1)}, bf16[256,512]{1,0:T(8,128)(2,1)S(1)}, bf16[256,512]{1,0:T(8,128)(2...) custom-call(s32[4]{0:T(128)S(1)} %copy-done.2, f32[1024,512]{1,0:T(8,128)} %get-tuple-element.202.lifted_ref, ...), custom_call_target="tpu_custom_call" | custom-call | flops 14000000000 | bytes 25165824 | tf_op jit(solution)/shard_map/attend_back/pallas_call | solution.py:676
  125.5 1.5 collective-permute-start.34
  127.1 1.5 collective-permute-start.35
  129.8 2.9 %settle_rows.1 = bf16[4,256,512]{2,1,0:T(8,128)(2,1)} custom-call(s32[4]{0:T(128)} %copy-done.1, bf16[256,512]{1,0:T(8,128)(2,1)} %copy-done, bf16[256,512]{1,0:T(8,128)(2,1)} %collective-permute-done.27.refs_1_, bf16[256,512]{1,0:T(8,128)(2,1)} %copy-done.7, bf16[256,512]{1,0:T(8,128)(2,1)} %copy-done.8), custom_call_target="tpu_custom_call" | custom-call | bytes 50331648 | tf_op jit(solution)/shard_map/settle_rows/pallas_call | solution.py:834
  133.8 2.9 %collective-permute-done.34 = bf16[1536,128]{1,0:T(8,128)(2,1)S(1)} collective-permute-done((bf16[1536,128]{1,0:T(8,128)(2,1)S(1)}, bf16[1536,128]{1,0:T(8,128)(2,1)S(1)}, u32[]{:S(2)}, u32[]{:S(2)}) %collective-permute-start.34) | collective-permute-done | bytes 393248 | tf_op jit(solution)/shard_map/ppermute | solution.py:883
  137.7 2.7 %collective-permute-start.38 = (bf16[576,128]{1,0:T(8,128)(2,1)S(1)}, bf16[576,128]{1,0:T(8,128)(2,1)S(1)}, u32[]{:S(2)}, u32[]{:S(2)}) collective-permute-start(bf16[576,128]{1,0:T(8,128)(2,1)S(1)} %pad_maximum_fusion.3), channel_id=1, source_target_pairs={{0,24},{1,25},{2,26},{3,27},{4,28},{5,29},{6,30},{7,31},{8,16},{9,... | collective-permute-start | bytes 442376 | tf_op jit(solution)/shard_map/ppermute | solution.py:883
  145.2 3.9 %collective-permute-done.37.refs_6_ = bf16[576,128]{1,0:T(8,128)(2,1)S(1)} collective-permute-done((bf16[576,128]{1,0:T(8,128)(2,1)S(1)}, bf16[576,128]{1,0:T(8,128)(2,1)S(1)}, u32[]{:S(2)}, u32[]{:S(2)}) %collective-permute-start.37) | collective-permute-done | bytes 147488 | tf_op jit(solution)/shard_map/ppermute | solution.py:883
  149.2 7.4 %collective-permute-done.36.refs_5_ = bf16[576,128]{1,0:T(8,128)(2,1)S(1)} collective-permute-done((bf16[576,128]{1,0:T(8,128)(2,1)S(1)}, bf16[576,128]{1,0:T(8,128)(2,1)S(1)}, u32[]{:S(2)}, u32[]{:S(2)}) %collective-permute-start.36) | collective-permute-done | bytes 147488 | tf_op jit(solution)/shard_map/ppermute | solution.py:883
  159.1 2.3 %collective-permute-start.41 = (bf16[1,336,128]{2,1,0:T(8,128)(2,1)S(1)}, bf16[1,336,128]{2,1,0:T(8,128)(2,1)S(1)}, u32[]{:S(2)}, u32[]{:S(2)}) collective-permute-start(bf16[1,336,128]{2,1,0:T(8,128)(2,1)S(1)} %get-tuple-element.337), channel_id=1, source_target_pairs={{0,8},{1,9},{2,10},{3,11},{4,12},{5,13},{6,14},{7,15},{8,0},{9,1},... | collective-permute-start | bytes 258056 | tf_op jit(solution)/shard_map/ppermute | solution.py:883
  161.4 2.0 %collective-permute-start.42 = (bf16[1,336,128]{2,1,0:T(8,128)(2,1)S(1)}, bf16[1,336,128]{2,1,0:T(8,128)(2,1)S(1)}, u32[]{:S(2)}, u32[]{:S(2)}) collective-permute-start(bf16[1,336,128]{2,1,0:T(8,128)(2,1)S(1)} %get-tuple-element.336), channel_id=1, source_target_pairs={{0,24},{1,25},{2,26},{3,27},{4,28},{5,29},{6,30},{7,31},{8,16},{9,... | collective-permute-start | bytes 258056 | tf_op jit(solution)/shard_map/ppermute | solution.py:883
  163.4 3.2 %collective-permute-done.40.refs_1_ = bf16[1,336,128]{2,1,0:T(8,128)(2,1)S(1)} collective-permute-done((bf16[1,336,128]{2,1,0:T(8,128)(2,1)S(1)}, bf16[1,336,128]{2,1,0:T(8,128)(2,1)S(1)}, u32[]{:S(2)}, u32[]{:S(2)}) %collective-permute-start.40) | collective-permute-done | bytes 86048 | tf_op jit(solution)/shard_map/ppermute | solution.py:883
  166.6 2.1 %collective-permute-done.42.refs_3_ = bf16[1,336,128]{2,1,0:T(8,128)(2,1)S(1)} collective-permute-done((bf16[1,336,128]{2,1,0:T(8,128)(2,1)S(1)}, bf16[1,336,128]{2,1,0:T(8,128)(2,1)S(1)}, u32[]{:S(2)}, u32[]{:S(2)}) %collective-permute-start.42) | collective-permute-done | bytes 86048 | tf_op jit(solution)/shard_map/ppermute | solution.py:883
  170.0 1.5 finish.1
  (119 shorter events, 28.5 us)
Async XLA Ops:
  3.5 9.7 %collective-permute-start.4 = (bf16[256,512]{1,0:T(8,128)(2,1)S(1)}, bf16[256,512]{1,0:T(8,128)(2,1)S(1)}, u32[]{:S(2)}, u32[]{:S(2)}) collective-permute-start(bf16[256,512]{1,0:T(8,128)(2,1)S(1)} %get-tuple-element.169), channel_id=1, source_target_pairs={{0,2},{1,3},{2,0},{3,1},{4,6},{5,7},{6,4},{7,5},{8,10},{9,11},{10,... | collective-permute-start | bytes 786440 | tf_op jit(solution)/shard_map/ppermute | solution.py:883
  6.1 12.3 %collective-permute-start.5 = (bf16[256,512]{1,0:T(8,128)(2,1)S(1)}, bf16[256,512]{1,0:T(8,128)(2,1)S(1)}, u32[]{:S(2)}, u32[]{:S(2)}) collective-permute-start(bf16[256,512]{1,0:T(8,128)(2,1)S(1)} %get-tuple-element.170), channel_id=1, source_target_pairs={{0,3},{1,2},{2,1},{3,0},{4,7},{5,6},{6,5},{7,4},{8,11},{9,10},{10,... | collective-permute-start | bytes 786440 | tf_op jit(solution)/shard_map/ppermute | solution.py:883
  6.1 12.2 %collective-permute-start.1 = (bf16[1,336,128]{2,1,0:T(8,128)(2,1)S(1)}, bf16[1,336,128]{2,1,0:T(8,128)(2,1)S(1)}, u32[]{:S(2)}, u32[]{:S(2)}) collective-permute-start(bf16[1,336,128]{2,1,0:T(8,128)(2,1)S(1)} %get-tuple-element.172), channel_id=1, source_target_pairs={{0,16},{1,17},{2,18},{3,19},{4,20},{5,21},{6,22},{7,23},{8,24},{9,... | collective-permute-start | bytes 258056 | tf_op jit(solution)/shard_map/ppermute | solution.py:883
  9.0 9.4 %collective-permute-start.2 = (bf16[1,336,128]{2,1,0:T(8,128)(2,1)S(1)}, bf16[1,336,128]{2,1,0:T(8,128)(2,1)S(1)}, u32[]{:S(2)}, u32[]{:S(2)}) collective-permute-start(bf16[1,336,128]{2,1,0:T(8,128)(2,1)S(1)} %get-tuple-element.172), channel_id=1, source_target_pairs={{0,8},{1,9},{2,10},{3,11},{4,12},{5,13},{6,14},{7,15},{8,0},{9,1},... | collective-permute-start | bytes 258056 | tf_op jit(solution)/shard_map/ppermute | solution.py:883
  10.5 7.8 %collective-permute-start.3 = (bf16[1,336,128]{2,1,0:T(8,128)(2,1)S(1)}, bf16[1,336,128]{2,1,0:T(8,128)(2,1)S(1)}, u32[]{:S(2)}, u32[]{:S(2)}) collective-permute-start(bf16[1,336,128]{2,1,0:T(8,128)(2,1)S(1)} %get-tuple-element.172), channel_id=1, source_target_pairs={{0,24},{1,25},{2,26},{3,27},{4,28},{5,29},{6,30},{7,31},{8,16},{9,... | collective-permute-start | bytes 258056 | tf_op jit(solution)/shard_map/ppermute | solution.py:883
  18.3 7.8 %collective-permute-start.10 = (bf16[1,576,128]{2,1,0:T(8,128)(2,1)S(1)}, bf16[1,576,128]{2,1,0:T(8,128)(2,1)S(1)}, u32[]{:S(2)}, u32[]{:S(2)}) collective-permute-start(bf16[1,576,128]{2,1,0:T(8,128)(2,1)S(1)} %get-tuple-element.192), channel_id=1, source_target_pairs={{0,8},{1,9},{2,10},{3,11},{4,12},{5,13},{6,14},{7,15},{8,0},{9,1},... | collective-permute-start | bytes 442376 | tf_op jit(solution)/shard_map/ppermute | solution.py:883
  20.1 18.8 %collective-permute-start.6 = (bf16[4,336,128]{2,1,0:T(8,128)(2,1)S(1)}, bf16[4,336,128]{2,1,0:T(8,128)(2,1)S(1)}, u32[]{:S(2)}, u32[]{:S(2)}) collective-permute-start(bf16[4,336,128]{2,1,0:T(8,128)(2,1)S(1)} %constant_dynamic-update-slice_fusion), channel_id=1, source_target_pairs={{0,2},{1,3},{2,0},{3,1},{4,6},{5,7},{6,4},{7,5},{8,10},{9,11},{10,... | collective-permute-start | bytes 1032200 | tf_op jit(solution)/shard_map/ppermute | solution.py:883
  21.7 17.2 %collective-permute-start.7 = (bf16[4,336,128]{2,1,0:T(8,128)(2,1)S(1)}, bf16[4,336,128]{2,1,0:T(8,128)(2,1)S(1)}, u32[]{:S(2)}, u32[]{:S(2)}) collective-permute-start(bf16[4,336,128]{2,1,0:T(8,128)(2,1)S(1)} %constant_dynamic-update-slice_fusion), channel_id=1, source_target_pairs={{0,4},{1,5},{2,6},{3,7},{4,0},{5,1},{6,2},{7,3},{8,12},{9,13},{10,... | collective-permute-start | bytes 1032200 | tf_op jit(solution)/shard_map/ppermute | solution.py:883
  23.2 15.7 %collective-permute-start.8 = (bf16[4,336,128]{2,1,0:T(8,128)(2,1)S(1)}, bf16[4,336,128]{2,1,0:T(8,128)(2,1)S(1)}, u32[]{:S(2)}, u32[]{:S(2)}) collective-permute-start(bf16[4,336,128]{2,1,0:T(8,128)(2,1)S(1)} %constant_dynamic-update-slice_fusion), channel_id=1, source_target_pairs={{0,6},{1,7},{2,4},{3,5},{4,2},{5,3},{6,0},{7,1},{8,14},{9,15},{10,... | collective-permute-start | bytes 1032200 | tf_op jit(solution)/shard_map/ppermute | solution.py:883
  23.7 8.4 %collective-permute-start.11 = (bf16[1,576,128]{2,1,0:T(8,128)(2,1)S(1)}, bf16[1,576,128]{2,1,0:T(8,128)(2,1)S(1)}, u32[]{:S(2)}, u32[]{:S(2)}) collective-permute-start(bf16[1,576,128]{2,1,0:T(8,128)(2,1)S(1)} %get-tuple-element.192), channel_id=1, source_target_pairs={{0,24},{1,25},{2,26},{3,27},{4,28},{5,29},{6,30},{7,31},{8,16},{9,... | collective-permute-start | bytes 442376 | tf_op jit(solution)/shard_map/ppermute | solution.py:883
  26.1 12.8 %collective-permute-start.9 = (bf16[1,576,128]{2,1,0:T(8,128)(2,1)S(1)}, bf16[1,576,128]{2,1,0:T(8,128)(2,1)S(1)}, u32[]{:S(2)}, u32[]{:S(2)}) collective-permute-start(bf16[1,576,128]{2,1,0:T(8,128)(2,1)S(1)} %get-tuple-element.192), channel_id=1, source_target_pairs={{0,16},{1,17},{2,18},{3,19},{4,20},{5,21},{6,22},{7,23},{8,24},{9,... | collective-permute-start | bytes 442376 | tf_op jit(solution)/shard_map/ppermute | solution.py:883
  39.1 17.3 %collective-permute-start.12 = (bf16[16,336,128]{2,1,0:T(8,128)(2,1)S(1)}, bf16[16,336,128]{2,1,0:T(8,128)(2,1)S(1)}, u32[]{:S(2)}, u32[]{:S(2)}) collective-permute-start(bf16[16,336,128]{2,1,0:T(8,128)(2,1)S(1)} %constant_dynamic-update-slice_fusion.4.refs_4_), channel_id=1, source_target_pairs={{0,1},{1,0},{2,3},{3,2},{4,5},{5,4},{6,7},{7,6},{8,9},{9,8},{10,11... | collective-permute-start | bytes 4128776 | tf_op jit(solution)/shard_map/ppermute | solution.py:883
  39.9 15.3 %collective-permute-start.14 = (bf16[4,576,128]{2,1,0:T(8,128)(2,1)S(1)}, bf16[4,576,128]{2,1,0:T(8,128)(2,1)S(1)}, u32[]{:S(2)}, u32[]{:S(2)}) collective-permute-start(bf16[4,576,128]{2,1,0:T(8,128)(2,1)S(1)} %constant_dynamic-update-slice_fusion.8.refs_4_), channel_id=1, source_target_pairs={{0,2},{1,3},{2,0},{3,1},{4,6},{5,7},{6,4},{7,5},{8,10},{9,11},{10,... | collective-permute-start | bytes 1769480 | tf_op jit(solution)/shard_map/ppermute | solution.py:883
  41.4 15.0 %collective-permute-start.15 = (bf16[4,576,128]{2,1,0:T(8,128)(2,1)S(1)}, bf16[4,576,128]{2,1,0:T(8,128)(2,1)S(1)}, u32[]{:S(2)}, u32[]{:S(2)}) collective-permute-start(bf16[4,576,128]{2,1,0:T(8,128)(2,1)S(1)} %constant_dynamic-update-slice_fusion.8.refs_4_), channel_id=1, source_target_pairs={{0,4},{1,5},{2,6},{3,7},{4,0},{5,1},{6,2},{7,3},{8,12},{9,13},{10,... | collective-permute-start | bytes 1769480 | tf_op jit(solution)/shard_map/ppermute | solution.py:883
  56.4 17.7 %collective-permute-start.17 = (bf16[4,576,128]{2,1,0:T(8,128)(2,1)S(1)}, bf16[4,576,128]{2,1,0:T(8,128)(2,1)S(1)}, u32[]{:S(2)}, u32[]{:S(2)}) collective-permute-start(bf16[4,576,128]{2,1,0:T(8,128)(2,1)S(1)} %collective-permute-done.14.refs_5_), channel_id=1, source_target_pairs={{0,4},{1,5},{2,6},{3,7},{4,0},{5,1},{6,2},{7,3},{8,12},{9,13},{10,... | collective-permute-start | bytes 1769480 | tf_op jit(solution)/shard_map/ppermute | solution.py:883
  58.0 16.2 %collective-permute-start.18 = (bf16[4,576,128]{2,1,0:T(8,128)(2,1)S(1)}, bf16[4,576,128]{2,1,0:T(8,128)(2,1)S(1)}, u32[]{:S(2)}, u32[]{:S(2)}) collective-permute-start(bf16[4,576,128]{2,1,0:T(8,128)(2,1)S(1)} %collective-permute-done.14.refs_5_), channel_id=1, source_target_pairs={{0,1},{1,0},{2,3},{3,2},{4,5},{5,4},{6,7},{7,6},{8,9},{9,8},{10,11... | collective-permute-start | bytes 1769480 | tf_op jit(solution)/shard_map/ppermute | solution.py:883
  58.0 16.2 %collective-permute-start.19 = (bf16[4,576,128]{2,1,0:T(8,128)(2,1)S(1)}, bf16[4,576,128]{2,1,0:T(8,128)(2,1)S(1)}, u32[]{:S(2)}, u32[]{:S(2)}) collective-permute-start(bf16[4,576,128]{2,1,0:T(8,128)(2,1)S(1)} %collective-permute-done.15.refs_6_), channel_id=1, source_target_pairs={{0,1},{1,0},{2,3},{3,2},{4,5},{5,4},{6,7},{7,6},{8,9},{9,8},{10,11... | collective-permute-start | bytes 1769480 | tf_op jit(solution)/shard_map/ppermute | solution.py:883
  58.5 15.7 %collective-permute-start.20 = (bf16[256,512]{1,0:T(8,128)(2,1)S(1)}, bf16[256,512]{1,0:T(8,128)(2,1)S(1)}, u32[]{:S(2)}, u32[]{:S(2)}) collective-permute-start(bf16[256,512]{1,0:T(8,128)(2,1)S(1)} %copy-done.10), channel_id=1, source_target_pairs={{0,2},{1,3},{2,0},{3,1},{4,6},{5,7},{6,4},{7,5},{8,10},{9,11},{10,... | collective-permute-start | bytes 786440 | tf_op jit(solution)/shard_map/ppermute | solution.py:883
  59.0 15.1 %collective-permute-start.21 = (bf16[256,512]{1,0:T(8,128)(2,1)S(1)}, bf16[256,512]{1,0:T(8,128)(2,1)S(1)}, u32[]{:S(2)}, u32[]{:S(2)}) collective-permute-start(bf16[256,512]{1,0:T(8,128)(2,1)S(1)} %copy-done.9), channel_id=1, source_target_pairs={{0,3},{1,2},{2,1},{3,0},{4,7},{5,6},{6,5},{7,4},{8,11},{9,10},{10,... | collective-permute-start | bytes 786440 | tf_op jit(solution)/shard_map/ppermute | solution.py:883
  101.3 23.1 %collective-permute-start.26 = (bf16[4608,128]{1,0:T(8,128)(2,1)S(1)}, bf16[4608,128]{1,0:T(8,128)(2,1)S(1)}, u32[]{:S(2)}, u32[]{:S(2)}) collective-permute-start(bf16[4608,128]{1,0:T(8,128)(2,1)S(1)} %get-tuple-element.227), channel_id=1, source_target_pairs={{0,1},{1,0},{2,3},{3,2},{4,5},{5,4},{6,7},{7,6},{8,9},{9,8},{10,11... | collective-permute-start | bytes 3538952 | tf_op jit(solution)/shard_map/ppermute | solution.py:883
  101.8 22.5 %collective-permute-start.28 = (bf16[256,512]{1,0:T(8,128)(2,1)S(1)}, bf16[256,512]{1,0:T(8,128)(2,1)S(1)}, u32[]{:S(2)}, u32[]{:S(2)}) collective-permute-start(bf16[256,512]{1,0:T(8,128)(2,1)S(1)} %get-tuple-element.230), channel_id=1, source_target_pairs={{0,2},{1,3},{2,0},{3,1},{4,6},{5,7},{6,4},{7,5},{8,10},{9,11},{10,... | collective-permute-start | bytes 786440 | tf_op jit(solution)/shard_map/ppermute | solution.py:883
  102.3 22.0 %collective-permute-start.29 = (bf16[256,512]{1,0:T(8,128)(2,1)S(1)}, bf16[256,512]{1,0:T(8,128)(2,1)S(1)}, u32[]{:S(2)}, u32[]{:S(2)}) collective-permute-start(bf16[256,512]{1,0:T(8,128)(2,1)S(1)} %get-tuple-element.231), channel_id=1, source_target_pairs={{0,3},{1,2},{2,1},{3,0},{4,7},{5,6},{6,5},{7,4},{8,11},{9,10},{10,... | collective-permute-start | bytes 786440 | tf_op jit(solution)/shard_map/ppermute | solution.py:883
  104.1 20.3 %collective-permute-start.24 = (bf16[3072,128]{1,0:T(8,128)(2,1)S(1)}, bf16[3072,128]{1,0:T(8,128)(2,1)S(1)}, u32[]{:S(2)}, u32[]{:S(2)}) collective-permute-start(bf16[3072,128]{1,0:T(8,128)(2,1)S(1)} %add_convert_fusion), channel_id=1, source_target_pairs={{0,4},{1,5},{2,6},{3,7},{4,0},{5,1},{6,2},{7,3},{8,12},{9,13},{10,... | collective-permute-start | bytes 2359304 | tf_op jit(solution)/shard_map/ppermute | solution.py:883
  104.7 19.7 %collective-permute-start.25 = (bf16[1536,128]{1,0:T(8,128)(2,1)S(1)}, bf16[1536,128]{1,0:T(8,128)(2,1)S(1)}, u32[]{:S(2)}, u32[]{:S(2)}) collective-permute-start(bf16[1536,128]{1,0:T(8,128)(2,1)S(1)} %add_convert_fusion.3), channel_id=1, source_target_pairs={{0,2},{1,3},{2,0},{3,1},{4,6},{5,7},{6,4},{7,5},{8,10},{9,11},{10,... | collective-permute-start | bytes 1179656 | tf_op jit(solution)/shard_map/ppermute | solution.py:883
  125.5 11.1 %collective-permute-start.34 = (bf16[1536,128]{1,0:T(8,128)(2,1)S(1)}, bf16[1536,128]{1,0:T(8,128)(2,1)S(1)}, u32[]{:S(2)}, u32[]{:S(2)}) collective-permute-start(bf16[1536,128]{1,0:T(8,128)(2,1)S(1)} %get-tuple-element.265), channel_id=1, source_target_pairs={{0,2},{1,3},{2,0},{3,1},{4,6},{5,7},{6,4},{7,5},{8,10},{9,11},{10,... | collective-permute-start | bytes 1179656 | tf_op jit(solution)/shard_map/ppermute | solution.py:883
  140.4 16.1 %collective-permute-start.31 = (bf16[4,336,128]{2,1,0:T(8,128)(2,1)S(1)}, bf16[4,336,128]{2,1,0:T(8,128)(2,1)S(1)}, u32[]{:S(2)}, u32[]{:S(2)}) collective-permute-start(bf16[4,336,128]{2,1,0:T(8,128)(2,1)S(1)} %copy-done.6), channel_id=1, source_target_pairs={{0,2},{1,3},{2,0},{3,1},{4,6},{5,7},{6,4},{7,5},{8,10},{9,11},{10,... | collective-permute-start | bytes 1032200 | tf_op jit(solution)/shard_map/ppermute | solution.py:883
  141.9 16.0 %collective-permute-start.32 = (bf16[4,336,128]{2,1,0:T(8,128)(2,1)S(1)}, bf16[4,336,128]{2,1,0:T(8,128)(2,1)S(1)}, u32[]{:S(2)}, u32[]{:S(2)}) collective-permute-start(bf16[4,336,128]{2,1,0:T(8,128)(2,1)S(1)} %copy-done.5), channel_id=1, source_target_pairs={{0,4},{1,5},{2,6},{3,7},{4,0},{5,1},{6,2},{7,3},{8,12},{9,13},{10,... | collective-permute-start | bytes 1032200 | tf_op jit(solution)/shard_map/ppermute | solution.py:883
  143.3 14.6 %collective-permute-start.33 = (bf16[4,336,128]{2,1,0:T(8,128)(2,1)S(1)}, bf16[4,336,128]{2,1,0:T(8,128)(2,1)S(1)}, u32[]{:S(2)}, u32[]{:S(2)}) collective-permute-start(bf16[4,336,128]{2,1,0:T(8,128)(2,1)S(1)} %get-tuple-element.263), channel_id=1, source_target_pairs={{0,6},{1,7},{2,4},{3,5},{4,2},{5,3},{6,0},{7,1},{8,14},{9,15},{10,... | collective-permute-start | bytes 1032200 | tf_op jit(solution)/shard_map/ppermute | solution.py:883
  145.2 11.3 %collective-permute-start.39 = (bf16[256,512]{1,0:T(8,128)(2,1)S(1)}, bf16[256,512]{1,0:T(8,128)(2,1)S(1)}, u32[]{:S(2)}, u32[]{:S(2)}) collective-permute-start(bf16[256,512]{1,0:T(8,128)(2,1)S(1)} %get-tuple-element.276), channel_id=1, source_target_pairs={{0,1},{1,0},{2,3},{3,2},{4,5},{5,4},{6,7},{7,6},{8,9},{9,8},{10,11... | collective-permute-start | bytes 786440 | tf_op jit(solution)/shard_map/ppermute | solution.py:883
  157.9 10.9 %collective-permute-start.43 = (bf16[256,512]{1,0:T(8,128)(2,1)S(1)}, bf16[256,512]{1,0:T(8,128)(2,1)S(1)}, u32[]{:S(2)}, u32[]{:S(2)}) collective-permute-start(bf16[256,512]{1,0:T(8,128)(2,1)S(1)} %get-tuple-element.286), channel_id=1, source_target_pairs={{0,2},{1,3},{2,0},{3,1},{4,6},{5,7},{6,4},{7,5},{8,10},{9,11},{10,... | collective-permute-start | bytes 786440 | tf_op jit(solution)/shard_map/ppermute | solution.py:883
  158.8 10.0 %collective-permute-start.44 = (bf16[256,512]{1,0:T(8,128)(2,1)S(1)}, bf16[256,512]{1,0:T(8,128)(2,1)S(1)}, u32[]{:S(2)}, u32[]{:S(2)}) collective-permute-start(bf16[256,512]{1,0:T(8,128)(2,1)S(1)} %get-tuple-element.287), channel_id=1, source_target_pairs={{0,3},{1,2},{2,1},{3,0},{4,7},{5,6},{6,5},{7,4},{8,11},{9,10},{10,... | collective-permute-start | bytes 786440 | tf_op jit(solution)/shard_map/ppermute | solution.py:883
  159.0 7.6 %collective-permute-start.40 = (bf16[1,336,128]{2,1,0:T(8,128)(2,1)S(1)}, bf16[1,336,128]{2,1,0:T(8,128)(2,1)S(1)}, u32[]{:S(2)}, u32[]{:S(2)}) collective-permute-start(bf16[1,336,128]{2,1,0:T(8,128)(2,1)S(1)} %get-tuple-element.338), channel_id=1, source_target_pairs={{0,16},{1,17},{2,18},{3,19},{4,20},{5,21},{6,22},{7,23},{8,24},{9,... | collective-permute-start | bytes 258056 | tf_op jit(solution)/shard_map/ppermute | solution.py:883
  (26 other events, 225.5 us)

commit v9 on v8

--- a/solution.py
+++ b/solution.py
@@ -85,7 +85,7 @@
         self.lengths = lengths
         self.owned = [n // devices for n in lengths]
         self.small_rows = 16
-        self.z_order = (0, 16, 8, 24)
+        self.z_order = (0, 24, 8, 16)
         starts = [0]
         for n in lengths:
             starts.append(starts[-1] + n // LANE)

time: 172 us -> 172 us (level)
  no operation moved by 1% of the time
where the time goes in v9:
time: 172 us; the launch traced here: 171 us
  Pallas kernels  66.5 us (39%)
  waiting for transfers between devices  53.5 us (31%)
  starting transfers between devices  43.3 us (25%)
  other arithmetic  5.81 us (3%)
    ppermute x45, waiting for transfers between devices, swap(): lax.ppermute(value, AXES, [(d, d ^ mask) for d in range(devices)])  53.5 us
    ppermute x45, starting transfers between devices, swap(): lax.ppermute(value, AXES, [(d, d ^ mask) for d in range(devices)])  43.3 us
    pallas_call x1, Pallas kernels, feed(): pl.pallas_call(functools.partial(feed_kernel, plan, count), grid_spec=plt...  24.2 us
    pallas_call x1, Pallas kernels, attend_back(): pl.pallas_call(functools.partial(attend_back_kernel, plan, count), grid_s...  19.1 us
    pallas_call x1, Pallas kernels, attend(): pl.pallas_call(functools.partial(attend_kernel, plan, count), grid_spec=p...  14.3 us
  transfers between devices with their start and end apart: 45, of which 17 were waited for; matrix products, arithmetic and copies ran while one was open for 2% of the time, Pallas kernels for 22%

profile of v9, /device:TPU:0, one launch (start us, length us, event | category | flops | bytes accessed | tf_op | source)
XLA Modules:
  0.0 171.3 jit_solution(14764495926102738302)
XLA Ops:
  0.7 2.3 %pack.1 = (bf16[256,512]{1,0:T(8,128)(2,1)S(1)}, bf16[256,512]{1,0:T(8,128)(2,1)S(1)}, bf16[256,512]{1,0:T(8,128)(2,1)S(1)}, bf16[256,512]{1,0:T(8,128)(2,1)S(1)...) custom-call(bf16[4,256,512]{2,1,0:T(8,128)(2,1)} %bitcast.41, bf16[16,1024]{1,0:T(8,128)(2,1)} %bitcast.43, ...), custom_call_target="tpu_custom_call" | custom-call | bytes 4194304 | tf_op jit(solution)/shard_map/pack/pallas_call | solution.py:751
  3.5 2.6 %collective-permute-start.4 = (bf16[256,512]{1,0:T(8,128)(2,1)S(1)}, bf16[256,512]{1,0:T(8,128)(2,1)S(1)}, u32[]{:S(2)}, u32[]{:S(2)}) collective-permute-start(bf16[256,512]{1,0:T(8,128)(2,1)S(1)} %get-tuple-element.169), channel_id=1, source_target_pairs={{0,2},{1,3},{2,0},{3,1},{4,6},{5,7},{6,4},{7,5},{8,10},{9,11},{10,... | collective-permute-start | bytes 786440 | tf_op jit(solution)/shard_map/ppermute | solution.py:883
  6.1 3.8 %collective-permute-start.1 = (bf16[1,336,128]{2,1,0:T(8,128)(2,1)S(1)}, bf16[1,336,128]{2,1,0:T(8,128)(2,1)S(1)}, u32[]{:S(2)}, u32[]{:S(2)}) collective-permute-start(bf16[1,336,128]{2,1,0:T(8,128)(2,1)S(1)} %get-tuple-element.172), channel_id=1, source_target_pairs={{0,24},{1,25},{2,26},{3,27},{4,28},{5,29},{6,30},{7,31},{8,16},{9,... | collective-permute-start | bytes 258056 | tf_op jit(solution)/shard_map/ppermute | solution.py:883
  10.5 2.7 %collective-permute-done.4.refs_2_ = bf16[256,512]{1,0:T(8,128)(2,1)S(1)} collective-permute-done((bf16[256,512]{1,0:T(8,128)(2,1)S(1)}, bf16[256,512]{1,0:T(8,128)(2,1)S(1)}, u32[]{:S(2)}, u32[]{:S(2)}) %collective-permute-start.4) | collective-permute-done | bytes 262176 | tf_op jit(solution)/shard_map/ppermute | solution.py:883
  13.2 5.1 %collective-permute-done.5.refs_3_ = bf16[256,512]{1,0:T(8,128)(2,1)S(1)} collective-permute-done((bf16[256,512]{1,0:T(8,128)(2,1)S(1)}, bf16[256,512]{1,0:T(8,128)(2,1)S(1)}, u32[]{:S(2)}, u32[]{:S(2)}) %collective-permute-start.5) | collective-permute-done | bytes 262176 | tf_op jit(solution)/shard_map/ppermute | solution.py:883
  18.3 1.7 %collective-permute-start.10 = (bf16[1,576,128]{2,1,0:T(8,128)(2,1)S(1)}, bf16[1,576,128]{2,1,0:T(8,128)(2,1)S(1)}, u32[]{:S(2)}, u32[]{:S(2)}) collective-permute-start(bf16[1,576,128]{2,1,0:T(8,128)(2,1)S(1)} %get-tuple-element.192), channel_id=1, source_target_pairs={{0,8},{1,9},{2,10},{3,11},{4,12},{5,13},{6,14},{7,15},{8,0},{9,1},... | collective-permute-start | bytes 442376 | tf_op jit(solution)/shard_map/ppermute | solution.py:883
  20.1 1.6 collective-permute-start.6
  21.7 1.5 collective-permute-start.7
  23.7 2.6 %collective-permute-start.11 = (bf16[1,576,128]{2,1,0:T(8,128)(2,1)S(1)}, bf16[1,576,128]{2,1,0:T(8,128)(2,1)S(1)}, u32[]{:S(2)}, u32[]{:S(2)}) collective-permute-start(bf16[1,576,128]{2,1,0:T(8,128)(2,1)S(1)} %get-tuple-element.192), channel_id=1, source_target_pairs={{0,16},{1,17},{2,18},{3,19},{4,20},{5,21},{6,22},{7,23},{8,24},{9,... | collective-permute-start | bytes 442376 | tf_op jit(solution)/shard_map/ppermute | solution.py:883
  26.3 1.8 %collective-permute-start.9 = (bf16[1,576,128]{2,1,0:T(8,128)(2,1)S(1)}, bf16[1,576,128]{2,1,0:T(8,128)(2,1)S(1)}, u32[]{:S(2)}, u32[]{:S(2)}) collective-permute-start(bf16[1,576,128]{2,1,0:T(8,128)(2,1)S(1)} %get-tuple-element.192), channel_id=1, source_target_pairs={{0,24},{1,25},{2,26},{3,27},{4,28},{5,29},{6,30},{7,31},{8,16},{9,... | collective-permute-start | bytes 442376 | tf_op jit(solution)/shard_map/ppermute | solution.py:883
  28.7 2.2 %cut_rows.1 = (bf16[256,512]{1,0:T(8,128)(2,1)}, bf16[256,512]{1,0:T(8,128)(2,1)}, bf16[256,512]{1,0:T(8,128)(2,1)}, bf16[256,512]{1,0:T(8,128)(2,1)}) custom-call(bf16[4,256,512]{2,1,0:T(8,128)(2,1)} %bitcast.42), custom_call_target="tpu_custom_call" | custom-call | bytes 4194304 | tf_op jit(solution)/shard_map/cut_rows/pallas_call | solution.py:856
  31.7 4.5 %collective-permute-done.11 = bf16[1,576,128]{2,1,0:T(8,128)(2,1)S(1)} collective-permute-done((bf16[1,576,128]{2,1,0:T(8,128)(2,1)S(1)}, bf16[1,576,128]{2,1,0:T(8,128)(2,1)S(1)}, u32[]{:S(2)}, u32[]{:S(2)}) %collective-permute-start.11) | collective-permute-done | bytes 147488 | tf_op jit(solution)/shard_map/ppermute | solution.py:883
  36.2 2.5 %collective-permute-done.7 = bf16[4,336,128]{2,1,0:T(8,128)(2,1)S(1)} collective-permute-done((bf16[4,336,128]{2,1,0:T(8,128)(2,1)S(1)}, bf16[4,336,128]{2,1,0:T(8,128)(2,1)S(1)}, u32[]{:S(2)}, u32[]{:S(2)}) %collective-permute-start.7) | collective-permute-done | bytes 344096 | tf_op jit(solution)/shard_map/ppermute | solution.py:883
  41.8 1.6 collective-permute-done.16.refs_1_
  43.4 11.6 %collective-permute-done.14.refs_5_ = bf16[4,576,128]{2,1,0:T(8,128)(2,1)S(1)} collective-permute-done((bf16[4,576,128]{2,1,0:T(8,128)(2,1)S(1)}, bf16[4,576,128]{2,1,0:T(8,128)(2,1)S(1)}, u32[]{:S(2)}, u32[]{:S(2)}) %collective-permute-start.14) | collective-permute-done | bytes 589856 | tf_op jit(solution)/shard_map/ppermute | solution.py:883
  57.3 1.5 collective-permute-start.20
  58.8 14.3 %attend.1 = (f32[1024,512]{1,0:T(8,128)}, bf16[1024,512]{1,0:T(8,128)(2,1)}, bf16[1024,512]{1,0:T(8,128)(2,1)}, bf16[1024,512]{1,0:T(8,128)(2,1)}, bf16[1024,512...) custom-call(s32[4]{0:T(128)S(1)} %pad_add_fusion.info_ref, ...), custom_call_target="tpu_custom_call" | custom-call | flops 5000000000 | bytes 14680064 | tf_op jit(solution)/shard_map/attend/pallas_call | solution.py:250
  73.9 1.6 collective-permute-done.22.refs_11_
  75.5 24.2 %feed.1 = (bf16[256,512]{1,0:T(8,128)(2,1)S(1)}, bf16[256,512]{1,0:T(8,128)(2,1)S(1)}, bf16[256,512]{1,0:T(8,128)(2,1)S(1)}, bf16[256,512]{1,0:T(8,128)(2,1)S(1)...) custom-call(s32[4]{0:T(128)} %copy-done.1, ...), custom_call_target="tpu_custom_call" | custom-call | flops 15000000512 | bytes 20971520 | tf_op jit(solution)/shard_map/feed/pallas_call | solution.py:482
  100.6 1.5 collective-permute-start.28
  105.0 19.1 %attend_back.1 = (bf16[256,512]{1,0:T(8,128)(2,1)S(1)}, bf16[256,512]{1,0:T(8,128)(2,1)S(1)}, bf16[256,512]{1,0:T(8,128)(2,1)S(1)}, bf16[256,512]{1,0:T(8,128)(2...) custom-call(s32[4]{0:T(128)S(1)} %copy-done.2, f32[1024,512]{1,0:T(8,128)} %get-tuple-element.202.lifted_ref, ...), custom_call_target="tpu_custom_call" | custom-call | flops 14000000000 | bytes 25165824 | tf_op jit(solution)/shard_map/attend_back/pallas_call | solution.py:676
  128.7 2.9 %settle_rows.1 = bf16[4,256,512]{2,1,0:T(8,128)(2,1)} custom-call(s32[4]{0:T(128)} %copy-done.1, bf16[256,512]{1,0:T(8,128)(2,1)} %copy-done, bf16[256,512]{1,0:T(8,128)(2,1)} %collective-permute-done.27.refs_1_, bf16[256,512]{1,0:T(8,128)(2,1)} %copy-done.7, bf16[256,512]{1,0:T(8,128)(2,1)} %copy-done.8), custom_call_target="tpu_custom_call" | custom-call | bytes 50331648 | tf_op jit(solution)/shard_map/settle_rows/pallas_call | solution.py:834
  131.6 1.6 collective-permute-done.35
  133.1 3.3 %collective-permute-done.34 = bf16[1536,128]{1,0:T(8,128)(2,1)S(1)} collective-permute-done((bf16[1536,128]{1,0:T(8,128)(2,1)S(1)}, bf16[1536,128]{1,0:T(8,128)(2,1)S(1)}, u32[]{:S(2)}, u32[]{:S(2)}) %collective-permute-start.34) | collective-permute-done | bytes 393248 | tf_op jit(solution)/shard_map/ppermute | solution.py:883
  137.5 2.7 %collective-permute-start.38 = (bf16[576,128]{1,0:T(8,128)(2,1)S(1)}, bf16[576,128]{1,0:T(8,128)(2,1)S(1)}, u32[]{:S(2)}, u32[]{:S(2)}) collective-permute-start(bf16[576,128]{1,0:T(8,128)(2,1)S(1)} %pad_maximum_fusion.3), channel_id=1, source_target_pairs={{0,16},{1,17},{2,18},{3,19},{4,20},{5,21},{6,22},{7,23},{8,24},{9,... | collective-permute-start | bytes 442376 | tf_op jit(solution)/shard_map/ppermute | solution.py:883
  144.2 2.5 %collective-permute-done.38.refs_7_ = bf16[576,128]{1,0:T(8,128)(2,1)S(1)} collective-permute-done((bf16[576,128]{1,0:T(8,128)(2,1)S(1)}, bf16[576,128]{1,0:T(8,128)(2,1)S(1)}, u32[]{:S(2)}, u32[]{:S(2)}) %collective-permute-start.38) | collective-permute-done | bytes 147488 | tf_op jit(solution)/shard_map/ppermute | solution.py:883
  146.7 3.0 %collective-permute-done.37.refs_6_ = bf16[576,128]{1,0:T(8,128)(2,1)S(1)} collective-permute-done((bf16[576,128]{1,0:T(8,128)(2,1)S(1)}, bf16[576,128]{1,0:T(8,128)(2,1)S(1)}, u32[]{:S(2)}, u32[]{:S(2)}) %collective-permute-start.37) | collective-permute-done | bytes 147488 | tf_op jit(solution)/shard_map/ppermute | solution.py:883
  150.7 6.1 %collective-permute-done.36.refs_5_ = bf16[576,128]{1,0:T(8,128)(2,1)S(1)} collective-permute-done((bf16[576,128]{1,0:T(8,128)(2,1)S(1)}, bf16[576,128]{1,0:T(8,128)(2,1)S(1)}, u32[]{:S(2)}, u32[]{:S(2)}) %collective-permute-start.36) | collective-permute-done | bytes 147488 | tf_op jit(solution)/shard_map/ppermute | solution.py:883
  159.5 3.3 %collective-permute-start.42 = (bf16[1,336,128]{2,1,0:T(8,128)(2,1)S(1)}, bf16[1,336,128]{2,1,0:T(8,128)(2,1)S(1)}, u32[]{:S(2)}, u32[]{:S(2)}) collective-permute-start(bf16[1,336,128]{2,1,0:T(8,128)(2,1)S(1)} %get-tuple-element.336), channel_id=1, source_target_pairs={{0,16},{1,17},{2,18},{3,19},{4,20},{5,21},{6,22},{7,23},{8,24},{9,... | collective-permute-start | bytes 258056 | tf_op jit(solution)/shard_map/ppermute | solution.py:883
  162.8 2.9 %collective-permute-done.40.refs_1_ = bf16[1,336,128]{2,1,0:T(8,128)(2,1)S(1)} collective-permute-done((bf16[1,336,128]{2,1,0:T(8,128)(2,1)S(1)}, bf16[1,336,128]{2,1,0:T(8,128)(2,1)S(1)}, u32[]{:S(2)}, u32[]{:S(2)}) %collective-permute-start.40) | collective-permute-done | bytes 86048 | tf_op jit(solution)/shard_map/ppermute | solution.py:883
  165.8 2.7 %collective-permute-done.41.refs_2_ = bf16[1,336,128]{2,1,0:T(8,128)(2,1)S(1)} collective-permute-done((bf16[1,336,128]{2,1,0:T(8,128)(2,1)S(1)}, bf16[1,336,128]{2,1,0:T(8,128)(2,1)S(1)}, u32[]{:S(2)}, u32[]{:S(2)}) %collective-permute-start.41) | collective-permute-done | bytes 86048 | tf_op jit(solution)/shard_map/ppermute | solution.py:883
  169.7 1.5 finish.1
  (119 shorter events, 27.2 us)
Async XLA Ops:
  3.5 9.7 %collective-permute-start.4 = (bf16[256,512]{1,0:T(8,128)(2,1)S(1)}, bf16[256,512]{1,0:T(8,128)(2,1)S(1)}, u32[]{:S(2)}, u32[]{:S(2)}) collective-permute-start(bf16[256,512]{1,0:T(8,128)(2,1)S(1)} %get-tuple-element.169), channel_id=1, source_target_pairs={{0,2},{1,3},{2,0},{3,1},{4,6},{5,7},{6,4},{7,5},{8,10},{9,11},{10,... | collective-permute-start | bytes 786440 | tf_op jit(solution)/shard_map/ppermute | solution.py:883
  6.1 12.3 %collective-permute-start.5 = (bf16[256,512]{1,0:T(8,128)(2,1)S(1)}, bf16[256,512]{1,0:T(8,128)(2,1)S(1)}, u32[]{:S(2)}, u32[]{:S(2)}) collective-permute-start(bf16[256,512]{1,0:T(8,128)(2,1)S(1)} %get-tuple-element.170), channel_id=1, source_target_pairs={{0,3},{1,2},{2,1},{3,0},{4,7},{5,6},{6,5},{7,4},{8,11},{9,10},{10,... | collective-permute-start | bytes 786440 | tf_op jit(solution)/shard_map/ppermute | solution.py:883
  6.1 12.2 %collective-permute-start.1 = (bf16[1,336,128]{2,1,0:T(8,128)(2,1)S(1)}, bf16[1,336,128]{2,1,0:T(8,128)(2,1)S(1)}, u32[]{:S(2)}, u32[]{:S(2)}) collective-permute-start(bf16[1,336,128]{2,1,0:T(8,128)(2,1)S(1)} %get-tuple-element.172), channel_id=1, source_target_pairs={{0,24},{1,25},{2,26},{3,27},{4,28},{5,29},{6,30},{7,31},{8,16},{9,... | collective-permute-start | bytes 258056 | tf_op jit(solution)/shard_map/ppermute | solution.py:883
  10.0 8.3 %collective-permute-start.2 = (bf16[1,336,128]{2,1,0:T(8,128)(2,1)S(1)}, bf16[1,336,128]{2,1,0:T(8,128)(2,1)S(1)}, u32[]{:S(2)}, u32[]{:S(2)}) collective-permute-start(bf16[1,336,128]{2,1,0:T(8,128)(2,1)S(1)} %get-tuple-element.172), channel_id=1, source_target_pairs={{0,8},{1,9},{2,10},{3,11},{4,12},{5,13},{6,14},{7,15},{8,0},{9,1},... | collective-permute-start | bytes 258056 | tf_op jit(solution)/shard_map/ppermute | solution.py:883
  20.1 16.1 %collective-permute-start.6 = (bf16[4,336,128]{2,1,0:T(8,128)(2,1)S(1)}, bf16[4,336,128]{2,1,0:T(8,128)(2,1)S(1)}, u32[]{:S(2)}, u32[]{:S(2)}) collective-permute-start(bf16[4,336,128]{2,1,0:T(8,128)(2,1)S(1)} %constant_dynamic-update-slice_fusion), channel_id=1, source_target_pairs={{0,2},{1,3},{2,0},{3,1},{4,6},{5,7},{6,4},{7,5},{8,10},{9,11},{10,... | collective-permute-start | bytes 1032200 | tf_op jit(solution)/shard_map/ppermute | solution.py:883
  21.7 17.1 %collective-permute-start.7 = (bf16[4,336,128]{2,1,0:T(8,128)(2,1)S(1)}, bf16[4,336,128]{2,1,0:T(8,128)(2,1)S(1)}, u32[]{:S(2)}, u32[]{:S(2)}) collective-permute-start(bf16[4,336,128]{2,1,0:T(8,128)(2,1)S(1)} %constant_dynamic-update-slice_fusion), channel_id=1, source_target_pairs={{0,4},{1,5},{2,6},{3,7},{4,0},{5,1},{6,2},{7,3},{8,12},{9,13},{10,... | collective-permute-start | bytes 1032200 | tf_op jit(solution)/shard_map/ppermute | solution.py:883
  23.2 15.5 %collective-permute-start.8 = (bf16[4,336,128]{2,1,0:T(8,128)(2,1)S(1)}, bf16[4,336,128]{2,1,0:T(8,128)(2,1)S(1)}, u32[]{:S(2)}, u32[]{:S(2)}) collective-permute-start(bf16[4,336,128]{2,1,0:T(8,128)(2,1)S(1)} %constant_dynamic-update-slice_fusion), channel_id=1, source_target_pairs={{0,6},{1,7},{2,4},{3,5},{4,2},{5,3},{6,0},{7,1},{8,14},{9,15},{10,... | collective-permute-start | bytes 1032200 | tf_op jit(solution)/shard_map/ppermute | solution.py:883
  23.7 12.5 %collective-permute-start.11 = (bf16[1,576,128]{2,1,0:T(8,128)(2,1)S(1)}, bf16[1,576,128]{2,1,0:T(8,128)(2,1)S(1)}, u32[]{:S(2)}, u32[]{:S(2)}) collective-permute-start(bf16[1,576,128]{2,1,0:T(8,128)(2,1)S(1)} %get-tuple-element.192), channel_id=1, source_target_pairs={{0,16},{1,17},{2,18},{3,19},{4,20},{5,21},{6,22},{7,23},{8,24},{9,... | collective-permute-start | bytes 442376 | tf_op jit(solution)/shard_map/ppermute | solution.py:883
  26.3 9.9 %collective-permute-start.9 = (bf16[1,576,128]{2,1,0:T(8,128)(2,1)S(1)}, bf16[1,576,128]{2,1,0:T(8,128)(2,1)S(1)}, u32[]{:S(2)}, u32[]{:S(2)}) collective-permute-start(bf16[1,576,128]{2,1,0:T(8,128)(2,1)S(1)} %get-tuple-element.192), channel_id=1, source_target_pairs={{0,24},{1,25},{2,26},{3,27},{4,28},{5,29},{6,30},{7,31},{8,16},{9,... | collective-permute-start | bytes 442376 | tf_op jit(solution)/shard_map/ppermute | solution.py:883
  39.0 17.0 %collective-permute-start.12 = (bf16[16,336,128]{2,1,0:T(8,128)(2,1)S(1)}, bf16[16,336,128]{2,1,0:T(8,128)(2,1)S(1)}, u32[]{:S(2)}, u32[]{:S(2)}) collective-permute-start(bf16[16,336,128]{2,1,0:T(8,128)(2,1)S(1)} %constant_dynamic-update-slice_fusion.4.refs_4_), channel_id=1, source_target_pairs={{0,1},{1,0},{2,3},{3,2},{4,5},{5,4},{6,7},{7,6},{8,9},{9,8},{10,11... | collective-permute-start | bytes 4128776 | tf_op jit(solution)/shard_map/ppermute | solution.py:883
  39.7 15.3 %collective-permute-start.14 = (bf16[4,576,128]{2,1,0:T(8,128)(2,1)S(1)}, bf16[4,576,128]{2,1,0:T(8,128)(2,1)S(1)}, u32[]{:S(2)}, u32[]{:S(2)}) collective-permute-start(bf16[4,576,128]{2,1,0:T(8,128)(2,1)S(1)} %constant_dynamic-update-slice_fusion.8.refs_4_), channel_id=1, source_target_pairs={{0,2},{1,3},{2,0},{3,1},{4,6},{5,7},{6,4},{7,5},{8,10},{9,11},{10,... | collective-permute-start | bytes 1769480 | tf_op jit(solution)/shard_map/ppermute | solution.py:883
  40.9 15.0 %collective-permute-start.15 = (bf16[4,576,128]{2,1,0:T(8,128)(2,1)S(1)}, bf16[4,576,128]{2,1,0:T(8,128)(2,1)S(1)}, u32[]{:S(2)}, u32[]{:S(2)}) collective-permute-start(bf16[4,576,128]{2,1,0:T(8,128)(2,1)S(1)} %constant_dynamic-update-slice_fusion.8.refs_4_), channel_id=1, source_target_pairs={{0,4},{1,5},{2,6},{3,7},{4,0},{5,1},{6,2},{7,3},{8,12},{9,13},{10,... | collective-permute-start | bytes 1769480 | tf_op jit(solution)/shard_map/ppermute | solution.py:883
  56.0 17.2 %collective-permute-start.17 = (bf16[4,576,128]{2,1,0:T(8,128)(2,1)S(1)}, bf16[4,576,128]{2,1,0:T(8,128)(2,1)S(1)}, u32[]{:S(2)}, u32[]{:S(2)}) collective-permute-start(bf16[4,576,128]{2,1,0:T(8,128)(2,1)S(1)} %collective-permute-done.14.refs_5_), channel_id=1, source_target_pairs={{0,4},{1,5},{2,6},{3,7},{4,0},{5,1},{6,2},{7,3},{8,12},{9,13},{10,... | collective-permute-start | bytes 1769480 | tf_op jit(solution)/shard_map/ppermute | solution.py:883
  56.8 16.3 %collective-permute-start.18 = (bf16[4,576,128]{2,1,0:T(8,128)(2,1)S(1)}, bf16[4,576,128]{2,1,0:T(8,128)(2,1)S(1)}, u32[]{:S(2)}, u32[]{:S(2)}) collective-permute-start(bf16[4,576,128]{2,1,0:T(8,128)(2,1)S(1)} %collective-permute-done.14.refs_5_), channel_id=1, source_target_pairs={{0,1},{1,0},{2,3},{3,2},{4,5},{5,4},{6,7},{7,6},{8,9},{9,8},{10,11... | collective-permute-start | bytes 1769480 | tf_op jit(solution)/shard_map/ppermute | solution.py:883
  56.8 16.4 %collective-permute-start.19 = (bf16[4,576,128]{2,1,0:T(8,128)(2,1)S(1)}, bf16[4,576,128]{2,1,0:T(8,128)(2,1)S(1)}, u32[]{:S(2)}, u32[]{:S(2)}) collective-permute-start(bf16[4,576,128]{2,1,0:T(8,128)(2,1)S(1)} %collective-permute-done.15.refs_6_), channel_id=1, source_target_pairs={{0,1},{1,0},{2,3},{3,2},{4,5},{5,4},{6,7},{7,6},{8,9},{9,8},{10,11... | collective-permute-start | bytes 1769480 | tf_op jit(solution)/shard_map/ppermute | solution.py:883
  57.3 15.8 %collective-permute-start.20 = (bf16[256,512]{1,0:T(8,128)(2,1)S(1)}, bf16[256,512]{1,0:T(8,128)(2,1)S(1)}, u32[]{:S(2)}, u32[]{:S(2)}) collective-permute-start(bf16[256,512]{1,0:T(8,128)(2,1)S(1)} %copy-done.10), channel_id=1, source_target_pairs={{0,2},{1,3},{2,0},{3,1},{4,6},{5,7},{6,4},{7,5},{8,10},{9,11},{10,... | collective-permute-start | bytes 786440 | tf_op jit(solution)/shard_map/ppermute | solution.py:883
  58.8 14.3 %collective-permute-start.21 = (bf16[256,512]{1,0:T(8,128)(2,1)S(1)}, bf16[256,512]{1,0:T(8,128)(2,1)S(1)}, u32[]{:S(2)}, u32[]{:S(2)}) collective-permute-start(bf16[256,512]{1,0:T(8,128)(2,1)S(1)} %copy-done.9), channel_id=1, source_target_pairs={{0,3},{1,2},{2,1},{3,0},{4,7},{5,6},{6,5},{7,4},{8,11},{9,10},{10,... | collective-permute-start | bytes 786440 | tf_op jit(solution)/shard_map/ppermute | solution.py:883
  100.1 24.0 %collective-permute-start.26 = (bf16[4608,128]{1,0:T(8,128)(2,1)S(1)}, bf16[4608,128]{1,0:T(8,128)(2,1)S(1)}, u32[]{:S(2)}, u32[]{:S(2)}) collective-permute-start(bf16[4608,128]{1,0:T(8,128)(2,1)S(1)} %get-tuple-element.227), channel_id=1, source_target_pairs={{0,1},{1,0},{2,3},{3,2},{4,5},{5,4},{6,7},{7,6},{8,9},{9,8},{10,11... | collective-permute-start | bytes 3538952 | tf_op jit(solution)/shard_map/ppermute | solution.py:883
  100.6 23.5 %collective-permute-start.28 = (bf16[256,512]{1,0:T(8,128)(2,1)S(1)}, bf16[256,512]{1,0:T(8,128)(2,1)S(1)}, u32[]{:S(2)}, u32[]{:S(2)}) collective-permute-start(bf16[256,512]{1,0:T(8,128)(2,1)S(1)} %get-tuple-element.230), channel_id=1, source_target_pairs={{0,2},{1,3},{2,0},{3,1},{4,6},{5,7},{6,4},{7,5},{8,10},{9,11},{10,... | collective-permute-start | bytes 786440 | tf_op jit(solution)/shard_map/ppermute | solution.py:883
  102.1 22.0 %collective-permute-start.29 = (bf16[256,512]{1,0:T(8,128)(2,1)S(1)}, bf16[256,512]{1,0:T(8,128)(2,1)S(1)}, u32[]{:S(2)}, u32[]{:S(2)}) collective-permute-start(bf16[256,512]{1,0:T(8,128)(2,1)S(1)} %get-tuple-element.231), channel_id=1, source_target_pairs={{0,3},{1,2},{2,1},{3,0},{4,7},{5,6},{6,5},{7,4},{8,11},{9,10},{10,... | collective-permute-start | bytes 786440 | tf_op jit(solution)/shard_map/ppermute | solution.py:883
  102.9 21.2 %collective-permute-start.24 = (bf16[3072,128]{1,0:T(8,128)(2,1)S(1)}, bf16[3072,128]{1,0:T(8,128)(2,1)S(1)}, u32[]{:S(2)}, u32[]{:S(2)}) collective-permute-start(bf16[3072,128]{1,0:T(8,128)(2,1)S(1)} %add_convert_fusion), channel_id=1, source_target_pairs={{0,4},{1,5},{2,6},{3,7},{4,0},{5,1},{6,2},{7,3},{8,12},{9,13},{10,... | collective-permute-start | bytes 2359304 | tf_op jit(solution)/shard_map/ppermute | solution.py:883
  104.2 19.9 %collective-permute-start.25 = (bf16[1536,128]{1,0:T(8,128)(2,1)S(1)}, bf16[1536,128]{1,0:T(8,128)(2,1)S(1)}, u32[]{:S(2)}, u32[]{:S(2)}) collective-permute-start(bf16[1536,128]{1,0:T(8,128)(2,1)S(1)} %add_convert_fusion.3), channel_id=1, source_target_pairs={{0,2},{1,3},{2,0},{3,1},{4,6},{5,7},{6,4},{7,5},{8,10},{9,11},{10,... | collective-permute-start | bytes 1179656 | tf_op jit(solution)/shard_map/ppermute | solution.py:883
  125.3 11.1 %collective-permute-start.34 = (bf16[1536,128]{1,0:T(8,128)(2,1)S(1)}, bf16[1536,128]{1,0:T(8,128)(2,1)S(1)}, u32[]{:S(2)}, u32[]{:S(2)}) collective-permute-start(bf16[1536,128]{1,0:T(8,128)(2,1)S(1)} %get-tuple-element.265), channel_id=1, source_target_pairs={{0,2},{1,3},{2,0},{3,1},{4,6},{5,7},{6,4},{7,5},{8,10},{9,11},{10,... | collective-permute-start | bytes 1179656 | tf_op jit(solution)/shard_map/ppermute | solution.py:883
  137.5 9.2 %collective-permute-start.38 = (bf16[576,128]{1,0:T(8,128)(2,1)S(1)}, bf16[576,128]{1,0:T(8,128)(2,1)S(1)}, u32[]{:S(2)}, u32[]{:S(2)}) collective-permute-start(bf16[576,128]{1,0:T(8,128)(2,1)S(1)} %pad_maximum_fusion.3), channel_id=1, source_target_pairs={{0,16},{1,17},{2,18},{3,19},{4,20},{5,21},{6,22},{7,23},{8,24},{9,... | collective-permute-start | bytes 442376 | tf_op jit(solution)/shard_map/ppermute | solution.py:883
  140.2 16.6 %collective-permute-start.31 = (bf16[4,336,128]{2,1,0:T(8,128)(2,1)S(1)}, bf16[4,336,128]{2,1,0:T(8,128)(2,1)S(1)}, u32[]{:S(2)}, u32[]{:S(2)}) collective-permute-start(bf16[4,336,128]{2,1,0:T(8,128)(2,1)S(1)} %copy-done.6), channel_id=1, source_target_pairs={{0,2},{1,3},{2,0},{3,1},{4,6},{5,7},{6,4},{7,5},{8,10},{9,11},{10,... | collective-permute-start | bytes 1032200 | tf_op jit(solution)/shard_map/ppermute | solution.py:883
  141.3 15.5 %collective-permute-start.32 = (bf16[4,336,128]{2,1,0:T(8,128)(2,1)S(1)}, bf16[4,336,128]{2,1,0:T(8,128)(2,1)S(1)}, u32[]{:S(2)}, u32[]{:S(2)}) collective-permute-start(bf16[4,336,128]{2,1,0:T(8,128)(2,1)S(1)} %copy-done.5), channel_id=1, source_target_pairs={{0,4},{1,5},{2,6},{3,7},{4,0},{5,1},{6,2},{7,3},{8,12},{9,13},{10,... | collective-permute-start | bytes 1032200 | tf_op jit(solution)/shard_map/ppermute | solution.py:883
  142.3 14.8 %collective-permute-start.33 = (bf16[4,336,128]{2,1,0:T(8,128)(2,1)S(1)}, bf16[4,336,128]{2,1,0:T(8,128)(2,1)S(1)}, u32[]{:S(2)}, u32[]{:S(2)}) collective-permute-start(bf16[4,336,128]{2,1,0:T(8,128)(2,1)S(1)} %get-tuple-element.263), channel_id=1, source_target_pairs={{0,6},{1,7},{2,4},{3,5},{4,2},{5,3},{6,0},{7,1},{8,14},{9,15},{10,... | collective-permute-start | bytes 1032200 | tf_op jit(solution)/shard_map/ppermute | solution.py:883
  146.7 10.1 %collective-permute-start.39 = (bf16[256,512]{1,0:T(8,128)(2,1)S(1)}, bf16[256,512]{1,0:T(8,128)(2,1)S(1)}, u32[]{:S(2)}, u32[]{:S(2)}) collective-permute-start(bf16[256,512]{1,0:T(8,128)(2,1)S(1)} %get-tuple-element.276), channel_id=1, source_target_pairs={{0,1},{1,0},{2,3},{3,2},{4,5},{5,4},{6,7},{7,6},{8,9},{9,8},{10,11... | collective-permute-start | bytes 786440 | tf_op jit(solution)/shard_map/ppermute | solution.py:883
  157.1 11.4 %collective-permute-start.43 = (bf16[256,512]{1,0:T(8,128)(2,1)S(1)}, bf16[256,512]{1,0:T(8,128)(2,1)S(1)}, u32[]{:S(2)}, u32[]{:S(2)}) collective-permute-start(bf16[256,512]{1,0:T(8,128)(2,1)S(1)} %get-tuple-element.286), channel_id=1, source_target_pairs={{0,2},{1,3},{2,0},{3,1},{4,6},{5,7},{6,4},{7,5},{8,10},{9,11},{10,... | collective-permute-start | bytes 786440 | tf_op jit(solution)/shard_map/ppermute | solution.py:883
  158.2 10.3 %collective-permute-start.44 = (bf16[256,512]{1,0:T(8,128)(2,1)S(1)}, bf16[256,512]{1,0:T(8,128)(2,1)S(1)}, u32[]{:S(2)}, u32[]{:S(2)}) collective-permute-start(bf16[256,512]{1,0:T(8,128)(2,1)S(1)} %get-tuple-element.287), channel_id=1, source_target_pairs={{0,3},{1,2},{2,1},{3,0},{4,7},{5,6},{6,5},{7,4},{8,11},{9,10},{10,... | collective-permute-start | bytes 786440 | tf_op jit(solution)/shard_map/ppermute | solution.py:883
  159.4 9.1 %collective-permute-start.41 = (bf16[1,336,128]{2,1,0:T(8,128)(2,1)S(1)}, bf16[1,336,128]{2,1,0:T(8,128)(2,1)S(1)}, u32[]{:S(2)}, u32[]{:S(2)}) collective-permute-start(bf16[1,336,128]{2,1,0:T(8,128)(2,1)S(1)} %get-tuple-element.337), channel_id=1, source_target_pairs={{0,8},{1,9},{2,10},{3,11},{4,12},{5,13},{6,14},{7,15},{8,0},{9,1},... | collective-permute-start | bytes 258056 | tf_op jit(solution)/shard_map/ppermute | solution.py:883
  159.5 8.9 %collective-permute-start.42 = (bf16[1,336,128]{2,1,0:T(8,128)(2,1)S(1)}, bf16[1,336,128]{2,1,0:T(8,128)(2,1)S(1)}, u32[]{:S(2)}, u32[]{:S(2)}) collective-permute-start(bf16[1,336,128]{2,1,0:T(8,128)(2,1)S(1)} %get-tuple-element.336), channel_id=1, source_target_pairs={{0,16},{1,17},{2,18},{3,19},{4,20},{5,21},{6,22},{7,23},{8,24},{9,... | collective-permute-start | bytes 258056 | tf_op jit(solution)/shard_map/ppermute | solution.py:883
  (26 other events, 225.3 us)

commit v10 on v9

--- a/solution.py
+++ b/solution.py
@@ -790,7 +790,7 @@
     for vector, ref in enumerate(vectors):
         size = plan.owned[vector]
         slot = lax.rem(info_ref[1], LANE // size)
-        row = pltpu.roll(small, LANE - slot * size, 1)
+        row = pltpu.roll(small, lax.rem(LANE - slot * size, LANE), 1)
         ref[...] = row[vector : vector + 1, :size]
 
 

time: 172 us -> 172 us (level)
  no operation moved by 1% of the time
where the time goes in v10:
time: 172 us; the launch traced here: 171 us
  Pallas kernels  66.5 us (39%)
  waiting for transfers between devices  53.5 us (31%)
  starting transfers between devices  43.3 us (25%)
  other arithmetic  5.81 us (3%)
    ppermute x45, waiting for transfers between devices, swap(): lax.ppermute(value, AXES, [(d, d ^ mask) for d in range(devices)])  53.5 us
    ppermute x45, starting transfers between devices, swap(): lax.ppermute(value, AXES, [(d, d ^ mask) for d in range(devices)])  43.3 us
    pallas_call x1, Pallas kernels, feed(): pl.pallas_call(functools.partial(feed_kernel, plan, count), grid_spec=plt...  24.2 us
    pallas_call x1, Pallas kernels, attend_back(): pl.pallas_call(functools.partial(attend_back_kernel, plan, count), grid_s...  19.1 us
    pallas_call x1, Pallas kernels, attend(): pl.pallas_call(functools.partial(attend_kernel, plan, count), grid_spec=p...  14.3 us
  transfers between devices with their start and end apart: 45, of which 17 were waited for; matrix products, arithmetic and copies ran while one was open for 2% of the time, Pallas kernels for 22%

profile of v10, /device:TPU:0, one launch (start us, length us, event | category | flops | bytes accessed | tf_op | source)
XLA Modules:
  0.0 171.3 jit_solution(17574837127683944102)
XLA Ops:
  0.7 2.3 %pack.1 = (bf16[256,512]{1,0:T(8,128)(2,1)S(1)}, bf16[256,512]{1,0:T(8,128)(2,1)S(1)}, bf16[256,512]{1,0:T(8,128)(2,1)S(1)}, bf16[256,512]{1,0:T(8,128)(2,1)S(1)...) custom-call(bf16[4,256,512]{2,1,0:T(8,128)(2,1)} %bitcast.41, bf16[16,1024]{1,0:T(8,128)(2,1)} %bitcast.43, ...), custom_call_target="tpu_custom_call" | custom-call | bytes 4194304 | tf_op jit(solution)/shard_map/pack/pallas_call | solution.py:751
  3.5 2.6 %collective-permute-start.4 = (bf16[256,512]{1,0:T(8,128)(2,1)S(1)}, bf16[256,512]{1,0:T(8,128)(2,1)S(1)}, u32[]{:S(2)}, u32[]{:S(2)}) collective-permute-start(bf16[256,512]{1,0:T(8,128)(2,1)S(1)} %get-tuple-element.169), channel_id=1, source_target_pairs={{0,2},{1,3},{2,0},{3,1},{4,6},{5,7},{6,4},{7,5},{8,10},{9,11},{10,... | collective-permute-start | bytes 786440 | tf_op jit(solution)/shard_map/ppermute | solution.py:883
  6.1 3.8 %collective-permute-start.1 = (bf16[1,336,128]{2,1,0:T(8,128)(2,1)S(1)}, bf16[1,336,128]{2,1,0:T(8,128)(2,1)S(1)}, u32[]{:S(2)}, u32[]{:S(2)}) collective-permute-start(bf16[1,336,128]{2,1,0:T(8,128)(2,1)S(1)} %get-tuple-element.172), channel_id=1, source_target_pairs={{0,24},{1,25},{2,26},{3,27},{4,28},{5,29},{6,30},{7,31},{8,16},{9,... | collective-permute-start | bytes 258056 | tf_op jit(solution)/shard_map/ppermute | solution.py:883
  10.5 2.7 %collective-permute-done.4.refs_2_ = bf16[256,512]{1,0:T(8,128)(2,1)S(1)} collective-permute-done((bf16[256,512]{1,0:T(8,128)(2,1)S(1)}, bf16[256,512]{1,0:T(8,128)(2,1)S(1)}, u32[]{:S(2)}, u32[]{:S(2)}) %collective-permute-start.4) | collective-permute-done | bytes 262176 | tf_op jit(solution)/shard_map/ppermute | solution.py:883
  13.2 5.1 %collective-permute-done.5.refs_3_ = bf16[256,512]{1,0:T(8,128)(2,1)S(1)} collective-permute-done((bf16[256,512]{1,0:T(8,128)(2,1)S(1)}, bf16[256,512]{1,0:T(8,128)(2,1)S(1)}, u32[]{:S(2)}, u32[]{:S(2)}) %collective-permute-start.5) | collective-permute-done | bytes 262176 | tf_op jit(solution)/shard_map/ppermute | solution.py:883
  18.3 1.7 %collective-permute-start.10 = (bf16[1,576,128]{2,1,0:T(8,128)(2,1)S(1)}, bf16[1,576,128]{2,1,0:T(8,128)(2,1)S(1)}, u32[]{:S(2)}, u32[]{:S(2)}) collective-permute-start(bf16[1,576,128]{2,1,0:T(8,128)(2,1)S(1)} %get-tuple-element.192), channel_id=1, source_target_pairs={{0,8},{1,9},{2,10},{3,11},{4,12},{5,13},{6,14},{7,15},{8,0},{9,1},... | collective-permute-start | bytes 442376 | tf_op jit(solution)/shard_map/ppermute | solution.py:883
  20.1 1.6 collective-permute-start.6
  21.7 1.5 collective-permute-start.7
  23.7 2.6 %collective-permute-start.11 = (bf16[1,576,128]{2,1,0:T(8,128)(2,1)S(1)}, bf16[1,576,128]{2,1,0:T(8,128)(2,1)S(1)}, u32[]{:S(2)}, u32[]{:S(2)}) collective-permute-start(bf16[1,576,128]{2,1,0:T(8,128)(2,1)S(1)} %get-tuple-element.192), channel_id=1, source_target_pairs={{0,16},{1,17},{2,18},{3,19},{4,20},{5,21},{6,22},{7,23},{8,24},{9,... | collective-permute-start | bytes 442376 | tf_op jit(solution)/shard_map/ppermute | solution.py:883
  26.3 1.8 %collective-permute-start.9 = (bf16[1,576,128]{2,1,0:T(8,128)(2,1)S(1)}, bf16[1,576,128]{2,1,0:T(8,128)(2,1)S(1)}, u32[]{:S(2)}, u32[]{:S(2)}) collective-permute-start(bf16[1,576,128]{2,1,0:T(8,128)(2,1)S(1)} %get-tuple-element.192), channel_id=1, source_target_pairs={{0,24},{1,25},{2,26},{3,27},{4,28},{5,29},{6,30},{7,31},{8,16},{9,... | collective-permute-start | bytes 442376 | tf_op jit(solution)/shard_map/ppermute | solution.py:883
  28.7 2.2 %cut_rows.1 = (bf16[256,512]{1,0:T(8,128)(2,1)}, bf16[256,512]{1,0:T(8,128)(2,1)}, bf16[256,512]{1,0:T(8,128)(2,1)}, bf16[256,512]{1,0:T(8,128)(2,1)}) custom-call(bf16[4,256,512]{2,1,0:T(8,128)(2,1)} %bitcast.42), custom_call_target="tpu_custom_call" | custom-call | bytes 4194304 | tf_op jit(solution)/shard_map/cut_rows/pallas_call | solution.py:856
  31.7 4.5 %collective-permute-done.11 = bf16[1,576,128]{2,1,0:T(8,128)(2,1)S(1)} collective-permute-done((bf16[1,576,128]{2,1,0:T(8,128)(2,1)S(1)}, bf16[1,576,128]{2,1,0:T(8,128)(2,1)S(1)}, u32[]{:S(2)}, u32[]{:S(2)}) %collective-permute-start.11) | collective-permute-done | bytes 147488 | tf_op jit(solution)/shard_map/ppermute | solution.py:883
  36.2 2.5 %collective-permute-done.7 = bf16[4,336,128]{2,1,0:T(8,128)(2,1)S(1)} collective-permute-done((bf16[4,336,128]{2,1,0:T(8,128)(2,1)S(1)}, bf16[4,336,128]{2,1,0:T(8,128)(2,1)S(1)}, u32[]{:S(2)}, u32[]{:S(2)}) %collective-permute-start.7) | collective-permute-done | bytes 344096 | tf_op jit(solution)/shard_map/ppermute | solution.py:883
  41.8 1.6 collective-permute-done.16.refs_1_
  43.4 11.6 %collective-permute-done.14.refs_5_ = bf16[4,576,128]{2,1,0:T(8,128)(2,1)S(1)} collective-permute-done((bf16[4,576,128]{2,1,0:T(8,128)(2,1)S(1)}, bf16[4,576,128]{2,1,0:T(8,128)(2,1)S(1)}, u32[]{:S(2)}, u32[]{:S(2)}) %collective-permute-start.14) | collective-permute-done | bytes 589856 | tf_op jit(solution)/shard_map/ppermute | solution.py:883
  57.3 1.5 collective-permute-start.20
  58.8 14.3 %attend.1 = (f32[1024,512]{1,0:T(8,128)}, bf16[1024,512]{1,0:T(8,128)(2,1)}, bf16[1024,512]{1,0:T(8,128)(2,1)}, bf16[1024,512]{1,0:T(8,128)(2,1)}, bf16[1024,512...) custom-call(s32[4]{0:T(128)S(1)} %pad_add_fusion.info_ref, ...), custom_call_target="tpu_custom_call" | custom-call | flops 5000000000 | bytes 14680064 | tf_op jit(solution)/shard_map/attend/pallas_call | solution.py:250
  73.9 1.6 collective-permute-done.22.refs_11_
  75.5 24.2 %feed.1 = (bf16[256,512]{1,0:T(8,128)(2,1)S(1)}, bf16[256,512]{1,0:T(8,128)(2,1)S(1)}, bf16[256,512]{1,0:T(8,128)(2,1)S(1)}, bf16[256,512]{1,0:T(8,128)(2,1)S(1)...) custom-call(s32[4]{0:T(128)} %copy-done.1, ...), custom_call_target="tpu_custom_call" | custom-call | flops 15000000512 | bytes 20971520 | tf_op jit(solution)/shard_map/feed/pallas_call | solution.py:482
  100.6 1.5 collective-permute-start.28
  105.0 19.1 %attend_back.1 = (bf16[256,512]{1,0:T(8,128)(2,1)S(1)}, bf16[256,512]{1,0:T(8,128)(2,1)S(1)}, bf16[256,512]{1,0:T(8,128)(2,1)S(1)}, bf16[256,512]{1,0:T(8,128)(2...) custom-call(s32[4]{0:T(128)S(1)} %copy-done.2, f32[1024,512]{1,0:T(8,128)} %get-tuple-element.202.lifted_ref, ...), custom_call_target="tpu_custom_call" | custom-call | flops 14000000000 | bytes 25165824 | tf_op jit(solution)/shard_map/attend_back/pallas_call | solution.py:676
  128.7 2.9 %settle_rows.1 = bf16[4,256,512]{2,1,0:T(8,128)(2,1)} custom-call(s32[4]{0:T(128)} %copy-done.1, bf16[256,512]{1,0:T(8,128)(2,1)} %copy-done, bf16[256,512]{1,0:T(8,128)(2,1)} %collective-permute-done.27.refs_1_, bf16[256,512]{1,0:T(8,128)(2,1)} %copy-done.7, bf16[256,512]{1,0:T(8,128)(2,1)} %copy-done.8), custom_call_target="tpu_custom_call" | custom-call | bytes 50331648 | tf_op jit(solution)/shard_map/settle_rows/pallas_call | solution.py:834
  131.6 1.6 collective-permute-done.35
  133.1 3.3 %collective-permute-done.34 = bf16[1536,128]{1,0:T(8,128)(2,1)S(1)} collective-permute-done((bf16[1536,128]{1,0:T(8,128)(2,1)S(1)}, bf16[1536,128]{1,0:T(8,128)(2,1)S(1)}, u32[]{:S(2)}, u32[]{:S(2)}) %collective-permute-start.34) | collective-permute-done | bytes 393248 | tf_op jit(solution)/shard_map/ppermute | solution.py:883
  137.5 2.7 %collective-permute-start.38 = (bf16[576,128]{1,0:T(8,128)(2,1)S(1)}, bf16[576,128]{1,0:T(8,128)(2,1)S(1)}, u32[]{:S(2)}, u32[]{:S(2)}) collective-permute-start(bf16[576,128]{1,0:T(8,128)(2,1)S(1)} %pad_maximum_fusion.3), channel_id=1, source_target_pairs={{0,16},{1,17},{2,18},{3,19},{4,20},{5,21},{6,22},{7,23},{8,24},{9,... | collective-permute-start | bytes 442376 | tf_op jit(solution)/shard_map/ppermute | solution.py:883
  144.2 2.5 %collective-permute-done.38.refs_7_ = bf16[576,128]{1,0:T(8,128)(2,1)S(1)} collective-permute-done((bf16[576,128]{1,0:T(8,128)(2,1)S(1)}, bf16[576,128]{1,0:T(8,128)(2,1)S(1)}, u32[]{:S(2)}, u32[]{:S(2)}) %collective-permute-start.38) | collective-permute-done | bytes 147488 | tf_op jit(solution)/shard_map/ppermute | solution.py:883
  146.7 3.0 %collective-permute-done.37.refs_6_ = bf16[576,128]{1,0:T(8,128)(2,1)S(1)} collective-permute-done((bf16[576,128]{1,0:T(8,128)(2,1)S(1)}, bf16[576,128]{1,0:T(8,128)(2,1)S(1)}, u32[]{:S(2)}, u32[]{:S(2)}) %collective-permute-start.37) | collective-permute-done | bytes 147488 | tf_op jit(solution)/shard_map/ppermute | solution.py:883
  150.7 6.1 %collective-permute-done.36.refs_5_ = bf16[576,128]{1,0:T(8,128)(2,1)S(1)} collective-permute-done((bf16[576,128]{1,0:T(8,128)(2,1)S(1)}, bf16[576,128]{1,0:T(8,128)(2,1)S(1)}, u32[]{:S(2)}, u32[]{:S(2)}) %collective-permute-start.36) | collective-permute-done | bytes 147488 | tf_op jit(solution)/shard_map/ppermute | solution.py:883
  159.5 3.3 %collective-permute-start.42 = (bf16[1,336,128]{2,1,0:T(8,128)(2,1)S(1)}, bf16[1,336,128]{2,1,0:T(8,128)(2,1)S(1)}, u32[]{:S(2)}, u32[]{:S(2)}) collective-permute-start(bf16[1,336,128]{2,1,0:T(8,128)(2,1)S(1)} %get-tuple-element.336), channel_id=1, source_target_pairs={{0,16},{1,17},{2,18},{3,19},{4,20},{5,21},{6,22},{7,23},{8,24},{9,... | collective-permute-start | bytes 258056 | tf_op jit(solution)/shard_map/ppermute | solution.py:883
  162.8 2.9 %collective-permute-done.40.refs_1_ = bf16[1,336,128]{2,1,0:T(8,128)(2,1)S(1)} collective-permute-done((bf16[1,336,128]{2,1,0:T(8,128)(2,1)S(1)}, bf16[1,336,128]{2,1,0:T(8,128)(2,1)S(1)}, u32[]{:S(2)}, u32[]{:S(2)}) %collective-permute-start.40) | collective-permute-done | bytes 86048 | tf_op jit(solution)/shard_map/ppermute | solution.py:883
  165.8 2.7 %collective-permute-done.41.refs_2_ = bf16[1,336,128]{2,1,0:T(8,128)(2,1)S(1)} collective-permute-done((bf16[1,336,128]{2,1,0:T(8,128)(2,1)S(1)}, bf16[1,336,128]{2,1,0:T(8,128)(2,1)S(1)}, u32[]{:S(2)}, u32[]{:S(2)}) %collective-permute-start.41) | collective-permute-done | bytes 86048 | tf_op jit(solution)/shard_map/ppermute | solution.py:883
  169.7 1.5 finish.1
  (119 shorter events, 27.2 us)
Async XLA Ops:
  3.5 9.7 %collective-permute-start.4 = (bf16[256,512]{1,0:T(8,128)(2,1)S(1)}, bf16[256,512]{1,0:T(8,128)(2,1)S(1)}, u32[]{:S(2)}, u32[]{:S(2)}) collective-permute-start(bf16[256,512]{1,0:T(8,128)(2,1)S(1)} %get-tuple-element.169), channel_id=1, source_target_pairs={{0,2},{1,3},{2,0},{3,1},{4,6},{5,7},{6,4},{7,5},{8,10},{9,11},{10,... | collective-permute-start | bytes 786440 | tf_op jit(solution)/shard_map/ppermute | solution.py:883
  6.1 12.3 %collective-permute-start.5 = (bf16[256,512]{1,0:T(8,128)(2,1)S(1)}, bf16[256,512]{1,0:T(8,128)(2,1)S(1)}, u32[]{:S(2)}, u32[]{:S(2)}) collective-permute-start(bf16[256,512]{1,0:T(8,128)(2,1)S(1)} %get-tuple-element.170), channel_id=1, source_target_pairs={{0,3},{1,2},{2,1},{3,0},{4,7},{5,6},{6,5},{7,4},{8,11},{9,10},{10,... | collective-permute-start | bytes 786440 | tf_op jit(solution)/shard_map/ppermute | solution.py:883
  6.1 12.2 %collective-permute-start.1 = (bf16[1,336,128]{2,1,0:T(8,128)(2,1)S(1)}, bf16[1,336,128]{2,1,0:T(8,128)(2,1)S(1)}, u32[]{:S(2)}, u32[]{:S(2)}) collective-permute-start(bf16[1,336,128]{2,1,0:T(8,128)(2,1)S(1)} %get-tuple-element.172), channel_id=1, source_target_pairs={{0,24},{1,25},{2,26},{3,27},{4,28},{5,29},{6,30},{7,31},{8,16},{9,... | collective-permute-start | bytes 258056 | tf_op jit(solution)/shard_map/ppermute | solution.py:883
  10.0 8.3 %collective-permute-start.2 = (bf16[1,336,128]{2,1,0:T(8,128)(2,1)S(1)}, bf16[1,336,128]{2,1,0:T(8,128)(2,1)S(1)}, u32[]{:S(2)}, u32[]{:S(2)}) collective-permute-start(bf16[1,336,128]{2,1,0:T(8,128)(2,1)S(1)} %get-tuple-element.172), channel_id=1, source_target_pairs={{0,8},{1,9},{2,10},{3,11},{4,12},{5,13},{6,14},{7,15},{8,0},{9,1},... | collective-permute-start | bytes 258056 | tf_op jit(solution)/shard_map/ppermute | solution.py:883
  20.1 16.1 %collective-permute-start.6 = (bf16[4,336,128]{2,1,0:T(8,128)(2,1)S(1)}, bf16[4,336,128]{2,1,0:T(8,128)(2,1)S(1)}, u32[]{:S(2)}, u32[]{:S(2)}) collective-permute-start(bf16[4,336,128]{2,1,0:T(8,128)(2,1)S(1)} %constant_dynamic-update-slice_fusion), channel_id=1, source_target_pairs={{0,2},{1,3},{2,0},{3,1},{4,6},{5,7},{6,4},{7,5},{8,10},{9,11},{10,... | collective-permute-start | bytes 1032200 | tf_op jit(solution)/shard_map/ppermute | solution.py:883
  21.7 17.1 %collective-permute-start.7 = (bf16[4,336,128]{2,1,0:T(8,128)(2,1)S(1)}, bf16[4,336,128]{2,1,0:T(8,128)(2,1)S(1)}, u32[]{:S(2)}, u32[]{:S(2)}) collective-permute-start(bf16[4,336,128]{2,1,0:T(8,128)(2,1)S(1)} %constant_dynamic-update-slice_fusion), channel_id=1, source_target_pairs={{0,4},{1,5},{2,6},{3,7},{4,0},{5,1},{6,2},{7,3},{8,12},{9,13},{10,... | collective-permute-start | bytes 1032200 | tf_op jit(solution)/shard_map/ppermute | solution.py:883
  23.2 15.5 %collective-permute-start.8 = (bf16[4,336,128]{2,1,0:T(8,128)(2,1)S(1)}, bf16[4,336,128]{2,1,0:T(8,128)(2,1)S(1)}, u32[]{:S(2)}, u32[]{:S(2)}) collective-permute-start(bf16[4,336,128]{2,1,0:T(8,128)(2,1)S(1)} %constant_dynamic-update-slice_fusion), channel_id=1, source_target_pairs={{0,6},{1,7},{2,4},{3,5},{4,2},{5,3},{6,0},{7,1},{8,14},{9,15},{10,... | collective-permute-start | bytes 1032200 | tf_op jit(solution)/shard_map/ppermute | solution.py:883
  23.7 12.5 %collective-permute-start.11 = (bf16[1,576,128]{2,1,0:T(8,128)(2,1)S(1)}, bf16[1,576,128]{2,1,0:T(8,128)(2,1)S(1)}, u32[]{:S(2)}, u32[]{:S(2)}) collective-permute-start(bf16[1,576,128]{2,1,0:T(8,128)(2,1)S(1)} %get-tuple-element.192), channel_id=1, source_target_pairs={{0,16},{1,17},{2,18},{3,19},{4,20},{5,21},{6,22},{7,23},{8,24},{9,... | collective-permute-start | bytes 442376 | tf_op jit(solution)/shard_map/ppermute | solution.py:883
  26.3 9.9 %collective-permute-start.9 = (bf16[1,576,128]{2,1,0:T(8,128)(2,1)S(1)}, bf16[1,576,128]{2,1,0:T(8,128)(2,1)S(1)}, u32[]{:S(2)}, u32[]{:S(2)}) collective-permute-start(bf16[1,576,128]{2,1,0:T(8,128)(2,1)S(1)} %get-tuple-element.192), channel_id=1, source_target_pairs={{0,24},{1,25},{2,26},{3,27},{4,28},{5,29},{6,30},{7,31},{8,16},{9,... | collective-permute-start | bytes 442376 | tf_op jit(solution)/shard_map/ppermute | solution.py:883
  39.0 17.0 %collective-permute-start.12 = (bf16[16,336,128]{2,1,0:T(8,128)(2,1)S(1)}, bf16[16,336,128]{2,1,0:T(8,128)(2,1)S(1)}, u32[]{:S(2)}, u32[]{:S(2)}) collective-permute-start(bf16[16,336,128]{2,1,0:T(8,128)(2,1)S(1)} %constant_dynamic-update-slice_fusion.4.refs_4_), channel_id=1, source_target_pairs={{0,1},{1,0},{2,3},{3,2},{4,5},{5,4},{6,7},{7,6},{8,9},{9,8},{10,11... | collective-permute-start | bytes 4128776 | tf_op jit(solution)/shard_map/ppermute | solution.py:883
  39.7 15.3 %collective-permute-start.14 = (bf16[4,576,128]{2,1,0:T(8,128)(2,1)S(1)}, bf16[4,576,128]{2,1,0:T(8,128)(2,1)S(1)}, u32[]{:S(2)}, u32[]{:S(2)}) collective-permute-start(bf16[4,576,128]{2,1,0:T(8,128)(2,1)S(1)} %constant_dynamic-update-slice_fusion.8.refs_4_), channel_id=1, source_target_pairs={{0,2},{1,3},{2,0},{3,1},{4,6},{5,7},{6,4},{7,5},{8,10},{9,11},{10,... | collective-permute-start | bytes 1769480 | tf_op jit(solution)/shard_map/ppermute | solution.py:883
  40.9 15.0 %collective-permute-start.15 = (bf16[4,576,128]{2,1,0:T(8,128)(2,1)S(1)}, bf16[4,576,128]{2,1,0:T(8,128)(2,1)S(1)}, u32[]{:S(2)}, u32[]{:S(2)}) collective-permute-start(bf16[4,576,128]{2,1,0:T(8,128)(2,1)S(1)} %constant_dynamic-update-slice_fusion.8.refs_4_), channel_id=1, source_target_pairs={{0,4},{1,5},{2,6},{3,7},{4,0},{5,1},{6,2},{7,3},{8,12},{9,13},{10,... | collective-permute-start | bytes 1769480 | tf_op jit(solution)/shard_map/ppermute | solution.py:883
  56.0 17.2 %collective-permute-start.17 = (bf16[4,576,128]{2,1,0:T(8,128)(2,1)S(1)}, bf16[4,576,128]{2,1,0:T(8,128)(2,1)S(1)}, u32[]{:S(2)}, u32[]{:S(2)}) collective-permute-start(bf16[4,576,128]{2,1,0:T(8,128)(2,1)S(1)} %collective-permute-done.14.refs_5_), channel_id=1, source_target_pairs={{0,4},{1,5},{2,6},{3,7},{4,0},{5,1},{6,2},{7,3},{8,12},{9,13},{10,... | collective-permute-start | bytes 1769480 | tf_op jit(solution)/shard_map/ppermute | solution.py:883
  56.8 16.3 %collective-permute-start.18 = (bf16[4,576,128]{2,1,0:T(8,128)(2,1)S(1)}, bf16[4,576,128]{2,1,0:T(8,128)(2,1)S(1)}, u32[]{:S(2)}, u32[]{:S(2)}) collective-permute-start(bf16[4,576,128]{2,1,0:T(8,128)(2,1)S(1)} %collective-permute-done.14.refs_5_), channel_id=1, source_target_pairs={{0,1},{1,0},{2,3},{3,2},{4,5},{5,4},{6,7},{7,6},{8,9},{9,8},{10,11... | collective-permute-start | bytes 1769480 | tf_op jit(solution)/shard_map/ppermute | solution.py:883
  56.8 16.4 %collective-permute-start.19 = (bf16[4,576,128]{2,1,0:T(8,128)(2,1)S(1)}, bf16[4,576,128]{2,1,0:T(8,128)(2,1)S(1)}, u32[]{:S(2)}, u32[]{:S(2)}) collective-permute-start(bf16[4,576,128]{2,1,0:T(8,128)(2,1)S(1)} %collective-permute-done.15.refs_6_), channel_id=1, source_target_pairs={{0,1},{1,0},{2,3},{3,2},{4,5},{5,4},{6,7},{7,6},{8,9},{9,8},{10,11... | collective-permute-start | bytes 1769480 | tf_op jit(solution)/shard_map/ppermute | solution.py:883
  57.3 15.8 %collective-permute-start.20 = (bf16[256,512]{1,0:T(8,128)(2,1)S(1)}, bf16[256,512]{1,0:T(8,128)(2,1)S(1)}, u32[]{:S(2)}, u32[]{:S(2)}) collective-permute-start(bf16[256,512]{1,0:T(8,128)(2,1)S(1)} %copy-done.10), channel_id=1, source_target_pairs={{0,2},{1,3},{2,0},{3,1},{4,6},{5,7},{6,4},{7,5},{8,10},{9,11},{10,... | collective-permute-start | bytes 786440 | tf_op jit(solution)/shard_map/ppermute | solution.py:883
  58.8 14.3 %collective-permute-start.21 = (bf16[256,512]{1,0:T(8,128)(2,1)S(1)}, bf16[256,512]{1,0:T(8,128)(2,1)S(1)}, u32[]{:S(2)}, u32[]{:S(2)}) collective-permute-start(bf16[256,512]{1,0:T(8,128)(2,1)S(1)} %copy-done.9), channel_id=1, source_target_pairs={{0,3},{1,2},{2,1},{3,0},{4,7},{5,6},{6,5},{7,4},{8,11},{9,10},{10,... | collective-permute-start | bytes 786440 | tf_op jit(solution)/shard_map/ppermute | solution.py:883
  100.1 24.0 %collective-permute-start.26 = (bf16[4608,128]{1,0:T(8,128)(2,1)S(1)}, bf16[4608,128]{1,0:T(8,128)(2,1)S(1)}, u32[]{:S(2)}, u32[]{:S(2)}) collective-permute-start(bf16[4608,128]{1,0:T(8,128)(2,1)S(1)} %get-tuple-element.227), channel_id=1, source_target_pairs={{0,1},{1,0},{2,3},{3,2},{4,5},{5,4},{6,7},{7,6},{8,9},{9,8},{10,11... | collective-permute-start | bytes 3538952 | tf_op jit(solution)/shard_map/ppermute | solution.py:883
  100.6 23.5 %collective-permute-start.28 = (bf16[256,512]{1,0:T(8,128)(2,1)S(1)}, bf16[256,512]{1,0:T(8,128)(2,1)S(1)}, u32[]{:S(2)}, u32[]{:S(2)}) collective-permute-start(bf16[256,512]{1,0:T(8,128)(2,1)S(1)} %get-tuple-element.230), channel_id=1, source_target_pairs={{0,2},{1,3},{2,0},{3,1},{4,6},{5,7},{6,4},{7,5},{8,10},{9,11},{10,... | collective-permute-start | bytes 786440 | tf_op jit(solution)/shard_map/ppermute | solution.py:883
  102.1 22.0 %collective-permute-start.29 = (bf16[256,512]{1,0:T(8,128)(2,1)S(1)}, bf16[256,512]{1,0:T(8,128)(2,1)S(1)}, u32[]{:S(2)}, u32[]{:S(2)}) collective-permute-start(bf16[256,512]{1,0:T(8,128)(2,1)S(1)} %get-tuple-element.231), channel_id=1, source_target_pairs={{0,3},{1,2},{2,1},{3,0},{4,7},{5,6},{6,5},{7,4},{8,11},{9,10},{10,... | collective-permute-start | bytes 786440 | tf_op jit(solution)/shard_map/ppermute | solution.py:883
  102.9 21.2 %collective-permute-start.24 = (bf16[3072,128]{1,0:T(8,128)(2,1)S(1)}, bf16[3072,128]{1,0:T(8,128)(2,1)S(1)}, u32[]{:S(2)}, u32[]{:S(2)}) collective-permute-start(bf16[3072,128]{1,0:T(8,128)(2,1)S(1)} %add_convert_fusion), channel_id=1, source_target_pairs={{0,4},{1,5},{2,6},{3,7},{4,0},{5,1},{6,2},{7,3},{8,12},{9,13},{10,... | collective-permute-start | bytes 2359304 | tf_op jit(solution)/shard_map/ppermute | solution.py:883
  104.2 19.9 %collective-permute-start.25 = (bf16[1536,128]{1,0:T(8,128)(2,1)S(1)}, bf16[1536,128]{1,0:T(8,128)(2,1)S(1)}, u32[]{:S(2)}, u32[]{:S(2)}) collective-permute-start(bf16[1536,128]{1,0:T(8,128)(2,1)S(1)} %add_convert_fusion.3), channel_id=1, source_target_pairs={{0,2},{1,3},{2,0},{3,1},{4,6},{5,7},{6,4},{7,5},{8,10},{9,11},{10,... | collective-permute-start | bytes 1179656 | tf_op jit(solution)/shard_map/ppermute | solution.py:883
  125.3 11.1 %collective-permute-start.34 = (bf16[1536,128]{1,0:T(8,128)(2,1)S(1)}, bf16[1536,128]{1,0:T(8,128)(2,1)S(1)}, u32[]{:S(2)}, u32[]{:S(2)}) collective-permute-start(bf16[1536,128]{1,0:T(8,128)(2,1)S(1)} %get-tuple-element.265), channel_id=1, source_target_pairs={{0,2},{1,3},{2,0},{3,1},{4,6},{5,7},{6,4},{7,5},{8,10},{9,11},{10,... | collective-permute-start | bytes 1179656 | tf_op jit(solution)/shard_map/ppermute | solution.py:883
  137.5 9.2 %collective-permute-start.38 = (bf16[576,128]{1,0:T(8,128)(2,1)S(1)}, bf16[576,128]{1,0:T(8,128)(2,1)S(1)}, u32[]{:S(2)}, u32[]{:S(2)}) collective-permute-start(bf16[576,128]{1,0:T(8,128)(2,1)S(1)} %pad_maximum_fusion.3), channel_id=1, source_target_pairs={{0,16},{1,17},{2,18},{3,19},{4,20},{5,21},{6,22},{7,23},{8,24},{9,... | collective-permute-start | bytes 442376 | tf_op jit(solution)/shard_map/ppermute | solution.py:883
  140.2 16.6 %collective-permute-start.31 = (bf16[4,336,128]{2,1,0:T(8,128)(2,1)S(1)}, bf16[4,336,128]{2,1,0:T(8,128)(2,1)S(1)}, u32[]{:S(2)}, u32[]{:S(2)}) collective-permute-start(bf16[4,336,128]{2,1,0:T(8,128)(2,1)S(1)} %copy-done.6), channel_id=1, source_target_pairs={{0,2},{1,3},{2,0},{3,1},{4,6},{5,7},{6,4},{7,5},{8,10},{9,11},{10,... | collective-permute-start | bytes 1032200 | tf_op jit(solution)/shard_map/ppermute | solution.py:883
  141.3 15.5 %collective-permute-start.32 = (bf16[4,336,128]{2,1,0:T(8,128)(2,1)S(1)}, bf16[4,336,128]{2,1,0:T(8,128)(2,1)S(1)}, u32[]{:S(2)}, u32[]{:S(2)}) collective-permute-start(bf16[4,336,128]{2,1,0:T(8,128)(2,1)S(1)} %copy-done.5), channel_id=1, source_target_pairs={{0,4},{1,5},{2,6},{3,7},{4,0},{5,1},{6,2},{7,3},{8,12},{9,13},{10,... | collective-permute-start | bytes 1032200 | tf_op jit(solution)/shard_map/ppermute | solution.py:883
  142.3 14.8 %collective-permute-start.33 = (bf16[4,336,128]{2,1,0:T(8,128)(2,1)S(1)}, bf16[4,336,128]{2,1,0:T(8,128)(2,1)S(1)}, u32[]{:S(2)}, u32[]{:S(2)}) collective-permute-start(bf16[4,336,128]{2,1,0:T(8,128)(2,1)S(1)} %get-tuple-element.263), channel_id=1, source_target_pairs={{0,6},{1,7},{2,4},{3,5},{4,2},{5,3},{6,0},{7,1},{8,14},{9,15},{10,... | collective-permute-start | bytes 1032200 | tf_op jit(solution)/shard_map/ppermute | solution.py:883
  146.7 10.1 %collective-permute-start.39 = (bf16[256,512]{1,0:T(8,128)(2,1)S(1)}, bf16[256,512]{1,0:T(8,128)(2,1)S(1)}, u32[]{:S(2)}, u32[]{:S(2)}) collective-permute-start(bf16[256,512]{1,0:T(8,128)(2,1)S(1)} %get-tuple-element.276), channel_id=1, source_target_pairs={{0,1},{1,0},{2,3},{3,2},{4,5},{5,4},{6,7},{7,6},{8,9},{9,8},{10,11... | collective-permute-start | bytes 786440 | tf_op jit(solution)/shard_map/ppermute | solution.py:883
  157.1 11.4 %collective-permute-start.43 = (bf16[256,512]{1,0:T(8,128)(2,1)S(1)}, bf16[256,512]{1,0:T(8,128)(2,1)S(1)}, u32[]{:S(2)}, u32[]{:S(2)}) collective-permute-start(bf16[256,512]{1,0:T(8,128)(2,1)S(1)} %get-tuple-element.286), channel_id=1, source_target_pairs={{0,2},{1,3},{2,0},{3,1},{4,6},{5,7},{6,4},{7,5},{8,10},{9,11},{10,... | collective-permute-start | bytes 786440 | tf_op jit(solution)/shard_map/ppermute | solution.py:883
  158.2 10.3 %collective-permute-start.44 = (bf16[256,512]{1,0:T(8,128)(2,1)S(1)}, bf16[256,512]{1,0:T(8,128)(2,1)S(1)}, u32[]{:S(2)}, u32[]{:S(2)}) collective-permute-start(bf16[256,512]{1,0:T(8,128)(2,1)S(1)} %get-tuple-element.287), channel_id=1, source_target_pairs={{0,3},{1,2},{2,1},{3,0},{4,7},{5,6},{6,5},{7,4},{8,11},{9,10},{10,... | collective-permute-start | bytes 786440 | tf_op jit(solution)/shard_map/ppermute | solution.py:883
  159.4 9.1 %collective-permute-start.41 = (bf16[1,336,128]{2,1,0:T(8,128)(2,1)S(1)}, bf16[1,336,128]{2,1,0:T(8,128)(2,1)S(1)}, u32[]{:S(2)}, u32[]{:S(2)}) collective-permute-start(bf16[1,336,128]{2,1,0:T(8,128)(2,1)S(1)} %get-tuple-element.337), channel_id=1, source_target_pairs={{0,8},{1,9},{2,10},{3,11},{4,12},{5,13},{6,14},{7,15},{8,0},{9,1},... | collective-permute-start | bytes 258056 | tf_op jit(solution)/shard_map/ppermute | solution.py:883
  159.5 8.9 %collective-permute-start.42 = (bf16[1,336,128]{2,1,0:T(8,128)(2,1)S(1)}, bf16[1,336,128]{2,1,0:T(8,128)(2,1)S(1)}, u32[]{:S(2)}, u32[]{:S(2)}) collective-permute-start(bf16[1,336,128]{2,1,0:T(8,128)(2,1)S(1)} %get-tuple-element.336), channel_id=1, source_target_pairs={{0,16},{1,17},{2,18},{3,19},{4,20},{5,21},{6,22},{7,23},{8,24},{9,... | collective-permute-start | bytes 258056 | tf_op jit(solution)/shard_map/ppermute | solution.py:883
  (26 other events, 225.3 us)

commit v11 on v10

--- a/solution.py
+++ b/solution.py
@@ -883,7 +883,10 @@
         return lax.ppermute(value, AXES, [(d, d ^ mask) for d in range(devices)]) if mask else value
 
     def exchange(pieces):
-        return [swap(piece, mask) for mask, piece in enumerate(pieces)]
+        moved = list(pieces)
+        for mask in reversed(range(1, count)):
+            moved[mask] = swap(pieces[mask], mask)
+        return moved
 
     def in_order(pieces):
         if count != 4 or share != 1:
@@ -970,7 +973,8 @@
         )
         terms = fold(terms, 4)
         early_terms = [swap(term, mask) for term, mask in zip(terms, plan.z_order)]
-        token_pieces[2:] = [swap(token_pieces[mask], mask) for mask in (2, 3)]
+        for mask in (3, 2):
+            token_pieces[mask] = swap(token_pieces[mask], mask)
         early_terms, token_pieces = lax.optimization_barrier((early_terms, token_pieces))
         tokens_back = in_order(token_pieces)
         values = finish(plan, info, early_terms, late_terms)

time: 172 us -> 172 us (level)
  no operation moved by 1% of the time
where the time goes in v11:
time: 172 us; the launch traced here: 171 us
  Pallas kernels  66.5 us (39%)
  waiting for transfers between devices  53.5 us (31%)
  starting transfers between devices  43.3 us (25%)
  other arithmetic  5.81 us (3%)
    ppermute x45, waiting for transfers between devices, swap(): lax.ppermute(value, AXES, [(d, d ^ mask) for d in range(devices)])  53.5 us
    ppermute x45, starting transfers between devices, swap(): lax.ppermute(value, AXES, [(d, d ^ mask) for d in range(devices)])  43.3 us
    pallas_call x1, Pallas kernels, feed(): pl.pallas_call(functools.partial(feed_kernel, plan, count), grid_spec=plt...  24.2 us
    pallas_call x1, Pallas kernels, attend_back(): pl.pallas_call(functools.partial(attend_back_kernel, plan, count), grid_s...  19.1 us
    pallas_call x1, Pallas kernels, attend(): pl.pallas_call(functools.partial(attend_kernel, plan, count), grid_spec=p...  14.3 us
  transfers between devices with their start and end apart: 45, of which 17 were waited for; matrix products, arithmetic and copies ran while one was open for 2% of the time, Pallas kernels for 22%

profile of v11, /device:TPU:0, one launch (start us, length us, event | category | flops | bytes accessed | tf_op | source)
XLA Modules:
  0.0 171.3 jit_solution(17574837127683944102)
XLA Ops:
  0.7 2.3 %pack.1 = (bf16[256,512]{1,0:T(8,128)(2,1)S(1)}, bf16[256,512]{1,0:T(8,128)(2,1)S(1)}, bf16[256,512]{1,0:T(8,128)(2,1)S(1)}, bf16[256,512]{1,0:T(8,128)(2,1)S(1)...) custom-call(bf16[4,256,512]{2,1,0:T(8,128)(2,1)} %bitcast.41, bf16[16,1024]{1,0:T(8,128)(2,1)} %bitcast.43, ...), custom_call_target="tpu_custom_call" | custom-call | bytes 4194304 | tf_op jit(solution)/shard_map/pack/pallas_call | solution.py:751
  3.5 2.6 %collective-permute-start.4 = (bf16[256,512]{1,0:T(8,128)(2,1)S(1)}, bf16[256,512]{1,0:T(8,128)(2,1)S(1)}, u32[]{:S(2)}, u32[]{:S(2)}) collective-permute-start(bf16[256,512]{1,0:T(8,128)(2,1)S(1)} %get-tuple-element.169), channel_id=1, source_target_pairs={{0,2},{1,3},{2,0},{3,1},{4,6},{5,7},{6,4},{7,5},{8,10},{9,11},{10,... | collective-permute-start | bytes 786440 | tf_op jit(solution)/shard_map/ppermute | solution.py:883
  6.1 3.8 %collective-permute-start.1 = (bf16[1,336,128]{2,1,0:T(8,128)(2,1)S(1)}, bf16[1,336,128]{2,1,0:T(8,128)(2,1)S(1)}, u32[]{:S(2)}, u32[]{:S(2)}) collective-permute-start(bf16[1,336,128]{2,1,0:T(8,128)(2,1)S(1)} %get-tuple-element.172), channel_id=1, source_target_pairs={{0,24},{1,25},{2,26},{3,27},{4,28},{5,29},{6,30},{7,31},{8,16},{9,... | collective-permute-start | bytes 258056 | tf_op jit(solution)/shard_map/ppermute | solution.py:883
  10.5 2.7 %collective-permute-done.4.refs_2_ = bf16[256,512]{1,0:T(8,128)(2,1)S(1)} collective-permute-done((bf16[256,512]{1,0:T(8,128)(2,1)S(1)}, bf16[256,512]{1,0:T(8,128)(2,1)S(1)}, u32[]{:S(2)}, u32[]{:S(2)}) %collective-permute-start.4) | collective-permute-done | bytes 262176 | tf_op jit(solution)/shard_map/ppermute | solution.py:883
  13.2 5.1 %collective-permute-done.5.refs_3_ = bf16[256,512]{1,0:T(8,128)(2,1)S(1)} collective-permute-done((bf16[256,512]{1,0:T(8,128)(2,1)S(1)}, bf16[256,512]{1,0:T(8,128)(2,1)S(1)}, u32[]{:S(2)}, u32[]{:S(2)}) %collective-permute-start.5) | collective-permute-done | bytes 262176 | tf_op jit(solution)/shard_map/ppermute | solution.py:883
  18.3 1.7 %collective-permute-start.10 = (bf16[1,576,128]{2,1,0:T(8,128)(2,1)S(1)}, bf16[1,576,128]{2,1,0:T(8,128)(2,1)S(1)}, u32[]{:S(2)}, u32[]{:S(2)}) collective-permute-start(bf16[1,576,128]{2,1,0:T(8,128)(2,1)S(1)} %get-tuple-element.192), channel_id=1, source_target_pairs={{0,8},{1,9},{2,10},{3,11},{4,12},{5,13},{6,14},{7,15},{8,0},{9,1},... | collective-permute-start | bytes 442376 | tf_op jit(solution)/shard_map/ppermute | solution.py:883
  20.1 1.6 collective-permute-start.6
  21.7 1.5 collective-permute-start.7
  23.7 2.6 %collective-permute-start.11 = (bf16[1,576,128]{2,1,0:T(8,128)(2,1)S(1)}, bf16[1,576,128]{2,1,0:T(8,128)(2,1)S(1)}, u32[]{:S(2)}, u32[]{:S(2)}) collective-permute-start(bf16[1,576,128]{2,1,0:T(8,128)(2,1)S(1)} %get-tuple-element.192), channel_id=1, source_target_pairs={{0,16},{1,17},{2,18},{3,19},{4,20},{5,21},{6,22},{7,23},{8,24},{9,... | collective-permute-start | bytes 442376 | tf_op jit(solution)/shard_map/ppermute | solution.py:883
  26.3 1.8 %collective-permute-start.9 = (bf16[1,576,128]{2,1,0:T(8,128)(2,1)S(1)}, bf16[1,576,128]{2,1,0:T(8,128)(2,1)S(1)}, u32[]{:S(2)}, u32[]{:S(2)}) collective-permute-start(bf16[1,576,128]{2,1,0:T(8,128)(2,1)S(1)} %get-tuple-element.192), channel_id=1, source_target_pairs={{0,24},{1,25},{2,26},{3,27},{4,28},{5,29},{6,30},{7,31},{8,16},{9,... | collective-permute-start | bytes 442376 | tf_op jit(solution)/shard_map/ppermute | solution.py:883
  28.7 2.2 %cut_rows.1 = (bf16[256,512]{1,0:T(8,128)(2,1)}, bf16[256,512]{1,0:T(8,128)(2,1)}, bf16[256,512]{1,0:T(8,128)(2,1)}, bf16[256,512]{1,0:T(8,128)(2,1)}) custom-call(bf16[4,256,512]{2,1,0:T(8,128)(2,1)} %bitcast.42), custom_call_target="tpu_custom_call" | custom-call | bytes 4194304 | tf_op jit(solution)/shard_map/cut_rows/pallas_call | solution.py:856
  31.7 4.5 %collective-permute-done.11 = bf16[1,576,128]{2,1,0:T(8,128)(2,1)S(1)} collective-permute-done((bf16[1,576,128]{2,1,0:T(8,128)(2,1)S(1)}, bf16[1,576,128]{2,1,0:T(8,128)(2,1)S(1)}, u32[]{:S(2)}, u32[]{:S(2)}) %collective-permute-start.11) | collective-permute-done | bytes 147488 | tf_op jit(solution)/shard_map/ppermute | solution.py:883
  36.2 2.5 %collective-permute-done.7 = bf16[4,336,128]{2,1,0:T(8,128)(2,1)S(1)} collective-permute-done((bf16[4,336,128]{2,1,0:T(8,128)(2,1)S(1)}, bf16[4,336,128]{2,1,0:T(8,128)(2,1)S(1)}, u32[]{:S(2)}, u32[]{:S(2)}) %collective-permute-start.7) | collective-permute-done | bytes 344096 | tf_op jit(solution)/shard_map/ppermute | solution.py:883
  41.8 1.6 collective-permute-done.16.refs_1_
  43.4 11.6 %collective-permute-done.14.refs_5_ = bf16[4,576,128]{2,1,0:T(8,128)(2,1)S(1)} collective-permute-done((bf16[4,576,128]{2,1,0:T(8,128)(2,1)S(1)}, bf16[4,576,128]{2,1,0:T(8,128)(2,1)S(1)}, u32[]{:S(2)}, u32[]{:S(2)}) %collective-permute-start.14) | collective-permute-done | bytes 589856 | tf_op jit(solution)/shard_map/ppermute | solution.py:883
  57.3 1.5 collective-permute-start.20
  58.8 14.3 %attend.1 = (f32[1024,512]{1,0:T(8,128)}, bf16[1024,512]{1,0:T(8,128)(2,1)}, bf16[1024,512]{1,0:T(8,128)(2,1)}, bf16[1024,512]{1,0:T(8,128)(2,1)}, bf16[1024,512...) custom-call(s32[4]{0:T(128)S(1)} %pad_add_fusion.info_ref, ...), custom_call_target="tpu_custom_call" | custom-call | flops 5000000000 | bytes 14680064 | tf_op jit(solution)/shard_map/attend/pallas_call | solution.py:250
  73.9 1.6 collective-permute-done.22.refs_11_
  75.5 24.2 %feed.1 = (bf16[256,512]{1,0:T(8,128)(2,1)S(1)}, bf16[256,512]{1,0:T(8,128)(2,1)S(1)}, bf16[256,512]{1,0:T(8,128)(2,1)S(1)}, bf16[256,512]{1,0:T(8,128)(2,1)S(1)...) custom-call(s32[4]{0:T(128)} %copy-done.1, ...), custom_call_target="tpu_custom_call" | custom-call | flops 15000000512 | bytes 20971520 | tf_op jit(solution)/shard_map/feed/pallas_call | solution.py:482
  100.6 1.5 collective-permute-start.28
  105.0 19.1 %attend_back.1 = (bf16[256,512]{1,0:T(8,128)(2,1)S(1)}, bf16[256,512]{1,0:T(8,128)(2,1)S(1)}, bf16[256,512]{1,0:T(8,128)(2,1)S(1)}, bf16[256,512]{1,0:T(8,128)(2...) custom-call(s32[4]{0:T(128)S(1)} %copy-done.2, f32[1024,512]{1,0:T(8,128)} %get-tuple-element.202.lifted_ref, ...), custom_call_target="tpu_custom_call" | custom-call | flops 14000000000 | bytes 25165824 | tf_op jit(solution)/shard_map/attend_back/pallas_call | solution.py:676
  128.7 2.9 %settle_rows.1 = bf16[4,256,512]{2,1,0:T(8,128)(2,1)} custom-call(s32[4]{0:T(128)} %copy-done.1, bf16[256,512]{1,0:T(8,128)(2,1)} %copy-done, bf16[256,512]{1,0:T(8,128)(2,1)} %collective-permute-done.27.refs_1_, bf16[256,512]{1,0:T(8,128)(2,1)} %copy-done.7, bf16[256,512]{1,0:T(8,128)(2,1)} %copy-done.8), custom_call_target="tpu_custom_call" | custom-call | bytes 50331648 | tf_op jit(solution)/shard_map/settle_rows/pallas_call | solution.py:834
  131.6 1.6 collective-permute-done.35
  133.1 3.3 %collective-permute-done.34 = bf16[1536,128]{1,0:T(8,128)(2,1)S(1)} collective-permute-done((bf16[1536,128]{1,0:T(8,128)(2,1)S(1)}, bf16[1536,128]{1,0:T(8,128)(2,1)S(1)}, u32[]{:S(2)}, u32[]{:S(2)}) %collective-permute-start.34) | collective-permute-done | bytes 393248 | tf_op jit(solution)/shard_map/ppermute | solution.py:883
  137.5 2.7 %collective-permute-start.38 = (bf16[576,128]{1,0:T(8,128)(2,1)S(1)}, bf16[576,128]{1,0:T(8,128)(2,1)S(1)}, u32[]{:S(2)}, u32[]{:S(2)}) collective-permute-start(bf16[576,128]{1,0:T(8,128)(2,1)S(1)} %pad_maximum_fusion.3), channel_id=1, source_target_pairs={{0,16},{1,17},{2,18},{3,19},{4,20},{5,21},{6,22},{7,23},{8,24},{9,... | collective-permute-start | bytes 442376 | tf_op jit(solution)/shard_map/ppermute | solution.py:883
  144.2 2.5 %collective-permute-done.38.refs_7_ = bf16[576,128]{1,0:T(8,128)(2,1)S(1)} collective-permute-done((bf16[576,128]{1,0:T(8,128)(2,1)S(1)}, bf16[576,128]{1,0:T(8,128)(2,1)S(1)}, u32[]{:S(2)}, u32[]{:S(2)}) %collective-permute-start.38) | collective-permute-done | bytes 147488 | tf_op jit(solution)/shard_map/ppermute | solution.py:883
  146.7 3.0 %collective-permute-done.37.refs_6_ = bf16[576,128]{1,0:T(8,128)(2,1)S(1)} collective-permute-done((bf16[576,128]{1,0:T(8,128)(2,1)S(1)}, bf16[576,128]{1,0:T(8,128)(2,1)S(1)}, u32[]{:S(2)}, u32[]{:S(2)}) %collective-permute-start.37) | collective-permute-done | bytes 147488 | tf_op jit(solution)/shard_map/ppermute | solution.py:883
  150.7 6.1 %collective-permute-done.36.refs_5_ = bf16[576,128]{1,0:T(8,128)(2,1)S(1)} collective-permute-done((bf16[576,128]{1,0:T(8,128)(2,1)S(1)}, bf16[576,128]{1,0:T(8,128)(2,1)S(1)}, u32[]{:S(2)}, u32[]{:S(2)}) %collective-permute-start.36) | collective-permute-done | bytes 147488 | tf_op jit(solution)/shard_map/ppermute | solution.py:883
  159.5 3.3 %collective-permute-start.42 = (bf16[1,336,128]{2,1,0:T(8,128)(2,1)S(1)}, bf16[1,336,128]{2,1,0:T(8,128)(2,1)S(1)}, u32[]{:S(2)}, u32[]{:S(2)}) collective-permute-start(bf16[1,336,128]{2,1,0:T(8,128)(2,1)S(1)} %get-tuple-element.336), channel_id=1, source_target_pairs={{0,16},{1,17},{2,18},{3,19},{4,20},{5,21},{6,22},{7,23},{8,24},{9,... | collective-permute-start | bytes 258056 | tf_op jit(solution)/shard_map/ppermute | solution.py:883
  162.8 2.9 %collective-permute-done.40.refs_1_ = bf16[1,336,128]{2,1,0:T(8,128)(2,1)S(1)} collective-permute-done((bf16[1,336,128]{2,1,0:T(8,128)(2,1)S(1)}, bf16[1,336,128]{2,1,0:T(8,128)(2,1)S(1)}, u32[]{:S(2)}, u32[]{:S(2)}) %collective-permute-start.40) | collective-permute-done | bytes 86048 | tf_op jit(solution)/shard_map/ppermute | solution.py:883
  165.8 2.7 %collective-permute-done.41.refs_2_ = bf16[1,336,128]{2,1,0:T(8,128)(2,1)S(1)} collective-permute-done((bf16[1,336,128]{2,1,0:T(8,128)(2,1)S(1)}, bf16[1,336,128]{2,1,0:T(8,128)(2,1)S(1)}, u32[]{:S(2)}, u32[]{:S(2)}) %collective-permute-start.41) | collective-permute-done | bytes 86048 | tf_op jit(solution)/shard_map/ppermute | solution.py:883
  169.7 1.5 finish.1
  (119 shorter events, 27.2 us)
Async XLA Ops:
  3.5 9.7 %collective-permute-start.4 = (bf16[256,512]{1,0:T(8,128)(2,1)S(1)}, bf16[256,512]{1,0:T(8,128)(2,1)S(1)}, u32[]{:S(2)}, u32[]{:S(2)}) collective-permute-start(bf16[256,512]{1,0:T(8,128)(2,1)S(1)} %get-tuple-element.169), channel_id=1, source_target_pairs={{0,2},{1,3},{2,0},{3,1},{4,6},{5,7},{6,4},{7,5},{8,10},{9,11},{10,... | collective-permute-start | bytes 786440 | tf_op jit(solution)/shard_map/ppermute | solution.py:883
  6.1 12.3 %collective-permute-start.5 = (bf16[256,512]{1,0:T(8,128)(2,1)S(1)}, bf16[256,512]{1,0:T(8,128)(2,1)S(1)}, u32[]{:S(2)}, u32[]{:S(2)}) collective-permute-start(bf16[256,512]{1,0:T(8,128)(2,1)S(1)} %get-tuple-element.170), channel_id=1, source_target_pairs={{0,3},{1,2},{2,1},{3,0},{4,7},{5,6},{6,5},{7,4},{8,11},{9,10},{10,... | collective-permute-start | bytes 786440 | tf_op jit(solution)/shard_map/ppermute | solution.py:883
  6.1 12.2 %collective-permute-start.1 = (bf16[1,336,128]{2,1,0:T(8,128)(2,1)S(1)}, bf16[1,336,128]{2,1,0:T(8,128)(2,1)S(1)}, u32[]{:S(2)}, u32[]{:S(2)}) collective-permute-start(bf16[1,336,128]{2,1,0:T(8,128)(2,1)S(1)} %get-tuple-element.172), channel_id=1, source_target_pairs={{0,24},{1,25},{2,26},{3,27},{4,28},{5,29},{6,30},{7,31},{8,16},{9,... | collective-permute-start | bytes 258056 | tf_op jit(solution)/shard_map/ppermute | solution.py:883
  10.0 8.3 %collective-permute-start.2 = (bf16[1,336,128]{2,1,0:T(8,128)(2,1)S(1)}, bf16[1,336,128]{2,1,0:T(8,128)(2,1)S(1)}, u32[]{:S(2)}, u32[]{:S(2)}) collective-permute-start(bf16[1,336,128]{2,1,0:T(8,128)(2,1)S(1)} %get-tuple-element.172), channel_id=1, source_target_pairs={{0,8},{1,9},{2,10},{3,11},{4,12},{5,13},{6,14},{7,15},{8,0},{9,1},... | collective-permute-start | bytes 258056 | tf_op jit(solution)/shard_map/ppermute | solution.py:883
  20.1 16.1 %collective-permute-start.6 = (bf16[4,336,128]{2,1,0:T(8,128)(2,1)S(1)}, bf16[4,336,128]{2,1,0:T(8,128)(2,1)S(1)}, u32[]{:S(2)}, u32[]{:S(2)}) collective-permute-start(bf16[4,336,128]{2,1,0:T(8,128)(2,1)S(1)} %constant_dynamic-update-slice_fusion), channel_id=1, source_target_pairs={{0,2},{1,3},{2,0},{3,1},{4,6},{5,7},{6,4},{7,5},{8,10},{9,11},{10,... | collective-permute-start | bytes 1032200 | tf_op jit(solution)/shard_map/ppermute | solution.py:883
  21.7 17.1 %collective-permute-start.7 = (bf16[4,336,128]{2,1,0:T(8,128)(2,1)S(1)}, bf16[4,336,128]{2,1,0:T(8,128)(2,1)S(1)}, u32[]{:S(2)}, u32[]{:S(2)}) collective-permute-start(bf16[4,336,128]{2,1,0:T(8,128)(2,1)S(1)} %constant_dynamic-update-slice_fusion), channel_id=1, source_target_pairs={{0,4},{1,5},{2,6},{3,7},{4,0},{5,1},{6,2},{7,3},{8,12},{9,13},{10,... | collective-permute-start | bytes 1032200 | tf_op jit(solution)/shard_map/ppermute | solution.py:883
  23.2 15.5 %collective-permute-start.8 = (bf16[4,336,128]{2,1,0:T(8,128)(2,1)S(1)}, bf16[4,336,128]{2,1,0:T(8,128)(2,1)S(1)}, u32[]{:S(2)}, u32[]{:S(2)}) collective-permute-start(bf16[4,336,128]{2,1,0:T(8,128)(2,1)S(1)} %constant_dynamic-update-slice_fusion), channel_id=1, source_target_pairs={{0,6},{1,7},{2,4},{3,5},{4,2},{5,3},{6,0},{7,1},{8,14},{9,15},{10,... | collective-permute-start | bytes 1032200 | tf_op jit(solution)/shard_map/ppermute | solution.py:883
  23.7 12.5 %collective-permute-start.11 = (bf16[1,576,128]{2,1,0:T(8,128)(2,1)S(1)}, bf16[1,576,128]{2,1,0:T(8,128)(2,1)S(1)}, u32[]{:S(2)}, u32[]{:S(2)}) collective-permute-start(bf16[1,576,128]{2,1,0:T(8,128)(2,1)S(1)} %get-tuple-element.192), channel_id=1, source_target_pairs={{0,16},{1,17},{2,18},{3,19},{4,20},{5,21},{6,22},{7,23},{8,24},{9,... | collective-permute-start | bytes 442376 | tf_op jit(solution)/shard_map/ppermute | solution.py:883
  26.3 9.9 %collective-permute-start.9 = (bf16[1,576,128]{2,1,0:T(8,128)(2,1)S(1)}, bf16[1,576,128]{2,1,0:T(8,128)(2,1)S(1)}, u32[]{:S(2)}, u32[]{:S(2)}) collective-permute-start(bf16[1,576,128]{2,1,0:T(8,128)(2,1)S(1)} %get-tuple-element.192), channel_id=1, source_target_pairs={{0,24},{1,25},{2,26},{3,27},{4,28},{5,29},{6,30},{7,31},{8,16},{9,... | collective-permute-start | bytes 442376 | tf_op jit(solution)/shard_map/ppermute | solution.py:883
  39.0 17.0 %collective-permute-start.12 = (bf16[16,336,128]{2,1,0:T(8,128)(2,1)S(1)}, bf16[16,336,128]{2,1,0:T(8,128)(2,1)S(1)}, u32[]{:S(2)}, u32[]{:S(2)}) collective-permute-start(bf16[16,336,128]{2,1,0:T(8,128)(2,1)S(1)} %constant_dynamic-update-slice_fusion.4.refs_4_), channel_id=1, source_target_pairs={{0,1},{1,0},{2,3},{3,2},{4,5},{5,4},{6,7},{7,6},{8,9},{9,8},{10,11... | collective-permute-start | bytes 4128776 | tf_op jit(solution)/shard_map/ppermute | solution.py:883
  39.7 15.3 %collective-permute-start.14 = (bf16[4,576,128]{2,1,0:T(8,128)(2,1)S(1)}, bf16[4,576,128]{2,1,0:T(8,128)(2,1)S(1)}, u32[]{:S(2)}, u32[]{:S(2)}) collective-permute-start(bf16[4,576,128]{2,1,0:T(8,128)(2,1)S(1)} %constant_dynamic-update-slice_fusion.8.refs_4_), channel_id=1, source_target_pairs={{0,2},{1,3},{2,0},{3,1},{4,6},{5,7},{6,4},{7,5},{8,10},{9,11},{10,... | collective-permute-start | bytes 1769480 | tf_op jit(solution)/shard_map/ppermute | solution.py:883
  40.9 15.0 %collective-permute-start.15 = (bf16[4,576,128]{2,1,0:T(8,128)(2,1)S(1)}, bf16[4,576,128]{2,1,0:T(8,128)(2,1)S(1)}, u32[]{:S(2)}, u32[]{:S(2)}) collective-permute-start(bf16[4,576,128]{2,1,0:T(8,128)(2,1)S(1)} %constant_dynamic-update-slice_fusion.8.refs_4_), channel_id=1, source_target_pairs={{0,4},{1,5},{2,6},{3,7},{4,0},{5,1},{6,2},{7,3},{8,12},{9,13},{10,... | collective-permute-start | bytes 1769480 | tf_op jit(solution)/shard_map/ppermute | solution.py:883
  56.0 17.2 %collective-permute-start.17 = (bf16[4,576,128]{2,1,0:T(8,128)(2,1)S(1)}, bf16[4,576,128]{2,1,0:T(8,128)(2,1)S(1)}, u32[]{:S(2)}, u32[]{:S(2)}) collective-permute-start(bf16[4,576,128]{2,1,0:T(8,128)(2,1)S(1)} %collective-permute-done.14.refs_5_), channel_id=1, source_target_pairs={{0,4},{1,5},{2,6},{3,7},{4,0},{5,1},{6,2},{7,3},{8,12},{9,13},{10,... | collective-permute-start | bytes 1769480 | tf_op jit(solution)/shard_map/ppermute | solution.py:883
  56.8 16.3 %collective-permute-start.18 = (bf16[4,576,128]{2,1,0:T(8,128)(2,1)S(1)}, bf16[4,576,128]{2,1,0:T(8,128)(2,1)S(1)}, u32[]{:S(2)}, u32[]{:S(2)}) collective-permute-start(bf16[4,576,128]{2,1,0:T(8,128)(2,1)S(1)} %collective-permute-done.14.refs_5_), channel_id=1, source_target_pairs={{0,1},{1,0},{2,3},{3,2},{4,5},{5,4},{6,7},{7,6},{8,9},{9,8},{10,11... | collective-permute-start | bytes 1769480 | tf_op jit(solution)/shard_map/ppermute | solution.py:883
  56.8 16.4 %collective-permute-start.19 = (bf16[4,576,128]{2,1,0:T(8,128)(2,1)S(1)}, bf16[4,576,128]{2,1,0:T(8,128)(2,1)S(1)}, u32[]{:S(2)}, u32[]{:S(2)}) collective-permute-start(bf16[4,576,128]{2,1,0:T(8,128)(2,1)S(1)} %collective-permute-done.15.refs_6_), channel_id=1, source_target_pairs={{0,1},{1,0},{2,3},{3,2},{4,5},{5,4},{6,7},{7,6},{8,9},{9,8},{10,11... | collective-permute-start | bytes 1769480 | tf_op jit(solution)/shard_map/ppermute | solution.py:883
  57.3 15.8 %collective-permute-start.20 = (bf16[256,512]{1,0:T(8,128)(2,1)S(1)}, bf16[256,512]{1,0:T(8,128)(2,1)S(1)}, u32[]{:S(2)}, u32[]{:S(2)}) collective-permute-start(bf16[256,512]{1,0:T(8,128)(2,1)S(1)} %copy-done.10), channel_id=1, source_target_pairs={{0,2},{1,3},{2,0},{3,1},{4,6},{5,7},{6,4},{7,5},{8,10},{9,11},{10,... | collective-permute-start | bytes 786440 | tf_op jit(solution)/shard_map/ppermute | solution.py:883
  58.8 14.3 %collective-permute-start.21 = (bf16[256,512]{1,0:T(8,128)(2,1)S(1)}, bf16[256,512]{1,0:T(8,128)(2,1)S(1)}, u32[]{:S(2)}, u32[]{:S(2)}) collective-permute-start(bf16[256,512]{1,0:T(8,128)(2,1)S(1)} %copy-done.9), channel_id=1, source_target_pairs={{0,3},{1,2},{2,1},{3,0},{4,7},{5,6},{6,5},{7,4},{8,11},{9,10},{10,... | collective-permute-start | bytes 786440 | tf_op jit(solution)/shard_map/ppermute | solution.py:883
  100.1 24.0 %collective-permute-start.26 = (bf16[4608,128]{1,0:T(8,128)(2,1)S(1)}, bf16[4608,128]{1,0:T(8,128)(2,1)S(1)}, u32[]{:S(2)}, u32[]{:S(2)}) collective-permute-start(bf16[4608,128]{1,0:T(8,128)(2,1)S(1)} %get-tuple-element.227), channel_id=1, source_target_pairs={{0,1},{1,0},{2,3},{3,2},{4,5},{5,4},{6,7},{7,6},{8,9},{9,8},{10,11... | collective-permute-start | bytes 3538952 | tf_op jit(solution)/shard_map/ppermute | solution.py:883
  100.6 23.5 %collective-permute-start.28 = (bf16[256,512]{1,0:T(8,128)(2,1)S(1)}, bf16[256,512]{1,0:T(8,128)(2,1)S(1)}, u32[]{:S(2)}, u32[]{:S(2)}) collective-permute-start(bf16[256,512]{1,0:T(8,128)(2,1)S(1)} %get-tuple-element.230), channel_id=1, source_target_pairs={{0,2},{1,3},{2,0},{3,1},{4,6},{5,7},{6,4},{7,5},{8,10},{9,11},{10,... | collective-permute-start | bytes 786440 | tf_op jit(solution)/shard_map/ppermute | solution.py:883
  102.1 22.0 %collective-permute-start.29 = (bf16[256,512]{1,0:T(8,128)(2,1)S(1)}, bf16[256,512]{1,0:T(8,128)(2,1)S(1)}, u32[]{:S(2)}, u32[]{:S(2)}) collective-permute-start(bf16[256,512]{1,0:T(8,128)(2,1)S(1)} %get-tuple-element.231), channel_id=1, source_target_pairs={{0,3},{1,2},{2,1},{3,0},{4,7},{5,6},{6,5},{7,4},{8,11},{9,10},{10,... | collective-permute-start | bytes 786440 | tf_op jit(solution)/shard_map/ppermute | solution.py:883
  102.9 21.2 %collective-permute-start.24 = (bf16[3072,128]{1,0:T(8,128)(2,1)S(1)}, bf16[3072,128]{1,0:T(8,128)(2,1)S(1)}, u32[]{:S(2)}, u32[]{:S(2)}) collective-permute-start(bf16[3072,128]{1,0:T(8,128)(2,1)S(1)} %add_convert_fusion), channel_id=1, source_target_pairs={{0,4},{1,5},{2,6},{3,7},{4,0},{5,1},{6,2},{7,3},{8,12},{9,13},{10,... | collective-permute-start | bytes 2359304 | tf_op jit(solution)/shard_map/ppermute | solution.py:883
  104.2 19.9 %collective-permute-start.25 = (bf16[1536,128]{1,0:T(8,128)(2,1)S(1)}, bf16[1536,128]{1,0:T(8,128)(2,1)S(1)}, u32[]{:S(2)}, u32[]{:S(2)}) collective-permute-start(bf16[1536,128]{1,0:T(8,128)(2,1)S(1)} %add_convert_fusion.3), channel_id=1, source_target_pairs={{0,2},{1,3},{2,0},{3,1},{4,6},{5,7},{6,4},{7,5},{8,10},{9,11},{10,... | collective-permute-start | bytes 1179656 | tf_op jit(solution)/shard_map/ppermute | solution.py:883
  125.3 11.1 %collective-permute-start.34 = (bf16[1536,128]{1,0:T(8,128)(2,1)S(1)}, bf16[1536,128]{1,0:T(8,128)(2,1)S(1)}, u32[]{:S(2)}, u32[]{:S(2)}) collective-permute-start(bf16[1536,128]{1,0:T(8,128)(2,1)S(1)} %get-tuple-element.265), channel_id=1, source_target_pairs={{0,2},{1,3},{2,0},{3,1},{4,6},{5,7},{6,4},{7,5},{8,10},{9,11},{10,... | collective-permute-start | bytes 1179656 | tf_op jit(solution)/shard_map/ppermute | solution.py:883
  137.5 9.2 %collective-permute-start.38 = (bf16[576,128]{1,0:T(8,128)(2,1)S(1)}, bf16[576,128]{1,0:T(8,128)(2,1)S(1)}, u32[]{:S(2)}, u32[]{:S(2)}) collective-permute-start(bf16[576,128]{1,0:T(8,128)(2,1)S(1)} %pad_maximum_fusion.3), channel_id=1, source_target_pairs={{0,16},{1,17},{2,18},{3,19},{4,20},{5,21},{6,22},{7,23},{8,24},{9,... | collective-permute-start | bytes 442376 | tf_op jit(solution)/shard_map/ppermute | solution.py:883
  140.2 16.6 %collective-permute-start.31 = (bf16[4,336,128]{2,1,0:T(8,128)(2,1)S(1)}, bf16[4,336,128]{2,1,0:T(8,128)(2,1)S(1)}, u32[]{:S(2)}, u32[]{:S(2)}) collective-permute-start(bf16[4,336,128]{2,1,0:T(8,128)(2,1)S(1)} %copy-done.6), channel_id=1, source_target_pairs={{0,2},{1,3},{2,0},{3,1},{4,6},{5,7},{6,4},{7,5},{8,10},{9,11},{10,... | collective-permute-start | bytes 1032200 | tf_op jit(solution)/shard_map/ppermute | solution.py:883
  141.3 15.5 %collective-permute-start.32 = (bf16[4,336,128]{2,1,0:T(8,128)(2,1)S(1)}, bf16[4,336,128]{2,1,0:T(8,128)(2,1)S(1)}, u32[]{:S(2)}, u32[]{:S(2)}) collective-permute-start(bf16[4,336,128]{2,1,0:T(8,128)(2,1)S(1)} %copy-done.5), channel_id=1, source_target_pairs={{0,4},{1,5},{2,6},{3,7},{4,0},{5,1},{6,2},{7,3},{8,12},{9,13},{10,... | collective-permute-start | bytes 1032200 | tf_op jit(solution)/shard_map/ppermute | solution.py:883
  142.3 14.8 %collective-permute-start.33 = (bf16[4,336,128]{2,1,0:T(8,128)(2,1)S(1)}, bf16[4,336,128]{2,1,0:T(8,128)(2,1)S(1)}, u32[]{:S(2)}, u32[]{:S(2)}) collective-permute-start(bf16[4,336,128]{2,1,0:T(8,128)(2,1)S(1)} %get-tuple-element.263), channel_id=1, source_target_pairs={{0,6},{1,7},{2,4},{3,5},{4,2},{5,3},{6,0},{7,1},{8,14},{9,15},{10,... | collective-permute-start | bytes 1032200 | tf_op jit(solution)/shard_map/ppermute | solution.py:883
  146.7 10.1 %collective-permute-start.39 = (bf16[256,512]{1,0:T(8,128)(2,1)S(1)}, bf16[256,512]{1,0:T(8,128)(2,1)S(1)}, u32[]{:S(2)}, u32[]{:S(2)}) collective-permute-start(bf16[256,512]{1,0:T(8,128)(2,1)S(1)} %get-tuple-element.276), channel_id=1, source_target_pairs={{0,1},{1,0},{2,3},{3,2},{4,5},{5,4},{6,7},{7,6},{8,9},{9,8},{10,11... | collective-permute-start | bytes 786440 | tf_op jit(solution)/shard_map/ppermute | solution.py:883
  157.1 11.4 %collective-permute-start.43 = (bf16[256,512]{1,0:T(8,128)(2,1)S(1)}, bf16[256,512]{1,0:T(8,128)(2,1)S(1)}, u32[]{:S(2)}, u32[]{:S(2)}) collective-permute-start(bf16[256,512]{1,0:T(8,128)(2,1)S(1)} %get-tuple-element.286), channel_id=1, source_target_pairs={{0,2},{1,3},{2,0},{3,1},{4,6},{5,7},{6,4},{7,5},{8,10},{9,11},{10,... | collective-permute-start | bytes 786440 | tf_op jit(solution)/shard_map/ppermute | solution.py:883
  158.2 10.3 %collective-permute-start.44 = (bf16[256,512]{1,0:T(8,128)(2,1)S(1)}, bf16[256,512]{1,0:T(8,128)(2,1)S(1)}, u32[]{:S(2)}, u32[]{:S(2)}) collective-permute-start(bf16[256,512]{1,0:T(8,128)(2,1)S(1)} %get-tuple-element.287), channel_id=1, source_target_pairs={{0,3},{1,2},{2,1},{3,0},{4,7},{5,6},{6,5},{7,4},{8,11},{9,10},{10,... | collective-permute-start | bytes 786440 | tf_op jit(solution)/shard_map/ppermute | solution.py:883
  159.4 9.1 %collective-permute-start.41 = (bf16[1,336,128]{2,1,0:T(8,128)(2,1)S(1)}, bf16[1,336,128]{2,1,0:T(8,128)(2,1)S(1)}, u32[]{:S(2)}, u32[]{:S(2)}) collective-permute-start(bf16[1,336,128]{2,1,0:T(8,128)(2,1)S(1)} %get-tuple-element.337), channel_id=1, source_target_pairs={{0,8},{1,9},{2,10},{3,11},{4,12},{5,13},{6,14},{7,15},{8,0},{9,1},... | collective-permute-start | bytes 258056 | tf_op jit(solution)/shard_map/ppermute | solution.py:883
  159.5 8.9 %collective-permute-start.42 = (bf16[1,336,128]{2,1,0:T(8,128)(2,1)S(1)}, bf16[1,336,128]{2,1,0:T(8,128)(2,1)S(1)}, u32[]{:S(2)}, u32[]{:S(2)}) collective-permute-start(bf16[1,336,128]{2,1,0:T(8,128)(2,1)S(1)} %get-tuple-element.336), channel_id=1, source_target_pairs={{0,16},{1,17},{2,18},{3,19},{4,20},{5,21},{6,22},{7,23},{8,24},{9,... | collective-permute-start | bytes 258056 | tf_op jit(solution)/shard_map/ppermute | solution.py:883
  (26 other events, 225.3 us)
